TPU v7x, 32 devices: a whole 2x2x4 slice. The times are simulated.
32 devices in a mesh: row: 8 (over z, core), col: 4 (over y, x).
Axes of the slice: x: 2, y: 2, z: 4, core: 2. Of those that a mesh axis runs over, the one named last changes fastest.
Arguments:
- vectors: float32 [12288, 128], P(('row', 'col')), may hold values from -6 to 6
- energies: float32 [12288], P(('row', 'col')), may hold values from 1 to 3
- intersections: bfloat16 [96, 512, 128], P(('row', 'col')), may hold values from -0.25 to 0.25
- coarse: bfloat16 [8, 8, 512, 512], P('col', 'row'), may hold values from -0.15625 to 0.15625
- fine_coarse: int32 [96], replicated, may hold values from 0 to 7, as said below
- coarse_slot: int32 [8], replicated, may hold values from 0 to 7, each once
- tile_codes: int32 [32, 96], P(('row', 'col')), may hold values from 0 to 287, as said below
- tile_count: int32 [32], P(('row', 'col')), may hold values from 12 to 96, as said below
Outputs:
- first_step: float32 [12288, 128], P(('row', 'col'))
- second_step: float32 [12288, 128], P(('row', 'col'))
Inputs may be any that keep to these rules, and one draw needn't show every extreme that they name: `fine_coarse`: fine block k lies on device d = k // 3; with c = d % (4) its coarse k-point lies in c * 2 to (c + 1) * 2 - 1. `coarse_slot`: each coarse k-point has its own position. `tile_codes`: each row lists distinct codes; a code e stands for output position e // (C 3) and input position e % (C 3) of the device's lists, with C = 4. Only the first tile_count[d] codes of row d are used; some device uses all 96.
All inputs are finite; a program needn't handle non-finite values.
Results may differ from a plain program's by a relative error of at most 0.0044.
Values may be sent and summed in bfloat16 or wider, within the bound.
No kernel may reach another device: no remote copies, remote signals or barrier semaphores. Data moves between devices by JAX's collectives and lax.ppermute only.
A program may use at most 128 MiB of HBM per device.

v0:
```python
import jax
import jax.numpy as jnp
from jax import lax
from jax.sharding import PartitionSpec as P

spectrum_center = 2.0
spectrum_half = 3.0
tile_batch = 16


def lookup(values_table, positions):
    matches = positions[:, None] == jnp.arange(values_table.shape[0], dtype=jnp.int32)[None, :]
    return jnp.sum(jnp.where(matches, values_table[None, :], 0), axis=1)


def on_device(
    vectors, energies, intersections, coarse, fine_coarse, coarse_slot, tile_codes, tile_count
):
    rows_count = lax.axis_size("row")
    cols_count = lax.axis_size("col")
    row_id = lax.axis_index("row")
    col_id = lax.axis_index("col")
    blocks_dev = intersections.shape[0]
    pairs_coarse = intersections.shape[1]
    tile_side = intersections.shape[2]
    width_vec = vectors.shape[1]
    points_col = coarse.shape[0]
    spread = cols_count * blocks_dev
    depth_out = rows_count * blocks_dev
    index_out = jnp.arange(depth_out, dtype=jnp.int32)
    index_in = jnp.arange(spread, dtype=jnp.int32)
    out_blocks = (
        index_out // blocks_dev * cols_count + col_id
    ) * blocks_dev + index_out % blocks_dev
    in_blocks = (row_id * cols_count + index_in // blocks_dev) * blocks_dev + index_in % blocks_dev
    over_out = lax.all_gather(intersections, "row", axis=0, tiled=True)
    over_in = lax.all_gather(intersections, "col", axis=0, tiled=True)
    in_slots = lookup(coarse_slot, lookup(fine_coarse, in_blocks))
    coarse_strip = lax.all_gather(coarse, "row", axis=1, tiled=True)
    picked = jnp.take(coarse_strip, in_slots, axis=1)
    projected = jnp.einsum(
        "aicd,idt->iact", picked, over_in, preferred_element_type=jnp.float32
    ).astype(jnp.bfloat16)
    projected_flat = projected.reshape(spread * points_col, pairs_coarse, tile_side)
    out_points = lookup(fine_coarse, out_blocks) - col_id * points_col
    tile_total = tile_count[0]
    slot_ids = jnp.arange(tile_codes.shape[1], dtype=jnp.int32)
    sort_keys = jnp.where(slot_ids < tile_total, tile_codes[0], depth_out * spread + slot_ids)
    ordering = jnp.argsort(sort_keys, stable=True)
    tile_list = jnp.take(tile_codes[0], ordering, axis=0)
    sorted_out = jnp.where(slot_ids < tile_total, tile_list // spread, depth_out)
    groups = (tile_total + tile_batch - 1) // tile_batch

    def make_tiles(offset):
        part_codes = lax.dynamic_slice_in_dim(tile_list, offset, tile_batch)
        out_idx = part_codes // spread
        in_idx = part_codes % spread
        local_point = lookup(out_points, out_idx)
        left_over = jnp.take(over_out, out_idx, axis=0)
        right_sel = jnp.take(projected_flat, in_idx * points_col + local_point, axis=0)
        fresh_tiles = jnp.einsum(
            "kct,kcu->ktu", left_over, right_sel, preferred_element_type=jnp.float32
        ).astype(jnp.bfloat16)
        live_mask = offset + jnp.arange(tile_batch, dtype=jnp.int32) < tile_total
        return (
            jnp.where(live_mask[:, None, None], fresh_tiles, jnp.zeros_like(fresh_tiles)),
            out_idx,
            in_idx,
        )

    def fill_group(group, buffer):
        fresh_tiles = make_tiles(group * tile_batch)[0]
        return lax.dynamic_update_slice_in_dim(buffer, fresh_tiles, group * tile_batch, 0)

    stored = lax.fori_loop(
        0, groups, fill_group, jnp.zeros((tile_list.shape[0], tile_side, tile_side), jnp.bfloat16)
    )

    def partial_range(pieces, start, count):
        first_tile = jnp.sum((sorted_out < start).astype(jnp.int32))
        last_tile = jnp.sum((sorted_out < start + count).astype(jnp.int32))
        first_group = first_tile // tile_batch
        last_group = (last_tile + tile_batch - 1) // tile_batch

        def add_group(group, partial_value):
            offset = group * tile_batch
            fresh_tiles = lax.dynamic_slice_in_dim(stored, offset, tile_batch)
            part_codes = lax.dynamic_slice_in_dim(tile_list, offset, tile_batch)
            out_idx = part_codes // spread
            in_idx = part_codes % spread
            inputs = jnp.take(pieces, in_idx, axis=0)
            product = jnp.einsum(
                "ktu,kun->ktn", fresh_tiles, inputs, preferred_element_type=jnp.float32
            )
            local_out = out_idx - start
            inside = (local_out >= 0) & (local_out < count)
            product = jnp.where(inside[:, None, None], product, jnp.zeros_like(product))
            return partial_value.at[jnp.clip(local_out, 0, count - 1)].add(product)

        return lax.fori_loop(
            first_group,
            last_group,
            add_group,
            jnp.zeros((count, tile_side, width_vec), jnp.float32),
        )

    def apply_kernel(field):
        pieces = lax.all_gather(field.astype(jnp.bfloat16), "col", axis=0, tiled=True)
        partial_value = partial_range(pieces, 0, depth_out)
        return lax.psum_scatter(partial_value, "row", scatter_dimension=0, tiled=True)

    start_vec = vectors.reshape(blocks_dev, tile_side, width_vec)
    pair_energy = energies.reshape(blocks_dev, tile_side, 1)

    def apply_shifted(field):
        return (pair_energy * field + apply_kernel(field) - spectrum_center * field) / spectrum_half

    first_step = apply_shifted(start_vec)
    second_step = 2.0 * apply_shifted(first_step) - start_vec
    return (
        first_step.reshape(blocks_dev * tile_side, width_vec),
        second_step.reshape(blocks_dev * tile_side, width_vec),
    )


def solution(mesh):
    in_specs = (
        P(("row", "col"), None),
        P(("row", "col")),
        P(("row", "col"), None, None),
        P("col", "row", None, None),
        P(),
        P(),
        P(("row", "col"), None),
        P(("row", "col")),
    )
    out_specs = (P(("row", "col"), None), P(("row", "col"), None))
    return jax.shard_map(
        on_device, mesh=mesh, in_specs=in_specs, out_specs=out_specs, check_vma=False
    )
```

profile of v0, /device:TPU:0, one launch (start us, length us, event | category | flops | bytes accessed | tf_op | source)
XLA Modules:
  0.0 366.0 jit_solution(11626295354753943800)
XLA Ops:
  7.3 0.7 all-gather.6.cloned.1.call-update
  8.0 0.7 all-gather.8.cloned.1.call-update
  8.7 0.7 all-gather.4.cloned.1.call-update
  10.8 2.5 sort.17
  13.4 1.2 gather_fusion.4
  18.6 11.0 %all_gather.18 = bf16[12,128,128]{2,1,0:T(8,128)(2,1)S(1)} all-gather(bf16[3,128,128]{2,1,0:T(8,128)(2,1)S(1)} %convert_element_type.26), channel_id=1, replica_groups=mesh['row'=8,'col'=4] {'col'}, dimensions={0}, use_global_device_ids=true | all-gather | bytes 491520 | tf_op jit(solution)/shard_map/all_gather | solution.py:108
  30.1 64.4 %all-gather.6.cloned.1.call-done = bf16[2,8,512,512]{3,2,1,0:T(8,128)(2,1)} async-done(((bf16[2,1,512,512]{3,2,1,0:T(8,128)(2,1)}), bf16[2,8,512,512]{3,2,1,0:T(8,128)(2,1)}) %all-gather.6.cloned.1.call-update) | async-done | bytes 8388624 | tf_op jit(solution)/shard_map/all_gather | solution.py:39
  94.5 9.4 %gather_fusion.5 = bf16[12,2,512,512]{3,2,1,0:T(8,128)(2,1)} fusion(bf16[2,8,512,512]{3,2,1,0:T(8,128)(2,1)} %all-gather.6.cloned.1.call-done, s32[1024]{0:T(1024)S(1)} %pad_clamp_fusion.4), kind=kCustom, calls=%fused_computation.5 | custom fusion | bytes 25165872 | tf_op jit(solution)/shard_map/jit(_take)/gather | solution.py:40
  103.9 21.9 %all-gather.8.cloned.1.call-done = bf16[12,512,128]{2,1,0:T(8,128)(2,1)} async-done(((bf16[3,512,128]{2,1,0:T(8,128)(2,1)}), bf16[12,512,128]{2,1,0:T(8,128)(2,1)}) %all-gather.8.cloned.1.call-update) | async-done | bytes 1572880 | tf_op jit(solution)/shard_map/all_gather | solution.py:37
  125.8 10.1 %fusion.41 = bf16[12,2,512,128]{3,2,1,0:T(8,128)(2,1)} fusion(bf16[12,2,512,512]{3,2,1,0:T(8,128)(2,1)} %gather_fusion.5, pred[12]{0:T(512)(128)(4,1)S(1)} %compare_and_fusion.6, bf16[12,512,128]{2,1,0:T(8,128)(2,1)} %all-gather.8.cloned.1.call-done), kind=kOutput, calls=%fused_computation.64 | convolution fusion | flops 1618477056 | bytes 17301516 | tf_op jit(solution)/shard_map/aicd,idt->iact/dot_general | solution.py:41
  136.0 29.8 %all-gather.4.cloned.1.call-done = bf16[24,512,128]{2,1,0:T(8,128)(2,1)} async-done(((bf16[3,512,128]{2,1,0:T(8,128)(2,1)}), bf16[24,512,128]{2,1,0:T(8,128)(2,1)}) %all-gather.4.cloned.1.call-update) | async-done | bytes 3145744 | tf_op jit(solution)/shard_map/all_gather | solution.py:36
  165.8 2.4 broadcast_in_dim.158
  168.2 33.7 %while.36 = (s32[]{:T(128)}, bf16[96,128,128]{2,1,0:T(8,128)(2,1)}, s32[]{:T(128)}, s32[]{:T(128)}, s32[96]{0:T(128)S(1)}, /*index=5*/bf16[24,512,128]{2,1,0:T(8...) while((s32[]{:T(128)}, bf16[96,128,128]{2,1,0:T(8,128)(2,1)}, ...), condition=%wide.region_8.10_spmd, body=%wide.region_6.9_spmd.sunk | while | flops 271060608 | bytes 13116599 | solution.py:75
  168.5 0.7 compare_and_fusion.12
  169.3 2.8 gather_fusion
  172.1 4.0 %gather_fusion.1 = bf16[16,512,128]{2,1,0:T(8,128)(2,1)} fusion(bf16[24,512,128]{2,1,0:T(8,128)(2,1)} %get-tuple-element.526, s32[1024]{0:T(1024)S(1)} %pad_clamp_fusion.11), kind=kCustom, calls=%fused_computation.clone.clone.1 | custom fusion | bytes 4194368 | tf_op jit(solution)/shard_map/while/body/jit(_take)/gather | solution.py:59
  176.1 3.3 fusion.68
  179.7 0.7 compare_and_fusion.12
  180.5 2.8 gather_fusion
  183.3 4.0 %gather_fusion.1 = bf16[16,512,128]{2,1,0:T(8,128)(2,1)} fusion(bf16[24,512,128]{2,1,0:T(8,128)(2,1)} %get-tuple-element.526, s32[1024]{0:T(1024)S(1)} %pad_clamp_fusion.11), kind=kCustom, calls=%fused_computation.clone.clone.1 | custom fusion | bytes 4194368 | tf_op jit(solution)/shard_map/while/body/jit(_take)/gather | solution.py:59
  187.4 3.3 fusion.68
  191.0 0.7 compare_and_fusion.12
  191.7 2.8 gather_fusion
  194.6 4.0 %gather_fusion.1 = bf16[16,512,128]{2,1,0:T(8,128)(2,1)} fusion(bf16[24,512,128]{2,1,0:T(8,128)(2,1)} %get-tuple-element.526, s32[1024]{0:T(1024)S(1)} %pad_clamp_fusion.11), kind=kCustom, calls=%fused_computation.clone.clone.1 | custom fusion | bytes 4194368 | tf_op jit(solution)/shard_map/while/body/jit(_take)/gather | solution.py:59
  198.6 3.3 fusion.68
  202.1 13.2 %while.37 = (s32[]{:T(128)}, f32[24,128,128]{2,1,0:T(8,128)S(1)}, s32[]{:T(128)}, s32[96]{0:T(128)S(1)}, bf16[96,128,128]{2,1,0:T(8,128)(2,1)}, /*index=5*/bf16[...) while((s32[]{:T(128)}, f32[24,128,128]{2,1,0:T(8,128)S(1)}, s32[]{:T(128)}, ...), condition=%wide.region_11.14_spmd, body=%wide.region_9.13_spmd.sunk | while | flops 67896728 | bytes 6296567 | solution.py:100
  203.4 1.4 convolution_select_fusion.4
  204.9 1.6 scatter_fusion
  207.8 1.4 convolution_select_fusion.4
  209.3 1.6 scatter_fusion
  212.2 1.4 convolution_select_fusion.4
  213.6 1.6 scatter_fusion
  215.3 1.1 copy-done.2
  216.5 77.3 %reduce-scatter.3.cloned.1.call-done = f32[3,128,128]{2,1,0:T(8,128)} async-done(((f32[24,128,128]{2,1,0:T(8,128)}), f32[3,128,128]{2,1,0:T(8,128)}) %reduce-scatter.3.cloned.1.call-update) | async-done | bytes 196624 | tf_op jit(solution)/shard_map/reduce_scatter | solution.py:110
  293.8 1.8 fusion.57
  295.6 9.2 %all_gather.19 = bf16[12,128,128]{2,1,0:T(8,128)(2,1)S(1)} all-gather(bf16[3,128,128]{2,1,0:T(8,128)(2,1)S(1)} %get-tuple-element.336), channel_id=1, replica_groups=mesh['row'=8,'col'=4] {'col'}, dimensions={0}, use_global_device_ids=true | all-gather | bytes 491520 | tf_op jit(solution)/shard_map/all_gather | solution.py:108
  304.9 13.3 %while.38 = (s32[]{:T(128)}, f32[24,128,128]{2,1,0:T(8,128)S(1)}, s32[]{:T(128)}, s32[96]{0:T(128)S(1)}, bf16[96,128,128]{2,1,0:T(8,128)(2,1)}, /*index=5*/bf16[...) while((s32[]{:T(128)}, f32[24,128,128]{2,1,0:T(8,128)S(1)}, s32[]{:T(128)}, ...), condition=%wide.region_15.18_spmd, body=%wide.region_13.17_spmd.sunk | while | flops 67896728 | bytes 6296567 | solution.py:100
  305.0 0.7 compare_and_fusion.14
  306.3 1.4 convolution_select_fusion.5
  307.8 1.6 scatter_fusion.1
  309.4 0.7 compare_and_fusion.14
  310.7 1.4 convolution_select_fusion.5
  312.2 1.6 scatter_fusion.1
  315.2 1.4 convolution_select_fusion.5
  316.6 1.6 scatter_fusion.1
  318.3 1.1 copy-done.1
  319.4 38.0 %reduce-scatter.5.cloned.1.call-done = f32[3,128,128]{2,1,0:T(8,128)} async-done(((f32[24,128,128]{2,1,0:T(8,128)}), f32[3,128,128]{2,1,0:T(8,128)}) %reduce-scatter.5.cloned.1.call-update) | async-done | bytes 196624 | tf_op jit(solution)/shard_map/reduce_scatter | solution.py:110
  357.5 2.0 multiply_subtract_fusion
  (87 shorter events, 9.8 us)
Async XLA Ops:
  7.2 6.2 %copy-start = (s32[1,96]{1,0:T(1,128)S(1)}, s32[1,96]{1,0:T(1,128)}, u32[]{:S(2)}) copy-start(s32[1,96]{1,0:T(1,128)} %param.24) | copy-start | bytes 1156
  7.2 11.4 %copy-start.3 = (f32[384,128]{1,0:T(8,128)S(1)}, f32[384,128]{1,0:T(8,128)}, u32[]{:S(2)}) copy-start(f32[384,128]{1,0:T(8,128)} %param.18) | copy-start | bytes 589828
  7.2 22.4 %copy-start.8 = (s32[96]{0:T(128)S(1)}, s32[96]{0:T(128)}, u32[]{:S(2)}) copy-start(s32[96]{0:T(128)} %param.22) | copy-start | bytes 1156
  7.2 22.6 %copy-start.7 = (s32[8]{0:T(128)S(1)}, s32[8]{0:T(128)}, u32[]{:S(2)}) copy-start(s32[8]{0:T(128)} %param.23) | copy-start | bytes 100
  7.2 87.3 %all-gather.6.cloned.1.call-start = ((), (), s32[]{:S(2)}) async-start(), calls=%async_computation.3 | async-start | bytes 9437184 | tf_op jit(solution)/shard_map/all_gather | solution.py:39
  7.9 117.9 %all-gather.8.cloned.1.call-start = ((), (), s32[]{:S(2)}) async-start(), calls=%async_computation.4 | async-start | bytes 1966080 | tf_op jit(solution)/shard_map/all_gather | solution.py:37
  8.7 157.1 %all-gather.4.cloned.1.call-start = ((), (), s32[]{:S(2)}) async-start(), calls=%async_computation.2 | async-start | bytes 3538944 | tf_op jit(solution)/shard_map/all_gather | solution.py:36
  9.4 284.3 %reduce-scatter.3.cloned.1.call-start = ((), (), s32[]{:S(2)}) async-start(), calls=%async_computation.5 | async-start | bytes 1769472 | tf_op jit(solution)/shard_map/reduce_scatter | solution.py:110
  202.1 91.7 %copy-start.4 = (f32[384]{0:T(512)S(1)}, f32[384]{0:T(512)}, u32[]{:S(2)}) copy-start(f32[384]{0:T(512)} %param.19) | copy-start | bytes 4612
  203.4 1.4 copy-start.5
  207.8 1.4 copy-start.5
  212.2 1.4 copy-start.5
  215.3 1.2 copy-start.2
  216.4 141.0 %reduce-scatter.5.cloned.1.call-start = ((), (), s32[]{:S(2)}) async-start(), calls=%async_computation.6 | async-start | bytes 1769472 | tf_op jit(solution)/shard_map/reduce_scatter | solution.py:110
  306.3 1.4 copy-start.6
  310.7 1.4 copy-start.6
  315.2 1.4 copy-start.6
  318.3 1.2 copy-start.1
Sparse Core Ops, SparseCore 0:
  9.6 84.7 all-gather.5
  96.3 29.4 all-gather.7
  127.5 38.2 all-gather.3
  216.6 77.1 reduce-scatter.2
  319.6 37.8 reduce-scatter.4
where the time goes:
time: 372 us; the launch traced here: 366 us
  waiting for transfers between devices  233 us (63%)
  local copies, waits for them, and re-layouts  40.2 us (11%)
  matrix products  28.6 us (8%)
  other arithmetic  24.9 us (7%)
  blocking collectives  20.2 us (5%)
  between operations  17.9 us (5%)
    reduce_scatter x2, waiting for transfers between devices, apply_kernel(): lax.psum_scatter(partial_value, 'row', scatter_dimension=0, tiled=True)  115 us
    all_gather x1, waiting for transfers between devices, on_device(): coarse_strip = lax.all_gather(coarse, 'row', axis=1, tiled=True)  64.4 us
    all_gather x1, waiting for transfers between devices, on_device(): over_out = lax.all_gather(intersections, 'row', axis=0, tiled=True)  29.8 us
    all_gather x1, waiting for transfers between devices, on_device(): over_in = lax.all_gather(intersections, 'col', axis=0, tiled=True)  21.9 us
    all_gather x2, blocking collectives, apply_kernel(): lax.all_gather(field.astype(jnp.bfloat16), 'col', axis=0, tiled=True)  20.2 us
    gather x3, local copies, waits for them, and re-layouts, make_tiles(): left_over = jnp.take(over_out, out_idx, axis=0)  12 us
    dot_general x1, matrix products, on_device(): jnp.einsum('aicd,idt->iact', picked, over_in, preferred_element_type=jnp....  10.1 us
    dot_general x3, matrix products, make_tiles(): jnp.einsum('kct,kcu->ktu', left_over, right_sel, preferred_element_type=j...  9.99 us
  transfers between devices with their start and end apart: 5, of which 5 were waited for; matrix products, arithmetic and copies ran while one was open for 7% of the time, Pallas kernels for 0%

commit v1 on v0

v1 whole, which is shorter than its diff:
```python
import functools

import jax
import jax.numpy as jnp
from jax import lax
from jax.experimental import pallas as pl
from jax.experimental.pallas import tpu as pltpu
from jax.sharding import PartitionSpec as P

spectrum_center = 2.0
spectrum_half = 3.0
axes = ("row", "col")
chunk_groups = 8
mib = 1 << 20


class Layout:
    def __init__(self, rows, cols, blocks, pairs, side, width, points, slots_dev, tile_max, unroll):
        self.rows, self.cols, self.blocks = rows, cols, blocks
        self.pairs, self.side, self.width = pairs, side, width
        self.points, self.slots_dev, self.tile_max = points, slots_dev, tile_max
        self.places = rows // 2
        self.near = max(self.places // 2, 1)
        self.owners = 2 if self.places > 1 else 1
        self.spread = cols * blocks
        self.inputs = self.owners * self.spread
        self.outputs = rows * blocks
        self.slots = 2 * self.near * slots_dev
        self.unroll = unroll
        most = self.owners * tile_max + self.inputs * (unroll - 1)
        self.groups = -(-most // (unroll * chunk_groups)) * chunk_groups


def plan_kernel(lay, ids, codes, counts, fine, stored, group_start, slot_of, entries, fill):
    place, core, col = ids[0], ids[1], ids[2]
    half = lax.div(place, lay.near)

    def clear(p, carry):
        owner = lax.div(p, lay.spread)
        rest = lax.rem(p, lay.spread)
        from_col = lax.bitwise_xor(lax.div(rest, lay.blocks), col)
        from_place = lax.bitwise_xor(place, owner * lay.near)
        block = ((from_place * 2 + core) * lay.cols + from_col) * lay.blocks + lax.rem(rest, lay.blocks)
        position = stored[fine[block]]
        at_row = lax.div(position, lay.slots_dev)
        at_place, at_core = lax.div(at_row, 2), lax.rem(at_row, 2)
        slot = (lax.bitwise_xor(at_place, place) * 2 + lax.bitwise_xor(at_core, core)) * lay.slots_dev
        slot = slot + lax.rem(position, lay.slots_dev)
        slot_of[p] = jnp.where(lax.div(at_place, lay.near) == half, slot, -1)
        fill[p] = 0
        return carry

    lax.fori_loop(0, lay.inputs, clear, 0)

    def input_of(owner, code):
        j = lax.rem(code, lay.spread)
        from_col = lax.bitwise_xor(lax.div(j, lay.blocks), col)
        return owner * lay.spread + from_col * lay.blocks + lax.rem(j, lay.blocks)

    for owner in range(lay.owners):

        def count(i, carry):
            p = input_of(owner, codes[owner, i])
            fill[p] = fill[p] + 1
            return carry

        lax.fori_loop(0, counts[owner], count, 0)

    def place_groups(p, start):
        group_start[p] = start
        used = jnp.where(slot_of[p] >= 0, fill[p], 0)
        fill[p] = start * lay.unroll
        return start + lax.div(used + (lay.unroll - 1), lay.unroll)

    total = lax.fori_loop(0, lay.inputs, place_groups, 0)
    group_start[lay.inputs] = total

    def blank(i, carry):
        entries[i] = lay.outputs * lay.points
        return carry

    lax.fori_loop(0, total * lay.unroll, blank, 0)

    for owner in range(lay.owners):

        def put(i, carry):
            code = codes[owner, i]
            p = input_of(owner, code)

            @pl.when(slot_of[p] >= 0)
            def _():
                out = lax.div(code, lay.spread)
                at_row = lax.div(out, lay.blocks)
                within = lax.rem(out, lay.blocks)
                far = lax.bitwise_xor(lax.div(at_row, 2), place)
                other = lax.bitwise_xor(lax.rem(at_row, 2), core)
                q = (other * lay.places + far) * lay.blocks + within
                a = fine[(at_row * lay.cols + col) * lay.blocks + within] - col * lay.points
                spot = fill[p]
                entries[spot] = q * lay.points + a
                fill[p] = spot + 1

            return carry

        lax.fori_loop(0, counts[owner], put, 0)


def make_plan(lay, ids, codes, counts, fine, stored):
    smem = pl.BlockSpec(memory_space=pltpu.SMEM)
    return pl.pallas_call(
        functools.partial(plan_kernel, lay),
        out_shape=(
            jax.ShapeDtypeStruct((lay.inputs + 1,), jnp.int32),
            jax.ShapeDtypeStruct((lay.inputs,), jnp.int32),
            jax.ShapeDtypeStruct((lay.groups * lay.unroll,), jnp.int32),
        ),
        in_specs=[smem] * 5,
        out_specs=(smem,) * 3,
        scratch_shapes=[pltpu.SMEM((lay.inputs,), jnp.int32)],
    )(ids, codes, counts, fine, stored)


def add_products(lay, group, entries, tiles, rounded_block, total):
    products = [
        jnp.dot(tiles[i], rounded_block, preferred_element_type=jnp.float32) for i in range(lay.unroll)
    ]
    for i in range(lay.unroll):
        q = lax.div(entries[group * lay.unroll + i], lay.points)
        total[q] = total[q] + products[i]


def tiles_kernel(lay, group_start, slot_of, entries, *refs):
    n_in = lay.owners * lay.cols
    n_out = 2 * lay.places
    n_coarse = 2 * lay.near
    refs = list(refs)
    given_in = [refs.pop(0) for _ in range(n_in)]
    given_out = [refs.pop(0) for _ in range(n_out)]
    given_coarse = [refs.pop(0) for _ in range(n_coarse)]
    given_vec = [refs.pop(0) for _ in range(lay.cols)]
    own_sum, other_sum, tiles_out = refs[:3]
    right, left, blocks, rounded, tiles, projected, total, sems, out_sems = refs[3:]
    copies = []

    def fetch(source, target):
        copies.append(pltpu.make_async_copy(source, target, sems.at[len(copies)]))
        copies[-1].start()

    for i in range(n_coarse):
        for a in range(lay.points):
            fetch(given_coarse[i].at[a], blocks.at[a, pl.ds(i * lay.slots_dev, lay.slots_dev)])
    for i in range(n_in):
        fetch(given_in[i], right.at[pl.ds(i * lay.blocks, lay.blocks)])
    for d in range(lay.cols):
        for g in range(lay.owners):
            fetch(given_vec[d].at[g], rounded.at[pl.ds((g * lay.cols + d) * lay.blocks, lay.blocks)])
    for i in range(n_out):
        fetch(given_out[i], left.at[pl.ds(i * lay.blocks, lay.blocks)])
    total[...] = jnp.zeros_like(total)
    for copy in copies:
        copy.wait()

    def visit(p, carry):
        first, last = group_start[p], group_start[p + 1]

        @pl.when(last > first)
        def _():
            slot = slot_of[p]
            for a in range(lay.points):
                projected[:, a * lay.side : (a + 1) * lay.side] = jnp.dot(
                    blocks[a, slot], right[p], preferred_element_type=jnp.float32
                ).astype(jnp.bfloat16)

            def group_step(group, inner):
                fresh = []
                for i in range(lay.unroll):
                    entry = entries[group * lay.unroll + i]
                    q = jnp.minimum(lax.div(entry, lay.points), lay.outputs - 1)
                    a = lax.rem(entry, lay.points)
                    both = jnp.dot(left[q], projected[...], preferred_element_type=jnp.float32)
                    tile = both[:, : lay.side]
                    for b in range(1, lay.points):
                        tile = jnp.where(a == b, both[:, b * lay.side : (b + 1) * lay.side], tile)
                    fresh.append(tile.astype(jnp.bfloat16))
                for i in range(lay.unroll):
                    tiles[group * lay.unroll + i] = fresh[i]
                add_products(lay, group, entries, fresh, rounded[p], total)
                return inner

            lax.fori_loop(first, last, group_step, 0)

        return carry

    lax.fori_loop(0, lay.inputs, visit, 0)
    used = group_start[lay.inputs]
    span = chunk_groups * lay.unroll

    def store(chunk):
        part = pl.ds(chunk * span, span)
        return pltpu.make_async_copy(tiles.at[part], tiles_out.at[part], out_sems.at[chunk])

    for chunk in range(lay.groups // chunk_groups):

        @pl.when(used > chunk * chunk_groups)
        def _():
            store(chunk).start()

    own = lay.places * lay.blocks
    own_sum[...] = total[0:own]
    other_sum[...] = total[own : 2 * own]
    for chunk in range(lay.groups // chunk_groups):

        @pl.when(used > chunk * chunk_groups)
        def _():
            store(chunk).wait()


def make_tiles(lay, plan, inputs, outputs, coarse, rounded):
    smem = pl.BlockSpec(memory_space=pltpu.SMEM)
    hbm = pl.BlockSpec(memory_space=pl.ANY)
    vmem = pl.BlockSpec(memory_space=pltpu.VMEM)
    own = lay.places * lay.blocks
    sums = jax.ShapeDtypeStruct((own, lay.side, lay.width), jnp.float32)
    n_copies = len(inputs) + len(outputs) + len(coarse) * lay.points + len(rounded) * lay.owners
    tiles = (lay.groups * lay.unroll, lay.side, lay.side)
    return pl.pallas_call(
        functools.partial(tiles_kernel, lay),
        out_shape=(sums, sums, jax.ShapeDtypeStruct(tiles, jnp.bfloat16)),
        in_specs=[smem] * 3 + [hbm] * (len(inputs) + len(outputs) + len(coarse) + len(rounded)),
        out_specs=(vmem, vmem, hbm),
        scratch_shapes=[
            pltpu.VMEM((lay.inputs, lay.pairs, lay.side), jnp.bfloat16),
            pltpu.VMEM((lay.outputs, lay.side, lay.pairs), jnp.bfloat16),
            pltpu.VMEM((lay.points, lay.slots, lay.pairs, lay.pairs), jnp.bfloat16),
            pltpu.VMEM((lay.inputs, lay.side, lay.width), jnp.bfloat16),
            pltpu.VMEM(tiles, jnp.bfloat16),
            pltpu.VMEM((lay.pairs, lay.points * lay.side), jnp.bfloat16),
            pltpu.VMEM((lay.outputs + 1, lay.side, lay.width), jnp.float32),
            pltpu.SemaphoreType.DMA((n_copies,)),
            pltpu.SemaphoreType.DMA((lay.groups // chunk_groups,)),
        ],
        compiler_params=pltpu.CompilerParams(vmem_limit_bytes=60 * mib),
        cost_estimate=pl.CostEstimate(flops=4_000_000_000, bytes_accessed=16_000_000, transcendentals=0),
    )(*plan, *inputs, *outputs, *coarse, *rounded)


def apply_kernel(lay, group_start, slot_of, entries, tiles_in, *refs):
    given_vec = refs[: lay.cols]
    own_sum, other_sum = refs[lay.cols : lay.cols + 2]
    rounded, tiles, total, sems, out_sems = refs[lay.cols + 2 :]
    used = group_start[lay.inputs]
    span = chunk_groups * lay.unroll

    def load(chunk):
        part = pl.ds(chunk * span, span)
        return pltpu.make_async_copy(tiles_in.at[part], tiles.at[part], out_sems.at[chunk])

    for chunk in range(lay.groups // chunk_groups):

        @pl.when(used > chunk * chunk_groups)
        def _():
            load(chunk).start()

    copies = []
    for d in range(lay.cols):
        for g in range(lay.owners):
            target = rounded.at[pl.ds((g * lay.cols + d) * lay.blocks, lay.blocks)]
            copies.append(pltpu.make_async_copy(given_vec[d].at[g], target, sems.at[len(copies)]))
            copies[-1].start()
    total[...] = jnp.zeros_like(total)
    for copy in copies:
        copy.wait()
    for chunk in range(lay.groups // chunk_groups):

        @pl.when(used > chunk * chunk_groups)
        def _():
            load(chunk).wait()

    def visit(p, carry):
        def group_step(group, inner):
            held = [tiles[group * lay.unroll + i] for i in range(lay.unroll)]
            add_products(lay, group, entries, held, rounded[p], total)
            return inner

        lax.fori_loop(group_start[p], group_start[p + 1], group_step, 0)
        return carry

    lax.fori_loop(0, lay.inputs, visit, 0)
    own = lay.places * lay.blocks
    own_sum[...] = total[0:own]
    other_sum[...] = total[own : 2 * own]


def apply_tiles(lay, plan, tiles, rounded):
    smem = pl.BlockSpec(memory_space=pltpu.SMEM)
    hbm = pl.BlockSpec(memory_space=pl.ANY)
    vmem = pl.BlockSpec(memory_space=pltpu.VMEM)
    own = lay.places * lay.blocks
    sums = jax.ShapeDtypeStruct((own, lay.side, lay.width), jnp.float32)
    return pl.pallas_call(
        functools.partial(apply_kernel, lay),
        out_shape=(sums, sums),
        in_specs=[smem] * 3 + [hbm] * (1 + len(rounded)),
        out_specs=(vmem, vmem),
        scratch_shapes=[
            pltpu.VMEM((lay.inputs, lay.side, lay.width), jnp.bfloat16),
            pltpu.VMEM(tiles.shape, jnp.bfloat16),
            pltpu.VMEM((lay.outputs + 1, lay.side, lay.width), jnp.float32),
            pltpu.SemaphoreType.DMA((len(rounded) * lay.owners,)),
            pltpu.SemaphoreType.DMA((lay.groups // chunk_groups,)),
        ],
        compiler_params=pltpu.CompilerParams(vmem_limit_bytes=50 * mib),
        cost_estimate=pl.CostEstimate(flops=400_000_000, bytes_accessed=4_000_000, transcendentals=0),
    )(*plan, tiles, *rounded)


def on_device(
    vectors, energies, intersections, coarse, fine_coarse, coarse_slot, tile_codes, tile_count
):
    rows = lax.axis_size("row")
    cols = lax.axis_size("col")
    row_id = lax.axis_index("row")
    col_id = lax.axis_index("col")
    blocks, pairs, side = intersections.shape
    width = vectors.shape[1]
    points, slots_dev = coarse.shape[:2]
    lay = Layout(rows, cols, blocks, pairs, side, width, points, slots_dev, tile_codes.shape[1], 4)
    if lay.groups * lay.unroll * side * side * 2 > 16 * mib:
        lay = Layout(rows, cols, blocks, pairs, side, width, points, slots_dev, tile_codes.shape[1], 1)
    near = lay.near

    def move(array, row_step, col_step):
        pairs_list = [
            (r * cols + c, (r ^ row_step) * cols + (c ^ col_step)) for r in range(rows) for c in range(cols)
        ]
        return lax.ppermute(array, axes, pairs_list)

    def along(array, step):
        return move(array, 2 * step, 0)

    def to_core(array):
        return move(array, 1, 0)

    def in_plane(array):
        return [array] + [move(array, 0, d) for d in range(1, cols)]

    start = vectors.reshape(blocks, side, width)
    energy = energies.reshape(blocks, side, 1)
    two_owners = lay.owners == 2
    codes, counts = tile_codes, tile_count
    if two_owners:
        codes = jnp.concatenate([tile_codes, along(tile_codes, near)], axis=0)
        counts = jnp.concatenate([tile_count, along(tile_count, near)], axis=0)
        starts = jnp.stack([start, along(start, near)])
        energies_both = jnp.stack([energy, along(energies, near).reshape(blocks, side, 1)])
    else:
        starts, energies_both = start[None], energy[None]
    ids = jnp.stack([row_id // 2, row_id % 2, col_id]).astype(jnp.int32)
    plan = make_plan(lay, ids, codes, counts, fine_coarse, coarse_slot)

    over_line = [intersections] + [along(intersections, d) for d in range(1, lay.places)]
    near_coarse = [coarse] + [along(coarse, e) for e in range(1, near)]
    blocks_coarse = []
    for part in near_coarse:
        blocks_coarse += [part, to_core(part)]
    inputs = in_plane(intersections)
    if two_owners:
        inputs = inputs + in_plane(over_line[near])
    lefts = [jnp.swapaxes(part, 1, 2) for part in over_line]
    lefts = lefts + [to_core(part) for part in lefts]
    rounded = in_plane(starts.astype(jnp.bfloat16))

    own_sum, other_sum, tiles = make_tiles(lay, plan, inputs, lefts, blocks_coarse, rounded)

    def over_core(own_part, other_part):
        return (own_part + to_core(other_part)).reshape(lay.places, blocks, side, width)

    merged = over_core(own_sum, other_sum)
    if two_owners:
        sums = jnp.stack([merged[0], merged[near]])
        for e in range(1, near):
            sent = jnp.stack([merged[e], merged[e ^ near]]).astype(jnp.bfloat16)
            sums = sums + along(sent, e).astype(jnp.float32)
        sums = sums + along(sums.astype(jnp.bfloat16), near)[::-1].astype(jnp.float32)
    else:
        sums = merged

    firsts = (energies_both * starts + sums - spectrum_center * starts) / spectrum_half
    own_sum, other_sum = apply_tiles(lay, plan, tiles, in_plane(firsts.astype(jnp.bfloat16)))
    merged = over_core(own_sum, other_sum)
    last = merged[0]
    for d in range(1, lay.places):
        last = last + along(merged[d].astype(jnp.bfloat16), d).astype(jnp.float32)
    first = firsts[0]
    second = 2.0 * ((energy * first + last - spectrum_center * first) / spectrum_half) - start
    return first.reshape(vectors.shape), second.reshape(vectors.shape)


def solution(mesh):
    in_specs = (
        P(axes, None),
        P(axes),
        P(axes, None, None),
        P("col", "row", None, None),
        P(),
        P(),
        P(axes, None),
        P(axes),
    )
    out_specs = (P(axes, None), P(axes, None))
    return jax.shard_map(
        on_device, mesh=mesh, in_specs=in_specs, out_specs=out_specs, check_vma=False
    )
```

time: 372 us -> 197 us (0.53); the launches traced: 366 us -> 200 us
  waiting for transfers between devices: 233 us -> 106 us
  starting transfers between devices: 0.19 us -> 45.6 us
  Pallas kernels: 0 us -> 33.2 us
  local copies, waits for them, and re-layouts: 40.2 us -> 7.56 us
  matrix products: 28.6 us -> 0 us
  blocking collectives: 20.2 us -> 0 us
  other arithmetic: 24.9 us -> 6.3 us
  between operations: 17.9 us -> 1.6 us
    all_gather x3 -> x0, waiting for transfers between devices: 116 us -> none  [the longest x1 64.4 us: on_device(): coarse_strip = lax.all_gather(coarse, 'row', axis=1, tiled=True)]
    reduce_scatter x2 -> x0, waiting for transfers between devices: 115 us -> none  [apply_kernel(): lax.psum_scatter(partial_value, 'row', scatter_dimension=0, tiled=True)]
    ppermute x0 -> x33, waiting for transfers between devices: none -> 106 us  [move(): return lax.ppermute(array, axes, pairs_list)]
    ppermute x0 -> x33, starting transfers between devices: none -> 45.6 us  [move(): return lax.ppermute(array, axes, pairs_list)]
    gather x14 -> x0, local copies, waits for them, and re-layouts: 35.1 us -> none  [the longest x3 12 us: make_tiles(): left_over = jnp.take(over_out, out_idx, axis=0)]
    pallas_call x0 -> x3, Pallas kernels: none -> 33.2 us  [the longest x1 20.5 us: make_tiles(): pl.pallas_call(functools.partial(tiles_kernel, lay), out_shape=(sums, sum...]
    dot_general x10 -> x0, matrix products: 28.6 us -> none  [the longest x1 10.1 us: on_device(): jnp.einsum('aicd,idt->iact', picked, over_in, preferred_element_type=jnp....]
    all_gather x2 -> x0, blocking collectives: 20.2 us -> none  [apply_kernel(): lax.all_gather(field.astype(jnp.bfloat16), 'col', axis=0, tiled=True)]
  transfers between devices with their start and end apart: 5 -> 33, of which waited for: 5 -> 18; matrix products, arithmetic and copies ran while one was open for 7% -> 5% of each run, Pallas kernels for 0% -> 4%
where the time goes in v1:
time: 197 us; the launch traced here: 200 us
  waiting for transfers between devices  106 us (54%)
  starting transfers between devices  45.6 us (23%)
  Pallas kernels  33.2 us (17%)
  local copies, waits for them, and re-layouts  7.56 us (4%)
  other arithmetic  6.3 us (3%)
    ppermute x33, waiting for transfers between devices, move(): return lax.ppermute(array, axes, pairs_list)  106 us
    ppermute x33, starting transfers between devices, move(): return lax.ppermute(array, axes, pairs_list)  45.6 us
    pallas_call x1, Pallas kernels, make_tiles(): pl.pallas_call(functools.partial(tiles_kernel, lay), out_shape=(sums, sum...  20.5 us
    pallas_call x1, Pallas kernels, make_plan(): pl.pallas_call(functools.partial(plan_kernel, lay), out_shape=(jax.ShapeD...  7.21 us
    pallas_call x1, Pallas kernels, apply_tiles(): pl.pallas_call(functools.partial(apply_kernel, lay), out_shape=(sums, sum...  5.5 us
  transfers between devices with their start and end apart: 33, of which 18 were waited for; matrix products, arithmetic and copies ran while one was open for 5% of the time, Pallas kernels for 4%

profile of v1, /device:TPU:0, one launch (start us, length us, event | category | flops | bytes accessed | tf_op | source)
XLA Modules:
  0.0 200.1 jit_solution(17393290210064737901)
XLA Ops:
  0.6 3.1 %collective-permute-start.18 = (bf16[2,1,512,512]{3,2,1,0:T(8,128)(2,1)}, bf16[2,1,512,512]{3,2,1,0:T(8,128)(2,1)S(1)}, u32[]{:S(2)}, u32[]{:S(2)}) collective-permute-start(bf16[2,1,512,512]{3,2,1,0:T(8,128)(2,1)} %refs_16_.1), channel_id=1, source_target_pairs={{0,8},{1,9},{2,10},{3,11},{4,12},{5,13},{6,14},{7,15},{8,0},{9,1},... | collective-permute-start | bytes 3145736 | tf_op jit(solution)/shard_map/ppermute | solution.py:336
  3.7 1.2 copy.10
  4.9 2.7 %collective-permute-start.7 = (bf16[3,512,128]{1,2,0:T(8,128)(2,1)S(1)}, bf16[3,512,128]{1,2,0:T(8,128)(2,1)S(1)}, u32[]{:S(2)}, u32[]{:S(2)}) collective-permute-start(bf16[3,512,128]{1,2,0:T(8,128)(2,1)S(1)} %copy.10), channel_id=1, source_target_pairs={{0,16},{1,17},{2,18},{3,19},{4,20},{5,21},{6,22},{7,23},{8,24},{9,... | collective-permute-start | bytes 1179656 | tf_op jit(solution)/shard_map/ppermute | solution.py:336
  7.9 31.2 %collective-permute-done.1 = f32[3,128,128]{2,1,0:T(8,128)S(1)} collective-permute-done((f32[3,128,128]{2,1,0:T(8,128)}, f32[3,128,128]{2,1,0:T(8,128)S(1)}, u32[]{:S(2)}, u32[]{:S(2)}) %collective-permute-start.1) | collective-permute-done | bytes 196640 | tf_op jit(solution)/shard_map/ppermute | solution.py:336
  39.1 0.9 fusion.refs_20_
  40.1 1.6 collective-permute-start.20
  41.6 3.3 %collective-permute-start.2 = (s32[1,96]{1,0:T(1,128)}, s32[1,96]{1,0:T(1,128)S(1)}, u32[]{:S(2)}, u32[]{:S(2)}) collective-permute-start(s32[1,96]{1,0:T(1,128)} %param.14), channel_id=1, source_target_pairs={{0,16},{1,17},{2,18},{3,19},{4,20},{5,21},{6,22},{7,23},{8,24},{9,... | collective-permute-start | bytes 1160 | tf_op jit(solution)/shard_map/ppermute | solution.py:336
  44.9 4.6 %collective-permute-done.3 = s32[1]{0:T(128)} collective-permute-done((s32[1]{0:T(128)}, s32[1]{0:T(128)}, u32[]{:S(2)}, u32[]{:S(2)}) %collective-permute-start.3) | collective-permute-done | bytes 36 | tf_op jit(solution)/shard_map/ppermute | solution.py:336
  49.6 1.5 collective-permute-start.21
  51.2 2.4 %collective-permute-start.12 = (bf16[3,512,128]{1,2,0:T(8,128)(2,1)S(1)}, bf16[3,512,128]{1,2,0:T(8,128)(2,1)}, u32[]{:S(2)}, u32[]{:S(2)}) collective-permute-start(bf16[3,512,128]{1,2,0:T(8,128)(2,1)S(1)} %copy.10), channel_id=1, source_target_pairs={{0,24},{1,25},{2,26},{3,27},{4,28},{5,29},{6,30},{7,31},{8,16},{9,... | collective-permute-start | bytes 1179656 | tf_op jit(solution)/shard_map/ppermute | solution.py:336
  53.7 0.7 copy-done.13
  54.3 0.9 collective-permute-done.21.refs_22_
  55.2 1.5 collective-permute-start.22
  56.7 5.9 %collective-permute-done.22.refs_23_ = bf16[2,3,128,128]{3,2,1,0:T(8,128)(2,1)} collective-permute-done((bf16[2,3,128,128]{3,2,1,0:T(8,128)(2,1)S(1)}, bf16[2,3,128,128]{3,2,1,0:T(8,128)(2,1)}, u32[]{:S(2)}, u32[]{:S(2)}) %collective-permute-start.22) | collective-permute-done | bytes 196640 | tf_op jit(solution)/shard_map/ppermute | solution.py:336
  63.2 0.8 collective-permute-start.5
  64.0 4.3 %collective-permute-done.12 = bf16[3,512,128]{1,2,0:T(8,128)(2,1)} collective-permute-done((bf16[3,512,128]{1,2,0:T(8,128)(2,1)S(1)}, bf16[3,512,128]{1,2,0:T(8,128)(2,1)}, u32[]{:S(2)}, u32[]{:S(2)}) %collective-permute-start.12) | collective-permute-done | bytes 393248 | tf_op jit(solution)/shard_map/ppermute | solution.py:336
  69.5 5.4 %collective-permute-done.4.refs_1_ = bf16[3,512,128]{2,1,0:T(8,128)(2,1)S(1)} collective-permute-done((bf16[3,512,128]{2,1,0:T(8,128)(2,1)}, bf16[3,512,128]{2,1,0:T(8,128)(2,1)S(1)}, u32[]{:S(2)}, u32[]{:S(2)}) %collective-permute-start.4) | collective-permute-done | bytes 393248 | tf_op jit(solution)/shard_map/ppermute | solution.py:336
  75.7 5.8 %collective-permute-done.5.refs_2_ = bf16[3,512,128]{2,1,0:T(8,128)(2,1)S(1)} collective-permute-done((bf16[3,512,128]{2,1,0:T(8,128)(2,1)}, bf16[3,512,128]{2,1,0:T(8,128)(2,1)S(1)}, u32[]{:S(2)}, u32[]{:S(2)}) %collective-permute-start.5) | collective-permute-done | bytes 393248 | tf_op jit(solution)/shard_map/ppermute | solution.py:336
  81.5 0.7 copy-done.11
  82.2 1.2 collective-permute-done.6.refs_3_
  83.4 2.8 %collective-permute-start.10 = (bf16[3,512,128]{1,2,0:T(8,128)(2,1)S(1)}, bf16[3,512,128]{1,2,0:T(8,128)(2,1)S(1)}, u32[]{:S(2)}, u32[]{:S(2)}) collective-permute-start(bf16[3,512,128]{1,2,0:T(8,128)(2,1)S(1)} %collective-permute-done.7), channel_id=1, source_target_pairs={{0,3},{1,2},{2,1},{3,0},{4,7},{5,6},{6,5},{7,4},{8,11},{9,10},{10,... | collective-permute-start | bytes 1179656 | tf_op jit(solution)/shard_map/ppermute | solution.py:336
  86.3 5.5 %collective-permute-done.8 = bf16[3,512,128]{1,2,0:T(8,128)(2,1)S(1)} collective-permute-done((bf16[3,512,128]{1,2,0:T(8,128)(2,1)S(1)}, bf16[3,512,128]{1,2,0:T(8,128)(2,1)S(1)}, u32[]{:S(2)}, u32[]{:S(2)}) %collective-permute-start.8) | collective-permute-done | bytes 393248 | tf_op jit(solution)/shard_map/ppermute | solution.py:336
  91.8 6.3 %collective-permute-done.9 = bf16[3,512,128]{1,2,0:T(8,128)(2,1)S(1)} collective-permute-done((bf16[3,512,128]{1,2,0:T(8,128)(2,1)S(1)}, bf16[3,512,128]{1,2,0:T(8,128)(2,1)S(1)}, u32[]{:S(2)}, u32[]{:S(2)}) %collective-permute-start.9) | collective-permute-done | bytes 393248 | tf_op jit(solution)/shard_map/ppermute | solution.py:336
  99.9 1.1 pad_add_fusion.2.counts
  101.0 1.2 pad_add_fusion.codes
  102.2 7.2 %shard_map.95 = (s32[25]{0:T(128)}, s32[24]{0:T(128)}, s32[288]{0:T(512)}) custom-call(s32[3]{0:T(128)} %pad_add_fusion.1.ids, s32[2,96]{1,0:T(2,128)} %pad_add_fusion.codes, s32[2]{0:T(128)} %pad_add_fusion.2.counts, s32[96]{0:T(128)} %fine.1, s32[8]{0:T(128)} %stored.1), custom_call_target="tpu_custom_call" | custom-call | tf_op jit(solution)/shard_map/pallas_call | solution.py:110
  109.5 0.9 copy.14.refs_4_
  110.4 0.9 copy.15.refs_5_
  111.3 0.9 copy.16.refs_6_
  112.2 0.9 copy.17.refs_7_
  113.3 20.5 %shard_map.96 = (f32[12,128,128]{2,1,0:T(8,128)}, f32[12,128,128]{2,1,0:T(8,128)}, bf16[288,128,128]{2,1,0:T(8,128)(2,1)}) custom-call(s32[25]{0:T(128)} %get-tuple-element.10.group_start, s32[24]{0:T(128)} %get-tuple-element.11.slot_of, s32[288]{0:T(512)} %get-tuple-element.12.entries, bf16[3,512,128]{2,1,0:T(8,128)(2,1)} %refs_0_.1, ...), custom_call_target="tpu_custom_call" | custom-call | flops 4000000000 | bytes 16000000 | tf_op jit(solution)/shard_map/pallas_call | solution.py:226
  133.8 5.3 %collective-permute-start.23 = (f32[12,128,128]{2,1,0:T(8,128)}, f32[12,128,128]{2,1,0:T(8,128)S(1)}, u32[]{:S(2)}, u32[]{:S(2)}) collective-permute-start(f32[12,128,128]{2,1,0:T(8,128)} %get-tuple-element.14), channel_id=1, source_target_pairs={{0,4},{1,5},{2,6},{3,7},{4,0},{5,1},{6,2},{7,3},{8,12},{9,13},{10,... | collective-permute-start | bytes 2359304 | tf_op jit(solution)/shard_map/ppermute | solution.py:336
  139.1 2.1 %collective-permute-done.23 = f32[12,128,128]{2,1,0:T(8,128)S(1)} collective-permute-done((f32[12,128,128]{2,1,0:T(8,128)}, f32[12,128,128]{2,1,0:T(8,128)S(1)}, u32[]{:S(2)}, u32[]{:S(2)}) %collective-permute-start.23) | collective-permute-done | bytes 786464 | tf_op jit(solution)/shard_map/ppermute | solution.py:336
  141.3 1.2 fusion.10
  142.7 7.1 %collective-permute-done.24 = bf16[2,3,128,128]{3,2,1,0:T(8,128)(2,1)S(1)} collective-permute-done((bf16[2,3,128,128]{3,2,1,0:T(8,128)(2,1)S(1)}, bf16[2,3,128,128]{3,2,1,0:T(8,128)(2,1)S(1)}, u32[]{:S(2)}, u32[]{:S(2)}) %collective-permute-start.24) | collective-permute-done | bytes 196640 | tf_op jit(solution)/shard_map/ppermute | solution.py:336
  149.9 2.9 %collective-permute-start = (f32[384]{0:T(512)S(1)}, f32[384]{0:T(512)S(1)}, u32[]{:S(2)}, u32[]{:S(2)}) collective-permute-start(f32[384]{0:T(512)S(1)} %copy-done.7), channel_id=1, source_target_pairs={{0,16},{1,17},{2,18},{3,19},{4,20},{5,21},{6,22},{7,23},{8,24},{9,... | collective-permute-start | bytes 4616 | tf_op jit(solution)/shard_map/ppermute | solution.py:336
  152.9 8.6 %collective-permute-done = f32[384]{0:T(512)S(1)} collective-permute-done((f32[384]{0:T(512)S(1)}, f32[384]{0:T(512)S(1)}, u32[]{:S(2)}, u32[]{:S(2)}) %collective-permute-start) | collective-permute-done | bytes 1568 | tf_op jit(solution)/shard_map/ppermute | solution.py:336
  161.7 8.0 %collective-permute-start.27 = (bf16[2,3,128,128]{3,2,1,0:T(8,128)(2,1)S(1)}, bf16[2,3,128,128]{3,2,1,0:T(8,128)(2,1)S(1)}, u32[]{:S(2)}, u32[]{:S(2)}) collective-permute-start(bf16[2,3,128,128]{3,2,1,0:T(8,128)(2,1)S(1)} %get-tuple-element.20.refs_0_), channel_id=1, source_target_pairs={{0,2},{1,3},{2,0},{3,1},{4,6},{5,7},{6,4},{7,5},{8,10},{9,11},{10,... | collective-permute-start | bytes 589832 | tf_op jit(solution)/shard_map/ppermute | solution.py:336
  169.7 1.4 collective-permute-start.28
  171.1 7.2 %collective-permute-done.27.refs_2_ = bf16[2,3,128,128]{3,2,1,0:T(8,128)(2,1)S(1)} collective-permute-done((bf16[2,3,128,128]{3,2,1,0:T(8,128)(2,1)S(1)}, bf16[2,3,128,128]{3,2,1,0:T(8,128)(2,1)S(1)}, u32[]{:S(2)}, u32[]{:S(2)}) %collective-permute-start.27) | collective-permute-done | bytes 196640 | tf_op jit(solution)/shard_map/ppermute | solution.py:336
  178.3 1.8 collective-permute-done.28.refs_3_
  180.1 5.5 %shard_map.97 = (f32[12,128,128]{2,1,0:T(8,128)S(1)}, f32[12,128,128]{2,1,0:T(8,128)S(1)}) custom-call(s32[25]{0:T(128)S(1)} %copy-done.1, s32[24]{0:T(128)S(1)} %copy-done.2, s32[288]{0:T(512)S(1)} %copy-done, bf16[288,128,128]{2,1,0:T(8,128)(2,1)} %get-tuple-element.15.tiles_in, bf16[2,3,128,128]{3,2,1,0:T(8,128)(2,1)S(1)} %get-tuple-element.20.refs_0_, ...), custom_call_target="tpu_custom_call" | custom-call | flops 400000000 | bytes 4000000 | tf_op jit(solution)/shard_map/pallas_call | solution.py:300
  186.2 1.9 collective-permute-done.29
  188.5 4.3 %collective-permute-start.32 = (bf16[3,128,128]{2,1,0:T(8,128)(2,1)S(1)}, bf16[3,128,128]{2,1,0:T(8,128)(2,1)S(1)}, u32[]{:S(2)}, u32[]{:S(2)}) collective-permute-start(bf16[3,128,128]{2,1,0:T(8,128)(2,1)S(1)} %get-tuple-element.27), channel_id=1, source_target_pairs={{0,24},{1,25},{2,26},{3,27},{4,28},{5,29},{6,30},{7,31},{8,16},{9,... | collective-permute-start | bytes 294920 | tf_op jit(solution)/shard_map/ppermute | solution.py:336
  192.8 0.7 slice.65
  193.5 1.1 collective-permute-done.30
  194.6 4.6 %collective-permute-done.31 = bf16[3,128,128]{2,1,0:T(8,128)(2,1)S(1)} collective-permute-done((bf16[3,128,128]{2,1,0:T(8,128)(2,1)S(1)}, bf16[3,128,128]{2,1,0:T(8,128)(2,1)S(1)}, u32[]{:S(2)}, u32[]{:S(2)}) %collective-permute-start.31) | collective-permute-done | bytes 98336 | tf_op jit(solution)/shard_map/ppermute | solution.py:336
  199.3 0.8 fusion.7
  (71 shorter events, 5.7 us)
Async XLA Ops:
  0.6 68.2 %collective-permute-start.18 = (bf16[2,1,512,512]{3,2,1,0:T(8,128)(2,1)}, bf16[2,1,512,512]{3,2,1,0:T(8,128)(2,1)S(1)}, u32[]{:S(2)}, u32[]{:S(2)}) collective-permute-start(bf16[2,1,512,512]{3,2,1,0:T(8,128)(2,1)} %refs_16_.1), channel_id=1, source_target_pairs={{0,8},{1,9},{2,10},{3,11},{4,12},{5,13},{6,14},{7,15},{8,0},{9,1},... | collective-permute-start | bytes 3145736 | tf_op jit(solution)/shard_map/ppermute | solution.py:336
  4.9 108.3 %copy-start.4 = (bf16[3,512,128]{1,2,0:T(8,128)(2,1)}, bf16[3,512,128]{1,2,0:T(8,128)(2,1)S(1)}, u32[]{:S(2)}) copy-start(bf16[3,512,128]{1,2,0:T(8,128)(2,1)S(1)} %copy.10) | copy-start | bytes 1179652
  4.9 46.3 %collective-permute-start.7 = (bf16[3,512,128]{1,2,0:T(8,128)(2,1)S(1)}, bf16[3,512,128]{1,2,0:T(8,128)(2,1)S(1)}, u32[]{:S(2)}, u32[]{:S(2)}) collective-permute-start(bf16[3,512,128]{1,2,0:T(8,128)(2,1)S(1)} %copy.10), channel_id=1, source_target_pairs={{0,16},{1,17},{2,18},{3,19},{4,20},{5,21},{6,22},{7,23},{8,24},{9,... | collective-permute-start | bytes 1179656 | tf_op jit(solution)/shard_map/ppermute | solution.py:336
  7.6 31.5 %collective-permute-start.1 = (f32[3,128,128]{2,1,0:T(8,128)}, f32[3,128,128]{2,1,0:T(8,128)S(1)}, u32[]{:S(2)}, u32[]{:S(2)}) collective-permute-start(f32[3,128,128]{2,1,0:T(8,128)} %bitcast.32), channel_id=1, source_target_pairs={{0,16},{1,17},{2,18},{3,19},{4,20},{5,21},{6,22},{7,23},{8,24},{9,... | collective-permute-start | bytes 589832 | tf_op jit(solution)/shard_map/ppermute | solution.py:336
  40.0 73.2 %copy-start.6 = (bf16[2,3,128,128]{3,2,1,0:T(8,128)(2,1)}, bf16[2,3,128,128]{3,2,1,0:T(8,128)(2,1)S(1)}, u32[]{:S(2)}) copy-start(bf16[2,3,128,128]{3,2,1,0:T(8,128)(2,1)S(1)} %fusion.refs_20_) | copy-start | bytes 589828
  40.1 13.6 %collective-permute-start.20 = (bf16[2,3,128,128]{3,2,1,0:T(8,128)(2,1)S(1)}, bf16[2,3,128,128]{3,2,1,0:T(8,128)(2,1)S(1)}, u32[]{:S(2)}, u32[]{:S(2)}) collective-permute-start(bf16[2,3,128,128]{3,2,1,0:T(8,128)(2,1)S(1)} %fusion.refs_20_), channel_id=1, source_target_pairs={{0,1},{1,0},{2,3},{3,2},{4,5},{5,4},{6,7},{7,6},{8,9},{9,8},{10,11... | collective-permute-start | bytes 589832 | tf_op jit(solution)/shard_map/ppermute | solution.py:336
  41.6 9.5 %collective-permute-start.2 = (s32[1,96]{1,0:T(1,128)}, s32[1,96]{1,0:T(1,128)S(1)}, u32[]{:S(2)}, u32[]{:S(2)}) collective-permute-start(s32[1,96]{1,0:T(1,128)} %param.14), channel_id=1, source_target_pairs={{0,16},{1,17},{2,18},{3,19},{4,20},{5,21},{6,22},{7,23},{8,24},{9,... | collective-permute-start | bytes 1160 | tf_op jit(solution)/shard_map/ppermute | solution.py:336
  44.9 4.7 %collective-permute-start.3 = (s32[1]{0:T(128)}, s32[1]{0:T(128)}, u32[]{:S(2)}, u32[]{:S(2)}) collective-permute-start(s32[1]{0:T(128)} %param.15), channel_id=1, source_target_pairs={{0,16},{1,17},{2,18},{3,19},{4,20},{5,21},{6,22},{7,23},{8,24},{9,... | collective-permute-start | bytes 20 | tf_op jit(solution)/shard_map/ppermute | solution.py:336
  49.6 5.7 %collective-permute-start.21 = (bf16[2,3,128,128]{3,2,1,0:T(8,128)(2,1)S(1)}, bf16[2,3,128,128]{3,2,1,0:T(8,128)(2,1)S(1)}, u32[]{:S(2)}, u32[]{:S(2)}) collective-permute-start(bf16[2,3,128,128]{3,2,1,0:T(8,128)(2,1)S(1)} %fusion.refs_20_), channel_id=1, source_target_pairs={{0,2},{1,3},{2,0},{3,1},{4,6},{5,7},{6,4},{7,5},{8,10},{9,11},{10,... | collective-permute-start | bytes 589832 | tf_op jit(solution)/shard_map/ppermute | solution.py:336
  51.1 12.1 %collective-permute-start.11 = (bf16[3,512,128]{1,2,0:T(8,128)(2,1)S(1)}, bf16[3,512,128]{1,2,0:T(8,128)(2,1)}, u32[]{:S(2)}, u32[]{:S(2)}) collective-permute-start(bf16[3,512,128]{1,2,0:T(8,128)(2,1)S(1)} %copy.10), channel_id=1, source_target_pairs={{0,8},{1,9},{2,10},{3,11},{4,12},{5,13},{6,14},{7,15},{8,0},{9,1},... | collective-permute-start | bytes 1179656 | tf_op jit(solution)/shard_map/ppermute | solution.py:336
  51.2 62.0 %copy-start.5 = (bf16[3,512,128]{1,2,0:T(8,128)(2,1)}, bf16[3,512,128]{1,2,0:T(8,128)(2,1)S(1)}, u32[]{:S(2)}) copy-start(bf16[3,512,128]{1,2,0:T(8,128)(2,1)S(1)} %collective-permute-done.7) | copy-start | bytes 1179652
  51.2 17.1 %collective-permute-start.12 = (bf16[3,512,128]{1,2,0:T(8,128)(2,1)S(1)}, bf16[3,512,128]{1,2,0:T(8,128)(2,1)}, u32[]{:S(2)}, u32[]{:S(2)}) collective-permute-start(bf16[3,512,128]{1,2,0:T(8,128)(2,1)S(1)} %copy.10), channel_id=1, source_target_pairs={{0,24},{1,25},{2,26},{3,27},{4,28},{5,29},{6,30},{7,31},{8,16},{9,... | collective-permute-start | bytes 1179656 | tf_op jit(solution)/shard_map/ppermute | solution.py:336
  53.7 0.7 copy-start.13
  54.3 14.5 %collective-permute-start.13 = (bf16[3,128,512]{2,1,0:T(8,128)(2,1)S(1)}, bf16[3,128,512]{2,1,0:T(8,128)(2,1)S(1)}, u32[]{:S(2)}, u32[]{:S(2)}) collective-permute-start(bf16[3,128,512]{2,1,0:T(8,128)(2,1)S(1)} %bitcast.38), channel_id=1, source_target_pairs={{0,4},{1,5},{2,6},{3,7},{4,0},{5,1},{6,2},{7,3},{8,12},{9,13},{10,... | collective-permute-start | bytes 1179656 | tf_op jit(solution)/shard_map/ppermute | solution.py:336
  55.2 1.5 copy-start.14
  55.2 7.4 %collective-permute-start.22 = (bf16[2,3,128,128]{3,2,1,0:T(8,128)(2,1)S(1)}, bf16[2,3,128,128]{3,2,1,0:T(8,128)(2,1)}, u32[]{:S(2)}, u32[]{:S(2)}) collective-permute-start(bf16[2,3,128,128]{3,2,1,0:T(8,128)(2,1)S(1)} %fusion.refs_20_), channel_id=1, source_target_pairs={{0,3},{1,2},{2,1},{3,0},{4,7},{5,6},{6,5},{7,4},{8,11},{9,10},{10,... | collective-permute-start | bytes 589832 | tf_op jit(solution)/shard_map/ppermute | solution.py:336
  62.7 12.3 %collective-permute-start.4 = (bf16[3,512,128]{2,1,0:T(8,128)(2,1)}, bf16[3,512,128]{2,1,0:T(8,128)(2,1)S(1)}, u32[]{:S(2)}, u32[]{:S(2)}) collective-permute-start(bf16[3,512,128]{2,1,0:T(8,128)(2,1)} %refs_0_.1), channel_id=1, source_target_pairs={{0,1},{1,0},{2,3},{3,2},{4,5},{5,4},{6,7},{7,6},{8,9},{9,8},{10,11... | collective-permute-start | bytes 1179656 | tf_op jit(solution)/shard_map/ppermute | solution.py:336
  63.2 18.2 %collective-permute-start.5 = (bf16[3,512,128]{2,1,0:T(8,128)(2,1)}, bf16[3,512,128]{2,1,0:T(8,128)(2,1)S(1)}, u32[]{:S(2)}, u32[]{:S(2)}) collective-permute-start(bf16[3,512,128]{2,1,0:T(8,128)(2,1)} %refs_0_.1), channel_id=1, source_target_pairs={{0,2},{1,3},{2,0},{3,1},{4,6},{5,7},{6,4},{7,5},{8,10},{9,11},{10,... | collective-permute-start | bytes 1179656 | tf_op jit(solution)/shard_map/ppermute | solution.py:336
  68.3 15.1 %collective-permute-start.6 = (bf16[3,512,128]{2,1,0:T(8,128)(2,1)}, bf16[3,512,128]{2,1,0:T(8,128)(2,1)S(1)}, u32[]{:S(2)}, u32[]{:S(2)}) collective-permute-start(bf16[3,512,128]{2,1,0:T(8,128)(2,1)} %refs_0_.1), channel_id=1, source_target_pairs={{0,3},{1,2},{2,1},{3,0},{4,7},{5,6},{6,5},{7,4},{8,11},{9,10},{10,... | collective-permute-start | bytes 1179656 | tf_op jit(solution)/shard_map/ppermute | solution.py:336
  68.8 0.8 copy-start.9
  68.8 44.4 %collective-permute-start.17 = (bf16[2,1,512,512]{3,2,1,0:T(8,128)(2,1)}, bf16[2,1,512,512]{3,2,1,0:T(8,128)(2,1)}, u32[]{:S(2)}, u32[]{:S(2)}) collective-permute-start(bf16[2,1,512,512]{3,2,1,0:T(8,128)(2,1)} %refs_16_.1), channel_id=1, source_target_pairs={{0,4},{1,5},{2,6},{3,7},{4,0},{5,1},{6,2},{7,3},{8,12},{9,13},{10,... | collective-permute-start | bytes 3145736 | tf_op jit(solution)/shard_map/ppermute | solution.py:336
  68.8 44.4 %copy-start.8 = (bf16[2,1,512,512]{3,2,1,0:T(8,128)(2,1)}, bf16[2,1,512,512]{3,2,1,0:T(8,128)(2,1)S(1)}, u32[]{:S(2)}) copy-start(bf16[2,1,512,512]{3,2,1,0:T(8,128)(2,1)S(1)} %collective-permute-done.18.refs_18_) | copy-start | bytes 3145732
  68.8 44.4 %collective-permute-start.19 = (bf16[2,1,512,512]{3,2,1,0:T(8,128)(2,1)S(1)}, bf16[2,1,512,512]{3,2,1,0:T(8,128)(2,1)}, u32[]{:S(2)}, u32[]{:S(2)}) collective-permute-start(bf16[2,1,512,512]{3,2,1,0:T(8,128)(2,1)S(1)} %collective-permute-done.18.refs_18_), channel_id=1, source_target_pairs={{0,4},{1,5},{2,6},{3,7},{4,0},{5,1},{6,2},{7,3},{8,12},{9,13},{10,... | collective-permute-start | bytes 3145736 | tf_op jit(solution)/shard_map/ppermute | solution.py:336
  74.9 0.7 copy-start.10
  74.9 16.9 %collective-permute-start.8 = (bf16[3,512,128]{1,2,0:T(8,128)(2,1)S(1)}, bf16[3,512,128]{1,2,0:T(8,128)(2,1)S(1)}, u32[]{:S(2)}, u32[]{:S(2)}) collective-permute-start(bf16[3,512,128]{1,2,0:T(8,128)(2,1)S(1)} %collective-permute-done.7), channel_id=1, source_target_pairs={{0,1},{1,0},{2,3},{3,2},{4,5},{5,4},{6,7},{7,6},{8,9},{9,8},{10,11... | collective-permute-start | bytes 1179656 | tf_op jit(solution)/shard_map/ppermute | solution.py:336
  81.4 0.7 copy-start.11
  81.4 16.7 %collective-permute-start.9 = (bf16[3,512,128]{1,2,0:T(8,128)(2,1)S(1)}, bf16[3,512,128]{1,2,0:T(8,128)(2,1)S(1)}, u32[]{:S(2)}, u32[]{:S(2)}) collective-permute-start(bf16[3,512,128]{1,2,0:T(8,128)(2,1)S(1)} %collective-permute-done.7), channel_id=1, source_target_pairs={{0,2},{1,3},{2,0},{3,1},{4,6},{5,7},{6,4},{7,5},{8,10},{9,11},{10,... | collective-permute-start | bytes 1179656 | tf_op jit(solution)/shard_map/ppermute | solution.py:336
  83.4 14.7 %copy-start.12 = (bf16[3,512,128]{2,1,0:T(8,128)(2,1)}, bf16[3,512,128]{2,1,0:T(8,128)(2,1)S(1)}, u32[]{:S(2)}) copy-start(bf16[3,512,128]{2,1,0:T(8,128)(2,1)S(1)} %collective-permute-done.6.refs_3_) | copy-start | bytes 1179652
  83.4 14.7 %collective-permute-start.10 = (bf16[3,512,128]{1,2,0:T(8,128)(2,1)S(1)}, bf16[3,512,128]{1,2,0:T(8,128)(2,1)S(1)}, u32[]{:S(2)}, u32[]{:S(2)}) collective-permute-start(bf16[3,512,128]{1,2,0:T(8,128)(2,1)S(1)} %collective-permute-done.7), channel_id=1, source_target_pairs={{0,3},{1,2},{2,1},{3,0},{4,7},{5,6},{6,5},{7,4},{8,11},{9,10},{10,... | collective-permute-start | bytes 1179656 | tf_op jit(solution)/shard_map/ppermute | solution.py:336
  91.8 21.4 %collective-permute-start.15 = (bf16[3,128,512]{2,1,0:T(8,128)(2,1)S(1)}, bf16[3,128,512]{2,1,0:T(8,128)(2,1)}, u32[]{:S(2)}, u32[]{:S(2)}) collective-permute-start(bf16[3,128,512]{2,1,0:T(8,128)(2,1)S(1)} %bitcast.40), channel_id=1, source_target_pairs={{0,4},{1,5},{2,6},{3,7},{4,0},{5,1},{6,2},{7,3},{8,12},{9,13},{10,... | collective-permute-start | bytes 1179656 | tf_op jit(solution)/shard_map/ppermute | solution.py:336
  98.1 15.1 %collective-permute-start.14 = (bf16[3,128,512]{2,1,0:T(8,128)(2,1)}, bf16[3,128,512]{2,1,0:T(8,128)(2,1)}, u32[]{:S(2)}, u32[]{:S(2)}) collective-permute-start(bf16[3,128,512]{2,1,0:T(8,128)(2,1)} %bitcast.10.refs_9_), channel_id=1, source_target_pairs={{0,4},{1,5},{2,6},{3,7},{4,0},{5,1},{6,2},{7,3},{8,12},{9,13},{10,... | collective-permute-start | bytes 1179656 | tf_op jit(solution)/shard_map/ppermute | solution.py:336
  98.1 15.0 %collective-permute-start.16 = (bf16[3,128,512]{2,1,0:T(8,128)(2,1)}, bf16[3,128,512]{2,1,0:T(8,128)(2,1)}, u32[]{:S(2)}, u32[]{:S(2)}) collective-permute-start(bf16[3,128,512]{2,1,0:T(8,128)(2,1)} %bitcast.12.refs_11_), channel_id=1, source_target_pairs={{0,4},{1,5},{2,6},{3,7},{4,0},{5,1},{6,2},{7,3},{8,12},{9,13},{10,... | collective-permute-start | bytes 1179656 | tf_op jit(solution)/shard_map/ppermute | solution.py:336
  113.3 36.7 %copy-start.7 = (f32[384]{0:T(512)S(1)}, f32[384]{0:T(512)}, u32[]{:S(2)}) copy-start(f32[384]{0:T(512)} %param.9) | copy-start | bytes 4612
  113.3 48.2 %copy-start.3 = (f32[384,128]{1,0:T(8,128)S(1)}, f32[384,128]{1,0:T(8,128)}, u32[]{:S(2)}) copy-start(f32[384,128]{1,0:T(8,128)} %param.8) | copy-start | bytes 589828
  113.3 66.8 %copy-start = (s32[288]{0:T(512)S(1)}, s32[288]{0:T(512)}, u32[]{:S(2)}) copy-start(s32[288]{0:T(512)} %get-tuple-element.12.entries) | copy-start | bytes 3460
  113.3 66.8 %copy-start.1 = (s32[25]{0:T(128)S(1)}, s32[25]{0:T(128)}, u32[]{:S(2)}) copy-start(s32[25]{0:T(128)} %get-tuple-element.10.group_start) | copy-start | bytes 304
  113.3 66.8 %copy-start.2 = (s32[24]{0:T(128)S(1)}, s32[24]{0:T(128)}, u32[]{:S(2)}) copy-start(s32[24]{0:T(128)} %get-tuple-element.11.slot_of) | copy-start | bytes 292
  133.8 7.5 %collective-permute-start.23 = (f32[12,128,128]{2,1,0:T(8,128)}, f32[12,128,128]{2,1,0:T(8,128)S(1)}, u32[]{:S(2)}, u32[]{:S(2)}) collective-permute-start(f32[12,128,128]{2,1,0:T(8,128)} %get-tuple-element.14), channel_id=1, source_target_pairs={{0,4},{1,5},{2,6},{3,7},{4,0},{5,1},{6,2},{7,3},{8,12},{9,13},{10,... | collective-permute-start | bytes 2359304 | tf_op jit(solution)/shard_map/ppermute | solution.py:336
  142.6 7.2 %collective-permute-start.24 = (bf16[2,3,128,128]{3,2,1,0:T(8,128)(2,1)S(1)}, bf16[2,3,128,128]{3,2,1,0:T(8,128)(2,1)S(1)}, u32[]{:S(2)}, u32[]{:S(2)}) collective-permute-start(bf16[2,3,128,128]{3,2,1,0:T(8,128)(2,1)S(1)} %pad_maximum_fusion.1), channel_id=1, source_target_pairs={{0,8},{1,9},{2,10},{3,11},{4,12},{5,13},{6,14},{7,15},{8,0},{9,1},... | collective-permute-start | bytes 589832 | tf_op jit(solution)/shard_map/ppermute | solution.py:336
  149.9 11.6 %collective-permute-start.25 = (bf16[2,3,128,128]{3,2,1,0:T(8,128)(2,1)S(1)}, bf16[2,3,128,128]{3,2,1,0:T(8,128)(2,1)S(1)}, u32[]{:S(2)}, u32[]{:S(2)}) collective-permute-start(bf16[2,3,128,128]{3,2,1,0:T(8,128)(2,1)S(1)} %fusion.1), channel_id=1, source_target_pairs={{0,16},{1,17},{2,18},{3,19},{4,20},{5,21},{6,22},{7,23},{8,24},{9,... | collective-permute-start | bytes 589832 | tf_op jit(solution)/shard_map/ppermute | solution.py:336
  149.9 11.5 %collective-permute-start = (f32[384]{0:T(512)S(1)}, f32[384]{0:T(512)S(1)}, u32[]{:S(2)}, u32[]{:S(2)}) collective-permute-start(f32[384]{0:T(512)S(1)} %copy-done.7), channel_id=1, source_target_pairs={{0,16},{1,17},{2,18},{3,19},{4,20},{5,21},{6,22},{7,23},{8,24},{9,... | collective-permute-start | bytes 4616 | tf_op jit(solution)/shard_map/ppermute | solution.py:336
  161.7 9.5 %collective-permute-start.26 = (bf16[2,3,128,128]{3,2,1,0:T(8,128)(2,1)S(1)}, bf16[2,3,128,128]{3,2,1,0:T(8,128)(2,1)S(1)}, u32[]{:S(2)}, u32[]{:S(2)}) collective-permute-start(bf16[2,3,128,128]{3,2,1,0:T(8,128)(2,1)S(1)} %get-tuple-element.20.refs_0_), channel_id=1, source_target_pairs={{0,1},{1,0},{2,3},{3,2},{4,5},{5,4},{6,7},{7,6},{8,9},{9,8},{10,11... | collective-permute-start | bytes 589832 | tf_op jit(solution)/shard_map/ppermute | solution.py:336
  161.7 16.5 %collective-permute-start.27 = (bf16[2,3,128,128]{3,2,1,0:T(8,128)(2,1)S(1)}, bf16[2,3,128,128]{3,2,1,0:T(8,128)(2,1)S(1)}, u32[]{:S(2)}, u32[]{:S(2)}) collective-permute-start(bf16[2,3,128,128]{3,2,1,0:T(8,128)(2,1)S(1)} %get-tuple-element.20.refs_0_), channel_id=1, source_target_pairs={{0,2},{1,3},{2,0},{3,1},{4,6},{5,7},{6,4},{7,5},{8,10},{9,11},{10,... | collective-permute-start | bytes 589832 | tf_op jit(solution)/shard_map/ppermute | solution.py:336
  169.7 10.4 %collective-permute-start.28 = (bf16[2,3,128,128]{3,2,1,0:T(8,128)(2,1)S(1)}, bf16[2,3,128,128]{3,2,1,0:T(8,128)(2,1)S(1)}, u32[]{:S(2)}, u32[]{:S(2)}) collective-permute-start(bf16[2,3,128,128]{3,2,1,0:T(8,128)(2,1)S(1)} %get-tuple-element.20.refs_0_), channel_id=1, source_target_pairs={{0,3},{1,2},{2,1},{3,0},{4,7},{5,6},{6,5},{7,4},{8,11},{9,10},{10,... | collective-permute-start | bytes 589832 | tf_op jit(solution)/shard_map/ppermute | solution.py:336
  185.6 2.5 %collective-permute-start.29 = (f32[12,128,128]{2,1,0:T(8,128)S(1)}, f32[12,128,128]{2,1,0:T(8,128)S(1)}, u32[]{:S(2)}, u32[]{:S(2)}) collective-permute-start(f32[12,128,128]{2,1,0:T(8,128)S(1)} %get-tuple-element.17), channel_id=1, source_target_pairs={{0,4},{1,5},{2,6},{3,7},{4,0},{5,1},{6,2},{7,3},{8,12},{9,13},{10,... | collective-permute-start | bytes 2359304 | tf_op jit(solution)/shard_map/ppermute | solution.py:336
  188.3 6.3 %collective-permute-start.30 = (bf16[3,128,128]{2,1,0:T(8,128)(2,1)S(1)}, bf16[3,128,128]{2,1,0:T(8,128)(2,1)S(1)}, u32[]{:S(2)}, u32[]{:S(2)}) collective-permute-start(bf16[3,128,128]{2,1,0:T(8,128)(2,1)S(1)} %get-tuple-element.26), channel_id=1, source_target_pairs={{0,8},{1,9},{2,10},{3,11},{4,12},{5,13},{6,14},{7,15},{8,0},{9,1},... | collective-permute-start | bytes 294920 | tf_op jit(solution)/shard_map/ppermute | solution.py:336
  188.4 10.9 %collective-permute-start.31 = (bf16[3,128,128]{2,1,0:T(8,128)(2,1)S(1)}, bf16[3,128,128]{2,1,0:T(8,128)(2,1)S(1)}, u32[]{:S(2)}, u32[]{:S(2)}) collective-permute-start(bf16[3,128,128]{2,1,0:T(8,128)(2,1)S(1)} %get-tuple-element.28), channel_id=1, source_target_pairs={{0,16},{1,17},{2,18},{3,19},{4,20},{5,21},{6,22},{7,23},{8,24},{9,... | collective-permute-start | bytes 294920 | tf_op jit(solution)/shard_map/ppermute | solution.py:336
  188.5 10.8 %collective-permute-start.32 = (bf16[3,128,128]{2,1,0:T(8,128)(2,1)S(1)}, bf16[3,128,128]{2,1,0:T(8,128)(2,1)S(1)}, u32[]{:S(2)}, u32[]{:S(2)}) collective-permute-start(bf16[3,128,128]{2,1,0:T(8,128)(2,1)S(1)} %get-tuple-element.27), channel_id=1, source_target_pairs={{0,24},{1,25},{2,26},{3,27},{4,28},{5,29},{6,30},{7,31},{8,16},{9,... | collective-permute-start | bytes 294920 | tf_op jit(solution)/shard_map/ppermute | solution.py:336

commit v2 on v1

--- a/solution.py
+++ b/solution.py
@@ -30,6 +30,9 @@
         most = self.owners * tile_max + self.inputs * (unroll - 1)
         self.groups = -(-most // (unroll * chunk_groups)) * chunk_groups
 
+    def line_steps(self):
+        return [d for d in range(1, self.places) if d != self.near]
+
 
 def plan_kernel(lay, ids, codes, counts, fine, stored, group_start, slot_of, entries, fill):
     place, core, col = ids[0], ids[1], ids[2]
@@ -117,6 +120,7 @@
         in_specs=[smem] * 5,
         out_specs=(smem,) * 3,
         scratch_shapes=[pltpu.SMEM((lay.inputs,), jnp.int32)],
+        cost_estimate=pl.CostEstimate(flops=0, bytes_accessed=20_000_000, transcendentals=0),
     )(ids, codes, counts, fine, stored)
 
 
@@ -129,15 +133,39 @@
         total[q] = total[q] + products[i]
 
 
+def turn_kernel(lay, *refs):
+    given, outs = refs[: lay.owners], refs[lay.owners :]
+    for g in range(lay.owners):
+        for t in range(lay.blocks):
+            turned = given[g][t, 0 : lay.pairs, :].T
+            outs[0][g * lay.blocks + t] = turned
+            if g == 0:
+                outs[1][t] = turned
+
+
+def turn(lay, *given):
+    vmem = pl.BlockSpec(memory_space=pltpu.VMEM)
+    return pl.pallas_call(
+        functools.partial(turn_kernel, lay),
+        out_shape=(
+            jax.ShapeDtypeStruct((lay.owners * lay.blocks, lay.side, lay.pairs), jnp.bfloat16),
+            jax.ShapeDtypeStruct((lay.blocks, lay.side, lay.pairs), jnp.bfloat16),
+        ),
+        in_specs=[vmem] * lay.owners,
+        out_specs=(vmem, vmem),
+        compiler_params=pltpu.CompilerParams(vmem_limit_bytes=16 * mib),
+        cost_estimate=pl.CostEstimate(flops=1_000_000, bytes_accessed=3_000_000, transcendentals=0),
+    )(*given)
+
+
 def tiles_kernel(lay, group_start, slot_of, entries, *refs):
     n_in = lay.owners * lay.cols
-    n_out = 2 * lay.places
     n_coarse = 2 * lay.near
+    lines = lay.line_steps()
     refs = list(refs)
     given_in = [refs.pop(0) for _ in range(n_in)]
-    given_out = [refs.pop(0) for _ in range(n_out)]
+    given_out = [refs.pop(0) for _ in range(2 * (1 + len(lines)))]
     given_coarse = [refs.pop(0) for _ in range(n_coarse)]
-    given_vec = [refs.pop(0) for _ in range(lay.cols)]
     own_sum, other_sum, tiles_out = refs[:3]
     right, left, blocks, rounded, tiles, projected, total, sems, out_sems = refs[3:]
     copies = []
@@ -150,12 +178,16 @@
         for a in range(lay.points):
             fetch(given_coarse[i].at[a], blocks.at[a, pl.ds(i * lay.slots_dev, lay.slots_dev)])
     for i in range(n_in):
-        fetch(given_in[i], right.at[pl.ds(i * lay.blocks, lay.blocks)])
-    for d in range(lay.cols):
+        part = pl.ds(i * lay.blocks, lay.blocks)
+        fetch(given_in[i].at[:, pl.ds(0, lay.pairs)], right.at[part])
+        fetch(given_in[i].at[:, pl.ds(lay.pairs, lay.side)], rounded.at[part])
+    for k in range(2):
+        held = given_out[k * (1 + len(lines)) :]
         for g in range(lay.owners):
-            fetch(given_vec[d].at[g], rounded.at[pl.ds((g * lay.cols + d) * lay.blocks, lay.blocks)])
-    for i in range(n_out):
-        fetch(given_out[i], left.at[pl.ds(i * lay.blocks, lay.blocks)])
+            spot = (k * lay.places + g * lay.near) * lay.blocks
+            fetch(held[0].at[pl.ds(g * lay.blocks, lay.blocks)], left.at[pl.ds(spot, lay.blocks)])
+        for i, d in enumerate(lines):
+            fetch(held[1 + i], left.at[pl.ds((k * lay.places + d) * lay.blocks, lay.blocks)])
     total[...] = jnp.zeros_like(total)
     for copy in copies:
         copy.wait()
@@ -215,18 +247,18 @@
             store(chunk).wait()
 
 
-def make_tiles(lay, plan, inputs, outputs, coarse, rounded):
+def make_tiles(lay, plan, inputs, outputs, coarse):
     smem = pl.BlockSpec(memory_space=pltpu.SMEM)
     hbm = pl.BlockSpec(memory_space=pl.ANY)
     vmem = pl.BlockSpec(memory_space=pltpu.VMEM)
     own = lay.places * lay.blocks
     sums = jax.ShapeDtypeStruct((own, lay.side, lay.width), jnp.float32)
-    n_copies = len(inputs) + len(outputs) + len(coarse) * lay.points + len(rounded) * lay.owners
+    n_copies = 2 * len(inputs) + 2 * lay.places + len(coarse) * lay.points
     tiles = (lay.groups * lay.unroll, lay.side, lay.side)
     return pl.pallas_call(
         functools.partial(tiles_kernel, lay),
         out_shape=(sums, sums, jax.ShapeDtypeStruct(tiles, jnp.bfloat16)),
-        in_specs=[smem] * 3 + [hbm] * (len(inputs) + len(outputs) + len(coarse) + len(rounded)),
+        in_specs=[smem] * 3 + [hbm] * (len(inputs) + len(outputs) + len(coarse)),
         out_specs=(vmem, vmem, hbm),
         scratch_shapes=[
             pltpu.VMEM((lay.inputs, lay.pairs, lay.side), jnp.bfloat16),
@@ -240,8 +272,8 @@
             pltpu.SemaphoreType.DMA((lay.groups // chunk_groups,)),
         ],
         compiler_params=pltpu.CompilerParams(vmem_limit_bytes=60 * mib),
-        cost_estimate=pl.CostEstimate(flops=4_000_000_000, bytes_accessed=16_000_000, transcendentals=0),
-    )(*plan, *inputs, *outputs, *coarse, *rounded)
+        cost_estimate=pl.CostEstimate(flops=4_000_000_000, bytes_accessed=50_000_000, transcendentals=0),
+    )(*plan, *inputs, *outputs, *coarse)
 
 
 def apply_kernel(lay, group_start, slot_of, entries, tiles_in, *refs):
@@ -347,52 +379,57 @@
     start = vectors.reshape(blocks, side, width)
     energy = energies.reshape(blocks, side, 1)
     two_owners = lay.owners == 2
-    codes, counts = tile_codes, tile_count
+    n_codes = tile_codes.shape[1]
+    listed = jnp.concatenate([tile_codes, tile_count[:, None]], axis=1)
     if two_owners:
-        codes = jnp.concatenate([tile_codes, along(tile_codes, near)], axis=0)
-        counts = jnp.concatenate([tile_count, along(tile_count, near)], axis=0)
-        starts = jnp.stack([start, along(start, near)])
-        energies_both = jnp.stack([energy, along(energies, near).reshape(blocks, side, 1)])
-    else:
-        starts, energies_both = start[None], energy[None]
+        listed = jnp.concatenate([listed, along(listed, near)], axis=0)
     ids = jnp.stack([row_id // 2, row_id % 2, col_id]).astype(jnp.int32)
-    plan = make_plan(lay, ids, codes, counts, fine_coarse, coarse_slot)
-
-    over_line = [intersections] + [along(intersections, d) for d in range(1, lay.places)]
-    near_coarse = [coarse] + [along(coarse, e) for e in range(1, near)]
+    plan = make_plan(lay, ids, listed[:, :n_codes], listed[:, n_codes], fine_coarse, coarse_slot)
+    joined = jnp.concatenate([intersections, start.astype(jnp.bfloat16)], axis=1)
+
+    partner = [along(joined, near)] if two_owners else []
+    inputs = in_plane(joined)
+    late_coarse, plan = lax.optimization_barrier((coarse, plan))
+    near_coarse = [coarse] + [along(late_coarse, e) for e in range(1, near)]
+    turned, turned_own = turn(lay, joined, *partner)
+    partner, inputs = lax.optimization_barrier((partner, inputs))
+    for part in partner:
+        inputs = inputs + in_plane(part)
+    lines = [along(turned_own, d) for d in lay.line_steps()]
+    held = (inputs, turned, near_coarse, lines)
+    inputs, turned, near_coarse, lines = lax.optimization_barrier(held)
     blocks_coarse = []
     for part in near_coarse:
         blocks_coarse += [part, to_core(part)]
-    inputs = in_plane(intersections)
-    if two_owners:
-        inputs = inputs + in_plane(over_line[near])
-    lefts = [jnp.swapaxes(part, 1, 2) for part in over_line]
+    lefts = [turned] + lines
     lefts = lefts + [to_core(part) for part in lefts]
-    rounded = in_plane(starts.astype(jnp.bfloat16))
-
-    own_sum, other_sum, tiles = make_tiles(lay, plan, inputs, lefts, blocks_coarse, rounded)
+
+    own_sum, other_sum, tiles = make_tiles(lay, plan, inputs, lefts, blocks_coarse)
 
     def over_core(own_part, other_part):
         return (own_part + to_core(other_part)).reshape(lay.places, blocks, side, width)
 
+    def shifted_part(field):
+        return energy * field - spectrum_center * field
+
     merged = over_core(own_sum, other_sum)
     if two_owners:
-        sums = jnp.stack([merged[0], merged[near]])
+        sums = jnp.stack([merged[0] + shifted_part(start), merged[near]])
         for e in range(1, near):
             sent = jnp.stack([merged[e], merged[e ^ near]]).astype(jnp.bfloat16)
             sums = sums + along(sent, e).astype(jnp.float32)
         sums = sums + along(sums.astype(jnp.bfloat16), near)[::-1].astype(jnp.float32)
     else:
-        sums = merged
-
-    firsts = (energies_both * starts + sums - spectrum_center * starts) / spectrum_half
+        sums = merged + shifted_part(start)[None]
+
+    firsts = sums / spectrum_half
+    first = firsts[0]
     own_sum, other_sum = apply_tiles(lay, plan, tiles, in_plane(firsts.astype(jnp.bfloat16)))
     merged = over_core(own_sum, other_sum)
     last = merged[0]
     for d in range(1, lay.places):
         last = last + along(merged[d].astype(jnp.bfloat16), d).astype(jnp.float32)
-    first = firsts[0]
-    second = 2.0 * ((energy * first + last - spectrum_center * first) / spectrum_half) - start
+    second = 2.0 * ((shifted_part(first) + last) / spectrum_half) - start
     return first.reshape(vectors.shape), second.reshape(vectors.shape)
 
 

time: 197 us -> 157 us (0.80); the launches traced: 200 us -> 156 us
  starting transfers between devices: 45.6 us -> 21.7 us
  waiting for transfers between devices: 106 us -> 85.1 us
  local copies, waits for them, and re-layouts: 7.56 us -> 3.36 us
  Pallas kernels: 33.2 us -> 37.1 us
    ppermute x33 -> x26, starting transfers between devices: 45.6 us -> 21.7 us  [move(): return lax.ppermute(array, axes, pairs_list)]
    ppermute x33 -> x26, waiting for transfers between devices: 106 us -> 85.1 us  [move(): return lax.ppermute(array, axes, pairs_list)]
    ppermute x4 -> x0, local copies, waits for them, and re-layouts: 3.72 us -> none  [move(): return lax.ppermute(array, axes, pairs_list)]
  transfers between devices with their start and end apart: 33 -> 26, of which waited for: 18 -> 17; matrix products, arithmetic and copies ran while one was open for 5% -> 3% of each run, Pallas kernels for 4% -> 6%
where the time goes in v2:
time: 157 us; the launch traced here: 156 us
  waiting for transfers between devices  85.1 us (54%)
  Pallas kernels  37.1 us (24%)
  starting transfers between devices  21.7 us (14%)
  other arithmetic  6.65 us (4%)
  local copies, waits for them, and re-layouts  3.36 us (2%)
  between operations  1.66 us (1%)
    ppermute x26, waiting for transfers between devices, move(): return lax.ppermute(array, axes, pairs_list)  85.1 us
    pallas_call x1, Pallas kernels, make_tiles(): pl.pallas_call(functools.partial(tiles_kernel, lay), out_shape=(sums, sum...  21.9 us
    ppermute x26, starting transfers between devices, move(): return lax.ppermute(array, axes, pairs_list)  21.7 us
    pallas_call x1, Pallas kernels, make_plan(): pl.pallas_call(functools.partial(plan_kernel, lay), out_shape=(jax.ShapeD...  8.57 us
    pallas_call x1, Pallas kernels, apply_tiles(): pl.pallas_call(functools.partial(apply_kernel, lay), out_shape=(sums, sum...  6.33 us
  transfers between devices with their start and end apart: 26, of which 17 were waited for; matrix products, arithmetic and copies ran while one was open for 3% of the time, Pallas kernels for 6%

profile of v2, /device:TPU:0, one launch (start us, length us, event | category | flops | bytes accessed | tf_op | source)
XLA Modules:
  0.0 155.5 jit_solution(6637041395133579025)
XLA Ops:
  1.3 0.7 pad_add_fusion.2
  2.0 4.0 %collective-permute-start = (s32[1,97]{1,0:T(1,128)S(1)}, s32[1,97]{1,0:T(1,128)S(1)}, u32[]{:S(2)}, u32[]{:S(2)}) collective-permute-start(s32[1,97]{1,0:T(1,128)S(1)} %pad_add_fusion.2), channel_id=1, source_target_pairs={{0,16},{1,17},{2,18},{3,19},{4,20},{5,21},{6,22},{7,23},{8,24},{9,... | collective-permute-start | bytes 1172 | tf_op jit(solution)/shard_map/ppermute | solution.py:368
  6.0 0.9 convert_element_type.28
  7.0 1.0 pad_maximum_fusion.refs_0_
  8.1 0.7 pad_add_fusion.1.ids
  8.8 0.7 pad_add_fusion
  9.5 0.7 slice_reduce_fusion.counts
  10.3 8.6 %shard_map.95 = (s32[25]{0:T(128)}, s32[24]{0:T(128)}, s32[288]{0:T(512)}) custom-call(s32[3]{0:T(128)} %pad_add_fusion.1.ids, s32[2,96]{1,0:T(2,128)} %bitcast.35, s32[2]{0:T(128)} %slice_reduce_fusion.counts, s32[96]{0:T(128)} %fine.1, s32[8]{0:T(128)} %stored.1), custom_call_target="tpu_custom_call" | custom-call | bytes 20000000 | tf_op jit(solution)/shard_map/pallas_call | solution.py:113
  19.0 0.5 collective-permute-start.4
  19.4 0.5 collective-permute-start.3
  20.0 2.5 %collective-permute-start.2 = (bf16[3,640,128]{2,1,0:T(8,128)(2,1)S(1)}, bf16[3,640,128]{2,1,0:T(8,128)(2,1)S(1)}, u32[]{:S(2)}, u32[]{:S(2)}) collective-permute-start(bf16[3,640,128]{2,1,0:T(8,128)(2,1)S(1)} %pad_maximum_fusion.refs_0_), channel_id=1, source_target_pairs={{0,1},{1,0},{2,3},{3,2},{4,5},{5,4},{6,7},{7,6},{8,9},{9,8},{10,11... | collective-permute-start | bytes 1474568 | tf_op jit(solution)/shard_map/ppermute | solution.py:368
  22.5 9.8 %collective-permute-done.1.refs_1_.refs_4_ = bf16[3,640,128]{2,1,0:T(8,128)(2,1)S(1)} collective-permute-done((bf16[3,640,128]{2,1,0:T(8,128)(2,1)S(1)}, bf16[3,640,128]{2,1,0:T(8,128)(2,1)S(1)}, u32[]{:S(2)}, u32[]{:S(2)}) %collective-permute-start.1) | collective-permute-done | bytes 491552 | tf_op jit(solution)/shard_map/ppermute | solution.py:368
  32.3 0.3 shard_map.96
  32.6 1.2 collective-permute-start.10
  33.8 0.2 collective-permute-done.4.refs_3_
  34.1 9.3 %collective-permute-done.3.refs_2_ = bf16[3,640,128]{2,1,0:T(8,128)(2,1)S(1)} collective-permute-done((bf16[3,640,128]{2,1,0:T(8,128)(2,1)S(1)}, bf16[3,640,128]{2,1,0:T(8,128)(2,1)S(1)}, u32[]{:S(2)}, u32[]{:S(2)}) %collective-permute-start.3) | collective-permute-done | bytes 491552 | tf_op jit(solution)/shard_map/ppermute | solution.py:368
  43.4 0.4 collective-permute-done.2.refs_1_
  43.8 1.2 collective-permute-start.7
  45.0 0.5 collective-permute-start.6
  45.6 1.7 %collective-permute-start.5 = (bf16[3,640,128]{2,1,0:T(8,128)(2,1)S(1)}, bf16[3,640,128]{2,1,0:T(8,128)(2,1)S(1)}, u32[]{:S(2)}, u32[]{:S(2)}) collective-permute-start(bf16[3,640,128]{2,1,0:T(8,128)(2,1)S(1)} %collective-permute-done.1.refs_1_.refs_4_), channel_id=1, source_target_pairs={{0,1},{1,0},{2,3},{3,2},{4,5},{5,4},{6,7},{7,6},{8,9},{9,8},{10,11... | collective-permute-start | bytes 1474568 | tf_op jit(solution)/shard_map/ppermute | solution.py:368
  47.3 7.4 %collective-permute-done.10.refs_10_ = bf16[3,128,512]{2,1,0:T(8,128)(2,1)S(1)} collective-permute-done((bf16[3,128,512]{2,1,0:T(8,128)(2,1)S(1)}, bf16[3,128,512]{2,1,0:T(8,128)(2,1)S(1)}, u32[]{:S(2)}, u32[]{:S(2)}) %collective-permute-start.10) | collective-permute-done | bytes 393248 | tf_op jit(solution)/shard_map/ppermute | solution.py:368
  54.7 15.7 %collective-permute-done.9.refs_9_ = bf16[3,128,512]{2,1,0:T(8,128)(2,1)S(1)} collective-permute-done((bf16[3,128,512]{2,1,0:T(8,128)(2,1)S(1)}, bf16[3,128,512]{2,1,0:T(8,128)(2,1)S(1)}, u32[]{:S(2)}, u32[]{:S(2)}) %collective-permute-start.9) | collective-permute-done | bytes 393248 | tf_op jit(solution)/shard_map/ppermute | solution.py:368
  70.5 0.6 copy-done.14
  71.2 0.2 copy-done.15
  71.4 0.5 collective-permute-start.11
  71.9 0.5 collective-permute-start.13
  72.4 4.0 %collective-permute-done.12.refs_12_ = bf16[3,128,512]{2,1,0:T(8,128)(2,1)S(1)} collective-permute-done((bf16[3,128,512]{2,1,0:T(8,128)(2,1)S(1)}, bf16[3,128,512]{2,1,0:T(8,128)(2,1)S(1)}, u32[]{:S(2)}, u32[]{:S(2)}) %collective-permute-start.12) | collective-permute-done | bytes 393248 | tf_op jit(solution)/shard_map/ppermute | solution.py:368
  76.4 0.6 collective-permute-done.13.refs_13_
  76.9 0.9 copy-done.10
  78.0 21.9 %shard_map.97 = (f32[12,128,128]{2,1,0:T(8,128)}, f32[12,128,128]{2,1,0:T(8,128)}, bf16[288,128,128]{2,1,0:T(8,128)(2,1)}) custom-call(s32[25]{0:T(128)} %get-tuple-element.37.group_start, s32[24]{0:T(128)} %get-tuple-element.38.slot_of, s32[288]{0:T(512)} %get-tuple-element.39.entries, bf16[3,640,128]{2,1,0:T(8,128)(2,1)} %copy-done, ...), custom_call_target="tpu_custom_call" | custom-call | flops 4000000000 | bytes 50000000 | tf_op jit(solution)/shard_map/pallas_call | solution.py:258
  100.0 2.5 %collective-permute-done.16 = f32[12,128,128]{2,1,0:T(8,128)S(1)} collective-permute-done((f32[12,128,128]{2,1,0:T(8,128)}, f32[12,128,128]{2,1,0:T(8,128)S(1)}, u32[]{:S(2)}, u32[]{:S(2)}) %collective-permute-start.16) | collective-permute-done | bytes 786464 | tf_op jit(solution)/shard_map/ppermute | solution.py:368
  102.5 1.3 fusion.10
  104.1 6.8 %collective-permute-done.17 = bf16[2,3,128,128]{3,2,1,0:T(8,128)(2,1)S(1)} collective-permute-done((bf16[2,3,128,128]{3,2,1,0:T(8,128)(2,1)S(1)}, bf16[2,3,128,128]{3,2,1,0:T(8,128)(2,1)S(1)}, u32[]{:S(2)}, u32[]{:S(2)}) %collective-permute-start.17) | collective-permute-done | bytes 196640 | tf_op jit(solution)/shard_map/ppermute | solution.py:368
  110.9 0.8 collective-permute-start.18
  111.8 10.5 %collective-permute-done.18 = bf16[2,3,128,128]{3,2,1,0:T(8,128)(2,1)S(1)} collective-permute-done((bf16[2,3,128,128]{3,2,1,0:T(8,128)(2,1)S(1)}, bf16[2,3,128,128]{3,2,1,0:T(8,128)(2,1)S(1)}, u32[]{:S(2)}, u32[]{:S(2)}) %collective-permute-start.18) | collective-permute-done | bytes 196640 | tf_op jit(solution)/shard_map/ppermute | solution.py:368
  122.4 2.0 %collective-permute-start.20 = (bf16[2,3,128,128]{3,2,1,0:T(8,128)(2,1)S(1)}, bf16[2,3,128,128]{3,2,1,0:T(8,128)(2,1)S(1)}, u32[]{:S(2)}, u32[]{:S(2)}) collective-permute-start(bf16[2,3,128,128]{3,2,1,0:T(8,128)(2,1)S(1)} %get-tuple-element.68.refs_0_), channel_id=1, source_target_pairs={{0,2},{1,3},{2,0},{3,1},{4,6},{5,7},{6,4},{7,5},{8,10},{9,11},{10,... | collective-permute-start | bytes 589832 | tf_op jit(solution)/shard_map/ppermute | solution.py:368
  124.5 1.4 collective-permute-start.19
  125.9 5.2 %collective-permute-done.21.refs_3_ = bf16[2,3,128,128]{3,2,1,0:T(8,128)(2,1)S(1)} collective-permute-done((bf16[2,3,128,128]{3,2,1,0:T(8,128)(2,1)S(1)}, bf16[2,3,128,128]{3,2,1,0:T(8,128)(2,1)S(1)}, u32[]{:S(2)}, u32[]{:S(2)}) %collective-permute-start.21) | collective-permute-done | bytes 196640 | tf_op jit(solution)/shard_map/ppermute | solution.py:368
  131.1 2.4 %collective-permute-done.20.refs_2_ = bf16[2,3,128,128]{3,2,1,0:T(8,128)(2,1)S(1)} collective-permute-done((bf16[2,3,128,128]{3,2,1,0:T(8,128)(2,1)S(1)}, bf16[2,3,128,128]{3,2,1,0:T(8,128)(2,1)S(1)}, u32[]{:S(2)}, u32[]{:S(2)}) %collective-permute-start.20) | collective-permute-done | bytes 196640 | tf_op jit(solution)/shard_map/ppermute | solution.py:368
  133.5 6.3 %shard_map.98 = (f32[12,128,128]{2,1,0:T(8,128)S(1)}, f32[12,128,128]{2,1,0:T(8,128)S(1)}) custom-call(s32[25]{0:T(128)S(1)} %copy-done.3, s32[24]{0:T(128)S(1)} %copy-done.4, s32[288]{0:T(512)S(1)} %copy-done.2, bf16[288,128,128]{2,1,0:T(8,128)(2,1)} %get-tuple-element.63.tiles_in, bf16[2,3,128,128]{3,2,1,0:T(8,128)(2,1)S(1)} %get-tuple-element.68.refs_0_, ...), custom_call_target="tpu_custom_call" | custom-call | flops 400000000 | bytes 4000000 | tf_op jit(solution)/shard_map/pallas_call | solution.py:332
  139.9 2.3 %collective-permute-done.22 = f32[12,128,128]{2,1,0:T(8,128)S(1)} collective-permute-done((f32[12,128,128]{2,1,0:T(8,128)S(1)}, f32[12,128,128]{2,1,0:T(8,128)S(1)}, u32[]{:S(2)}, u32[]{:S(2)}) %collective-permute-start.22) | collective-permute-done | bytes 786464 | tf_op jit(solution)/shard_map/ppermute | solution.py:368
  142.4 0.9 collective-permute-start.25
  143.3 2.6 %collective-permute-start.24 = (bf16[3,128,128]{2,1,0:T(8,128)(2,1)S(1)}, bf16[3,128,128]{2,1,0:T(8,128)(2,1)S(1)}, u32[]{:S(2)}, u32[]{:S(2)}) collective-permute-start(bf16[3,128,128]{2,1,0:T(8,128)(2,1)S(1)} %get-tuple-element.76), channel_id=1, source_target_pairs={{0,16},{1,17},{2,18},{3,19},{4,20},{5,21},{6,22},{7,23},{8,24},{9,... | collective-permute-start | bytes 294920 | tf_op jit(solution)/shard_map/ppermute | solution.py:368
  145.9 0.7 slice.70
  146.6 2.1 %collective-permute-done.23 = bf16[3,128,128]{2,1,0:T(8,128)(2,1)S(1)} collective-permute-done((bf16[3,128,128]{2,1,0:T(8,128)(2,1)S(1)}, bf16[3,128,128]{2,1,0:T(8,128)(2,1)S(1)}, u32[]{:S(2)}, u32[]{:S(2)}) %collective-permute-start.23) | collective-permute-done | bytes 98336 | tf_op jit(solution)/shard_map/ppermute | solution.py:368
  148.7 1.4 collective-permute-done.25
  150.0 4.7 %collective-permute-done.24 = bf16[3,128,128]{2,1,0:T(8,128)(2,1)S(1)} collective-permute-done((bf16[3,128,128]{2,1,0:T(8,128)(2,1)S(1)}, bf16[3,128,128]{2,1,0:T(8,128)(2,1)S(1)}, u32[]{:S(2)}, u32[]{:S(2)}) %collective-permute-start.24) | collective-permute-done | bytes 98336 | tf_op jit(solution)/shard_map/ppermute | solution.py:368
  154.7 0.8 fusion.5
  (66 shorter events, 1.2 us)
Async XLA Ops:
  2.0 6.8 %collective-permute-start = (s32[1,97]{1,0:T(1,128)S(1)}, s32[1,97]{1,0:T(1,128)S(1)}, u32[]{:S(2)}, u32[]{:S(2)}) collective-permute-start(s32[1,97]{1,0:T(1,128)S(1)} %pad_add_fusion.2), channel_id=1, source_target_pairs={{0,16},{1,17},{2,18},{3,19},{4,20},{5,21},{6,22},{7,23},{8,24},{9,... | collective-permute-start | bytes 1172 | tf_op jit(solution)/shard_map/ppermute | solution.py:368
  8.0 69.9 %copy-start = (bf16[3,640,128]{2,1,0:T(8,128)(2,1)}, bf16[3,640,128]{2,1,0:T(8,128)(2,1)S(1)}, u32[]{:S(2)}) copy-start(bf16[3,640,128]{2,1,0:T(8,128)(2,1)S(1)} %pad_maximum_fusion.refs_0_) | copy-start | bytes 1474564
  8.0 24.3 %collective-permute-start.1 = (bf16[3,640,128]{2,1,0:T(8,128)(2,1)S(1)}, bf16[3,640,128]{2,1,0:T(8,128)(2,1)S(1)}, u32[]{:S(2)}, u32[]{:S(2)}) collective-permute-start(bf16[3,640,128]{2,1,0:T(8,128)(2,1)S(1)} %pad_maximum_fusion.refs_0_), channel_id=1, source_target_pairs={{0,16},{1,17},{2,18},{3,19},{4,20},{5,21},{6,22},{7,23},{8,24},{9,... | collective-permute-start | bytes 1474568 | tf_op jit(solution)/shard_map/ppermute | solution.py:368
  9.5 0.8 copy-start.8
  18.9 85.1 %copy-start.6 = (f32[384,128]{1,0:T(8,128)S(1)}, f32[384,128]{1,0:T(8,128)}, u32[]{:S(2)}) copy-start(f32[384,128]{1,0:T(8,128)} %param.8) | copy-start | bytes 589828
  18.9 85.1 %copy-start.7 = (f32[384]{0:T(512)S(1)}, f32[384]{0:T(512)}, u32[]{:S(2)}) copy-start(f32[384]{0:T(512)} %param.9) | copy-start | bytes 4612
  18.9 51.5 %collective-permute-start.8 = (bf16[2,1,512,512]{3,2,1,0:T(8,128)(2,1)}, bf16[2,1,512,512]{3,2,1,0:T(8,128)(2,1)S(1)}, u32[]{:S(2)}, u32[]{:S(2)}) collective-permute-start(bf16[2,1,512,512]{3,2,1,0:T(8,128)(2,1)} %refs_14_), channel_id=1, source_target_pairs={{0,8},{1,9},{2,10},{3,11},{4,12},{5,13},{6,14},{7,15},{8,0},{9,1},... | collective-permute-start | bytes 3145736 | tf_op jit(solution)/shard_map/ppermute | solution.py:368
  19.0 15.1 %collective-permute-start.4 = (bf16[3,640,128]{2,1,0:T(8,128)(2,1)S(1)}, bf16[3,640,128]{2,1,0:T(8,128)(2,1)S(1)}, u32[]{:S(2)}, u32[]{:S(2)}) collective-permute-start(bf16[3,640,128]{2,1,0:T(8,128)(2,1)S(1)} %pad_maximum_fusion.refs_0_), channel_id=1, source_target_pairs={{0,3},{1,2},{2,1},{3,0},{4,7},{5,6},{6,5},{7,4},{8,11},{9,10},{10,... | collective-permute-start | bytes 1474568 | tf_op jit(solution)/shard_map/ppermute | solution.py:368
  19.4 23.9 %collective-permute-start.3 = (bf16[3,640,128]{2,1,0:T(8,128)(2,1)S(1)}, bf16[3,640,128]{2,1,0:T(8,128)(2,1)S(1)}, u32[]{:S(2)}, u32[]{:S(2)}) collective-permute-start(bf16[3,640,128]{2,1,0:T(8,128)(2,1)S(1)} %pad_maximum_fusion.refs_0_), channel_id=1, source_target_pairs={{0,2},{1,3},{2,0},{3,1},{4,6},{5,7},{6,4},{7,5},{8,10},{9,11},{10,... | collective-permute-start | bytes 1474568 | tf_op jit(solution)/shard_map/ppermute | solution.py:368
  20.0 23.8 %collective-permute-start.2 = (bf16[3,640,128]{2,1,0:T(8,128)(2,1)S(1)}, bf16[3,640,128]{2,1,0:T(8,128)(2,1)S(1)}, u32[]{:S(2)}, u32[]{:S(2)}) collective-permute-start(bf16[3,640,128]{2,1,0:T(8,128)(2,1)S(1)} %pad_maximum_fusion.refs_0_), channel_id=1, source_target_pairs={{0,1},{1,0},{2,3},{3,2},{4,5},{5,4},{6,7},{7,6},{8,9},{9,8},{10,11... | collective-permute-start | bytes 1474568 | tf_op jit(solution)/shard_map/ppermute | solution.py:368
  32.3 45.6 %copy-start.1 = (bf16[3,640,128]{2,1,0:T(8,128)(2,1)}, bf16[3,640,128]{2,1,0:T(8,128)(2,1)S(1)}, u32[]{:S(2)}) copy-start(bf16[3,640,128]{2,1,0:T(8,128)(2,1)S(1)} %collective-permute-done.1.refs_1_.refs_4_) | copy-start | bytes 1474564
  32.6 45.4 %copy-start.5 = (bf16[6,128,512]{2,1,0:T(8,128)(2,1)}, bf16[6,128,512]{2,1,0:T(8,128)(2,1)S(1)}, u32[]{:S(2)}) copy-start(bf16[6,128,512]{2,1,0:T(8,128)(2,1)S(1)} %get-tuple-element.56.refs_8_) | copy-start | bytes 2359300
  32.6 22.1 %collective-permute-start.10 = (bf16[3,128,512]{2,1,0:T(8,128)(2,1)S(1)}, bf16[3,128,512]{2,1,0:T(8,128)(2,1)S(1)}, u32[]{:S(2)}, u32[]{:S(2)}) collective-permute-start(bf16[3,128,512]{2,1,0:T(8,128)(2,1)S(1)} %get-tuple-element.47), channel_id=1, source_target_pairs={{0,24},{1,25},{2,26},{3,27},{4,28},{5,29},{6,30},{7,31},{8,16},{9,... | collective-permute-start | bytes 1179656 | tf_op jit(solution)/shard_map/ppermute | solution.py:368
  34.1 43.9 %copy-start.11 = (bf16[3,640,128]{2,1,0:T(8,128)(2,1)}, bf16[3,640,128]{2,1,0:T(8,128)(2,1)S(1)}, u32[]{:S(2)}) copy-start(bf16[3,640,128]{2,1,0:T(8,128)(2,1)S(1)} %collective-permute-done.4.refs_3_) | copy-start | bytes 1474564
  43.4 34.6 %copy-start.12 = (bf16[3,640,128]{2,1,0:T(8,128)(2,1)}, bf16[3,640,128]{2,1,0:T(8,128)(2,1)S(1)}, u32[]{:S(2)}) copy-start(bf16[3,640,128]{2,1,0:T(8,128)(2,1)S(1)} %collective-permute-done.3.refs_2_) | copy-start | bytes 1474564
  43.8 34.1 %copy-start.13 = (bf16[3,640,128]{2,1,0:T(8,128)(2,1)}, bf16[3,640,128]{2,1,0:T(8,128)(2,1)S(1)}, u32[]{:S(2)}) copy-start(bf16[3,640,128]{2,1,0:T(8,128)(2,1)S(1)} %collective-permute-done.2.refs_1_) | copy-start | bytes 1474564
  43.8 26.6 %collective-permute-start.7 = (bf16[3,640,128]{2,1,0:T(8,128)(2,1)S(1)}, bf16[3,640,128]{2,1,0:T(8,128)(2,1)S(1)}, u32[]{:S(2)}, u32[]{:S(2)}) collective-permute-start(bf16[3,640,128]{2,1,0:T(8,128)(2,1)S(1)} %collective-permute-done.1.refs_1_.refs_4_), channel_id=1, source_target_pairs={{0,3},{1,2},{2,1},{3,0},{4,7},{5,6},{6,5},{7,4},{8,11},{9,10},{10,... | collective-permute-start | bytes 1474568 | tf_op jit(solution)/shard_map/ppermute | solution.py:368
  45.0 25.3 %collective-permute-start.6 = (bf16[3,640,128]{2,1,0:T(8,128)(2,1)S(1)}, bf16[3,640,128]{2,1,0:T(8,128)(2,1)S(1)}, u32[]{:S(2)}, u32[]{:S(2)}) collective-permute-start(bf16[3,640,128]{2,1,0:T(8,128)(2,1)S(1)} %collective-permute-done.1.refs_1_.refs_4_), channel_id=1, source_target_pairs={{0,2},{1,3},{2,0},{3,1},{4,6},{5,7},{6,4},{7,5},{8,10},{9,11},{10,... | collective-permute-start | bytes 1474568 | tf_op jit(solution)/shard_map/ppermute | solution.py:368
  45.6 24.8 %collective-permute-start.5 = (bf16[3,640,128]{2,1,0:T(8,128)(2,1)S(1)}, bf16[3,640,128]{2,1,0:T(8,128)(2,1)S(1)}, u32[]{:S(2)}, u32[]{:S(2)}) collective-permute-start(bf16[3,640,128]{2,1,0:T(8,128)(2,1)S(1)} %collective-permute-done.1.refs_1_.refs_4_), channel_id=1, source_target_pairs={{0,1},{1,0},{2,3},{3,2},{4,5},{5,4},{6,7},{7,6},{8,9},{9,8},{10,11... | collective-permute-start | bytes 1474568 | tf_op jit(solution)/shard_map/ppermute | solution.py:368
  54.7 23.2 %copy-start.17 = (bf16[3,128,512]{2,1,0:T(8,128)(2,1)}, bf16[3,128,512]{2,1,0:T(8,128)(2,1)S(1)}, u32[]{:S(2)}) copy-start(bf16[3,128,512]{2,1,0:T(8,128)(2,1)S(1)} %collective-permute-done.10.refs_10_) | copy-start | bytes 1179652
  54.7 15.7 %collective-permute-start.9 = (bf16[3,128,512]{2,1,0:T(8,128)(2,1)S(1)}, bf16[3,128,512]{2,1,0:T(8,128)(2,1)S(1)}, u32[]{:S(2)}, u32[]{:S(2)}) collective-permute-start(bf16[3,128,512]{2,1,0:T(8,128)(2,1)S(1)} %get-tuple-element.47), channel_id=1, source_target_pairs={{0,8},{1,9},{2,10},{3,11},{4,12},{5,13},{6,14},{7,15},{8,0},{9,1},... | collective-permute-start | bytes 1179656 | tf_op jit(solution)/shard_map/ppermute | solution.py:368
  70.4 7.5 %copy-start.18 = (bf16[3,128,512]{2,1,0:T(8,128)(2,1)}, bf16[3,128,512]{2,1,0:T(8,128)(2,1)S(1)}, u32[]{:S(2)}) copy-start(bf16[3,128,512]{2,1,0:T(8,128)(2,1)S(1)} %collective-permute-done.9.refs_9_) | copy-start | bytes 1179652
  70.4 0.8 copy-start.14
  70.4 1.0 copy-start.15
  70.4 7.5 %copy-start.16 = (bf16[3,640,128]{2,1,0:T(8,128)(2,1)}, bf16[3,640,128]{2,1,0:T(8,128)(2,1)S(1)}, u32[]{:S(2)}) copy-start(bf16[3,640,128]{2,1,0:T(8,128)(2,1)S(1)} %collective-permute-done.5.refs_5_) | copy-start | bytes 1474564
  70.4 7.6 %copy-start.9 = (bf16[2,1,512,512]{3,2,1,0:T(8,128)(2,1)}, bf16[2,1,512,512]{3,2,1,0:T(8,128)(2,1)S(1)}, u32[]{:S(2)}) copy-start(bf16[2,1,512,512]{3,2,1,0:T(8,128)(2,1)S(1)} %collective-permute-done.8.refs_16_) | copy-start | bytes 3145732
  70.4 63.1 %copy-start.2 = (s32[288]{0:T(512)S(1)}, s32[288]{0:T(512)}, u32[]{:S(2)}) copy-start(s32[288]{0:T(512)} %get-tuple-element.39.entries) | copy-start | bytes 3460
  70.4 63.0 %copy-start.3 = (s32[25]{0:T(128)S(1)}, s32[25]{0:T(128)}, u32[]{:S(2)}) copy-start(s32[25]{0:T(128)} %get-tuple-element.37.group_start) | copy-start | bytes 304
  70.4 63.0 %copy-start.4 = (s32[24]{0:T(128)S(1)}, s32[24]{0:T(128)}, u32[]{:S(2)}) copy-start(s32[24]{0:T(128)} %get-tuple-element.38.slot_of) | copy-start | bytes 292
  70.4 7.4 %collective-permute-start.14 = (bf16[2,1,512,512]{3,2,1,0:T(8,128)(2,1)}, bf16[2,1,512,512]{3,2,1,0:T(8,128)(2,1)}, u32[]{:S(2)}, u32[]{:S(2)}) collective-permute-start(bf16[2,1,512,512]{3,2,1,0:T(8,128)(2,1)} %refs_14_), channel_id=1, source_target_pairs={{0,4},{1,5},{2,6},{3,7},{4,0},{5,1},{6,2},{7,3},{8,12},{9,13},{10,... | collective-permute-start | bytes 3145736 | tf_op jit(solution)/shard_map/ppermute | solution.py:368
  71.4 6.6 %collective-permute-start.15 = (bf16[2,1,512,512]{3,2,1,0:T(8,128)(2,1)S(1)}, bf16[2,1,512,512]{3,2,1,0:T(8,128)(2,1)}, u32[]{:S(2)}, u32[]{:S(2)}) collective-permute-start(bf16[2,1,512,512]{3,2,1,0:T(8,128)(2,1)S(1)} %collective-permute-done.8.refs_16_), channel_id=1, source_target_pairs={{0,4},{1,5},{2,6},{3,7},{4,0},{5,1},{6,2},{7,3},{8,12},{9,13},{10,... | collective-permute-start | bytes 3145736 | tf_op jit(solution)/shard_map/ppermute | solution.py:368
  71.4 5.6 %collective-permute-start.11 = (bf16[6,128,512]{2,1,0:T(8,128)(2,1)S(1)}, bf16[6,128,512]{2,1,0:T(8,128)(2,1)S(1)}, u32[]{:S(2)}, u32[]{:S(2)}) collective-permute-start(bf16[6,128,512]{2,1,0:T(8,128)(2,1)S(1)} %get-tuple-element.56.refs_8_), channel_id=1, source_target_pairs={{0,4},{1,5},{2,6},{3,7},{4,0},{5,1},{6,2},{7,3},{8,12},{9,13},{10,... | collective-permute-start | bytes 2359304 | tf_op jit(solution)/shard_map/ppermute | solution.py:368
  71.9 4.5 %collective-permute-start.12 = (bf16[3,128,512]{2,1,0:T(8,128)(2,1)S(1)}, bf16[3,128,512]{2,1,0:T(8,128)(2,1)S(1)}, u32[]{:S(2)}, u32[]{:S(2)}) collective-permute-start(bf16[3,128,512]{2,1,0:T(8,128)(2,1)S(1)} %collective-permute-done.9.refs_9_), channel_id=1, source_target_pairs={{0,4},{1,5},{2,6},{3,7},{4,0},{5,1},{6,2},{7,3},{8,12},{9,13},{10,... | collective-permute-start | bytes 1179656 | tf_op jit(solution)/shard_map/ppermute | solution.py:368
  71.9 5.1 %collective-permute-start.13 = (bf16[3,128,512]{2,1,0:T(8,128)(2,1)S(1)}, bf16[3,128,512]{2,1,0:T(8,128)(2,1)S(1)}, u32[]{:S(2)}, u32[]{:S(2)}) collective-permute-start(bf16[3,128,512]{2,1,0:T(8,128)(2,1)S(1)} %collective-permute-done.10.refs_10_), channel_id=1, source_target_pairs={{0,4},{1,5},{2,6},{3,7},{4,0},{5,1},{6,2},{7,3},{8,12},{9,13},{10,... | collective-permute-start | bytes 1179656 | tf_op jit(solution)/shard_map/ppermute | solution.py:368
  76.4 1.5 copy-start.19
  76.9 1.0 copy-start.20
  76.9 0.9 copy-start.10
  99.9 2.6 %collective-permute-start.16 = (f32[12,128,128]{2,1,0:T(8,128)}, f32[12,128,128]{2,1,0:T(8,128)S(1)}, u32[]{:S(2)}, u32[]{:S(2)}) collective-permute-start(f32[12,128,128]{2,1,0:T(8,128)} %get-tuple-element.62), channel_id=1, source_target_pairs={{0,4},{1,5},{2,6},{3,7},{4,0},{5,1},{6,2},{7,3},{8,12},{9,13},{10,... | collective-permute-start | bytes 2359304 | tf_op jit(solution)/shard_map/ppermute | solution.py:368
  103.9 7.0 %collective-permute-start.17 = (bf16[2,3,128,128]{3,2,1,0:T(8,128)(2,1)S(1)}, bf16[2,3,128,128]{3,2,1,0:T(8,128)(2,1)S(1)}, u32[]{:S(2)}, u32[]{:S(2)}) collective-permute-start(bf16[2,3,128,128]{3,2,1,0:T(8,128)(2,1)S(1)} %pad_maximum_fusion.1), channel_id=1, source_target_pairs={{0,8},{1,9},{2,10},{3,11},{4,12},{5,13},{6,14},{7,15},{8,0},{9,1},... | collective-permute-start | bytes 589832 | tf_op jit(solution)/shard_map/ppermute | solution.py:368
  110.9 11.3 %collective-permute-start.18 = (bf16[2,3,128,128]{3,2,1,0:T(8,128)(2,1)S(1)}, bf16[2,3,128,128]{3,2,1,0:T(8,128)(2,1)S(1)}, u32[]{:S(2)}, u32[]{:S(2)}) collective-permute-start(bf16[2,3,128,128]{3,2,1,0:T(8,128)(2,1)S(1)} %fusion), channel_id=1, source_target_pairs={{0,16},{1,17},{2,18},{3,19},{4,20},{5,21},{6,22},{7,23},{8,24},{9,... | collective-permute-start | bytes 589832 | tf_op jit(solution)/shard_map/ppermute | solution.py:368
  122.3 8.8 %collective-permute-start.21 = (bf16[2,3,128,128]{3,2,1,0:T(8,128)(2,1)S(1)}, bf16[2,3,128,128]{3,2,1,0:T(8,128)(2,1)S(1)}, u32[]{:S(2)}, u32[]{:S(2)}) collective-permute-start(bf16[2,3,128,128]{3,2,1,0:T(8,128)(2,1)S(1)} %get-tuple-element.68.refs_0_), channel_id=1, source_target_pairs={{0,3},{1,2},{2,1},{3,0},{4,7},{5,6},{6,5},{7,4},{8,11},{9,10},{10,... | collective-permute-start | bytes 589832 | tf_op jit(solution)/shard_map/ppermute | solution.py:368
  122.4 11.1 %collective-permute-start.20 = (bf16[2,3,128,128]{3,2,1,0:T(8,128)(2,1)S(1)}, bf16[2,3,128,128]{3,2,1,0:T(8,128)(2,1)S(1)}, u32[]{:S(2)}, u32[]{:S(2)}) collective-permute-start(bf16[2,3,128,128]{3,2,1,0:T(8,128)(2,1)S(1)} %get-tuple-element.68.refs_0_), channel_id=1, source_target_pairs={{0,2},{1,3},{2,0},{3,1},{4,6},{5,7},{6,4},{7,5},{8,10},{9,11},{10,... | collective-permute-start | bytes 589832 | tf_op jit(solution)/shard_map/ppermute | solution.py:368
  124.5 9.0 %collective-permute-start.19 = (bf16[2,3,128,128]{3,2,1,0:T(8,128)(2,1)S(1)}, bf16[2,3,128,128]{3,2,1,0:T(8,128)(2,1)S(1)}, u32[]{:S(2)}, u32[]{:S(2)}) collective-permute-start(bf16[2,3,128,128]{3,2,1,0:T(8,128)(2,1)S(1)} %get-tuple-element.68.refs_0_), channel_id=1, source_target_pairs={{0,1},{1,0},{2,3},{3,2},{4,5},{5,4},{6,7},{7,6},{8,9},{9,8},{10,11... | collective-permute-start | bytes 589832 | tf_op jit(solution)/shard_map/ppermute | solution.py:368
  139.8 2.4 %collective-permute-start.22 = (f32[12,128,128]{2,1,0:T(8,128)S(1)}, f32[12,128,128]{2,1,0:T(8,128)S(1)}, u32[]{:S(2)}, u32[]{:S(2)}) collective-permute-start(f32[12,128,128]{2,1,0:T(8,128)S(1)} %get-tuple-element.65), channel_id=1, source_target_pairs={{0,4},{1,5},{2,6},{3,7},{4,0},{5,1},{6,2},{7,3},{8,12},{9,13},{10,... | collective-permute-start | bytes 2359304 | tf_op jit(solution)/shard_map/ppermute | solution.py:368
  142.3 6.3 %collective-permute-start.23 = (bf16[3,128,128]{2,1,0:T(8,128)(2,1)S(1)}, bf16[3,128,128]{2,1,0:T(8,128)(2,1)S(1)}, u32[]{:S(2)}, u32[]{:S(2)}) collective-permute-start(bf16[3,128,128]{2,1,0:T(8,128)(2,1)S(1)} %get-tuple-element.74), channel_id=1, source_target_pairs={{0,8},{1,9},{2,10},{3,11},{4,12},{5,13},{6,14},{7,15},{8,0},{9,1},... | collective-permute-start | bytes 294920 | tf_op jit(solution)/shard_map/ppermute | solution.py:368
  142.4 7.6 %collective-permute-start.25 = (bf16[3,128,128]{2,1,0:T(8,128)(2,1)S(1)}, bf16[3,128,128]{2,1,0:T(8,128)(2,1)S(1)}, u32[]{:S(2)}, u32[]{:S(2)}) collective-permute-start(bf16[3,128,128]{2,1,0:T(8,128)(2,1)S(1)} %get-tuple-element.75), channel_id=1, source_target_pairs={{0,24},{1,25},{2,26},{3,27},{4,28},{5,29},{6,30},{7,31},{8,16},{9,... | collective-permute-start | bytes 294920 | tf_op jit(solution)/shard_map/ppermute | solution.py:368
  143.3 11.5 %collective-permute-start.24 = (bf16[3,128,128]{2,1,0:T(8,128)(2,1)S(1)}, bf16[3,128,128]{2,1,0:T(8,128)(2,1)S(1)}, u32[]{:S(2)}, u32[]{:S(2)}) collective-permute-start(bf16[3,128,128]{2,1,0:T(8,128)(2,1)S(1)} %get-tuple-element.76), channel_id=1, source_target_pairs={{0,16},{1,17},{2,18},{3,19},{4,20},{5,21},{6,22},{7,23},{8,24},{9,... | collective-permute-start | bytes 294920 | tf_op jit(solution)/shard_map/ppermute | solution.py:368

commit v3 on v2

v3 whole, which is shorter than its diff:
```python
import functools

import jax
import jax.numpy as jnp
from jax import lax
from jax.experimental import pallas as pl
from jax.experimental.pallas import tpu as pltpu
from jax.sharding import PartitionSpec as P

spectrum_center = 2.0
spectrum_half = 3.0
axes = ("row", "col")
chunk_groups = 8
mib = 1 << 20


class Layout:
    def __init__(self, rows, cols, blocks, pairs, side, width, points, slots_dev, tile_max, unroll):
        self.rows, self.cols, self.blocks = rows, cols, blocks
        self.pairs, self.side, self.width = pairs, side, width
        self.points, self.slots_dev, self.tile_max = points, slots_dev, tile_max
        self.places = rows // 2
        self.near = max(self.places // 2, 1)
        self.owners = 2 if self.places > 1 else 1
        self.spread = cols * blocks
        self.inputs = self.owners * self.spread
        self.outputs = rows * blocks
        self.slots = 2 * self.near * slots_dev
        self.unroll = unroll
        self.vmem = (32 if unroll > 1 else 60) * mib
        most = self.owners * tile_max + self.inputs * (unroll - 1) + unroll
        self.groups = -(-most // (unroll * chunk_groups)) * chunk_groups

    def line_steps(self):
        return [d for d in range(1, self.places) if d != self.near]


def plan_kernel(lay, ids, listed, fine, stored, slot_of, valid, sizes, group_input, entries, fill):
    place, core, col = ids[0], ids[1], ids[2]
    half = lax.div(place, lay.near)
    blank = lay.outputs * lay.points

    for owner in range(lay.owners):

        def examine(i, found):
            p = owner * lay.spread + i
            from_col = lax.bitwise_xor(lax.div(i, lay.blocks), col)
            from_place = lax.bitwise_xor(place, owner * lay.near)
            block = ((from_place * 2 + core) * lay.cols + from_col) * lay.blocks + lax.rem(i, lay.blocks)
            position = stored[fine[block]]
            at_row = lax.div(position, lay.slots_dev)
            at_place, at_core = lax.div(at_row, 2), lax.rem(at_row, 2)
            slot = (lax.bitwise_xor(at_place, place) * 2 + lax.bitwise_xor(at_core, core)) * lay.slots_dev
            slot = slot + lax.rem(position, lay.slots_dev)
            here = lax.div(at_place, lay.near) == half
            slot_of[p] = jnp.where(here, slot, -1)
            valid[owner * (lay.spread + 1) + found] = i
            fill[p] = 0
            return found + here.astype(jnp.int32)

        sizes[1 + owner] = lax.fori_loop(0, lay.spread, examine, 0)

    def input_of(owner, code):
        j = lax.rem(code, lay.spread)
        from_col = lax.bitwise_xor(lax.div(j, lay.blocks), col)
        return owner * lay.spread + from_col * lay.blocks + lax.rem(j, lay.blocks)

    for owner in range(lay.owners):

        def count(i, carry):
            p = input_of(owner, listed[owner, i])
            fill[p] = fill[p] + 1
            return carry

        lax.fori_loop(0, listed[owner, lay.tile_max], count, 0)

    group_input[0] = 0

    def place_groups(p, start):
        used = jnp.where(slot_of[p] >= 0, fill[p], 0)
        fill[p] = start * lay.unroll
        end = start + lax.div(used + (lay.unroll - 1), lay.unroll)

        def name(group, carry):
            group_input[group] = p
            return carry

        lax.fori_loop(start, end, name, 0)
        return end

    total = lax.fori_loop(0, lay.inputs, place_groups, 1)
    sizes[0] = total

    def clear(i, carry):
        entries[i] = blank
        return carry

    lax.fori_loop(0, total * lay.unroll, clear, 0)

    for owner in range(lay.owners):

        def put(i, carry):
            code = listed[owner, i]
            p = input_of(owner, code)

            @pl.when(slot_of[p] >= 0)
            def _():
                out = lax.div(code, lay.spread)
                at_row = lax.div(out, lay.blocks)
                within = lax.rem(out, lay.blocks)
                far = lax.bitwise_xor(lax.div(at_row, 2), place)
                other = lax.bitwise_xor(lax.rem(at_row, 2), core)
                q = (other * lay.places + far) * lay.blocks + within
                a = fine[(at_row * lay.cols + col) * lay.blocks + within] - col * lay.points
                spot = fill[p]
                entries[spot] = q * lay.points + a
                fill[p] = spot + 1

            return carry

        lax.fori_loop(0, listed[owner, lay.tile_max], put, 0)


def make_plan(lay, ids, listed, fine, stored):
    smem = pl.BlockSpec(memory_space=pltpu.SMEM)
    lengths = (
        lay.inputs,
        lay.owners * (lay.spread + 1),
        1 + lay.owners,
        lay.groups,
        lay.groups * lay.unroll,
    )
    return pl.pallas_call(
        functools.partial(plan_kernel, lay),
        out_shape=tuple(jax.ShapeDtypeStruct((n,), jnp.int32) for n in lengths),
        in_specs=[smem] * 4,
        out_specs=(smem,) * 5,
        scratch_shapes=[pltpu.SMEM((lay.inputs,), jnp.int32)],
        cost_estimate=pl.CostEstimate(flops=0, bytes_accessed=20_000_000, transcendentals=0),
    )(ids, listed, fine, stored)


def project_kernel(lay, owner, slot_of, valid, sizes, *refs):
    n_coarse = 2 * (2 * lay.near - 1)
    given_in, given_coarse = refs[: lay.cols], list(refs[lay.cols : lay.cols + n_coarse])
    out, right, blocks, sems = refs[lay.cols + n_coarse :]
    copies = []

    def fetch(source, target):
        copies.append(pltpu.make_async_copy(source, target, sems.at[len(copies)]))
        copies[-1].start()

    for i in range(lay.cols):
        fetch(given_in[i].at[:, pl.ds(0, lay.pairs)], right.at[pl.ds(i * lay.blocks, lay.blocks)])
    for i in range(2 * lay.near):
        first = given_coarse.pop(0)
        for a in range(first.shape[0]):
            fetch(first.at[a], blocks.at[a, pl.ds(i * lay.slots_dev, lay.slots_dev)])
        if i < 2:
            continue
        rest = given_coarse.pop(0)
        for a in range(1, lay.points):
            for at in range(lay.slots_dev):
                row = lay.blocks * lay.side + ((a - 1) * lay.slots_dev + at) * lay.pairs
                fetch(rest.at[pl.ds(row, lay.pairs)], blocks.at[a, i * lay.slots_dev + at])
    for copy in copies:
        copy.wait()
    found = sizes[1 + owner]

    def visit(step, carry):
        for lane in range(2):
            i = valid[owner * (lay.spread + 1) + jnp.minimum(2 * step + lane, found - 1)]
            slot = slot_of[owner * lay.spread + i]
            for a in range(lay.points):
                out[i, :, a * lay.side : (a + 1) * lay.side] = jnp.dot(
                    blocks[a, slot], right[i], preferred_element_type=jnp.float32
                ).astype(jnp.bfloat16)
        return carry

    lax.fori_loop(0, lax.div(found + 1, 2), visit, 0)


def project(lay, owner, plan, inputs, coarse):
    smem = pl.BlockSpec(memory_space=pltpu.SMEM)
    hbm = pl.BlockSpec(memory_space=pl.ANY)
    shape = (lay.spread, lay.pairs, lay.points * lay.side)
    return pl.pallas_call(
        functools.partial(project_kernel, lay, owner),
        out_shape=jax.ShapeDtypeStruct(shape, jnp.bfloat16),
        in_specs=[smem] * 3 + [hbm] * (len(inputs) + len(coarse)),
        out_specs=pl.BlockSpec(memory_space=pltpu.VMEM),
        scratch_shapes=[
            pltpu.VMEM((lay.spread, lay.pairs, lay.side), jnp.bfloat16),
            pltpu.VMEM((lay.points, lay.slots, lay.pairs, lay.pairs), jnp.bfloat16),
            pltpu.SemaphoreType.DMA((len(inputs) + lay.slots * lay.points,)),
        ],
        compiler_params=pltpu.CompilerParams(vmem_limit_bytes=32 * mib),
        cost_estimate=pl.CostEstimate(flops=1_000_000_000, bytes_accessed=20_000_000, transcendentals=0),
    )(*plan[:3], *inputs, *coarse)


def add_products(lay, group, group_input, entries, tiles, rounded, total):
    vector = rounded[group_input[group]]
    products = [
        jnp.dot(tiles[group * lay.unroll + i], vector, preferred_element_type=jnp.float32)
        for i in range(lay.unroll)
    ]
    for i in range(lay.unroll):
        q = lax.div(entries[group * lay.unroll + i], lay.points)
        total[q] = total[q] + products[i]


def turn_kernel(lay, *refs):
    given, rest, outs = refs[: lay.owners], refs[lay.owners], refs[lay.owners + 1 :]
    for g in range(lay.owners):
        for t in range(lay.blocks):
            turned = given[g][t, 0 : lay.pairs, :].T
            outs[0][g * lay.blocks + t] = turned
            if g == 0:
                outs[1][t] = turned
                outs[2][t * lay.side : (t + 1) * lay.side, :] = turned
    outs[2][lay.blocks * lay.side :, :] = rest[...]


def turn(lay, rest, *given):
    vmem = pl.BlockSpec(memory_space=pltpu.VMEM)
    return pl.pallas_call(
        functools.partial(turn_kernel, lay),
        out_shape=(
            jax.ShapeDtypeStruct((lay.owners * lay.blocks, lay.side, lay.pairs), jnp.bfloat16),
            jax.ShapeDtypeStruct((lay.blocks, lay.side, lay.pairs), jnp.bfloat16),
            jax.ShapeDtypeStruct((lay.blocks * lay.side + rest.shape[0], lay.pairs), jnp.bfloat16),
        ),
        in_specs=[vmem] * (lay.owners + 1),
        out_specs=(vmem,) * 3,
        compiler_params=pltpu.CompilerParams(vmem_limit_bytes=16 * mib),
        cost_estimate=pl.CostEstimate(flops=1_000_000, bytes_accessed=3_000_000, transcendentals=0),
    )(*given, rest)


def tiles_kernel(lay, sizes, group_input, entries, *refs):
    n_in = lay.owners * lay.cols
    lines = lay.line_steps()
    refs = list(refs)
    given_in = [refs.pop(0) for _ in range(n_in)]
    given_out = [refs.pop(0) for _ in range(2 * (1 + len(lines)))]
    given_projected = [refs.pop(0) for _ in range(lay.owners)]
    own_sum, other_sum, tiles_out = refs[:3]
    left, projected, rounded, tiles, total, sems, out_sems = refs[3:]
    copies = []

    def fetch(source, target):
        copies.append(pltpu.make_async_copy(source, target, sems.at[len(copies)]))
        copies[-1].start()

    for k in range(2):
        held = given_out[k * (1 + len(lines)) :]
        for g in range(lay.owners):
            spot = (k * lay.places + g * lay.near) * lay.blocks
            fetch(held[0].at[pl.ds(g * lay.blocks, lay.blocks)], left.at[pl.ds(spot, lay.blocks)])
        for i, d in enumerate(lines):
            spot = (k * lay.places + d) * lay.blocks
            if d > lay.near:
                fetch(held[1 + i], left.at[pl.ds(spot, lay.blocks)])
            else:
                for t in range(lay.blocks):
                    fetch(held[1 + i].at[pl.ds(t * lay.side, lay.side)], left.at[spot + t])
    for g in range(lay.owners):
        fetch(given_projected[g], projected.at[pl.ds(g * lay.spread, lay.spread)])
    for i in range(n_in):
        part = pl.ds(i * lay.blocks, lay.blocks)
        fetch(given_in[i].at[:, pl.ds(lay.pairs, lay.side)], rounded.at[part])
    total[...] = jnp.zeros_like(total)
    for copy in copies:
        copy.wait()
    used = sizes[0]

    def group_step(group, carry):
        p = group_input[group]
        for i in range(lay.unroll):
            entry = entries[group * lay.unroll + i]
            q = jnp.minimum(lax.div(entry, lay.points), lay.outputs - 1)
            a = lax.rem(entry, lay.points)
            both = jnp.dot(left[q], projected[p], preferred_element_type=jnp.float32)
            tile = both[:, : lay.side]
            for b in range(1, lay.points):
                tile = jnp.where(a == b, both[:, b * lay.side : (b + 1) * lay.side], tile)
            tiles[group * lay.unroll + i] = tile.astype(jnp.bfloat16)
        add_products(lay, group - 1, group_input, entries, tiles, rounded, total)
        return carry

    lax.fori_loop(1, used, group_step, 0)
    span = chunk_groups * lay.unroll

    def store(chunk):
        part = pl.ds(chunk * span, span)
        return pltpu.make_async_copy(tiles.at[part], tiles_out.at[part], out_sems.at[chunk])

    for chunk in range(lay.groups // chunk_groups):

        @pl.when(used > chunk * chunk_groups)
        def _():
            store(chunk).start()

    add_products(lay, used - 1, group_input, entries, tiles, rounded, total)
    own = lay.places * lay.blocks
    own_sum[...] = total[0:own]
    other_sum[...] = total[own : 2 * own]
    for chunk in range(lay.groups // chunk_groups):

        @pl.when(used > chunk * chunk_groups)
        def _():
            store(chunk).wait()


def make_tiles(lay, plan, inputs, outputs, projected):
    smem = pl.BlockSpec(memory_space=pltpu.SMEM)
    hbm = pl.BlockSpec(memory_space=pl.ANY)
    vmem = pl.BlockSpec(memory_space=pltpu.VMEM)
    own = lay.places * lay.blocks
    sums = jax.ShapeDtypeStruct((own, lay.side, lay.width), jnp.float32)
    n_copies = len(inputs) + 2 * lay.places * lay.blocks + len(projected)
    tiles = (lay.groups * lay.unroll, lay.side, lay.side)
    return pl.pallas_call(
        functools.partial(tiles_kernel, lay),
        out_shape=(sums, sums, jax.ShapeDtypeStruct(tiles, jnp.bfloat16)),
        in_specs=[smem] * 3 + [hbm] * (len(inputs) + len(outputs) + len(projected)),
        out_specs=(vmem, vmem, hbm),
        scratch_shapes=[
            pltpu.VMEM((lay.outputs, lay.side, lay.pairs), jnp.bfloat16),
            pltpu.VMEM((lay.inputs, lay.pairs, lay.points * lay.side), jnp.bfloat16),
            pltpu.VMEM((lay.inputs, lay.side, lay.width), jnp.bfloat16),
            pltpu.VMEM(tiles, jnp.bfloat16),
            pltpu.VMEM((lay.outputs + 1, lay.side, lay.width), jnp.float32),
            pltpu.SemaphoreType.DMA((n_copies,)),
            pltpu.SemaphoreType.DMA((lay.groups // chunk_groups,)),
        ],
        compiler_params=pltpu.CompilerParams(vmem_limit_bytes=lay.vmem),
        cost_estimate=pl.CostEstimate(flops=4_000_000_000, bytes_accessed=30_000_000, transcendentals=0),
    )(plan[2], *plan[3:], *inputs, *outputs, *projected)


def apply_kernel(lay, sizes, group_input, entries, tiles_in, *refs):
    given_vec = refs[: lay.cols]
    own_sum, other_sum = refs[lay.cols : lay.cols + 2]
    rounded, tiles, total, sems, out_sems = refs[lay.cols + 2 :]
    used = sizes[0]
    span = chunk_groups * lay.unroll

    def load(chunk):
        part = pl.ds(chunk * span, span)
        return pltpu.make_async_copy(tiles_in.at[part], tiles.at[part], out_sems.at[chunk])

    for chunk in range(lay.groups // chunk_groups):

        @pl.when(used > chunk * chunk_groups)
        def _():
            load(chunk).start()

    copies = []
    for d in range(lay.cols):
        for g in range(lay.owners):
            target = rounded.at[pl.ds((g * lay.cols + d) * lay.blocks, lay.blocks)]
            copies.append(pltpu.make_async_copy(given_vec[d].at[g], target, sems.at[len(copies)]))
            copies[-1].start()
    total[...] = jnp.zeros_like(total)
    for copy in copies:
        copy.wait()
    for chunk in range(lay.groups // chunk_groups):

        @pl.when(used > chunk * chunk_groups)
        def _():
            load(chunk).wait()

    def group_step(group, carry):
        add_products(lay, group, group_input, entries, tiles, rounded, total)
        return carry

    lax.fori_loop(1, used, group_step, 0)
    own = lay.places * lay.blocks
    own_sum[...] = total[0:own]
    other_sum[...] = total[own : 2 * own]


def apply_tiles(lay, plan, tiles, rounded):
    smem = pl.BlockSpec(memory_space=pltpu.SMEM)
    hbm = pl.BlockSpec(memory_space=pl.ANY)
    vmem = pl.BlockSpec(memory_space=pltpu.VMEM)
    own = lay.places * lay.blocks
    sums = jax.ShapeDtypeStruct((own, lay.side, lay.width), jnp.float32)
    return pl.pallas_call(
        functools.partial(apply_kernel, lay),
        out_shape=(sums, sums),
        in_specs=[smem] * 3 + [hbm] * (1 + len(rounded)),
        out_specs=(vmem, vmem),
        scratch_shapes=[
            pltpu.VMEM((lay.inputs, lay.side, lay.width), jnp.bfloat16),
            pltpu.VMEM(tiles.shape, jnp.bfloat16),
            pltpu.VMEM((lay.outputs + 1, lay.side, lay.width), jnp.float32),
            pltpu.SemaphoreType.DMA((len(rounded) * lay.owners,)),
            pltpu.SemaphoreType.DMA((lay.groups // chunk_groups,)),
        ],
        compiler_params=pltpu.CompilerParams(vmem_limit_bytes=lay.vmem),
        cost_estimate=pl.CostEstimate(flops=400_000_000, bytes_accessed=4_000_000, transcendentals=0),
    )(plan[2], *plan[3:], tiles, *rounded)


def on_device(
    vectors, energies, intersections, coarse, fine_coarse, coarse_slot, tile_codes, tile_count
):
    rows = lax.axis_size("row")
    cols = lax.axis_size("col")
    row_id = lax.axis_index("row")
    col_id = lax.axis_index("col")
    blocks, pairs, side = intersections.shape
    width = vectors.shape[1]
    points, slots_dev = coarse.shape[:2]
    lay = Layout(rows, cols, blocks, pairs, side, width, points, slots_dev, tile_codes.shape[1], 4)
    if lay.groups * lay.unroll * side * side * 2 > 16 * mib:
        lay = Layout(rows, cols, blocks, pairs, side, width, points, slots_dev, tile_codes.shape[1], 1)
    near = lay.near

    def move(array, row_step, col_step):
        pairs_list = [
            (r * cols + c, (r ^ row_step) * cols + (c ^ col_step)) for r in range(rows) for c in range(cols)
        ]
        return lax.ppermute(array, axes, pairs_list)

    def along(array, step):
        return move(array, 2 * step, 0)

    def to_core(array):
        return move(array, 1, 0)

    def in_plane(array):
        return [array] + [move(array, 0, d) for d in range(1, cols)]

    start = vectors.reshape(blocks, side, width)
    energy = energies.reshape(blocks, side, 1)
    two_owners = lay.owners == 2
    ids = jnp.stack([row_id // 2, row_id % 2, col_id]).astype(jnp.int32)
    listed = jnp.concatenate([tile_codes, tile_count[:, None]], axis=1)
    n_listed = listed.shape[1]
    digits = jnp.concatenate([listed[0] >> 8, listed[0] & 255]).astype(jnp.bfloat16)
    depth = 16 * -(-2 * n_listed // (16 * width * blocks))
    digits = jnp.pad(digits, (0, blocks * depth * width - 2 * n_listed)).reshape(blocks, depth, width)
    joined = jnp.concatenate([intersections, start.astype(jnp.bfloat16), digits], axis=1)

    partner = [along(joined, near)] if two_owners else []
    inputs = in_plane(joined)
    near_coarse = [along(coarse[:1], e) for e in range(1, near)]
    rest = coarse[1:].reshape(-1, pairs)
    partner, inputs, near_coarse, rest = lax.optimization_barrier((partner, inputs, near_coarse, rest))
    if two_owners:
        sent = partner[0][:, pairs + side :].reshape(-1)[: 2 * n_listed].astype(jnp.int32)
        listed = jnp.concatenate([listed, ((sent[:n_listed] << 8) + sent[n_listed:])[None]], axis=0)
    plan = make_plan(lay, ids, listed, fine_coarse, coarse_slot)
    turned, turned_own, mixed = turn(lay, rest, joined, *partner)
    for part in partner:
        inputs = inputs + in_plane(part)
    lines = [along(mixed if d < near else turned_own, d) for d in lay.line_steps()]
    held = (inputs, turned, lines, near_coarse, plan)
    inputs, turned, lines, near_coarse, plan = lax.optimization_barrier(held)
    blocks_coarse = [coarse, to_core(coarse)]
    lefts = [turned] + lines
    lefts_core = [to_core(part) for part in lefts]
    for e in range(1, near):
        first_rows = near_coarse[e - 1]
        blocks_coarse += [first_rows, lefts[e], to_core(first_rows), lefts_core[e]]
    lefts = lefts + lefts_core
    projected = [
        project(lay, g, plan, inputs[g * cols : (g + 1) * cols], blocks_coarse) for g in range(lay.owners)
    ]
    own_sum, other_sum, tiles = make_tiles(lay, plan, inputs, lefts, projected)

    def over_core(own_part, other_part):
        return (own_part + to_core(other_part)).reshape(lay.places, blocks, side, width)

    def shifted_part(field):
        return energy * field - spectrum_center * field

    merged = over_core(own_sum, other_sum)
    if two_owners:
        sums = jnp.stack([merged[0] + shifted_part(start), merged[near]])
        for e in range(1, near):
            sent = jnp.stack([merged[e], merged[e ^ near]]).astype(jnp.bfloat16)
            sums = sums + along(sent, e).astype(jnp.float32)
        sums = sums + along(sums.astype(jnp.bfloat16), near)[::-1].astype(jnp.float32)
    else:
        sums = merged + shifted_part(start)[None]

    firsts = sums / spectrum_half
    first = firsts[0]
    own_sum, other_sum = apply_tiles(lay, plan, tiles, in_plane(firsts.astype(jnp.bfloat16)))
    merged = over_core(own_sum, other_sum)
    last = merged[0]
    for d in range(1, lay.places):
        last = last + along(merged[d].astype(jnp.bfloat16), d).astype(jnp.float32)
    second = 2.0 * ((shifted_part(first) + last) / spectrum_half) - start
    return first.reshape(vectors.shape), second.reshape(vectors.shape)


def solution(mesh):
    in_specs = (
        P(axes, None),
        P(axes),
        P(axes, None, None),
        P("col", "row", None, None),
        P(),
        P(),
        P(axes, None),
        P(axes),
    )
    out_specs = (P(axes, None), P(axes, None))
    return jax.shard_map(
        on_device, mesh=mesh, in_specs=in_specs, out_specs=out_specs, check_vma=False
    )
```

time: 157 us -> 173 us (1.10)
  starting transfers between devices: 21.7 us -> 34.7 us
  local copies, waits for them, and re-layouts: 3.36 us -> 11.6 us
  waiting for transfers between devices: 85.1 us -> 82.1 us
  Pallas kernels: 37.1 us -> 35.1 us
    ppermute x26 -> x25, starting transfers between devices: 21.7 us -> 34.7 us  [move(): return lax.ppermute(array, axes, pairs_list)]
    pallas_call x1, Pallas kernels: 21.9 us -> 12.6 us  [make_tiles(): pl.pallas_call(functools.partial(tiles_kernel, lay), out_shape=(sums, sum...]
    unnamed x42 -> x38, local copies, waits for them, and re-layouts: 1.88 us -> 8.83 us
    pallas_call x1 -> x3, Pallas kernels: 8.57 us -> 15.4 us  [the longest x2 7.87 us: project(): pl.pallas_call(functools.partial(project_kernel, lay, owner), out_shape=j...]
    ppermute x26 -> x25, waiting for transfers between devices: 85.1 us -> 82.1 us  [move(): return lax.ppermute(array, axes, pairs_list)]
    pallas_call x1, Pallas kernels: 0.25 us -> 2.22 us  [turn(): pl.pallas_call(functools.partial(turn_kernel, lay), out_shape=(jax.ShapeD...]
  transfers between devices with their start and end apart: 26 -> 25, of which waited for: 17 -> 13; matrix products, arithmetic and copies ran while one was open for 3% -> 3% of each run, Pallas kernels for 6% -> 9%
where the time goes in v3:
time: 173 us; the launch traced here: 171 us
  waiting for transfers between devices  82.1 us (47%)
  Pallas kernels  35.1 us (20%)
  starting transfers between devices  34.7 us (20%)
  local copies, waits for them, and re-layouts  11.6 us (7%)
  other arithmetic  5.48 us (3%)
    ppermute x25, waiting for transfers between devices, move(): return lax.ppermute(array, axes, pairs_list)  82.1 us
    ppermute x25, starting transfers between devices, move(): return lax.ppermute(array, axes, pairs_list)  34.7 us
    pallas_call x1, Pallas kernels, make_tiles(): pl.pallas_call(functools.partial(tiles_kernel, lay), out_shape=(sums, sum...  12.6 us
    unnamed x38, local copies, waits for them, and re-layouts  8.83 us
    pallas_call x2, Pallas kernels, project(): pl.pallas_call(functools.partial(project_kernel, lay, owner), out_shape=j...  7.87 us
    pallas_call x1, Pallas kernels, make_plan(): pl.pallas_call(functools.partial(plan_kernel, lay), out_shape=tuple((jax....  7.58 us
    pallas_call x1, Pallas kernels, apply_tiles(): pl.pallas_call(functools.partial(apply_kernel, lay), out_shape=(sums, sum...  4.75 us
  transfers between devices with their start and end apart: 25, of which 13 were waited for; matrix products, arithmetic and copies ran while one was open for 3% of the time, Pallas kernels for 9%

profile of v3, /device:TPU:0, one launch (start us, length us, event | category | flops | bytes accessed | tf_op | source)
XLA Modules:
  0.0 170.7 jit_solution(14941942288267778628)
XLA Ops:
  0.7 1.4 slice_bitcast_fusion
  2.0 3.1 %collective-permute-start.4 = (bf16[1,1,512,512]{3,2,1,0:T(8,128)(2,1)S(1)}, bf16[1,1,512,512]{3,2,1,0:T(8,128)(2,1)}, u32[]{:S(2)}, u32[]{:S(2)}) collective-permute-start(bf16[1,1,512,512]{3,2,1,0:T(8,128)(2,1)S(1)} %get-tuple-element.83), channel_id=1, source_target_pairs={{0,8},{1,9},{2,10},{3,11},{4,12},{5,13},{6,14},{7,15},{8,0},{9,1},... | collective-permute-start | bytes 1572872 | tf_op jit(solution)/shard_map/ppermute | solution.py:427
  5.7 0.9 convert_element_type.34
  6.7 0.7 convert_bitcast_fusion.1
  7.5 1.0 pad_maximum_fusion.refs_0_
  8.5 2.5 %collective-permute-start.3 = (bf16[3,656,128]{2,1,0:T(8,128)(2,1)S(1)}, bf16[3,656,128]{2,1,0:T(8,128)(2,1)S(1)}, u32[]{:S(2)}, u32[]{:S(2)}) collective-permute-start(bf16[3,656,128]{2,1,0:T(8,128)(2,1)S(1)} %pad_maximum_fusion.refs_0_), channel_id=1, source_target_pairs={{0,3},{1,2},{2,1},{3,0},{4,7},{5,6},{6,5},{7,4},{8,11},{9,10},{10,... | collective-permute-start | bytes 1511432 | tf_op jit(solution)/shard_map/ppermute | solution.py:427
  11.6 0.5 collective-permute-start.1
  12.1 2.6 %collective-permute-start = (bf16[3,656,128]{2,1,0:T(8,128)(2,1)S(1)}, bf16[3,656,128]{2,1,0:T(8,128)(2,1)}, u32[]{:S(2)}, u32[]{:S(2)}) collective-permute-start(bf16[3,656,128]{2,1,0:T(8,128)(2,1)S(1)} %pad_maximum_fusion.refs_0_), channel_id=1, source_target_pairs={{0,16},{1,17},{2,18},{3,19},{4,20},{5,21},{6,22},{7,23},{8,24},{9,... | collective-permute-start | bytes 1511432 | tf_op jit(solution)/shard_map/ppermute | solution.py:427
  14.7 9.3 %collective-permute-done.3.refs_3_ = bf16[3,656,128]{2,1,0:T(8,128)(2,1)S(1)} collective-permute-done((bf16[3,656,128]{2,1,0:T(8,128)(2,1)S(1)}, bf16[3,656,128]{2,1,0:T(8,128)(2,1)S(1)}, u32[]{:S(2)}, u32[]{:S(2)}) %collective-permute-start.3) | collective-permute-done | bytes 503840 | tf_op jit(solution)/shard_map/ppermute | solution.py:427
  24.0 0.8 copy-done.2
  24.7 8.5 %collective-permute-done.2.refs_2_ = bf16[3,656,128]{2,1,0:T(8,128)(2,1)S(1)} collective-permute-done((bf16[3,656,128]{2,1,0:T(8,128)(2,1)S(1)}, bf16[3,656,128]{2,1,0:T(8,128)(2,1)S(1)}, u32[]{:S(2)}, u32[]{:S(2)}) %collective-permute-start.2) | collective-permute-done | bytes 503840 | tf_op jit(solution)/shard_map/ppermute | solution.py:427
  33.3 0.8 copy-done.4
  34.1 0.8 copy-done.6
  34.8 1.2 collective-permute-done.refs_1_.refs_0_.refs_4_
  36.1 2.2 %shard_map.95 = (bf16[6,128,512]{2,1,0:T(8,128)(2,1)S(1)}, bf16[3,128,512]{2,1,0:T(8,128)(2,1)S(1)}, bf16[896,512]{1,0:T(8,128)(2,1)}) custom-call(bf16[3,656,128]{2,1,0:T(8,128)(2,1)S(1)} %pad_maximum_fusion.refs_0_, bf16[3,656,128]{2,1,0:T(8,128)(2,1)} %collective-permute-done.refs_1_.refs_0_.refs_4_, bf16[512,512]{1,0:T(8,128)(2,1)S(1)} %get-tuple-element.44.refs_2_), custom_call_target="tpu_custom_call" | custom-call | flops 1000000 | bytes 3000000 | tf_op jit(solution)/shard_map/pallas_call | solution.py:227
  38.3 0.9 copy-done.14
  39.2 2.8 %collective-permute-start.9 = (bf16[3,128,512]{2,1,0:T(8,128)(2,1)S(1)}, bf16[3,128,512]{2,1,0:T(8,128)(2,1)}, u32[]{:S(2)}, u32[]{:S(2)}) collective-permute-start(bf16[3,128,512]{2,1,0:T(8,128)(2,1)S(1)} %get-tuple-element.47), channel_id=1, source_target_pairs={{0,24},{1,25},{2,26},{3,27},{4,28},{5,29},{6,30},{7,31},{8,16},{9,... | collective-permute-start | bytes 1179656 | tf_op jit(solution)/shard_map/ppermute | solution.py:427
  42.0 0.7 pad_add_fusion.2.ids
  42.6 0.7 slice.66
  43.4 2.1 %collective-permute-start.7 = (bf16[3,656,128]{2,1,0:T(8,128)(2,1)}, bf16[3,656,128]{2,1,0:T(8,128)(2,1)}, u32[]{:S(2)}, u32[]{:S(2)}) collective-permute-start(bf16[3,656,128]{2,1,0:T(8,128)(2,1)} %collective-permute-done.refs_1_.refs_0_.refs_4_), channel_id=1, source_target_pairs={{0,3},{1,2},{2,1},{3,0},{4,7},{5,6},{6,5},{7,4},{8,11},{9,10},{10,... | collective-permute-start | bytes 1511432 | tf_op jit(solution)/shard_map/ppermute | solution.py:427
  45.4 0.9 collective-permute-start.6
  46.3 0.5 collective-permute-start.5
  46.9 24.1 %collective-permute-done.9.refs_10_ = bf16[3,128,512]{2,1,0:T(8,128)(2,1)} collective-permute-done((bf16[3,128,512]{2,1,0:T(8,128)(2,1)S(1)}, bf16[3,128,512]{2,1,0:T(8,128)(2,1)}, u32[]{:S(2)}, u32[]{:S(2)}) %collective-permute-start.9) | collective-permute-done | bytes 393248 | tf_op jit(solution)/shard_map/ppermute | solution.py:427
  71.1 0.6 pad_add_fusion.listed
  71.7 7.6 %shard_map.96 = (s32[24]{0:T(128)}, s32[26]{0:T(128)}, s32[3]{0:T(128)}, s32[72]{0:T(128)}, s32[288]{0:T(512)}) custom-call(s32[3]{0:T(128)} %pad_add_fusion.2.ids, s32[2,97]{1,0:T(2,128)} %pad_add_fusion.listed, s32[96]{0:T(128)} %fine.1, s32[8]{0:T(128)} %stored.1), custom_call_target="tpu_custom_call" | custom-call | bytes 20000000 | tf_op jit(solution)/shard_map/pallas_call | solution.py:133
  80.4 3.5 %collective-permute-done.14.refs_8_ = bf16[1,1,512,512]{3,2,1,0:T(8,128)(2,1)S(1)} collective-permute-done((bf16[1,1,512,512]{3,2,1,0:T(8,128)(2,1)}, bf16[1,1,512,512]{3,2,1,0:T(8,128)(2,1)S(1)}, u32[]{:S(2)}, u32[]{:S(2)}) %collective-permute-start.14) | collective-permute-done | bytes 524320 | tf_op jit(solution)/shard_map/ppermute | solution.py:427
  84.0 0.6 copy-done.8
  84.6 0.6 copy-done.11
  85.2 0.7 copy-done.12
  85.8 3.6 %shard_map.98.refs_15_ = bf16[12,512,256]{2,1,0:T(8,128)(2,1)S(1)} custom-call(s32[24]{0:T(128)S(1)} %copy-done.11, s32[26]{0:T(128)S(1)} %copy-done.12, s32[3]{0:T(128)S(1)} %copy-done.8, bf16[3,656,128]{2,1,0:T(8,128)(2,1)} %collective-permute-done.refs_1_.refs_0_.refs_4_, bf16[3,656,128]{2,1,0:T(8,128)(2,1)} %collective-permute-done.5.refs_1_.refs_5_, ...), custom_call_target="tpu_custom_call" | custom-call | flops 1000000000 | bytes 20000000 | tf_op jit(solution)/shard_map/pallas_call | solution.py:187
  89.6 4.2 %shard_map.97.refs_14_ = bf16[12,512,256]{2,1,0:T(8,128)(2,1)S(1)} custom-call(s32[24]{0:T(128)S(1)} %copy-done.11, s32[26]{0:T(128)S(1)} %copy-done.12, s32[3]{0:T(128)S(1)} %copy-done.8, bf16[3,656,128]{2,1,0:T(8,128)(2,1)S(1)} %pad_maximum_fusion.refs_0_, bf16[3,656,128]{2,1,0:T(8,128)(2,1)S(1)} %copy-done.7, bf16[3,656,128]{2,1,0:T(8,128)(2,1)S(1)} %copy-done.5, ...), custom_call_target="tpu_custom_call" | custom-call | flops 1000000000 | bytes 20000000 | tf_op jit(solution)/shard_map/pallas_call | solution.py:187
  93.9 12.6 %shard_map.99 = (f32[12,128,128]{2,1,0:T(8,128)S(1)}, f32[12,128,128]{2,1,0:T(8,128)S(1)}, bf16[288,128,128]{2,1,0:T(8,128)(2,1)}) custom-call(s32[3]{0:T(128)S(1)} %copy-done.9, s32[72]{0:T(128)S(1)} %copy-done.13, s32[288]{0:T(512)S(1)} %copy-done.10, bf16[3,656,128]{2,1,0:T(8,128)(2,1)S(1)} %pad_maximum_fusion.refs_0_, ...), custom_call_target="tpu_custom_call" | custom-call | flops 4000000000 | bytes 30000000 | tf_op jit(solution)/shard_map/pallas_call | solution.py:324
  106.6 2.3 %collective-permute-done.15 = f32[12,128,128]{2,1,0:T(8,128)S(1)} collective-permute-done((f32[12,128,128]{2,1,0:T(8,128)S(1)}, f32[12,128,128]{2,1,0:T(8,128)S(1)}, u32[]{:S(2)}, u32[]{:S(2)}) %collective-permute-start.15) | collective-permute-done | bytes 786464 | tf_op jit(solution)/shard_map/ppermute | solution.py:427
  109.3 6.8 %collective-permute-done.16 = bf16[2,3,128,128]{3,2,1,0:T(8,128)(2,1)S(1)} collective-permute-done((bf16[2,3,128,128]{3,2,1,0:T(8,128)(2,1)S(1)}, bf16[2,3,128,128]{3,2,1,0:T(8,128)(2,1)S(1)}, u32[]{:S(2)}, u32[]{:S(2)}) %collective-permute-start.16) | collective-permute-done | bytes 196640 | tf_op jit(solution)/shard_map/ppermute | solution.py:427
  116.1 7.7 %collective-permute-start.17 = (bf16[2,3,128,128]{3,2,1,0:T(8,128)(2,1)S(1)}, bf16[2,3,128,128]{3,2,1,0:T(8,128)(2,1)S(1)}, u32[]{:S(2)}, u32[]{:S(2)}) collective-permute-start(bf16[2,3,128,128]{3,2,1,0:T(8,128)(2,1)S(1)} %fusion), channel_id=1, source_target_pairs={{0,16},{1,17},{2,18},{3,19},{4,20},{5,21},{6,22},{7,23},{8,24},{9,... | collective-permute-start | bytes 589832 | tf_op jit(solution)/shard_map/ppermute | solution.py:427
  123.8 8.9 %collective-permute-done.17 = bf16[2,3,128,128]{3,2,1,0:T(8,128)(2,1)S(1)} collective-permute-done((bf16[2,3,128,128]{3,2,1,0:T(8,128)(2,1)S(1)}, bf16[2,3,128,128]{3,2,1,0:T(8,128)(2,1)S(1)}, u32[]{:S(2)}, u32[]{:S(2)}) %collective-permute-start.17) | collective-permute-done | bytes 196640 | tf_op jit(solution)/shard_map/ppermute | solution.py:427
  133.0 3.4 %collective-permute-start.18 = (bf16[2,3,128,128]{3,2,1,0:T(8,128)(2,1)S(1)}, bf16[2,3,128,128]{3,2,1,0:T(8,128)(2,1)S(1)}, u32[]{:S(2)}, u32[]{:S(2)}) collective-permute-start(bf16[2,3,128,128]{3,2,1,0:T(8,128)(2,1)S(1)} %get-tuple-element.78.refs_0_), channel_id=1, source_target_pairs={{0,1},{1,0},{2,3},{3,2},{4,5},{5,4},{6,7},{7,6},{8,9},{9,8},{10,11... | collective-permute-start | bytes 589832 | tf_op jit(solution)/shard_map/ppermute | solution.py:427
  136.4 5.2 %collective-permute-done.20.refs_3_ = bf16[2,3,128,128]{3,2,1,0:T(8,128)(2,1)S(1)} collective-permute-done((bf16[2,3,128,128]{3,2,1,0:T(8,128)(2,1)S(1)}, bf16[2,3,128,128]{3,2,1,0:T(8,128)(2,1)S(1)}, u32[]{:S(2)}, u32[]{:S(2)}) %collective-permute-start.20) | collective-permute-done | bytes 196640 | tf_op jit(solution)/shard_map/ppermute | solution.py:427
  141.6 1.5 collective-permute-done.19.refs_2_
  143.1 3.7 %copy-done = bf16[288,128,128]{2,1,0:T(8,128)(2,1)S(1)} copy-done((bf16[288,128,128]{2,1,0:T(8,128)(2,1)S(1)}, bf16[288,128,128]{2,1,0:T(8,128)(2,1)}, u32[]{:S(2)}) %copy-start) | copy-done | bytes 9437208
  146.8 4.8 %shard_map.100 = (f32[12,128,128]{2,1,0:T(8,128)S(1)}, f32[12,128,128]{2,1,0:T(8,128)S(1)}) custom-call(s32[3]{0:T(128)S(1)} %copy-done.9, s32[72]{0:T(128)S(1)} %copy-done.13, s32[288]{0:T(512)S(1)} %copy-done.10, bf16[288,128,128]{2,1,0:T(8,128)(2,1)S(1)} %copy-done, bf16[2,3,128,128]{3,2,1,0:T(8,128)(2,1)S(1)} %get-tuple-element.78.refs_0_, ...), custom_call_target="tpu_custom_call" | custom-call | flops 400000000 | bytes 4000000 | tf_op jit(solution)/shard_map/pallas_call | solution.py:391
  151.6 2.3 %collective-permute-done.21 = f32[12,128,128]{2,1,0:T(8,128)S(1)} collective-permute-done((f32[12,128,128]{2,1,0:T(8,128)S(1)}, f32[12,128,128]{2,1,0:T(8,128)S(1)}, u32[]{:S(2)}, u32[]{:S(2)}) %collective-permute-start.21) | collective-permute-done | bytes 786464 | tf_op jit(solution)/shard_map/ppermute | solution.py:427
  154.1 2.7 %collective-permute-start.22 = (bf16[3,128,128]{2,1,0:T(8,128)(2,1)S(1)}, bf16[3,128,128]{2,1,0:T(8,128)(2,1)S(1)}, u32[]{:S(2)}, u32[]{:S(2)}) collective-permute-start(bf16[3,128,128]{2,1,0:T(8,128)(2,1)S(1)} %get-tuple-element.86), channel_id=1, source_target_pairs={{0,8},{1,9},{2,10},{3,11},{4,12},{5,13},{6,14},{7,15},{8,0},{9,1},... | collective-permute-start | bytes 294920 | tf_op jit(solution)/shard_map/ppermute | solution.py:427
  156.8 3.4 %collective-permute-start.24 = (bf16[3,128,128]{2,1,0:T(8,128)(2,1)S(1)}, bf16[3,128,128]{2,1,0:T(8,128)(2,1)S(1)}, u32[]{:S(2)}, u32[]{:S(2)}) collective-permute-start(bf16[3,128,128]{2,1,0:T(8,128)(2,1)S(1)} %get-tuple-element.87), channel_id=1, source_target_pairs={{0,24},{1,25},{2,26},{3,27},{4,28},{5,29},{6,30},{7,31},{8,16},{9,... | collective-permute-start | bytes 294920 | tf_op jit(solution)/shard_map/ppermute | solution.py:427
  160.8 0.7 slice.87
  161.4 4.5 %collective-permute-done.24 = bf16[3,128,128]{2,1,0:T(8,128)(2,1)S(1)} collective-permute-done((bf16[3,128,128]{2,1,0:T(8,128)(2,1)S(1)}, bf16[3,128,128]{2,1,0:T(8,128)(2,1)S(1)}, u32[]{:S(2)}, u32[]{:S(2)}) %collective-permute-start.24) | collective-permute-done | bytes 98336 | tf_op jit(solution)/shard_map/ppermute | solution.py:427
  166.0 3.9 %collective-permute-done.23 = bf16[3,128,128]{2,1,0:T(8,128)(2,1)S(1)} collective-permute-done((bf16[3,128,128]{2,1,0:T(8,128)(2,1)S(1)}, bf16[3,128,128]{2,1,0:T(8,128)(2,1)S(1)}, u32[]{:S(2)}, u32[]{:S(2)}) %collective-permute-start.23) | collective-permute-done | bytes 98336 | tf_op jit(solution)/shard_map/ppermute | solution.py:427
  169.9 0.8 fusion.5
  (66 shorter events, 3.2 us)
Async XLA Ops:
  0.6 70.4 %copy-start.1 = (bf16[2,1,512,512]{3,2,1,0:T(8,128)(2,1)S(1)}, bf16[2,1,512,512]{3,2,1,0:T(8,128)(2,1)}, u32[]{:S(2)}) copy-start(bf16[2,1,512,512]{3,2,1,0:T(8,128)(2,1)} %refs_4_.3) | copy-start | bytes 3145732
  0.6 70.4 %copy-start.18 = (s32[1,96]{1,0:T(1,128)S(1)}, s32[1,96]{1,0:T(1,128)}, u32[]{:S(2)}) copy-start(s32[1,96]{1,0:T(1,128)} %param.14) | copy-start | bytes 1156
  2.0 34.0 %collective-permute-start.4 = (bf16[1,1,512,512]{3,2,1,0:T(8,128)(2,1)S(1)}, bf16[1,1,512,512]{3,2,1,0:T(8,128)(2,1)}, u32[]{:S(2)}, u32[]{:S(2)}) collective-permute-start(bf16[1,1,512,512]{3,2,1,0:T(8,128)(2,1)S(1)} %get-tuple-element.83), channel_id=1, source_target_pairs={{0,8},{1,9},{2,10},{3,11},{4,12},{5,13},{6,14},{7,15},{8,0},{9,1},... | collective-permute-start | bytes 1572872 | tf_op jit(solution)/shard_map/ppermute | solution.py:427
  8.5 15.4 %collective-permute-start.3 = (bf16[3,656,128]{2,1,0:T(8,128)(2,1)S(1)}, bf16[3,656,128]{2,1,0:T(8,128)(2,1)S(1)}, u32[]{:S(2)}, u32[]{:S(2)}) collective-permute-start(bf16[3,656,128]{2,1,0:T(8,128)(2,1)S(1)} %pad_maximum_fusion.refs_0_), channel_id=1, source_target_pairs={{0,3},{1,2},{2,1},{3,0},{4,7},{5,6},{6,5},{7,4},{8,11},{9,10},{10,... | collective-permute-start | bytes 1511432 | tf_op jit(solution)/shard_map/ppermute | solution.py:427
  11.1 22.2 %collective-permute-start.2 = (bf16[3,656,128]{2,1,0:T(8,128)(2,1)S(1)}, bf16[3,656,128]{2,1,0:T(8,128)(2,1)S(1)}, u32[]{:S(2)}, u32[]{:S(2)}) collective-permute-start(bf16[3,656,128]{2,1,0:T(8,128)(2,1)S(1)} %pad_maximum_fusion.refs_0_), channel_id=1, source_target_pairs={{0,2},{1,3},{2,0},{3,1},{4,6},{5,7},{6,4},{7,5},{8,10},{9,11},{10,... | collective-permute-start | bytes 1511432 | tf_op jit(solution)/shard_map/ppermute | solution.py:427
  11.6 22.5 %collective-permute-start.1 = (bf16[3,656,128]{2,1,0:T(8,128)(2,1)S(1)}, bf16[3,656,128]{2,1,0:T(8,128)(2,1)S(1)}, u32[]{:S(2)}, u32[]{:S(2)}) collective-permute-start(bf16[3,656,128]{2,1,0:T(8,128)(2,1)S(1)} %pad_maximum_fusion.refs_0_), channel_id=1, source_target_pairs={{0,1},{1,0},{2,3},{3,2},{4,5},{5,4},{6,7},{7,6},{8,9},{9,8},{10,11... | collective-permute-start | bytes 1511432 | tf_op jit(solution)/shard_map/ppermute | solution.py:427
  12.1 23.9 %collective-permute-start = (bf16[3,656,128]{2,1,0:T(8,128)(2,1)S(1)}, bf16[3,656,128]{2,1,0:T(8,128)(2,1)}, u32[]{:S(2)}, u32[]{:S(2)}) collective-permute-start(bf16[3,656,128]{2,1,0:T(8,128)(2,1)S(1)} %pad_maximum_fusion.refs_0_), channel_id=1, source_target_pairs={{0,16},{1,17},{2,18},{3,19},{4,20},{5,21},{6,22},{7,23},{8,24},{9,... | collective-permute-start | bytes 1511432 | tf_op jit(solution)/shard_map/ppermute | solution.py:427
  24.0 0.8 copy-start.2
  33.2 0.8 copy-start.4
  34.1 0.8 copy-start.6
  38.3 0.9 copy-start.14
  39.2 40.2 %collective-permute-start.8 = (bf16[896,512]{1,0:T(8,128)(2,1)}, bf16[896,512]{1,0:T(8,128)(2,1)S(1)}, u32[]{:S(2)}, u32[]{:S(2)}) collective-permute-start(bf16[896,512]{1,0:T(8,128)(2,1)} %get-tuple-element.46), channel_id=1, source_target_pairs={{0,8},{1,9},{2,10},{3,11},{4,12},{5,13},{6,14},{7,15},{8,0},{9,1},... | collective-permute-start | bytes 2752520 | tf_op jit(solution)/shard_map/ppermute | solution.py:427
  39.2 31.8 %collective-permute-start.9 = (bf16[3,128,512]{2,1,0:T(8,128)(2,1)S(1)}, bf16[3,128,512]{2,1,0:T(8,128)(2,1)}, u32[]{:S(2)}, u32[]{:S(2)}) collective-permute-start(bf16[3,128,512]{2,1,0:T(8,128)(2,1)S(1)} %get-tuple-element.47), channel_id=1, source_target_pairs={{0,24},{1,25},{2,26},{3,27},{4,28},{5,29},{6,30},{7,31},{8,16},{9,... | collective-permute-start | bytes 1179656 | tf_op jit(solution)/shard_map/ppermute | solution.py:427
  43.4 35.9 %collective-permute-start.7 = (bf16[3,656,128]{2,1,0:T(8,128)(2,1)}, bf16[3,656,128]{2,1,0:T(8,128)(2,1)}, u32[]{:S(2)}, u32[]{:S(2)}) collective-permute-start(bf16[3,656,128]{2,1,0:T(8,128)(2,1)} %collective-permute-done.refs_1_.refs_0_.refs_4_), channel_id=1, source_target_pairs={{0,3},{1,2},{2,1},{3,0},{4,7},{5,6},{6,5},{7,4},{8,11},{9,10},{10,... | collective-permute-start | bytes 1511432 | tf_op jit(solution)/shard_map/ppermute | solution.py:427
  45.4 33.9 %collective-permute-start.6 = (bf16[3,656,128]{2,1,0:T(8,128)(2,1)}, bf16[3,656,128]{2,1,0:T(8,128)(2,1)}, u32[]{:S(2)}, u32[]{:S(2)}) collective-permute-start(bf16[3,656,128]{2,1,0:T(8,128)(2,1)} %collective-permute-done.refs_1_.refs_0_.refs_4_), channel_id=1, source_target_pairs={{0,2},{1,3},{2,0},{3,1},{4,6},{5,7},{6,4},{7,5},{8,10},{9,11},{10,... | collective-permute-start | bytes 1511432 | tf_op jit(solution)/shard_map/ppermute | solution.py:427
  46.3 33.0 %collective-permute-start.5 = (bf16[3,656,128]{2,1,0:T(8,128)(2,1)}, bf16[3,656,128]{2,1,0:T(8,128)(2,1)}, u32[]{:S(2)}, u32[]{:S(2)}) collective-permute-start(bf16[3,656,128]{2,1,0:T(8,128)(2,1)} %collective-permute-done.refs_1_.refs_0_.refs_4_), channel_id=1, source_target_pairs={{0,1},{1,0},{2,3},{3,2},{4,5},{5,4},{6,7},{7,6},{8,9},{9,8},{10,11... | collective-permute-start | bytes 1511432 | tf_op jit(solution)/shard_map/ppermute | solution.py:427
  71.0 9.5 %collective-permute-start.13 = (bf16[2,1,512,512]{3,2,1,0:T(8,128)(2,1)S(1)}, bf16[2,1,512,512]{3,2,1,0:T(8,128)(2,1)S(1)}, u32[]{:S(2)}, u32[]{:S(2)}) collective-permute-start(bf16[2,1,512,512]{3,2,1,0:T(8,128)(2,1)S(1)} %copy-done.1), channel_id=1, source_target_pairs={{0,4},{1,5},{2,6},{3,7},{4,0},{5,1},{6,2},{7,3},{8,12},{9,13},{10,... | collective-permute-start | bytes 3145736 | tf_op jit(solution)/shard_map/ppermute | solution.py:427
  79.3 10.2 %copy-start.3 = (bf16[3,656,128]{2,1,0:T(8,128)(2,1)S(1)}, bf16[3,656,128]{2,1,0:T(8,128)(2,1)}, u32[]{:S(2)}) copy-start(bf16[3,656,128]{2,1,0:T(8,128)(2,1)} %copy-done.2) | copy-start | bytes 1511428
  79.3 10.2 %copy-start.5 = (bf16[3,656,128]{2,1,0:T(8,128)(2,1)S(1)}, bf16[3,656,128]{2,1,0:T(8,128)(2,1)}, u32[]{:S(2)}) copy-start(bf16[3,656,128]{2,1,0:T(8,128)(2,1)} %copy-done.4) | copy-start | bytes 1511428
  79.3 10.2 %copy-start.7 = (bf16[3,656,128]{2,1,0:T(8,128)(2,1)S(1)}, bf16[3,656,128]{2,1,0:T(8,128)(2,1)}, u32[]{:S(2)}) copy-start(bf16[3,656,128]{2,1,0:T(8,128)(2,1)} %copy-done.6) | copy-start | bytes 1511428
  79.4 4.6 %collective-permute-start.11 = (bf16[896,512]{1,0:T(8,128)(2,1)S(1)}, bf16[896,512]{1,0:T(8,128)(2,1)S(1)}, u32[]{:S(2)}, u32[]{:S(2)}) collective-permute-start(bf16[896,512]{1,0:T(8,128)(2,1)S(1)} %collective-permute-done.8.refs_7_.refs_9_), channel_id=1, source_target_pairs={{0,4},{1,5},{2,6},{3,7},{4,0},{5,1},{6,2},{7,3},{8,12},{9,13},{10,... | collective-permute-start | bytes 2752520 | tf_op jit(solution)/shard_map/ppermute | solution.py:427
  79.4 14.4 %collective-permute-start.10 = (bf16[6,128,512]{2,1,0:T(8,128)(2,1)}, bf16[6,128,512]{2,1,0:T(8,128)(2,1)S(1)}, u32[]{:S(2)}, u32[]{:S(2)}) collective-permute-start(bf16[6,128,512]{2,1,0:T(8,128)(2,1)} %copy-done.14), channel_id=1, source_target_pairs={{0,4},{1,5},{2,6},{3,7},{4,0},{5,1},{6,2},{7,3},{8,12},{9,13},{10,... | collective-permute-start | bytes 2359304 | tf_op jit(solution)/shard_map/ppermute | solution.py:427
  79.9 4.0 %collective-permute-start.14 = (bf16[1,1,512,512]{3,2,1,0:T(8,128)(2,1)}, bf16[1,1,512,512]{3,2,1,0:T(8,128)(2,1)S(1)}, u32[]{:S(2)}, u32[]{:S(2)}) collective-permute-start(bf16[1,1,512,512]{3,2,1,0:T(8,128)(2,1)} %collective-permute-done.4.refs_6_), channel_id=1, source_target_pairs={{0,4},{1,5},{2,6},{3,7},{4,0},{5,1},{6,2},{7,3},{8,12},{9,13},{10,... | collective-permute-start | bytes 1572872 | tf_op jit(solution)/shard_map/ppermute | solution.py:427
  80.0 13.8 %collective-permute-start.12 = (bf16[3,128,512]{2,1,0:T(8,128)(2,1)}, bf16[3,128,512]{2,1,0:T(8,128)(2,1)S(1)}, u32[]{:S(2)}, u32[]{:S(2)}) collective-permute-start(bf16[3,128,512]{2,1,0:T(8,128)(2,1)} %collective-permute-done.9.refs_10_), channel_id=1, source_target_pairs={{0,4},{1,5},{2,6},{3,7},{4,0},{5,1},{6,2},{7,3},{8,12},{9,13},{10,... | collective-permute-start | bytes 1179656 | tf_op jit(solution)/shard_map/ppermute | solution.py:427
  84.0 0.6 copy-start.8
  84.6 0.6 copy-start.11
  85.2 0.7 copy-start.12
  89.5 4.3 %copy-start.9 = (s32[3]{0:T(128)S(1)}, s32[3]{0:T(128)}, u32[]{:S(2)}) copy-start(s32[3]{0:T(128)} %get-tuple-element.54.sizes) | copy-start | bytes 40
  89.5 4.3 %copy-start.10 = (s32[288]{0:T(512)S(1)}, s32[288]{0:T(512)}, u32[]{:S(2)}) copy-start(s32[288]{0:T(512)} %get-tuple-element.56.entries) | copy-start | bytes 3460
  89.5 4.3 %copy-start.13 = (s32[72]{0:T(128)S(1)}, s32[72]{0:T(128)}, u32[]{:S(2)}) copy-start(s32[72]{0:T(128)} %get-tuple-element.55.group_input) | copy-start | bytes 868
  89.6 4.3 %copy-start.15 = (bf16[6,128,512]{2,1,0:T(8,128)(2,1)S(1)}, bf16[6,128,512]{2,1,0:T(8,128)(2,1)}, u32[]{:S(2)}) copy-start(bf16[6,128,512]{2,1,0:T(8,128)(2,1)} %copy-done.14) | copy-start | bytes 2359300
  106.5 2.6 %copy-start.16 = (f32[384,128]{1,0:T(8,128)S(1)}, f32[384,128]{1,0:T(8,128)}, u32[]{:S(2)}) copy-start(f32[384,128]{1,0:T(8,128)} %param.8) | copy-start | bytes 589828
  106.5 2.6 %copy-start.17 = (f32[384]{0:T(512)S(1)}, f32[384]{0:T(512)}, u32[]{:S(2)}) copy-start(f32[384]{0:T(512)} %param.9) | copy-start | bytes 4612
  106.5 2.4 %collective-permute-start.15 = (f32[12,128,128]{2,1,0:T(8,128)S(1)}, f32[12,128,128]{2,1,0:T(8,128)S(1)}, u32[]{:S(2)}, u32[]{:S(2)}) collective-permute-start(f32[12,128,128]{2,1,0:T(8,128)S(1)} %get-tuple-element.72), channel_id=1, source_target_pairs={{0,4},{1,5},{2,6},{3,7},{4,0},{5,1},{6,2},{7,3},{8,12},{9,13},{10,... | collective-permute-start | bytes 2359304 | tf_op jit(solution)/shard_map/ppermute | solution.py:427
  109.1 7.0 %collective-permute-start.16 = (bf16[2,3,128,128]{3,2,1,0:T(8,128)(2,1)S(1)}, bf16[2,3,128,128]{3,2,1,0:T(8,128)(2,1)S(1)}, u32[]{:S(2)}, u32[]{:S(2)}) collective-permute-start(bf16[2,3,128,128]{3,2,1,0:T(8,128)(2,1)S(1)} %pad_maximum_fusion.1), channel_id=1, source_target_pairs={{0,8},{1,9},{2,10},{3,11},{4,12},{5,13},{6,14},{7,15},{8,0},{9,1},... | collective-permute-start | bytes 589832 | tf_op jit(solution)/shard_map/ppermute | solution.py:427
  116.1 16.6 %collective-permute-start.17 = (bf16[2,3,128,128]{3,2,1,0:T(8,128)(2,1)S(1)}, bf16[2,3,128,128]{3,2,1,0:T(8,128)(2,1)S(1)}, u32[]{:S(2)}, u32[]{:S(2)}) collective-permute-start(bf16[2,3,128,128]{3,2,1,0:T(8,128)(2,1)S(1)} %fusion), channel_id=1, source_target_pairs={{0,16},{1,17},{2,18},{3,19},{4,20},{5,21},{6,22},{7,23},{8,24},{9,... | collective-permute-start | bytes 589832 | tf_op jit(solution)/shard_map/ppermute | solution.py:427
  132.8 8.8 %collective-permute-start.20 = (bf16[2,3,128,128]{3,2,1,0:T(8,128)(2,1)S(1)}, bf16[2,3,128,128]{3,2,1,0:T(8,128)(2,1)S(1)}, u32[]{:S(2)}, u32[]{:S(2)}) collective-permute-start(bf16[2,3,128,128]{3,2,1,0:T(8,128)(2,1)S(1)} %get-tuple-element.78.refs_0_), channel_id=1, source_target_pairs={{0,3},{1,2},{2,1},{3,0},{4,7},{5,6},{6,5},{7,4},{8,11},{9,10},{10,... | collective-permute-start | bytes 589832 | tf_op jit(solution)/shard_map/ppermute | solution.py:427
  132.9 10.2 %collective-permute-start.19 = (bf16[2,3,128,128]{3,2,1,0:T(8,128)(2,1)S(1)}, bf16[2,3,128,128]{3,2,1,0:T(8,128)(2,1)S(1)}, u32[]{:S(2)}, u32[]{:S(2)}) collective-permute-start(bf16[2,3,128,128]{3,2,1,0:T(8,128)(2,1)S(1)} %get-tuple-element.78.refs_0_), channel_id=1, source_target_pairs={{0,2},{1,3},{2,0},{3,1},{4,6},{5,7},{6,4},{7,5},{8,10},{9,11},{10,... | collective-permute-start | bytes 589832 | tf_op jit(solution)/shard_map/ppermute | solution.py:427
  133.0 10.2 %collective-permute-start.18 = (bf16[2,3,128,128]{3,2,1,0:T(8,128)(2,1)S(1)}, bf16[2,3,128,128]{3,2,1,0:T(8,128)(2,1)S(1)}, u32[]{:S(2)}, u32[]{:S(2)}) collective-permute-start(bf16[2,3,128,128]{3,2,1,0:T(8,128)(2,1)S(1)} %get-tuple-element.78.refs_0_), channel_id=1, source_target_pairs={{0,1},{1,0},{2,3},{3,2},{4,5},{5,4},{6,7},{7,6},{8,9},{9,8},{10,11... | collective-permute-start | bytes 589832 | tf_op jit(solution)/shard_map/ppermute | solution.py:427
  143.1 3.7 %copy-start = (bf16[288,128,128]{2,1,0:T(8,128)(2,1)S(1)}, bf16[288,128,128]{2,1,0:T(8,128)(2,1)}, u32[]{:S(2)}) copy-start(bf16[288,128,128]{2,1,0:T(8,128)(2,1)} %get-tuple-element.73.tiles_in) | copy-start | bytes 28311556
  151.6 2.4 %collective-permute-start.21 = (f32[12,128,128]{2,1,0:T(8,128)S(1)}, f32[12,128,128]{2,1,0:T(8,128)S(1)}, u32[]{:S(2)}, u32[]{:S(2)}) collective-permute-start(f32[12,128,128]{2,1,0:T(8,128)S(1)} %get-tuple-element.75), channel_id=1, source_target_pairs={{0,4},{1,5},{2,6},{3,7},{4,0},{5,1},{6,2},{7,3},{8,12},{9,13},{10,... | collective-permute-start | bytes 2359304 | tf_op jit(solution)/shard_map/ppermute | solution.py:427
  154.1 7.4 %collective-permute-start.22 = (bf16[3,128,128]{2,1,0:T(8,128)(2,1)S(1)}, bf16[3,128,128]{2,1,0:T(8,128)(2,1)S(1)}, u32[]{:S(2)}, u32[]{:S(2)}) collective-permute-start(bf16[3,128,128]{2,1,0:T(8,128)(2,1)S(1)} %get-tuple-element.86), channel_id=1, source_target_pairs={{0,8},{1,9},{2,10},{3,11},{4,12},{5,13},{6,14},{7,15},{8,0},{9,1},... | collective-permute-start | bytes 294920 | tf_op jit(solution)/shard_map/ppermute | solution.py:427
  156.8 9.2 %collective-permute-start.24 = (bf16[3,128,128]{2,1,0:T(8,128)(2,1)S(1)}, bf16[3,128,128]{2,1,0:T(8,128)(2,1)S(1)}, u32[]{:S(2)}, u32[]{:S(2)}) collective-permute-start(bf16[3,128,128]{2,1,0:T(8,128)(2,1)S(1)} %get-tuple-element.87), channel_id=1, source_target_pairs={{0,24},{1,25},{2,26},{3,27},{4,28},{5,29},{6,30},{7,31},{8,16},{9,... | collective-permute-start | bytes 294920 | tf_op jit(solution)/shard_map/ppermute | solution.py:427
  160.3 9.6 %collective-permute-start.23 = (bf16[3,128,128]{2,1,0:T(8,128)(2,1)S(1)}, bf16[3,128,128]{2,1,0:T(8,128)(2,1)S(1)}, u32[]{:S(2)}, u32[]{:S(2)}) collective-permute-start(bf16[3,128,128]{2,1,0:T(8,128)(2,1)S(1)} %get-tuple-element.88), channel_id=1, source_target_pairs={{0,16},{1,17},{2,18},{3,19},{4,20},{5,21},{6,22},{7,23},{8,24},{9,... | collective-permute-start | bytes 294920 | tf_op jit(solution)/shard_map/ppermute | solution.py:427

commit v4 on v3

--- a/solution.py
+++ b/solution.py
@@ -27,7 +27,7 @@
         self.outputs = rows * blocks
         self.slots = 2 * self.near * slots_dev
         self.unroll = unroll
-        self.vmem = (32 if unroll > 1 else 60) * mib
+        self.vmem = 60 * mib
         most = self.owners * tile_max + self.inputs * (unroll - 1) + unroll
         self.groups = -(-most // (unroll * chunk_groups)) * chunk_groups
 
@@ -88,7 +88,11 @@
         lax.fori_loop(start, end, name, 0)
         return end
 
-    total = lax.fori_loop(0, lay.inputs, place_groups, 1)
+    total = 1
+    for owner in range(lay.owners):
+        if owner > 0:
+            sizes[lay.owners + owner] = total
+        total = lax.fori_loop(owner * lay.spread, (owner + 1) * lay.spread, place_groups, total)
     sizes[0] = total
 
     def clear(i, carry):
@@ -126,7 +130,7 @@
     lengths = (
         lay.inputs,
         lay.owners * (lay.spread + 1),
-        1 + lay.owners,
+        2 * lay.owners,
         lay.groups,
         lay.groups * lay.unroll,
     )
@@ -194,48 +198,63 @@
             pltpu.VMEM((lay.points, lay.slots, lay.pairs, lay.pairs), jnp.bfloat16),
             pltpu.SemaphoreType.DMA((len(inputs) + lay.slots * lay.points,)),
         ],
-        compiler_params=pltpu.CompilerParams(vmem_limit_bytes=32 * mib),
+        compiler_params=pltpu.CompilerParams(vmem_limit_bytes=lay.vmem),
         cost_estimate=pl.CostEstimate(flops=1_000_000_000, bytes_accessed=20_000_000, transcendentals=0),
     )(*plan[:3], *inputs, *coarse)
 
 
 def add_products(lay, group, group_input, entries, tiles, rounded, total):
-    vector = rounded[group_input[group]]
-    products = [
-        jnp.dot(tiles[group * lay.unroll + i], vector, preferred_element_type=jnp.float32)
-        for i in range(lay.unroll)
-    ]
+    held = tiles[pl.ds(group * lay.unroll, lay.unroll)].reshape(lay.unroll * lay.side, lay.side)
+    products = jnp.dot(held, rounded[group_input[group]], preferred_element_type=jnp.float32)
     for i in range(lay.unroll):
         q = lax.div(entries[group * lay.unroll + i], lay.points)
-        total[q] = total[q] + products[i]
-
-
-def turn_kernel(lay, *refs):
-    given, rest, outs = refs[: lay.owners], refs[lay.owners], refs[lay.owners + 1 :]
-    for g in range(lay.owners):
-        for t in range(lay.blocks):
-            turned = given[g][t, 0 : lay.pairs, :].T
-            outs[0][g * lay.blocks + t] = turned
-            if g == 0:
-                outs[1][t] = turned
-                outs[2][t * lay.side : (t + 1) * lay.side, :] = turned
-    outs[2][lay.blocks * lay.side :, :] = rest[...]
-
-
-def turn(lay, rest, *given):
+        total[q] = total[q] + products[i * lay.side : (i + 1) * lay.side]
+
+
+def turn_own_kernel(lay, given, coarse, turned, mixed):
+    for t in range(lay.blocks):
+        block = given[t, 0 : lay.pairs, :].T
+        turned[t] = block
+        mixed[t * lay.side : (t + 1) * lay.side, :] = block
+    row = lay.blocks * lay.side
+    for a in range(1, lay.points):
+        for at in range(lay.slots_dev):
+            mixed[row : row + lay.pairs, :] = coarse[a, at]
+            row += lay.pairs
+
+
+def turn_own(lay, joined, coarse):
+    vmem = pl.BlockSpec(memory_space=pltpu.VMEM)
+    rows = lay.blocks * lay.side + (lay.points - 1) * lay.slots_dev * lay.pairs
+    return pl.pallas_call(
+        functools.partial(turn_own_kernel, lay),
+        out_shape=(
+            jax.ShapeDtypeStruct((lay.blocks, lay.side, lay.pairs), jnp.bfloat16),
+            jax.ShapeDtypeStruct((rows, lay.pairs), jnp.bfloat16),
+        ),
+        in_specs=[vmem] * 2,
+        out_specs=(vmem,) * 2,
+        compiler_params=pltpu.CompilerParams(vmem_limit_bytes=16 * mib),
+        cost_estimate=pl.CostEstimate(flops=1_000_000, bytes_accessed=5_000_000, transcendentals=0),
+    )(joined, coarse)
+
+
+def turn_both_kernel(lay, given, own, out):
+    out[0 : lay.blocks] = own[...]
+    for t in range(lay.blocks):
+        out[lay.blocks + t] = given[t, 0 : lay.pairs, :].T
+
+
+def turn_both(lay, partner, own):
     vmem = pl.BlockSpec(memory_space=pltpu.VMEM)
     return pl.pallas_call(
-        functools.partial(turn_kernel, lay),
-        out_shape=(
-            jax.ShapeDtypeStruct((lay.owners * lay.blocks, lay.side, lay.pairs), jnp.bfloat16),
-            jax.ShapeDtypeStruct((lay.blocks, lay.side, lay.pairs), jnp.bfloat16),
-            jax.ShapeDtypeStruct((lay.blocks * lay.side + rest.shape[0], lay.pairs), jnp.bfloat16),
-        ),
-        in_specs=[vmem] * (lay.owners + 1),
-        out_specs=(vmem,) * 3,
+        functools.partial(turn_both_kernel, lay),
+        out_shape=jax.ShapeDtypeStruct((2 * lay.blocks, lay.side, lay.pairs), jnp.bfloat16),
+        in_specs=[vmem] * 2,
+        out_specs=vmem,
         compiler_params=pltpu.CompilerParams(vmem_limit_bytes=16 * mib),
-        cost_estimate=pl.CostEstimate(flops=1_000_000, bytes_accessed=3_000_000, transcendentals=0),
-    )(*given, rest)
+        cost_estimate=pl.CostEstimate(flops=1_000_000, bytes_accessed=5_000_000, transcendentals=0),
+    )(partner, own)
 
 
 def tiles_kernel(lay, sizes, group_input, entries, *refs):
@@ -246,7 +265,7 @@
     given_out = [refs.pop(0) for _ in range(2 * (1 + len(lines)))]
     given_projected = [refs.pop(0) for _ in range(lay.owners)]
     own_sum, other_sum, tiles_out = refs[:3]
-    left, projected, rounded, tiles, total, sems, out_sems = refs[3:]
+    left, rounded, tiles, total, sems, out_sems = refs[3:]
     copies = []
 
     def fetch(source, target):
@@ -265,8 +284,6 @@
             else:
                 for t in range(lay.blocks):
                     fetch(held[1 + i].at[pl.ds(t * lay.side, lay.side)], left.at[spot + t])
-    for g in range(lay.owners):
-        fetch(given_projected[g], projected.at[pl.ds(g * lay.spread, lay.spread)])
     for i in range(n_in):
         part = pl.ds(i * lay.blocks, lay.blocks)
         fetch(given_in[i].at[:, pl.ds(lay.pairs, lay.side)], rounded.at[part])
@@ -275,21 +292,27 @@
         copy.wait()
     used = sizes[0]
 
-    def group_step(group, carry):
-        p = group_input[group]
-        for i in range(lay.unroll):
-            entry = entries[group * lay.unroll + i]
-            q = jnp.minimum(lax.div(entry, lay.points), lay.outputs - 1)
-            a = lax.rem(entry, lay.points)
-            both = jnp.dot(left[q], projected[p], preferred_element_type=jnp.float32)
-            tile = both[:, : lay.side]
-            for b in range(1, lay.points):
-                tile = jnp.where(a == b, both[:, b * lay.side : (b + 1) * lay.side], tile)
-            tiles[group * lay.unroll + i] = tile.astype(jnp.bfloat16)
-        add_products(lay, group - 1, group_input, entries, tiles, rounded, total)
-        return carry
-
-    lax.fori_loop(1, used, group_step, 0)
+    for g in range(lay.owners):
+
+        def group_step(group, carry):
+            right = given_projected[g][group_input[group] - g * lay.spread]
+            numbers = [entries[group * lay.unroll + i] for i in range(lay.unroll)]
+            places = [jnp.minimum(lax.div(n, lay.points), lay.outputs - 1) for n in numbers]
+            lefts = jnp.concatenate([left[q] for q in places], axis=0)
+            both = jnp.dot(lefts, right, preferred_element_type=jnp.float32)
+            for i in range(lay.unroll):
+                mine = both[i * lay.side : (i + 1) * lay.side]
+                tile = mine[:, : lay.side]
+                for b in range(1, lay.points):
+                    at_b = mine[:, b * lay.side : (b + 1) * lay.side]
+                    tile = jnp.where(lax.rem(numbers[i], lay.points) == b, at_b, tile)
+                tiles[group * lay.unroll + i] = tile.astype(jnp.bfloat16)
+            add_products(lay, group - 1, group_input, entries, tiles, rounded, total)
+            return carry
+
+        first = 1 if g == 0 else sizes[lay.owners + g]
+        last = used if g == lay.owners - 1 else sizes[lay.owners + g + 1]
+        lax.fori_loop(first, last, group_step, 0)
     span = chunk_groups * lay.unroll
 
     def store(chunk):
@@ -319,16 +342,15 @@
     vmem = pl.BlockSpec(memory_space=pltpu.VMEM)
     own = lay.places * lay.blocks
     sums = jax.ShapeDtypeStruct((own, lay.side, lay.width), jnp.float32)
-    n_copies = len(inputs) + 2 * lay.places * lay.blocks + len(projected)
+    n_copies = len(inputs) + 2 * lay.places * lay.blocks
     tiles = (lay.groups * lay.unroll, lay.side, lay.side)
     return pl.pallas_call(
         functools.partial(tiles_kernel, lay),
         out_shape=(sums, sums, jax.ShapeDtypeStruct(tiles, jnp.bfloat16)),
-        in_specs=[smem] * 3 + [hbm] * (len(inputs) + len(outputs) + len(projected)),
+        in_specs=[smem] * 3 + [hbm] * (len(inputs) + len(outputs)) + [vmem] * len(projected),
         out_specs=(vmem, vmem, hbm),
         scratch_shapes=[
             pltpu.VMEM((lay.outputs, lay.side, lay.pairs), jnp.bfloat16),
-            pltpu.VMEM((lay.inputs, lay.pairs, lay.points * lay.side), jnp.bfloat16),
             pltpu.VMEM((lay.inputs, lay.side, lay.width), jnp.bfloat16),
             pltpu.VMEM(tiles, jnp.bfloat16),
             pltpu.VMEM((lay.outputs + 1, lay.side, lay.width), jnp.float32),
@@ -448,19 +470,22 @@
 
     partner = [along(joined, near)] if two_owners else []
     inputs = in_plane(joined)
-    near_coarse = [along(coarse[:1], e) for e in range(1, near)]
-    rest = coarse[1:].reshape(-1, pairs)
-    partner, inputs, near_coarse, rest = lax.optimization_barrier((partner, inputs, near_coarse, rest))
+    late_coarse, late_joined = lax.optimization_barrier((coarse, joined))
+    near_coarse = [along(late_coarse[:1], e) for e in range(1, near)]
+    turned, mixed = turn_own(lay, late_joined, late_coarse)
+    held = (partner, inputs, near_coarse, turned, mixed)
+    partner, inputs, near_coarse, turned, mixed = lax.optimization_barrier(held)
     if two_owners:
         sent = partner[0][:, pairs + side :].reshape(-1)[: 2 * n_listed].astype(jnp.int32)
         listed = jnp.concatenate([listed, ((sent[:n_listed] << 8) + sent[n_listed:])[None]], axis=0)
     plan = make_plan(lay, ids, listed, fine_coarse, coarse_slot)
-    turned, turned_own, mixed = turn(lay, rest, joined, *partner)
     for part in partner:
         inputs = inputs + in_plane(part)
-    lines = [along(mixed if d < near else turned_own, d) for d in lay.line_steps()]
-    held = (inputs, turned, lines, near_coarse, plan)
-    inputs, turned, lines, near_coarse, plan = lax.optimization_barrier(held)
+    lines = [along(mixed if d < near else turned, d) for d in lay.line_steps()]
+    for part in partner:
+        turned = turn_both(lay, part, turned)
+    held = (inputs, turned, lines, near_coarse, plan, coarse)
+    inputs, turned, lines, near_coarse, plan, coarse = lax.optimization_barrier(held)
     blocks_coarse = [coarse, to_core(coarse)]
     lefts = [turned] + lines
     lefts_core = [to_core(part) for part in lefts]

time: 173 us -> 168 us (0.971)
  local copies, waits for them, and re-layouts: 11.6 us -> 4.79 us
  Pallas kernels: 35.1 us -> 40 us
  waiting for transfers between devices: 82.1 us -> 78.9 us
  other arithmetic: 5.48 us -> 7.92 us
    unnamed x38 -> x34, local copies, waits for them, and re-layouts: 8.83 us -> 2.8 us
    pallas_call x2, Pallas kernels: 7.87 us -> 13.7 us  [project(): pl.pallas_call(functools.partial(project_kernel, lay, owner), out_shape=j...]
    ppermute x25, waiting for transfers between devices: 82.1 us -> 78.9 us  [move(): return lax.ppermute(array, axes, pairs_list)]
    another operation x2, other arithmetic: 0.24 us -> 2.67 us
  transfers between devices with their start and end apart: 25 -> 25, of which waited for: 13 -> 16; matrix products, arithmetic and copies ran while one was open for 3% -> 1% of each run, Pallas kernels for 9% -> 13%
where the time goes in v4:
time: 168 us; the launch traced here: 166 us
  waiting for transfers between devices  78.9 us (47%)
  Pallas kernels  40 us (24%)
  starting transfers between devices  33.2 us (20%)
  other arithmetic  7.92 us (5%)
  local copies, waits for them, and re-layouts  4.79 us (3%)
  between operations  1.69 us (1%)
    ppermute x25, waiting for transfers between devices, move(): return lax.ppermute(array, axes, pairs_list)  78.9 us
    ppermute x25, starting transfers between devices, move(): return lax.ppermute(array, axes, pairs_list)  33.2 us
    pallas_call x2, Pallas kernels, project(): pl.pallas_call(functools.partial(project_kernel, lay, owner), out_shape=j...  13.7 us
    pallas_call x1, Pallas kernels, make_tiles(): pl.pallas_call(functools.partial(tiles_kernel, lay), out_shape=(sums, sum...  13.1 us
    pallas_call x1, Pallas kernels, make_plan(): pl.pallas_call(functools.partial(plan_kernel, lay), out_shape=tuple((jax....  6.13 us
    pallas_call x1, Pallas kernels, apply_tiles(): pl.pallas_call(functools.partial(apply_kernel, lay), out_shape=(sums, sum...  5.73 us
  transfers between devices with their start and end apart: 25, of which 16 were waited for; matrix products, arithmetic and copies ran while one was open for 1% of the time, Pallas kernels for 13%

profile of v4, /device:TPU:0, one launch (start us, length us, event | category | flops | bytes accessed | tf_op | source)
XLA Modules:
  0.0 166.5 jit_solution(7064161949631575181)
XLA Ops:
  1.4 0.9 convert_element_type.34
  2.3 0.7 convert_bitcast_fusion.1
  3.1 1.0 pad_maximum_fusion.given.refs_0_
  4.2 1.3 slice.61
  5.5 3.1 %collective-permute-start.4 = (bf16[1,1,512,512]{3,2,1,0:T(8,128)(2,1)S(1)}, bf16[1,1,512,512]{3,2,1,0:T(8,128)(2,1)}, u32[]{:S(2)}, u32[]{:S(2)}) collective-permute-start(bf16[1,1,512,512]{3,2,1,0:T(8,128)(2,1)S(1)} %slice.61), channel_id=1, source_target_pairs={{0,8},{1,9},{2,10},{3,11},{4,12},{5,13},{6,14},{7,15},{8,0},{9,1},... | collective-permute-start | bytes 1572872 | tf_op jit(solution)/shard_map/ppermute | solution.py:449
  8.5 2.4 %collective-permute-start.3 = (bf16[3,656,128]{2,1,0:T(8,128)(2,1)S(1)}, bf16[3,656,128]{2,1,0:T(8,128)(2,1)S(1)}, u32[]{:S(2)}, u32[]{:S(2)}) collective-permute-start(bf16[3,656,128]{2,1,0:T(8,128)(2,1)S(1)} %pad_maximum_fusion.given.refs_0_), channel_id=1, source_target_pairs={{0,3},{1,2},{2,1},{3,0},{4,7},{5,6},{6,5},{7,4},{8,11},{9,10},{10,... | collective-permute-start | bytes 1511432 | tf_op jit(solution)/shard_map/ppermute | solution.py:449
  11.0 0.5 collective-permute-start.2
  11.5 0.5 collective-permute-start.1
  12.0 2.6 %collective-permute-start = (bf16[3,656,128]{2,1,0:T(8,128)(2,1)S(1)}, bf16[3,656,128]{2,1,0:T(8,128)(2,1)S(1)}, u32[]{:S(2)}, u32[]{:S(2)}) collective-permute-start(bf16[3,656,128]{2,1,0:T(8,128)(2,1)S(1)} %pad_maximum_fusion.given.refs_0_), channel_id=1, source_target_pairs={{0,16},{1,17},{2,18},{3,19},{4,20},{5,21},{6,22},{7,23},{8,24},{9,... | collective-permute-start | bytes 1511432 | tf_op jit(solution)/shard_map/ppermute | solution.py:449
  14.6 1.2 copy-done
  15.8 1.1 shard_map.95
  17.0 6.9 %collective-permute-done.3.refs_3_ = bf16[3,656,128]{2,1,0:T(8,128)(2,1)S(1)} collective-permute-done((bf16[3,656,128]{2,1,0:T(8,128)(2,1)S(1)}, bf16[3,656,128]{2,1,0:T(8,128)(2,1)S(1)}, u32[]{:S(2)}, u32[]{:S(2)}) %collective-permute-start.3) | collective-permute-done | bytes 503840 | tf_op jit(solution)/shard_map/ppermute | solution.py:449
  23.9 9.3 %collective-permute-done.2.refs_2_ = bf16[3,656,128]{2,1,0:T(8,128)(2,1)S(1)} collective-permute-done((bf16[3,656,128]{2,1,0:T(8,128)(2,1)S(1)}, bf16[3,656,128]{2,1,0:T(8,128)(2,1)S(1)}, u32[]{:S(2)}, u32[]{:S(2)}) %collective-permute-start.2) | collective-permute-done | bytes 503840 | tf_op jit(solution)/shard_map/ppermute | solution.py:449
  33.3 2.6 %collective-permute-done.given.refs_0_.refs_4_ = bf16[3,656,128]{2,1,0:T(8,128)(2,1)S(1)} collective-permute-done((bf16[3,656,128]{2,1,0:T(8,128)(2,1)S(1)}, bf16[3,656,128]{2,1,0:T(8,128)(2,1)S(1)}, u32[]{:S(2)}, u32[]{:S(2)}) %collective-permute-start) | collective-permute-done | bytes 503840 | tf_op jit(solution)/shard_map/ppermute | solution.py:449
  36.0 0.7 pad_add_fusion.2.ids
  36.7 2.5 %collective-permute-start.7 = (bf16[3,656,128]{2,1,0:T(8,128)(2,1)S(1)}, bf16[3,656,128]{2,1,0:T(8,128)(2,1)}, u32[]{:S(2)}, u32[]{:S(2)}) collective-permute-start(bf16[3,656,128]{2,1,0:T(8,128)(2,1)S(1)} %collective-permute-done.given.refs_0_.refs_4_), channel_id=1, source_target_pairs={{0,3},{1,2},{2,1},{3,0},{4,7},{5,6},{6,5},{7,4},{8,11},{9,10},{10,... | collective-permute-start | bytes 1511432 | tf_op jit(solution)/shard_map/ppermute | solution.py:449
  39.6 0.5 collective-permute-start.5
  40.2 2.5 %collective-permute-start.9 = (bf16[3,128,512]{2,1,0:T(8,128)(2,1)S(1)}, bf16[3,128,512]{2,1,0:T(8,128)(2,1)}, u32[]{:S(2)}, u32[]{:S(2)}) collective-permute-start(bf16[3,128,512]{2,1,0:T(8,128)(2,1)S(1)} %get-tuple-element.51.own), channel_id=1, source_target_pairs={{0,24},{1,25},{2,26},{3,27},{4,28},{5,29},{6,30},{7,31},{8,16},{9,... | collective-permute-start | bytes 1179656 | tf_op jit(solution)/shard_map/ppermute | solution.py:449
  42.7 0.6 pad_add_fusion.listed
  43.4 6.1 %shard_map.97 = (s32[24]{0:T(128)}, s32[26]{0:T(128)}, s32[4]{0:T(128)}, s32[72]{0:T(128)}, s32[288]{0:T(512)}) custom-call(s32[3]{0:T(128)} %pad_add_fusion.2.ids, s32[2,97]{1,0:T(2,128)} %pad_add_fusion.listed, s32[96]{0:T(128)} %fine.1, s32[8]{0:T(128)} %stored.1), custom_call_target="tpu_custom_call" | custom-call | bytes 20000000 | tf_op jit(solution)/shard_map/pallas_call | solution.py:137
  49.7 17.5 %collective-permute-done.9.refs_10_ = bf16[3,128,512]{2,1,0:T(8,128)(2,1)} collective-permute-done((bf16[3,128,512]{2,1,0:T(8,128)(2,1)S(1)}, bf16[3,128,512]{2,1,0:T(8,128)(2,1)}, u32[]{:S(2)}, u32[]{:S(2)}) %collective-permute-start.9) | collective-permute-done | bytes 393248 | tf_op jit(solution)/shard_map/ppermute | solution.py:449
  68.4 4.6 %collective-permute-done.14.refs_8_ = bf16[1,1,512,512]{3,2,1,0:T(8,128)(2,1)S(1)} collective-permute-done((bf16[1,1,512,512]{3,2,1,0:T(8,128)(2,1)}, bf16[1,1,512,512]{3,2,1,0:T(8,128)(2,1)S(1)}, u32[]{:S(2)}, u32[]{:S(2)}) %collective-permute-start.14) | collective-permute-done | bytes 524320 | tf_op jit(solution)/shard_map/ppermute | solution.py:449
  73.0 0.7 collective-permute-done.11.refs_9_.refs_12_
  73.8 7.2 %shard_map.99.refs_15_ = bf16[12,512,256]{2,1,0:T(8,128)(2,1)} custom-call(s32[24]{0:T(128)} %get-tuple-element.73.slot_of, s32[26]{0:T(128)} %get-tuple-element.74.valid, s32[4]{0:T(128)} %get-tuple-element.59.sizes, bf16[3,656,128]{2,1,0:T(8,128)(2,1)} %copy-done.3, bf16[3,656,128]{2,1,0:T(8,128)(2,1)} %collective-permute-done.5.refs_1_.refs_5_, ...), custom_call_target="tpu_custom_call" | custom-call | flops 1000000000 | bytes 20000000 | tf_op jit(solution)/shard_map/pallas_call | solution.py:191
  81.0 6.6 %shard_map.98.refs_14_ = bf16[12,512,256]{2,1,0:T(8,128)(2,1)} custom-call(s32[24]{0:T(128)} %get-tuple-element.73.slot_of, s32[26]{0:T(128)} %get-tuple-element.74.valid, s32[4]{0:T(128)} %get-tuple-element.59.sizes, bf16[3,656,128]{2,1,0:T(8,128)(2,1)} %copy-done.2, bf16[3,656,128]{2,1,0:T(8,128)(2,1)} %copy-done.10, bf16[3,656,128]{2,1,0:T(8,128)(2,1)} %copy-done.9, ...), custom_call_target="tpu_custom_call" | custom-call | flops 1000000000 | bytes 20000000 | tf_op jit(solution)/shard_map/pallas_call | solution.py:191
  87.6 0.8 copy-done.16
  88.3 13.1 %shard_map.100 = (f32[12,128,128]{2,1,0:T(8,128)}, f32[12,128,128]{2,1,0:T(8,128)}, bf16[288,128,128]{2,1,0:T(8,128)(2,1)}) custom-call(s32[4]{0:T(128)} %get-tuple-element.59.sizes, s32[72]{0:T(128)} %get-tuple-element.60.group_input, s32[288]{0:T(512)} %get-tuple-element.61.entries, bf16[3,656,128]{2,1,0:T(8,128)(2,1)} %copy-done.2, ...), custom_call_target="tpu_custom_call" | custom-call | flops 4000000000 | bytes 30000000 | tf_op jit(solution)/shard_map/pallas_call | solution.py:347
  101.5 2.1 %collective-permute-start.15 = (f32[12,128,128]{2,1,0:T(8,128)}, f32[12,128,128]{2,1,0:T(8,128)S(1)}, u32[]{:S(2)}, u32[]{:S(2)}) collective-permute-start(f32[12,128,128]{2,1,0:T(8,128)} %get-tuple-element.78), channel_id=1, source_target_pairs={{0,4},{1,5},{2,6},{3,7},{4,0},{5,1},{6,2},{7,3},{8,12},{9,13},{10,... | collective-permute-start | bytes 2359304 | tf_op jit(solution)/shard_map/ppermute | solution.py:449
  103.6 2.1 %collective-permute-done.15 = f32[12,128,128]{2,1,0:T(8,128)S(1)} collective-permute-done((f32[12,128,128]{2,1,0:T(8,128)}, f32[12,128,128]{2,1,0:T(8,128)S(1)}, u32[]{:S(2)}, u32[]{:S(2)}) %collective-permute-start.15) | collective-permute-done | bytes 786464 | tf_op jit(solution)/shard_map/ppermute | solution.py:449
  105.7 1.3 fusion.13
  107.3 7.0 %collective-permute-done.16 = bf16[2,3,128,128]{3,2,1,0:T(8,128)(2,1)S(1)} collective-permute-done((bf16[2,3,128,128]{3,2,1,0:T(8,128)(2,1)S(1)}, bf16[2,3,128,128]{3,2,1,0:T(8,128)(2,1)S(1)}, u32[]{:S(2)}, u32[]{:S(2)}) %collective-permute-start.16) | collective-permute-done | bytes 196640 | tf_op jit(solution)/shard_map/ppermute | solution.py:449
  114.4 3.3 %collective-permute-start.17 = (bf16[2,3,128,128]{3,2,1,0:T(8,128)(2,1)S(1)}, bf16[2,3,128,128]{3,2,1,0:T(8,128)(2,1)S(1)}, u32[]{:S(2)}, u32[]{:S(2)}) collective-permute-start(bf16[2,3,128,128]{3,2,1,0:T(8,128)(2,1)S(1)} %fusion), channel_id=1, source_target_pairs={{0,16},{1,17},{2,18},{3,19},{4,20},{5,21},{6,22},{7,23},{8,24},{9,... | collective-permute-start | bytes 589832 | tf_op jit(solution)/shard_map/ppermute | solution.py:449
  117.7 8.9 %collective-permute-done.17 = bf16[2,3,128,128]{3,2,1,0:T(8,128)(2,1)S(1)} collective-permute-done((bf16[2,3,128,128]{3,2,1,0:T(8,128)(2,1)S(1)}, bf16[2,3,128,128]{3,2,1,0:T(8,128)(2,1)S(1)}, u32[]{:S(2)}, u32[]{:S(2)}) %collective-permute-start.17) | collective-permute-done | bytes 196640 | tf_op jit(solution)/shard_map/ppermute | solution.py:449
  126.7 2.0 %collective-permute-start.20 = (bf16[2,3,128,128]{3,2,1,0:T(8,128)(2,1)S(1)}, bf16[2,3,128,128]{3,2,1,0:T(8,128)(2,1)S(1)}, u32[]{:S(2)}, u32[]{:S(2)}) collective-permute-start(bf16[2,3,128,128]{3,2,1,0:T(8,128)(2,1)S(1)} %get-tuple-element.84.refs_0_), channel_id=1, source_target_pairs={{0,3},{1,2},{2,1},{3,0},{4,7},{5,6},{6,5},{7,4},{8,11},{9,10},{10,... | collective-permute-start | bytes 589832 | tf_op jit(solution)/shard_map/ppermute | solution.py:449
  128.8 2.6 %collective-permute-start.19 = (bf16[2,3,128,128]{3,2,1,0:T(8,128)(2,1)S(1)}, bf16[2,3,128,128]{3,2,1,0:T(8,128)(2,1)S(1)}, u32[]{:S(2)}, u32[]{:S(2)}) collective-permute-start(bf16[2,3,128,128]{3,2,1,0:T(8,128)(2,1)S(1)} %get-tuple-element.84.refs_0_), channel_id=1, source_target_pairs={{0,2},{1,3},{2,0},{3,1},{4,6},{5,7},{6,4},{7,5},{8,10},{9,11},{10,... | collective-permute-start | bytes 589832 | tf_op jit(solution)/shard_map/ppermute | solution.py:449
  131.4 3.5 %collective-permute-done.20.refs_3_ = bf16[2,3,128,128]{3,2,1,0:T(8,128)(2,1)S(1)} collective-permute-done((bf16[2,3,128,128]{3,2,1,0:T(8,128)(2,1)S(1)}, bf16[2,3,128,128]{3,2,1,0:T(8,128)(2,1)S(1)}, u32[]{:S(2)}, u32[]{:S(2)}) %collective-permute-start.20) | collective-permute-done | bytes 196640 | tf_op jit(solution)/shard_map/ppermute | solution.py:449
  134.9 3.6 %collective-permute-done.19.refs_2_ = bf16[2,3,128,128]{3,2,1,0:T(8,128)(2,1)S(1)} collective-permute-done((bf16[2,3,128,128]{3,2,1,0:T(8,128)(2,1)S(1)}, bf16[2,3,128,128]{3,2,1,0:T(8,128)(2,1)S(1)}, u32[]{:S(2)}, u32[]{:S(2)}) %collective-permute-start.19) | collective-permute-done | bytes 196640 | tf_op jit(solution)/shard_map/ppermute | solution.py:449
  138.6 1.1 collective-permute-done.18.refs_1_
  139.6 0.7 copy-done.13
  140.3 5.7 %shard_map.101 = (f32[12,128,128]{2,1,0:T(8,128)}, f32[12,128,128]{2,1,0:T(8,128)}) custom-call(s32[4]{0:T(128)} %get-tuple-element.59.sizes, s32[72]{0:T(128)} %get-tuple-element.60.group_input, s32[288]{0:T(512)} %get-tuple-element.61.entries, bf16[288,128,128]{2,1,0:T(8,128)(2,1)} %get-tuple-element.79.tiles_in, bf16[2,3,128,128]{3,2,1,0:T(8,128)(2,1)} %copy-done.7, ...), custom_call_target="tpu_custom_call" | custom-call | flops 400000000 | bytes 4000000 | tf_op jit(solution)/shard_map/pallas_call | solution.py:413
  146.1 2.5 %collective-permute-done.21 = f32[12,128,128]{2,1,0:T(8,128)S(1)} collective-permute-done((f32[12,128,128]{2,1,0:T(8,128)}, f32[12,128,128]{2,1,0:T(8,128)S(1)}, u32[]{:S(2)}, u32[]{:S(2)}) %collective-permute-start.21) | collective-permute-done | bytes 786464 | tf_op jit(solution)/shard_map/ppermute | solution.py:449
  148.6 1.3 fusion.11
  149.9 1.4 collective-permute-start.22
  151.3 4.7 %collective-permute-start.24 = (bf16[3,128,128]{2,1,0:T(8,128)(2,1)S(1)}, bf16[3,128,128]{2,1,0:T(8,128)(2,1)S(1)}, u32[]{:S(2)}, u32[]{:S(2)}) collective-permute-start(bf16[3,128,128]{2,1,0:T(8,128)(2,1)S(1)} %get-tuple-element.91), channel_id=1, source_target_pairs={{0,24},{1,25},{2,26},{3,27},{4,28},{5,29},{6,30},{7,31},{8,16},{9,... | collective-permute-start | bytes 294920 | tf_op jit(solution)/shard_map/ppermute | solution.py:449
  156.5 0.7 slice.83
  157.2 4.5 %collective-permute-done.24 = bf16[3,128,128]{2,1,0:T(8,128)(2,1)S(1)} collective-permute-done((bf16[3,128,128]{2,1,0:T(8,128)(2,1)S(1)}, bf16[3,128,128]{2,1,0:T(8,128)(2,1)S(1)}, u32[]{:S(2)}, u32[]{:S(2)}) %collective-permute-start.24) | collective-permute-done | bytes 98336 | tf_op jit(solution)/shard_map/ppermute | solution.py:449
  161.8 3.9 %collective-permute-done.23 = bf16[3,128,128]{2,1,0:T(8,128)(2,1)S(1)} collective-permute-done((bf16[3,128,128]{2,1,0:T(8,128)(2,1)S(1)}, bf16[3,128,128]{2,1,0:T(8,128)(2,1)S(1)}, u32[]{:S(2)}, u32[]{:S(2)}) %collective-permute-start.23) | collective-permute-done | bytes 98336 | tf_op jit(solution)/shard_map/ppermute | solution.py:449
  165.7 0.8 fusion.5
  (63 shorter events, 3.3 us)
Async XLA Ops:
  0.6 42.1 %copy-start.15 = (s32[1,96]{1,0:T(1,128)S(1)}, s32[1,96]{1,0:T(1,128)}, u32[]{:S(2)}) copy-start(s32[1,96]{1,0:T(1,128)} %param.14) | copy-start | bytes 1156
  0.6 66.6 %copy-start.1 = (bf16[2,1,512,512]{3,2,1,0:T(8,128)(2,1)S(1)}, bf16[2,1,512,512]{3,2,1,0:T(8,128)(2,1)}, u32[]{:S(2)}) copy-start(bf16[2,1,512,512]{3,2,1,0:T(8,128)(2,1)} %refs_4_.1) | copy-start | bytes 3145732
  4.2 76.8 %copy-start.2 = (bf16[3,656,128]{2,1,0:T(8,128)(2,1)}, bf16[3,656,128]{2,1,0:T(8,128)(2,1)S(1)}, u32[]{:S(2)}) copy-start(bf16[3,656,128]{2,1,0:T(8,128)(2,1)S(1)} %pad_maximum_fusion.given.refs_0_) | copy-start | bytes 1511428
  5.5 30.4 %collective-permute-start.4 = (bf16[1,1,512,512]{3,2,1,0:T(8,128)(2,1)S(1)}, bf16[1,1,512,512]{3,2,1,0:T(8,128)(2,1)}, u32[]{:S(2)}, u32[]{:S(2)}) collective-permute-start(bf16[1,1,512,512]{3,2,1,0:T(8,128)(2,1)S(1)} %slice.61), channel_id=1, source_target_pairs={{0,8},{1,9},{2,10},{3,11},{4,12},{5,13},{6,14},{7,15},{8,0},{9,1},... | collective-permute-start | bytes 1572872 | tf_op jit(solution)/shard_map/ppermute | solution.py:449
  8.5 15.4 %collective-permute-start.3 = (bf16[3,656,128]{2,1,0:T(8,128)(2,1)S(1)}, bf16[3,656,128]{2,1,0:T(8,128)(2,1)S(1)}, u32[]{:S(2)}, u32[]{:S(2)}) collective-permute-start(bf16[3,656,128]{2,1,0:T(8,128)(2,1)S(1)} %pad_maximum_fusion.given.refs_0_), channel_id=1, source_target_pairs={{0,3},{1,2},{2,1},{3,0},{4,7},{5,6},{6,5},{7,4},{8,11},{9,10},{10,... | collective-permute-start | bytes 1511432 | tf_op jit(solution)/shard_map/ppermute | solution.py:449
  11.0 22.2 %collective-permute-start.2 = (bf16[3,656,128]{2,1,0:T(8,128)(2,1)S(1)}, bf16[3,656,128]{2,1,0:T(8,128)(2,1)S(1)}, u32[]{:S(2)}, u32[]{:S(2)}) collective-permute-start(bf16[3,656,128]{2,1,0:T(8,128)(2,1)S(1)} %pad_maximum_fusion.given.refs_0_), channel_id=1, source_target_pairs={{0,2},{1,3},{2,0},{3,1},{4,6},{5,7},{6,4},{7,5},{8,10},{9,11},{10,... | collective-permute-start | bytes 1511432 | tf_op jit(solution)/shard_map/ppermute | solution.py:449
  11.5 21.8 %collective-permute-start.1 = (bf16[3,656,128]{2,1,0:T(8,128)(2,1)S(1)}, bf16[3,656,128]{2,1,0:T(8,128)(2,1)S(1)}, u32[]{:S(2)}, u32[]{:S(2)}) collective-permute-start(bf16[3,656,128]{2,1,0:T(8,128)(2,1)S(1)} %pad_maximum_fusion.given.refs_0_), channel_id=1, source_target_pairs={{0,1},{1,0},{2,3},{3,2},{4,5},{5,4},{6,7},{7,6},{8,9},{9,8},{10,11... | collective-permute-start | bytes 1511432 | tf_op jit(solution)/shard_map/ppermute | solution.py:449
  12.0 23.8 %collective-permute-start = (bf16[3,656,128]{2,1,0:T(8,128)(2,1)S(1)}, bf16[3,656,128]{2,1,0:T(8,128)(2,1)S(1)}, u32[]{:S(2)}, u32[]{:S(2)}) collective-permute-start(bf16[3,656,128]{2,1,0:T(8,128)(2,1)S(1)} %pad_maximum_fusion.given.refs_0_), channel_id=1, source_target_pairs={{0,16},{1,17},{2,18},{3,19},{4,20},{5,21},{6,22},{7,23},{8,24},{9,... | collective-permute-start | bytes 1511432 | tf_op jit(solution)/shard_map/ppermute | solution.py:449
  14.6 1.2 copy-start
  23.9 12.0 %copy-start.8 = (bf16[3,656,128]{2,1,0:T(8,128)(2,1)}, bf16[3,656,128]{2,1,0:T(8,128)(2,1)S(1)}, u32[]{:S(2)}) copy-start(bf16[3,656,128]{2,1,0:T(8,128)(2,1)S(1)} %collective-permute-done.3.refs_3_) | copy-start | bytes 1511428
  33.2 2.7 %copy-start.9 = (bf16[3,656,128]{2,1,0:T(8,128)(2,1)}, bf16[3,656,128]{2,1,0:T(8,128)(2,1)S(1)}, u32[]{:S(2)}) copy-start(bf16[3,656,128]{2,1,0:T(8,128)(2,1)S(1)} %collective-permute-done.2.refs_2_) | copy-start | bytes 1511428
  33.3 2.6 %copy-start.10 = (bf16[3,656,128]{2,1,0:T(8,128)(2,1)}, bf16[3,656,128]{2,1,0:T(8,128)(2,1)S(1)}, u32[]{:S(2)}) copy-start(bf16[3,656,128]{2,1,0:T(8,128)(2,1)S(1)} %collective-permute-done.1.refs_1_) | copy-start | bytes 1511428
  35.9 37.8 %copy-start.3 = (bf16[3,656,128]{2,1,0:T(8,128)(2,1)}, bf16[3,656,128]{2,1,0:T(8,128)(2,1)S(1)}, u32[]{:S(2)}) copy-start(bf16[3,656,128]{2,1,0:T(8,128)(2,1)S(1)} %collective-permute-done.given.refs_0_.refs_4_) | copy-start | bytes 1511428
  35.9 31.3 %collective-permute-start.8 = (bf16[896,512]{1,0:T(8,128)(2,1)}, bf16[896,512]{1,0:T(8,128)(2,1)}, u32[]{:S(2)}, u32[]{:S(2)}) collective-permute-start(bf16[896,512]{1,0:T(8,128)(2,1)} %get-tuple-element.52), channel_id=1, source_target_pairs={{0,8},{1,9},{2,10},{3,11},{4,12},{5,13},{6,14},{7,15},{8,0},{9,1},... | collective-permute-start | bytes 2752520 | tf_op jit(solution)/shard_map/ppermute | solution.py:449
  36.7 30.5 %collective-permute-start.7 = (bf16[3,656,128]{2,1,0:T(8,128)(2,1)S(1)}, bf16[3,656,128]{2,1,0:T(8,128)(2,1)}, u32[]{:S(2)}, u32[]{:S(2)}) collective-permute-start(bf16[3,656,128]{2,1,0:T(8,128)(2,1)S(1)} %collective-permute-done.given.refs_0_.refs_4_), channel_id=1, source_target_pairs={{0,3},{1,2},{2,1},{3,0},{4,7},{5,6},{6,5},{7,4},{8,11},{9,10},{10,... | collective-permute-start | bytes 1511432 | tf_op jit(solution)/shard_map/ppermute | solution.py:449
  39.1 28.1 %collective-permute-start.6 = (bf16[3,656,128]{2,1,0:T(8,128)(2,1)S(1)}, bf16[3,656,128]{2,1,0:T(8,128)(2,1)}, u32[]{:S(2)}, u32[]{:S(2)}) collective-permute-start(bf16[3,656,128]{2,1,0:T(8,128)(2,1)S(1)} %collective-permute-done.given.refs_0_.refs_4_), channel_id=1, source_target_pairs={{0,2},{1,3},{2,0},{3,1},{4,6},{5,7},{6,4},{7,5},{8,10},{9,11},{10,... | collective-permute-start | bytes 1511432 | tf_op jit(solution)/shard_map/ppermute | solution.py:449
  39.6 27.6 %collective-permute-start.5 = (bf16[3,656,128]{2,1,0:T(8,128)(2,1)S(1)}, bf16[3,656,128]{2,1,0:T(8,128)(2,1)}, u32[]{:S(2)}, u32[]{:S(2)}) collective-permute-start(bf16[3,656,128]{2,1,0:T(8,128)(2,1)S(1)} %collective-permute-done.given.refs_0_.refs_4_), channel_id=1, source_target_pairs={{0,1},{1,0},{2,3},{3,2},{4,5},{5,4},{6,7},{7,6},{8,9},{9,8},{10,11... | collective-permute-start | bytes 1511432 | tf_op jit(solution)/shard_map/ppermute | solution.py:449
  40.2 27.0 %collective-permute-start.9 = (bf16[3,128,512]{2,1,0:T(8,128)(2,1)S(1)}, bf16[3,128,512]{2,1,0:T(8,128)(2,1)}, u32[]{:S(2)}, u32[]{:S(2)}) collective-permute-start(bf16[3,128,512]{2,1,0:T(8,128)(2,1)S(1)} %get-tuple-element.51.own), channel_id=1, source_target_pairs={{0,24},{1,25},{2,26},{3,27},{4,28},{5,29},{6,30},{7,31},{8,16},{9,... | collective-permute-start | bytes 1179656 | tf_op jit(solution)/shard_map/ppermute | solution.py:449
  49.7 31.3 %copy-start.4 = (bf16[6,128,512]{2,1,0:T(8,128)(2,1)}, bf16[6,128,512]{2,1,0:T(8,128)(2,1)S(1)}, u32[]{:S(2)}) copy-start(bf16[6,128,512]{2,1,0:T(8,128)(2,1)S(1)} %shard_map.96.refs_8_) | copy-start | bytes 2359300
  67.2 6.5 %collective-permute-start.13 = (bf16[2,1,512,512]{3,2,1,0:T(8,128)(2,1)S(1)}, bf16[2,1,512,512]{3,2,1,0:T(8,128)(2,1)}, u32[]{:S(2)}, u32[]{:S(2)}) collective-permute-start(bf16[2,1,512,512]{3,2,1,0:T(8,128)(2,1)S(1)} %copy-done.1), channel_id=1, source_target_pairs={{0,4},{1,5},{2,6},{3,7},{4,0},{5,1},{6,2},{7,3},{8,12},{9,13},{10,... | collective-permute-start | bytes 3145736 | tf_op jit(solution)/shard_map/ppermute | solution.py:449
  67.3 6.4 %collective-permute-start.11 = (bf16[896,512]{1,0:T(8,128)(2,1)}, bf16[896,512]{1,0:T(8,128)(2,1)}, u32[]{:S(2)}, u32[]{:S(2)}) collective-permute-start(bf16[896,512]{1,0:T(8,128)(2,1)} %collective-permute-done.8.refs_7_.refs_9_), channel_id=1, source_target_pairs={{0,4},{1,5},{2,6},{3,7},{4,0},{5,1},{6,2},{7,3},{8,12},{9,13},{10,... | collective-permute-start | bytes 2752520 | tf_op jit(solution)/shard_map/ppermute | solution.py:449
  67.8 19.8 %collective-permute-start.10 = (bf16[6,128,512]{2,1,0:T(8,128)(2,1)S(1)}, bf16[6,128,512]{2,1,0:T(8,128)(2,1)}, u32[]{:S(2)}, u32[]{:S(2)}) collective-permute-start(bf16[6,128,512]{2,1,0:T(8,128)(2,1)S(1)} %shard_map.96.refs_8_), channel_id=1, source_target_pairs={{0,4},{1,5},{2,6},{3,7},{4,0},{5,1},{6,2},{7,3},{8,12},{9,13},{10,... | collective-permute-start | bytes 2359304 | tf_op jit(solution)/shard_map/ppermute | solution.py:449
  67.9 5.1 %collective-permute-start.14 = (bf16[1,1,512,512]{3,2,1,0:T(8,128)(2,1)}, bf16[1,1,512,512]{3,2,1,0:T(8,128)(2,1)S(1)}, u32[]{:S(2)}, u32[]{:S(2)}) collective-permute-start(bf16[1,1,512,512]{3,2,1,0:T(8,128)(2,1)} %collective-permute-done.4.refs_6_), channel_id=1, source_target_pairs={{0,4},{1,5},{2,6},{3,7},{4,0},{5,1},{6,2},{7,3},{8,12},{9,13},{10,... | collective-permute-start | bytes 1572872 | tf_op jit(solution)/shard_map/ppermute | solution.py:449
  68.3 19.2 %collective-permute-start.12 = (bf16[3,128,512]{2,1,0:T(8,128)(2,1)}, bf16[3,128,512]{2,1,0:T(8,128)(2,1)S(1)}, u32[]{:S(2)}, u32[]{:S(2)}) collective-permute-start(bf16[3,128,512]{2,1,0:T(8,128)(2,1)} %collective-permute-done.9.refs_10_), channel_id=1, source_target_pairs={{0,4},{1,5},{2,6},{3,7},{4,0},{5,1},{6,2},{7,3},{8,12},{9,13},{10,... | collective-permute-start | bytes 1179656 | tf_op jit(solution)/shard_map/ppermute | solution.py:449
  73.0 0.8 copy-start.5
  87.6 0.8 copy-start.16
  101.5 5.7 %copy-start.6 = (f32[384,128]{1,0:T(8,128)S(1)}, f32[384,128]{1,0:T(8,128)}, u32[]{:S(2)}) copy-start(f32[384,128]{1,0:T(8,128)} %param.8) | copy-start | bytes 589828
  101.5 5.7 %copy-start.14 = (f32[384]{0:T(512)S(1)}, f32[384]{0:T(512)}, u32[]{:S(2)}) copy-start(f32[384]{0:T(512)} %param.9) | copy-start | bytes 4612
  101.5 4.2 %collective-permute-start.15 = (f32[12,128,128]{2,1,0:T(8,128)}, f32[12,128,128]{2,1,0:T(8,128)S(1)}, u32[]{:S(2)}, u32[]{:S(2)}) collective-permute-start(f32[12,128,128]{2,1,0:T(8,128)} %get-tuple-element.78), channel_id=1, source_target_pairs={{0,4},{1,5},{2,6},{3,7},{4,0},{5,1},{6,2},{7,3},{8,12},{9,13},{10,... | collective-permute-start | bytes 2359304 | tf_op jit(solution)/shard_map/ppermute | solution.py:449
  107.1 7.2 %collective-permute-start.16 = (bf16[2,3,128,128]{3,2,1,0:T(8,128)(2,1)S(1)}, bf16[2,3,128,128]{3,2,1,0:T(8,128)(2,1)S(1)}, u32[]{:S(2)}, u32[]{:S(2)}) collective-permute-start(bf16[2,3,128,128]{3,2,1,0:T(8,128)(2,1)S(1)} %pad_maximum_fusion.1), channel_id=1, source_target_pairs={{0,8},{1,9},{2,10},{3,11},{4,12},{5,13},{6,14},{7,15},{8,0},{9,1},... | collective-permute-start | bytes 589832 | tf_op jit(solution)/shard_map/ppermute | solution.py:449
  114.4 12.2 %collective-permute-start.17 = (bf16[2,3,128,128]{3,2,1,0:T(8,128)(2,1)S(1)}, bf16[2,3,128,128]{3,2,1,0:T(8,128)(2,1)S(1)}, u32[]{:S(2)}, u32[]{:S(2)}) collective-permute-start(bf16[2,3,128,128]{3,2,1,0:T(8,128)(2,1)S(1)} %fusion), channel_id=1, source_target_pairs={{0,16},{1,17},{2,18},{3,19},{4,20},{5,21},{6,22},{7,23},{8,24},{9,... | collective-permute-start | bytes 589832 | tf_op jit(solution)/shard_map/ppermute | solution.py:449
  126.7 12.9 %copy-start.7 = (bf16[2,3,128,128]{3,2,1,0:T(8,128)(2,1)}, bf16[2,3,128,128]{3,2,1,0:T(8,128)(2,1)S(1)}, u32[]{:S(2)}) copy-start(bf16[2,3,128,128]{3,2,1,0:T(8,128)(2,1)S(1)} %get-tuple-element.84.refs_0_) | copy-start | bytes 589828
  126.7 8.2 %collective-permute-start.20 = (bf16[2,3,128,128]{3,2,1,0:T(8,128)(2,1)S(1)}, bf16[2,3,128,128]{3,2,1,0:T(8,128)(2,1)S(1)}, u32[]{:S(2)}, u32[]{:S(2)}) collective-permute-start(bf16[2,3,128,128]{3,2,1,0:T(8,128)(2,1)S(1)} %get-tuple-element.84.refs_0_), channel_id=1, source_target_pairs={{0,3},{1,2},{2,1},{3,0},{4,7},{5,6},{6,5},{7,4},{8,11},{9,10},{10,... | collective-permute-start | bytes 589832 | tf_op jit(solution)/shard_map/ppermute | solution.py:449
  128.8 9.8 %collective-permute-start.19 = (bf16[2,3,128,128]{3,2,1,0:T(8,128)(2,1)S(1)}, bf16[2,3,128,128]{3,2,1,0:T(8,128)(2,1)S(1)}, u32[]{:S(2)}, u32[]{:S(2)}) collective-permute-start(bf16[2,3,128,128]{3,2,1,0:T(8,128)(2,1)S(1)} %get-tuple-element.84.refs_0_), channel_id=1, source_target_pairs={{0,2},{1,3},{2,0},{3,1},{4,6},{5,7},{6,4},{7,5},{8,10},{9,11},{10,... | collective-permute-start | bytes 589832 | tf_op jit(solution)/shard_map/ppermute | solution.py:449
  131.4 8.2 %collective-permute-start.18 = (bf16[2,3,128,128]{3,2,1,0:T(8,128)(2,1)S(1)}, bf16[2,3,128,128]{3,2,1,0:T(8,128)(2,1)S(1)}, u32[]{:S(2)}, u32[]{:S(2)}) collective-permute-start(bf16[2,3,128,128]{3,2,1,0:T(8,128)(2,1)S(1)} %get-tuple-element.84.refs_0_), channel_id=1, source_target_pairs={{0,1},{1,0},{2,3},{3,2},{4,5},{5,4},{6,7},{7,6},{8,9},{9,8},{10,11... | collective-permute-start | bytes 589832 | tf_op jit(solution)/shard_map/ppermute | solution.py:449
  134.9 4.7 %copy-start.11 = (bf16[2,3,128,128]{3,2,1,0:T(8,128)(2,1)}, bf16[2,3,128,128]{3,2,1,0:T(8,128)(2,1)S(1)}, u32[]{:S(2)}) copy-start(bf16[2,3,128,128]{3,2,1,0:T(8,128)(2,1)S(1)} %collective-permute-done.20.refs_3_) | copy-start | bytes 589828
  138.6 1.1 copy-start.12
  139.6 0.7 copy-start.13
  146.0 2.6 %collective-permute-start.21 = (f32[12,128,128]{2,1,0:T(8,128)}, f32[12,128,128]{2,1,0:T(8,128)S(1)}, u32[]{:S(2)}, u32[]{:S(2)}) collective-permute-start(f32[12,128,128]{2,1,0:T(8,128)} %get-tuple-element.81), channel_id=1, source_target_pairs={{0,4},{1,5},{2,6},{3,7},{4,0},{5,1},{6,2},{7,3},{8,12},{9,13},{10,... | collective-permute-start | bytes 2359304 | tf_op jit(solution)/shard_map/ppermute | solution.py:449
  149.9 7.3 %collective-permute-start.22 = (bf16[3,128,128]{2,1,0:T(8,128)(2,1)S(1)}, bf16[3,128,128]{2,1,0:T(8,128)(2,1)S(1)}, u32[]{:S(2)}, u32[]{:S(2)}) collective-permute-start(bf16[3,128,128]{2,1,0:T(8,128)(2,1)S(1)} %get-tuple-element.90), channel_id=1, source_target_pairs={{0,8},{1,9},{2,10},{3,11},{4,12},{5,13},{6,14},{7,15},{8,0},{9,1},... | collective-permute-start | bytes 294920 | tf_op jit(solution)/shard_map/ppermute | solution.py:449
  151.3 10.4 %collective-permute-start.24 = (bf16[3,128,128]{2,1,0:T(8,128)(2,1)S(1)}, bf16[3,128,128]{2,1,0:T(8,128)(2,1)S(1)}, u32[]{:S(2)}, u32[]{:S(2)}) collective-permute-start(bf16[3,128,128]{2,1,0:T(8,128)(2,1)S(1)} %get-tuple-element.91), channel_id=1, source_target_pairs={{0,24},{1,25},{2,26},{3,27},{4,28},{5,29},{6,30},{7,31},{8,16},{9,... | collective-permute-start | bytes 294920 | tf_op jit(solution)/shard_map/ppermute | solution.py:449
  156.0 9.6 %collective-permute-start.23 = (bf16[3,128,128]{2,1,0:T(8,128)(2,1)S(1)}, bf16[3,128,128]{2,1,0:T(8,128)(2,1)S(1)}, u32[]{:S(2)}, u32[]{:S(2)}) collective-permute-start(bf16[3,128,128]{2,1,0:T(8,128)(2,1)S(1)} %get-tuple-element.92), channel_id=1, source_target_pairs={{0,16},{1,17},{2,18},{3,19},{4,20},{5,21},{6,22},{7,23},{8,24},{9,... | collective-permute-start | bytes 294920 | tf_op jit(solution)/shard_map/ppermute | solution.py:449

commit v5 on v4

--- a/solution.py
+++ b/solution.py
@@ -144,65 +144,6 @@
     )(ids, listed, fine, stored)
 
 
-def project_kernel(lay, owner, slot_of, valid, sizes, *refs):
-    n_coarse = 2 * (2 * lay.near - 1)
-    given_in, given_coarse = refs[: lay.cols], list(refs[lay.cols : lay.cols + n_coarse])
-    out, right, blocks, sems = refs[lay.cols + n_coarse :]
-    copies = []
-
-    def fetch(source, target):
-        copies.append(pltpu.make_async_copy(source, target, sems.at[len(copies)]))
-        copies[-1].start()
-
-    for i in range(lay.cols):
-        fetch(given_in[i].at[:, pl.ds(0, lay.pairs)], right.at[pl.ds(i * lay.blocks, lay.blocks)])
-    for i in range(2 * lay.near):
-        first = given_coarse.pop(0)
-        for a in range(first.shape[0]):
-            fetch(first.at[a], blocks.at[a, pl.ds(i * lay.slots_dev, lay.slots_dev)])
-        if i < 2:
-            continue
-        rest = given_coarse.pop(0)
-        for a in range(1, lay.points):
-            for at in range(lay.slots_dev):
-                row = lay.blocks * lay.side + ((a - 1) * lay.slots_dev + at) * lay.pairs
-                fetch(rest.at[pl.ds(row, lay.pairs)], blocks.at[a, i * lay.slots_dev + at])
-    for copy in copies:
-        copy.wait()
-    found = sizes[1 + owner]
-
-    def visit(step, carry):
-        for lane in range(2):
-            i = valid[owner * (lay.spread + 1) + jnp.minimum(2 * step + lane, found - 1)]
-            slot = slot_of[owner * lay.spread + i]
-            for a in range(lay.points):
-                out[i, :, a * lay.side : (a + 1) * lay.side] = jnp.dot(
-                    blocks[a, slot], right[i], preferred_element_type=jnp.float32
-                ).astype(jnp.bfloat16)
-        return carry
-
-    lax.fori_loop(0, lax.div(found + 1, 2), visit, 0)
-
-
-def project(lay, owner, plan, inputs, coarse):
-    smem = pl.BlockSpec(memory_space=pltpu.SMEM)
-    hbm = pl.BlockSpec(memory_space=pl.ANY)
-    shape = (lay.spread, lay.pairs, lay.points * lay.side)
-    return pl.pallas_call(
-        functools.partial(project_kernel, lay, owner),
-        out_shape=jax.ShapeDtypeStruct(shape, jnp.bfloat16),
-        in_specs=[smem] * 3 + [hbm] * (len(inputs) + len(coarse)),
-        out_specs=pl.BlockSpec(memory_space=pltpu.VMEM),
-        scratch_shapes=[
-            pltpu.VMEM((lay.spread, lay.pairs, lay.side), jnp.bfloat16),
-            pltpu.VMEM((lay.points, lay.slots, lay.pairs, lay.pairs), jnp.bfloat16),
-            pltpu.SemaphoreType.DMA((len(inputs) + lay.slots * lay.points,)),
-        ],
-        compiler_params=pltpu.CompilerParams(vmem_limit_bytes=lay.vmem),
-        cost_estimate=pl.CostEstimate(flops=1_000_000_000, bytes_accessed=20_000_000, transcendentals=0),
-    )(*plan[:3], *inputs, *coarse)
-
-
 def add_products(lay, group, group_input, entries, tiles, rounded, total):
     held = tiles[pl.ds(group * lay.unroll, lay.unroll)].reshape(lay.unroll * lay.side, lay.side)
     products = jnp.dot(held, rounded[group_input[group]], preferred_element_type=jnp.float32)
@@ -257,21 +198,44 @@
     )(partner, own)
 
 
-def tiles_kernel(lay, sizes, group_input, entries, *refs):
-    n_in = lay.owners * lay.cols
+def tiles_kernel(lay, slot_of, valid, sizes, group_input, entries, *refs):
     lines = lay.line_steps()
     refs = list(refs)
-    given_in = [refs.pop(0) for _ in range(n_in)]
+    given_in = [refs.pop(0) for _ in range(lay.owners * lay.cols)]
     given_out = [refs.pop(0) for _ in range(2 * (1 + len(lines)))]
-    given_projected = [refs.pop(0) for _ in range(lay.owners)]
+    given_coarse = [refs.pop(0) for _ in range(2 * (2 * lay.near - 1))]
     own_sum, other_sum, tiles_out = refs[:3]
-    left, rounded, tiles, total, sems, out_sems = refs[3:]
-    copies = []
+    right, left, blocks, projected, rounded, tiles, total, sems, sum_sems, out_sems = refs[3:]
+    started, waited = [], []
 
     def fetch(source, target):
-        copies.append(pltpu.make_async_copy(source, target, sems.at[len(copies)]))
-        copies[-1].start()
-
+        started.append(pltpu.make_async_copy(source, target, sems.at[len(started) + len(waited)]))
+        started[-1].start()
+
+    def arrive(count):
+        for copy in started[:count]:
+            copy.wait()
+        waited.extend(started[:count])
+        del started[:count]
+
+    def fetch_inputs(owner):
+        for i in range(owner * lay.cols, (owner + 1) * lay.cols):
+            part = pl.ds(i * lay.blocks, lay.blocks)
+            fetch(given_in[i].at[:, pl.ds(0, lay.pairs)], right.at[part])
+
+    for i in range(2 * lay.near):
+        first = given_coarse.pop(0)
+        for a in range(first.shape[0]):
+            fetch(first.at[a], blocks.at[a, pl.ds(i * lay.slots_dev, lay.slots_dev)])
+        if i < 2:
+            continue
+        rest = given_coarse.pop(0)
+        for a in range(1, lay.points):
+            for at in range(lay.slots_dev):
+                row = lay.blocks * lay.side + ((a - 1) * lay.slots_dev + at) * lay.pairs
+                fetch(rest.at[pl.ds(row, lay.pairs)], blocks.at[a, i * lay.slots_dev + at])
+    fetch_inputs(0)
+    for_projection = len(started)
     for k in range(2):
         held = given_out[k * (1 + len(lines)) :]
         for g in range(lay.owners):
@@ -284,22 +248,38 @@
             else:
                 for t in range(lay.blocks):
                     fetch(held[1 + i].at[pl.ds(t * lay.side, lay.side)], left.at[spot + t])
-    for i in range(n_in):
+    for i, ref in enumerate(given_in):
         part = pl.ds(i * lay.blocks, lay.blocks)
-        fetch(given_in[i].at[:, pl.ds(lay.pairs, lay.side)], rounded.at[part])
+        fetch(ref.at[:, pl.ds(lay.pairs, lay.side)], rounded.at[part])
+    for_tiles = len(started) - for_projection
+    for owner in range(1, lay.owners):
+        fetch_inputs(owner)
     total[...] = jnp.zeros_like(total)
-    for copy in copies:
-        copy.wait()
+    arrive(for_projection)
     used = sizes[0]
 
-    for g in range(lay.owners):
+    for owner in range(lay.owners):
+        found = sizes[1 + owner]
+
+        def visit(step, carry):
+            for lane in range(2):
+                i = valid[owner * (lay.spread + 1) + jnp.minimum(2 * step + lane, found - 1)]
+                p = owner * lay.spread + i
+                for a in range(lay.points):
+                    projected[i, :, a * lay.side : (a + 1) * lay.side] = jnp.dot(
+                        blocks[a, slot_of[p]], right[p], preferred_element_type=jnp.float32
+                    ).astype(jnp.bfloat16)
+            return carry
+
+        lax.fori_loop(0, lax.div(found + 1, 2), visit, 0)
+        arrive(for_tiles if owner == 0 else 0)
 
         def group_step(group, carry):
-            right = given_projected[g][group_input[group] - g * lay.spread]
+            block = projected[group_input[group] - owner * lay.spread]
             numbers = [entries[group * lay.unroll + i] for i in range(lay.unroll)]
             places = [jnp.minimum(lax.div(n, lay.points), lay.outputs - 1) for n in numbers]
             lefts = jnp.concatenate([left[q] for q in places], axis=0)
-            both = jnp.dot(lefts, right, preferred_element_type=jnp.float32)
+            both = jnp.dot(lefts, block, preferred_element_type=jnp.float32)
             for i in range(lay.unroll):
                 mine = both[i * lay.side : (i + 1) * lay.side]
                 tile = mine[:, : lay.side]
@@ -310,9 +290,12 @@
             add_products(lay, group - 1, group_input, entries, tiles, rounded, total)
             return carry
 
-        first = 1 if g == 0 else sizes[lay.owners + g]
-        last = used if g == lay.owners - 1 else sizes[lay.owners + g + 1]
+        first = 1 if owner == 0 else sizes[lay.owners + owner]
+        last = used if owner == lay.owners - 1 else sizes[lay.owners + owner + 1]
         lax.fori_loop(first, last, group_step, 0)
+        if owner < lay.owners - 1:
+            arrive(lay.cols)
+
     span = chunk_groups * lay.unroll
 
     def store(chunk):
@@ -326,9 +309,7 @@
             store(chunk).start()
 
     add_products(lay, used - 1, group_input, entries, tiles, rounded, total)
-    own = lay.places * lay.blocks
-    own_sum[...] = total[0:own]
-    other_sum[...] = total[own : 2 * own]
+    give_sums(lay, total, own_sum, other_sum, sum_sems)
     for chunk in range(lay.groups // chunk_groups):
 
         @pl.when(used > chunk * chunk_groups)
@@ -336,36 +317,50 @@
             store(chunk).wait()
 
 
-def make_tiles(lay, plan, inputs, outputs, projected):
+def give_sums(lay, total, own_sum, other_sum, sems):
+    own = lay.places * lay.blocks
+    for copy in (
+        pltpu.make_async_copy(total.at[pl.ds(own, own)], other_sum, sems.at[1]),
+        pltpu.make_async_copy(total.at[pl.ds(0, own)], own_sum, sems.at[0]),
+    ):
+        copy.start()
+    pltpu.make_async_copy(total.at[pl.ds(own, own)], other_sum, sems.at[1]).wait()
+    pltpu.make_async_copy(total.at[pl.ds(0, own)], own_sum, sems.at[0]).wait()
+
+
+def make_tiles(lay, plan, inputs, outputs, coarse):
     smem = pl.BlockSpec(memory_space=pltpu.SMEM)
     hbm = pl.BlockSpec(memory_space=pl.ANY)
-    vmem = pl.BlockSpec(memory_space=pltpu.VMEM)
     own = lay.places * lay.blocks
     sums = jax.ShapeDtypeStruct((own, lay.side, lay.width), jnp.float32)
-    n_copies = len(inputs) + 2 * lay.places * lay.blocks
+    n_copies = 2 * len(inputs) + 2 * lay.places * lay.blocks + lay.slots * lay.points
     tiles = (lay.groups * lay.unroll, lay.side, lay.side)
     return pl.pallas_call(
         functools.partial(tiles_kernel, lay),
         out_shape=(sums, sums, jax.ShapeDtypeStruct(tiles, jnp.bfloat16)),
-        in_specs=[smem] * 3 + [hbm] * (len(inputs) + len(outputs)) + [vmem] * len(projected),
-        out_specs=(vmem, vmem, hbm),
+        in_specs=[smem] * 5 + [hbm] * (len(inputs) + len(outputs) + len(coarse)),
+        out_specs=(hbm,) * 3,
         scratch_shapes=[
+            pltpu.VMEM((lay.inputs, lay.pairs, lay.side), jnp.bfloat16),
             pltpu.VMEM((lay.outputs, lay.side, lay.pairs), jnp.bfloat16),
+            pltpu.VMEM((lay.points, lay.slots, lay.pairs, lay.pairs), jnp.bfloat16),
+            pltpu.VMEM((lay.spread, lay.pairs, lay.points * lay.side), jnp.bfloat16),
             pltpu.VMEM((lay.inputs, lay.side, lay.width), jnp.bfloat16),
             pltpu.VMEM(tiles, jnp.bfloat16),
             pltpu.VMEM((lay.outputs + 1, lay.side, lay.width), jnp.float32),
             pltpu.SemaphoreType.DMA((n_copies,)),
+            pltpu.SemaphoreType.DMA((2,)),
             pltpu.SemaphoreType.DMA((lay.groups // chunk_groups,)),
         ],
         compiler_params=pltpu.CompilerParams(vmem_limit_bytes=lay.vmem),
         cost_estimate=pl.CostEstimate(flops=4_000_000_000, bytes_accessed=30_000_000, transcendentals=0),
-    )(plan[2], *plan[3:], *inputs, *outputs, *projected)
+    )(*plan, *inputs, *outputs, *coarse)
 
 
 def apply_kernel(lay, sizes, group_input, entries, tiles_in, *refs):
     given_vec = refs[: lay.cols]
     own_sum, other_sum = refs[lay.cols : lay.cols + 2]
-    rounded, tiles, total, sems, out_sems = refs[lay.cols + 2 :]
+    rounded, tiles, total, sems, sum_sems, out_sems = refs[lay.cols + 2 :]
     used = sizes[0]
     span = chunk_groups * lay.unroll
 
@@ -399,32 +394,30 @@
         return carry
 
     lax.fori_loop(1, used, group_step, 0)
-    own = lay.places * lay.blocks
-    own_sum[...] = total[0:own]
-    other_sum[...] = total[own : 2 * own]
+    give_sums(lay, total, own_sum, other_sum, sum_sems)
 
 
 def apply_tiles(lay, plan, tiles, rounded):
     smem = pl.BlockSpec(memory_space=pltpu.SMEM)
     hbm = pl.BlockSpec(memory_space=pl.ANY)
-    vmem = pl.BlockSpec(memory_space=pltpu.VMEM)
     own = lay.places * lay.blocks
     sums = jax.ShapeDtypeStruct((own, lay.side, lay.width), jnp.float32)
     return pl.pallas_call(
         functools.partial(apply_kernel, lay),
         out_shape=(sums, sums),
         in_specs=[smem] * 3 + [hbm] * (1 + len(rounded)),
-        out_specs=(vmem, vmem),
+        out_specs=(hbm, hbm),
         scratch_shapes=[
             pltpu.VMEM((lay.inputs, lay.side, lay.width), jnp.bfloat16),
             pltpu.VMEM(tiles.shape, jnp.bfloat16),
             pltpu.VMEM((lay.outputs + 1, lay.side, lay.width), jnp.float32),
             pltpu.SemaphoreType.DMA((len(rounded) * lay.owners,)),
+            pltpu.SemaphoreType.DMA((2,)),
             pltpu.SemaphoreType.DMA((lay.groups // chunk_groups,)),
         ],
         compiler_params=pltpu.CompilerParams(vmem_limit_bytes=lay.vmem),
         cost_estimate=pl.CostEstimate(flops=400_000_000, bytes_accessed=4_000_000, transcendentals=0),
-    )(plan[2], *plan[3:], tiles, *rounded)
+    )(*plan[2:], tiles, *rounded)
 
 
 def on_device(
@@ -468,8 +461,8 @@
     digits = jnp.pad(digits, (0, blocks * depth * width - 2 * n_listed)).reshape(blocks, depth, width)
     joined = jnp.concatenate([intersections, start.astype(jnp.bfloat16), digits], axis=1)
 
+    inputs = in_plane(joined)
     partner = [along(joined, near)] if two_owners else []
-    inputs = in_plane(joined)
     late_coarse, late_joined = lax.optimization_barrier((coarse, joined))
     near_coarse = [along(late_coarse[:1], e) for e in range(1, near)]
     turned, mixed = turn_own(lay, late_joined, late_coarse)
@@ -493,10 +486,7 @@
         first_rows = near_coarse[e - 1]
         blocks_coarse += [first_rows, lefts[e], to_core(first_rows), lefts_core[e]]
     lefts = lefts + lefts_core
-    projected = [
-        project(lay, g, plan, inputs[g * cols : (g + 1) * cols], blocks_coarse) for g in range(lay.owners)
-    ]
-    own_sum, other_sum, tiles = make_tiles(lay, plan, inputs, lefts, projected)
+    own_sum, other_sum, tiles = make_tiles(lay, plan, inputs, lefts, blocks_coarse)
 
     def over_core(own_part, other_part):
         return (own_part + to_core(other_part)).reshape(lay.places, blocks, side, width)

time: 168 us -> 157 us (0.935)
  Pallas kernels: 40 us -> 30.1 us
  starting transfers between devices: 33.2 us -> 31.2 us
    pallas_call x2 -> x0, Pallas kernels: 13.7 us -> none  [project(): pl.pallas_call(functools.partial(project_kernel, lay, owner), out_shape=j...]
    pallas_call x1, Pallas kernels: 13.1 us -> 17.5 us  [make_tiles(): pl.pallas_call(functools.partial(tiles_kernel, lay), out_shape=(sums, sum...]
    ppermute x25, starting transfers between devices: 33.2 us -> 31.2 us  [move(): return lax.ppermute(array, axes, pairs_list)]
    unnamed x34 -> x36, local copies, waits for them, and re-layouts: 2.8 us -> 4.03 us
  transfers between devices with their start and end apart: 25 -> 25, of which waited for: 16 -> 16; matrix products, arithmetic and copies ran while one was open for 1% -> 2% of each run, Pallas kernels for 13% -> 4%
where the time goes in v5:
time: 157 us; the launch traced here: 156 us
  waiting for transfers between devices  78.4 us (50%)
  starting transfers between devices  31.2 us (20%)
  Pallas kernels  30.1 us (19%)
  other arithmetic  8.6 us (5%)
  local copies, waits for them, and re-layouts  6.02 us (4%)
  between operations  1.6 us (1%)
    ppermute x25, waiting for transfers between devices, move(): return lax.ppermute(array, axes, pairs_list)  78.4 us
    ppermute x25, starting transfers between devices, move(): return lax.ppermute(array, axes, pairs_list)  31.2 us
    pallas_call x1, Pallas kernels, make_tiles(): pl.pallas_call(functools.partial(tiles_kernel, lay), out_shape=(sums, sum...  17.5 us
    pallas_call x1, Pallas kernels, apply_tiles(): pl.pallas_call(functools.partial(apply_kernel, lay), out_shape=(sums, sum...  6.27 us
    pallas_call x1, Pallas kernels, make_plan(): pl.pallas_call(functools.partial(plan_kernel, lay), out_shape=tuple((jax....  6.02 us
    unnamed x36, local copies, waits for them, and re-layouts  4.03 us
  transfers between devices with their start and end apart: 25, of which 16 were waited for; matrix products, arithmetic and copies ran while one was open for 2% of the time, Pallas kernels for 4%

profile of v5, /device:TPU:0, one launch (start us, length us, event | category | flops | bytes accessed | tf_op | source)
XLA Modules:
  0.0 155.9 jit_solution(10677766439188638665)
XLA Ops:
  1.3 0.9 convert_element_type.34
  2.2 0.7 convert_bitcast_fusion.1
  3.0 1.0 pad_maximum_fusion.given.refs_0_
  4.1 1.3 slice.61
  5.3 3.1 %collective-permute-start.4 = (bf16[1,1,512,512]{3,2,1,0:T(8,128)(2,1)S(1)}, bf16[1,1,512,512]{3,2,1,0:T(8,128)(2,1)S(1)}, u32[]{:S(2)}, u32[]{:S(2)}) collective-permute-start(bf16[1,1,512,512]{3,2,1,0:T(8,128)(2,1)S(1)} %slice.61), channel_id=1, source_target_pairs={{0,8},{1,9},{2,10},{3,11},{4,12},{5,13},{6,14},{7,15},{8,0},{9,1},... | collective-permute-start | bytes 1572872 | tf_op jit(solution)/shard_map/ppermute | solution.py:442
  8.4 2.4 %collective-permute-start.3 = (bf16[3,656,128]{2,1,0:T(8,128)(2,1)S(1)}, bf16[3,656,128]{2,1,0:T(8,128)(2,1)S(1)}, u32[]{:S(2)}, u32[]{:S(2)}) collective-permute-start(bf16[3,656,128]{2,1,0:T(8,128)(2,1)S(1)} %pad_maximum_fusion.given.refs_0_), channel_id=1, source_target_pairs={{0,3},{1,2},{2,1},{3,0},{4,7},{5,6},{6,5},{7,4},{8,11},{9,10},{10,... | collective-permute-start | bytes 1511432 | tf_op jit(solution)/shard_map/ppermute | solution.py:442
  10.9 0.5 collective-permute-start.2
  11.4 0.5 collective-permute-start.1
  11.9 2.6 %collective-permute-start = (bf16[3,656,128]{2,1,0:T(8,128)(2,1)S(1)}, bf16[3,656,128]{2,1,0:T(8,128)(2,1)S(1)}, u32[]{:S(2)}, u32[]{:S(2)}) collective-permute-start(bf16[3,656,128]{2,1,0:T(8,128)(2,1)S(1)} %pad_maximum_fusion.given.refs_0_), channel_id=1, source_target_pairs={{0,16},{1,17},{2,18},{3,19},{4,20},{5,21},{6,22},{7,23},{8,24},{9,... | collective-permute-start | bytes 1511432 | tf_op jit(solution)/shard_map/ppermute | solution.py:442
  14.5 1.2 copy-done
  15.9 7.9 %collective-permute-done.3.refs_3_ = bf16[3,656,128]{2,1,0:T(8,128)(2,1)S(1)} collective-permute-done((bf16[3,656,128]{2,1,0:T(8,128)(2,1)S(1)}, bf16[3,656,128]{2,1,0:T(8,128)(2,1)S(1)}, u32[]{:S(2)}, u32[]{:S(2)}) %collective-permute-start.3) | collective-permute-done | bytes 503840 | tf_op jit(solution)/shard_map/ppermute | solution.py:442
  23.8 9.3 %collective-permute-done.2.refs_2_ = bf16[3,656,128]{2,1,0:T(8,128)(2,1)S(1)} collective-permute-done((bf16[3,656,128]{2,1,0:T(8,128)(2,1)S(1)}, bf16[3,656,128]{2,1,0:T(8,128)(2,1)S(1)}, u32[]{:S(2)}, u32[]{:S(2)}) %collective-permute-start.2) | collective-permute-done | bytes 503840 | tf_op jit(solution)/shard_map/ppermute | solution.py:442
  33.2 2.6 %collective-permute-done.given.refs_4_ = bf16[3,656,128]{2,1,0:T(8,128)(2,1)S(1)} collective-permute-done((bf16[3,656,128]{2,1,0:T(8,128)(2,1)S(1)}, bf16[3,656,128]{2,1,0:T(8,128)(2,1)S(1)}, u32[]{:S(2)}, u32[]{:S(2)}) %collective-permute-start) | collective-permute-done | bytes 503840 | tf_op jit(solution)/shard_map/ppermute | solution.py:442
  35.9 0.8 pad_add_fusion.2.ids
  36.7 2.4 %collective-permute-start.7 = (bf16[3,656,128]{2,1,0:T(8,128)(2,1)S(1)}, bf16[3,656,128]{2,1,0:T(8,128)(2,1)}, u32[]{:S(2)}, u32[]{:S(2)}) collective-permute-start(bf16[3,656,128]{2,1,0:T(8,128)(2,1)S(1)} %collective-permute-done.given.refs_4_), channel_id=1, source_target_pairs={{0,3},{1,2},{2,1},{3,0},{4,7},{5,6},{6,5},{7,4},{8,11},{9,10},{10,... | collective-permute-start | bytes 1511432 | tf_op jit(solution)/shard_map/ppermute | solution.py:442
  39.1 0.5 collective-permute-start.6
  39.6 0.5 collective-permute-start.5
  40.2 2.5 %collective-permute-start.9 = (bf16[3,128,512]{2,1,0:T(8,128)(2,1)S(1)}, bf16[3,128,512]{2,1,0:T(8,128)(2,1)}, u32[]{:S(2)}, u32[]{:S(2)}) collective-permute-start(bf16[3,128,512]{2,1,0:T(8,128)(2,1)S(1)} %get-tuple-element.51.own), channel_id=1, source_target_pairs={{0,24},{1,25},{2,26},{3,27},{4,28},{5,29},{6,30},{7,31},{8,16},{9,... | collective-permute-start | bytes 1179656 | tf_op jit(solution)/shard_map/ppermute | solution.py:442
  42.7 1.3 pad_add_fusion.listed
  44.0 6.0 %shard_map.97 = (s32[24]{0:T(128)}, s32[26]{0:T(128)}, s32[4]{0:T(128)}, s32[72]{0:T(128)}, s32[288]{0:T(512)}) custom-call(s32[3]{0:T(128)} %pad_add_fusion.2.ids, s32[2,97]{1,0:T(2,128)} %pad_add_fusion.listed, s32[96]{0:T(128)} %fine.1, s32[8]{0:T(128)} %stored.1), custom_call_target="tpu_custom_call" | custom-call | bytes 20000000 | tf_op jit(solution)/shard_map/pallas_call | solution.py:137
  50.2 15.8 %collective-permute-done.9.refs_10_ = bf16[3,128,512]{2,1,0:T(8,128)(2,1)} collective-permute-done((bf16[3,128,512]{2,1,0:T(8,128)(2,1)S(1)}, bf16[3,128,512]{2,1,0:T(8,128)(2,1)}, u32[]{:S(2)}, u32[]{:S(2)}) %collective-permute-start.9) | collective-permute-done | bytes 393248 | tf_op jit(solution)/shard_map/ppermute | solution.py:442
  66.1 0.5 collective-permute-start.11
  66.7 0.4 collective-permute-start.14
  67.2 4.1 %collective-permute-done.12.refs_13_ = bf16[3,128,512]{2,1,0:T(8,128)(2,1)S(1)} collective-permute-done((bf16[3,128,512]{2,1,0:T(8,128)(2,1)}, bf16[3,128,512]{2,1,0:T(8,128)(2,1)S(1)}, u32[]{:S(2)}, u32[]{:S(2)}) %collective-permute-start.12) | collective-permute-done | bytes 393248 | tf_op jit(solution)/shard_map/ppermute | solution.py:442
  71.3 1.2 collective-permute-done.14.refs_18_
  72.5 0.9 copy-done.11
  73.6 1.0 copy-done.10
  74.6 17.5 %shard_map.98 = (f32[12,128,128]{2,1,0:T(8,128)}, f32[12,128,128]{2,1,0:T(8,128)}, bf16[288,128,128]{2,1,0:T(8,128)(2,1)}) custom-call(s32[24]{0:T(128)} %get-tuple-element.59.slot_of, s32[26]{0:T(128)} %get-tuple-element.60.valid, s32[4]{0:T(128)} %get-tuple-element.61.sizes, s32[72]{0:T(128)} %get-tuple-element.62.group_input, ...), custom_call_target="tpu_custom_call" | custom-call | flops 4000000000 | bytes 30000000 | tf_op jit(solution)/shard_map/pallas_call | solution.py:338
  92.2 2.5 %collective-permute-done.15 = f32[12,128,128]{2,1,0:T(8,128)S(1)} collective-permute-done((f32[12,128,128]{2,1,0:T(8,128)}, f32[12,128,128]{2,1,0:T(8,128)S(1)}, u32[]{:S(2)}, u32[]{:S(2)}) %collective-permute-start.15) | collective-permute-done | bytes 786464 | tf_op jit(solution)/shard_map/ppermute | solution.py:442
  94.7 1.3 fusion.13
  96.2 6.8 %collective-permute-done.16 = bf16[2,3,128,128]{3,2,1,0:T(8,128)(2,1)S(1)} collective-permute-done((bf16[2,3,128,128]{3,2,1,0:T(8,128)(2,1)S(1)}, bf16[2,3,128,128]{3,2,1,0:T(8,128)(2,1)S(1)}, u32[]{:S(2)}, u32[]{:S(2)}) %collective-permute-start.16) | collective-permute-done | bytes 196640 | tf_op jit(solution)/shard_map/ppermute | solution.py:442
  103.0 3.9 %collective-permute-start.17 = (bf16[2,3,128,128]{3,2,1,0:T(8,128)(2,1)S(1)}, bf16[2,3,128,128]{3,2,1,0:T(8,128)(2,1)S(1)}, u32[]{:S(2)}, u32[]{:S(2)}) collective-permute-start(bf16[2,3,128,128]{3,2,1,0:T(8,128)(2,1)S(1)} %fusion), channel_id=1, source_target_pairs={{0,16},{1,17},{2,18},{3,19},{4,20},{5,21},{6,22},{7,23},{8,24},{9,... | collective-permute-start | bytes 589832 | tf_op jit(solution)/shard_map/ppermute | solution.py:442
  107.0 8.9 %collective-permute-done.17 = bf16[2,3,128,128]{3,2,1,0:T(8,128)(2,1)S(1)} collective-permute-done((bf16[2,3,128,128]{3,2,1,0:T(8,128)(2,1)S(1)}, bf16[2,3,128,128]{3,2,1,0:T(8,128)(2,1)S(1)}, u32[]{:S(2)}, u32[]{:S(2)}) %collective-permute-start.17) | collective-permute-done | bytes 196640 | tf_op jit(solution)/shard_map/ppermute | solution.py:442
  116.0 6.5 %collective-permute-start.20 = (bf16[2,3,128,128]{3,2,1,0:T(8,128)(2,1)S(1)}, bf16[2,3,128,128]{3,2,1,0:T(8,128)(2,1)S(1)}, u32[]{:S(2)}, u32[]{:S(2)}) collective-permute-start(bf16[2,3,128,128]{3,2,1,0:T(8,128)(2,1)S(1)} %get-tuple-element.84.refs_0_), channel_id=1, source_target_pairs={{0,3},{1,2},{2,1},{3,0},{4,7},{5,6},{6,5},{7,4},{8,11},{9,10},{10,... | collective-permute-start | bytes 589832 | tf_op jit(solution)/shard_map/ppermute | solution.py:442
  122.5 0.6 collective-permute-start.18
  123.1 5.1 %collective-permute-done.20.refs_3_ = bf16[2,3,128,128]{3,2,1,0:T(8,128)(2,1)S(1)} collective-permute-done((bf16[2,3,128,128]{3,2,1,0:T(8,128)(2,1)S(1)}, bf16[2,3,128,128]{3,2,1,0:T(8,128)(2,1)S(1)}, u32[]{:S(2)}, u32[]{:S(2)}) %collective-permute-start.20) | collective-permute-done | bytes 196640 | tf_op jit(solution)/shard_map/ppermute | solution.py:442
  128.2 3.5 %collective-permute-done.19.refs_2_ = bf16[2,3,128,128]{3,2,1,0:T(8,128)(2,1)S(1)} collective-permute-done((bf16[2,3,128,128]{3,2,1,0:T(8,128)(2,1)S(1)}, bf16[2,3,128,128]{3,2,1,0:T(8,128)(2,1)S(1)}, u32[]{:S(2)}, u32[]{:S(2)}) %collective-permute-start.19) | collective-permute-done | bytes 196640 | tf_op jit(solution)/shard_map/ppermute | solution.py:442
  131.7 0.7 copy-done.7
  132.5 6.3 %shard_map.99 = (f32[12,128,128]{2,1,0:T(8,128)}, f32[12,128,128]{2,1,0:T(8,128)}) custom-call(s32[4]{0:T(128)} %get-tuple-element.61.sizes, s32[72]{0:T(128)} %get-tuple-element.62.group_input, s32[288]{0:T(512)} %get-tuple-element.63.entries, bf16[288,128,128]{2,1,0:T(8,128)(2,1)} %get-tuple-element.79.tiles_in, bf16[2,3,128,128]{3,2,1,0:T(8,128)(2,1)} %copy-done.5, ...), custom_call_target="tpu_custom_call" | custom-call | flops 400000000 | bytes 4000000 | tf_op jit(solution)/shard_map/pallas_call | solution.py:405
  138.8 2.5 %collective-permute-done.21 = f32[12,128,128]{2,1,0:T(8,128)S(1)} collective-permute-done((f32[12,128,128]{2,1,0:T(8,128)}, f32[12,128,128]{2,1,0:T(8,128)S(1)}, u32[]{:S(2)}, u32[]{:S(2)}) %collective-permute-start.21) | collective-permute-done | bytes 786464 | tf_op jit(solution)/shard_map/ppermute | solution.py:442
  141.3 1.3 fusion.11
  142.7 1.9 %collective-permute-start.24 = (bf16[3,128,128]{2,1,0:T(8,128)(2,1)S(1)}, bf16[3,128,128]{2,1,0:T(8,128)(2,1)S(1)}, u32[]{:S(2)}, u32[]{:S(2)}) collective-permute-start(bf16[3,128,128]{2,1,0:T(8,128)(2,1)S(1)} %get-tuple-element.91), channel_id=1, source_target_pairs={{0,24},{1,25},{2,26},{3,27},{4,28},{5,29},{6,30},{7,31},{8,16},{9,... | collective-permute-start | bytes 294920 | tf_op jit(solution)/shard_map/ppermute | solution.py:442
  144.6 1.6 %collective-permute-start.23 = (bf16[3,128,128]{2,1,0:T(8,128)(2,1)S(1)}, bf16[3,128,128]{2,1,0:T(8,128)(2,1)S(1)}, u32[]{:S(2)}, u32[]{:S(2)}) collective-permute-start(bf16[3,128,128]{2,1,0:T(8,128)(2,1)S(1)} %get-tuple-element.92), channel_id=1, source_target_pairs={{0,16},{1,17},{2,18},{3,19},{4,20},{5,21},{6,22},{7,23},{8,24},{9,... | collective-permute-start | bytes 294920 | tf_op jit(solution)/shard_map/ppermute | solution.py:442
  146.2 0.7 slice.83
  146.9 0.9 collective-permute-done.22
  147.8 2.6 %collective-permute-done.24 = bf16[3,128,128]{2,1,0:T(8,128)(2,1)S(1)} collective-permute-done((bf16[3,128,128]{2,1,0:T(8,128)(2,1)S(1)}, bf16[3,128,128]{2,1,0:T(8,128)(2,1)S(1)}, u32[]{:S(2)}, u32[]{:S(2)}) %collective-permute-start.24) | collective-permute-done | bytes 98336 | tf_op jit(solution)/shard_map/ppermute | solution.py:442
  150.3 4.7 %collective-permute-done.23 = bf16[3,128,128]{2,1,0:T(8,128)(2,1)S(1)} collective-permute-done((bf16[3,128,128]{2,1,0:T(8,128)(2,1)S(1)}, bf16[3,128,128]{2,1,0:T(8,128)(2,1)S(1)}, u32[]{:S(2)}, u32[]{:S(2)}) %collective-permute-start.23) | collective-permute-done | bytes 98336 | tf_op jit(solution)/shard_map/ppermute | solution.py:442
  155.1 0.8 fusion.5
  (63 shorter events, 1.7 us)
Async XLA Ops:
  4.1 69.5 %copy-start.1 = (bf16[3,656,128]{2,1,0:T(8,128)(2,1)}, bf16[3,656,128]{2,1,0:T(8,128)(2,1)S(1)}, u32[]{:S(2)}) copy-start(bf16[3,656,128]{2,1,0:T(8,128)(2,1)S(1)} %pad_maximum_fusion.given.refs_0_) | copy-start | bytes 1511428
  5.3 30.4 %collective-permute-start.4 = (bf16[1,1,512,512]{3,2,1,0:T(8,128)(2,1)S(1)}, bf16[1,1,512,512]{3,2,1,0:T(8,128)(2,1)S(1)}, u32[]{:S(2)}, u32[]{:S(2)}) collective-permute-start(bf16[1,1,512,512]{3,2,1,0:T(8,128)(2,1)S(1)} %slice.61), channel_id=1, source_target_pairs={{0,8},{1,9},{2,10},{3,11},{4,12},{5,13},{6,14},{7,15},{8,0},{9,1},... | collective-permute-start | bytes 1572872 | tf_op jit(solution)/shard_map/ppermute | solution.py:442
  8.4 15.4 %collective-permute-start.3 = (bf16[3,656,128]{2,1,0:T(8,128)(2,1)S(1)}, bf16[3,656,128]{2,1,0:T(8,128)(2,1)S(1)}, u32[]{:S(2)}, u32[]{:S(2)}) collective-permute-start(bf16[3,656,128]{2,1,0:T(8,128)(2,1)S(1)} %pad_maximum_fusion.given.refs_0_), channel_id=1, source_target_pairs={{0,3},{1,2},{2,1},{3,0},{4,7},{5,6},{6,5},{7,4},{8,11},{9,10},{10,... | collective-permute-start | bytes 1511432 | tf_op jit(solution)/shard_map/ppermute | solution.py:442
  10.9 22.2 %collective-permute-start.2 = (bf16[3,656,128]{2,1,0:T(8,128)(2,1)S(1)}, bf16[3,656,128]{2,1,0:T(8,128)(2,1)S(1)}, u32[]{:S(2)}, u32[]{:S(2)}) collective-permute-start(bf16[3,656,128]{2,1,0:T(8,128)(2,1)S(1)} %pad_maximum_fusion.given.refs_0_), channel_id=1, source_target_pairs={{0,2},{1,3},{2,0},{3,1},{4,6},{5,7},{6,4},{7,5},{8,10},{9,11},{10,... | collective-permute-start | bytes 1511432 | tf_op jit(solution)/shard_map/ppermute | solution.py:442
  11.4 21.8 %collective-permute-start.1 = (bf16[3,656,128]{2,1,0:T(8,128)(2,1)S(1)}, bf16[3,656,128]{2,1,0:T(8,128)(2,1)S(1)}, u32[]{:S(2)}, u32[]{:S(2)}) collective-permute-start(bf16[3,656,128]{2,1,0:T(8,128)(2,1)S(1)} %pad_maximum_fusion.given.refs_0_), channel_id=1, source_target_pairs={{0,1},{1,0},{2,3},{3,2},{4,5},{5,4},{6,7},{7,6},{8,9},{9,8},{10,11... | collective-permute-start | bytes 1511432 | tf_op jit(solution)/shard_map/ppermute | solution.py:442
  11.9 23.8 %collective-permute-start = (bf16[3,656,128]{2,1,0:T(8,128)(2,1)S(1)}, bf16[3,656,128]{2,1,0:T(8,128)(2,1)S(1)}, u32[]{:S(2)}, u32[]{:S(2)}) collective-permute-start(bf16[3,656,128]{2,1,0:T(8,128)(2,1)S(1)} %pad_maximum_fusion.given.refs_0_), channel_id=1, source_target_pairs={{0,16},{1,17},{2,18},{3,19},{4,20},{5,21},{6,22},{7,23},{8,24},{9,... | collective-permute-start | bytes 1511432 | tf_op jit(solution)/shard_map/ppermute | solution.py:442
  14.5 1.2 copy-start
  23.8 12.1 %copy-start.14 = (bf16[3,656,128]{2,1,0:T(8,128)(2,1)}, bf16[3,656,128]{2,1,0:T(8,128)(2,1)S(1)}, u32[]{:S(2)}) copy-start(bf16[3,656,128]{2,1,0:T(8,128)(2,1)S(1)} %collective-permute-done.3.refs_3_) | copy-start | bytes 1511428
  33.1 2.8 %copy-start.15 = (bf16[3,656,128]{2,1,0:T(8,128)(2,1)}, bf16[3,656,128]{2,1,0:T(8,128)(2,1)S(1)}, u32[]{:S(2)}) copy-start(bf16[3,656,128]{2,1,0:T(8,128)(2,1)S(1)} %collective-permute-done.2.refs_2_) | copy-start | bytes 1511428
  33.2 2.7 %copy-start.16 = (bf16[3,656,128]{2,1,0:T(8,128)(2,1)}, bf16[3,656,128]{2,1,0:T(8,128)(2,1)S(1)}, u32[]{:S(2)}) copy-start(bf16[3,656,128]{2,1,0:T(8,128)(2,1)S(1)} %collective-permute-done.1.refs_1_) | copy-start | bytes 1511428
  35.8 37.8 %copy-start.3 = (bf16[3,656,128]{2,1,0:T(8,128)(2,1)}, bf16[3,656,128]{2,1,0:T(8,128)(2,1)S(1)}, u32[]{:S(2)}) copy-start(bf16[3,656,128]{2,1,0:T(8,128)(2,1)S(1)} %collective-permute-done.given.refs_4_) | copy-start | bytes 1511428
  35.8 37.8 %copy-start.12 = (bf16[1,1,512,512]{3,2,1,0:T(8,128)(2,1)}, bf16[1,1,512,512]{3,2,1,0:T(8,128)(2,1)S(1)}, u32[]{:S(2)}) copy-start(bf16[1,1,512,512]{3,2,1,0:T(8,128)(2,1)S(1)} %collective-permute-done.4.refs_16_) | copy-start | bytes 1572868
  35.8 30.2 %collective-permute-start.8 = (bf16[896,512]{1,0:T(8,128)(2,1)S(1)}, bf16[896,512]{1,0:T(8,128)(2,1)}, u32[]{:S(2)}, u32[]{:S(2)}) collective-permute-start(bf16[896,512]{1,0:T(8,128)(2,1)S(1)} %get-tuple-element.52), channel_id=1, source_target_pairs={{0,8},{1,9},{2,10},{3,11},{4,12},{5,13},{6,14},{7,15},{8,0},{9,1},... | collective-permute-start | bytes 2752520 | tf_op jit(solution)/shard_map/ppermute | solution.py:442
  36.7 29.4 %collective-permute-start.7 = (bf16[3,656,128]{2,1,0:T(8,128)(2,1)S(1)}, bf16[3,656,128]{2,1,0:T(8,128)(2,1)}, u32[]{:S(2)}, u32[]{:S(2)}) collective-permute-start(bf16[3,656,128]{2,1,0:T(8,128)(2,1)S(1)} %collective-permute-done.given.refs_4_), channel_id=1, source_target_pairs={{0,3},{1,2},{2,1},{3,0},{4,7},{5,6},{6,5},{7,4},{8,11},{9,10},{10,... | collective-permute-start | bytes 1511432 | tf_op jit(solution)/shard_map/ppermute | solution.py:442
  39.1 26.9 %collective-permute-start.6 = (bf16[3,656,128]{2,1,0:T(8,128)(2,1)S(1)}, bf16[3,656,128]{2,1,0:T(8,128)(2,1)}, u32[]{:S(2)}, u32[]{:S(2)}) collective-permute-start(bf16[3,656,128]{2,1,0:T(8,128)(2,1)S(1)} %collective-permute-done.given.refs_4_), channel_id=1, source_target_pairs={{0,2},{1,3},{2,0},{3,1},{4,6},{5,7},{6,4},{7,5},{8,10},{9,11},{10,... | collective-permute-start | bytes 1511432 | tf_op jit(solution)/shard_map/ppermute | solution.py:442
  39.6 26.4 %collective-permute-start.5 = (bf16[3,656,128]{2,1,0:T(8,128)(2,1)S(1)}, bf16[3,656,128]{2,1,0:T(8,128)(2,1)}, u32[]{:S(2)}, u32[]{:S(2)}) collective-permute-start(bf16[3,656,128]{2,1,0:T(8,128)(2,1)S(1)} %collective-permute-done.given.refs_4_), channel_id=1, source_target_pairs={{0,1},{1,0},{2,3},{3,2},{4,5},{5,4},{6,7},{7,6},{8,9},{9,8},{10,11... | collective-permute-start | bytes 1511432 | tf_op jit(solution)/shard_map/ppermute | solution.py:442
  40.2 25.9 %collective-permute-start.9 = (bf16[3,128,512]{2,1,0:T(8,128)(2,1)S(1)}, bf16[3,128,512]{2,1,0:T(8,128)(2,1)}, u32[]{:S(2)}, u32[]{:S(2)}) collective-permute-start(bf16[3,128,512]{2,1,0:T(8,128)(2,1)S(1)} %get-tuple-element.51.own), channel_id=1, source_target_pairs={{0,24},{1,25},{2,26},{3,27},{4,28},{5,29},{6,30},{7,31},{8,16},{9,... | collective-permute-start | bytes 1179656 | tf_op jit(solution)/shard_map/ppermute | solution.py:442
  50.2 23.4 %copy-start.2 = (bf16[6,128,512]{2,1,0:T(8,128)(2,1)}, bf16[6,128,512]{2,1,0:T(8,128)(2,1)S(1)}, u32[]{:S(2)}) copy-start(bf16[6,128,512]{2,1,0:T(8,128)(2,1)S(1)} %shard_map.96.refs_8_) | copy-start | bytes 2359300
  50.2 45.9 %copy-start.4 = (f32[384,128]{1,0:T(8,128)S(1)}, f32[384,128]{1,0:T(8,128)}, u32[]{:S(2)}) copy-start(f32[384,128]{1,0:T(8,128)} %param.8) | copy-start | bytes 589828
  50.2 45.9 %copy-start.9 = (f32[384]{0:T(512)S(1)}, f32[384]{0:T(512)}, u32[]{:S(2)}) copy-start(f32[384]{0:T(512)} %param.9) | copy-start | bytes 4612
  66.0 7.6 %collective-permute-start.13 = (bf16[2,1,512,512]{3,2,1,0:T(8,128)(2,1)}, bf16[2,1,512,512]{3,2,1,0:T(8,128)(2,1)S(1)}, u32[]{:S(2)}, u32[]{:S(2)}) collective-permute-start(bf16[2,1,512,512]{3,2,1,0:T(8,128)(2,1)} %refs_14_), channel_id=1, source_target_pairs={{0,4},{1,5},{2,6},{3,7},{4,0},{5,1},{6,2},{7,3},{8,12},{9,13},{10,... | collective-permute-start | bytes 3145736 | tf_op jit(solution)/shard_map/ppermute | solution.py:442
  66.1 7.4 %collective-permute-start.11 = (bf16[896,512]{1,0:T(8,128)(2,1)}, bf16[896,512]{1,0:T(8,128)(2,1)}, u32[]{:S(2)}, u32[]{:S(2)}) collective-permute-start(bf16[896,512]{1,0:T(8,128)(2,1)} %collective-permute-done.8.refs_9_.refs_17_), channel_id=1, source_target_pairs={{0,4},{1,5},{2,6},{3,7},{4,0},{5,1},{6,2},{7,3},{8,12},{9,13},{10,... | collective-permute-start | bytes 2752520 | tf_op jit(solution)/shard_map/ppermute | solution.py:442
  66.6 5.9 %collective-permute-start.10 = (bf16[6,128,512]{2,1,0:T(8,128)(2,1)S(1)}, bf16[6,128,512]{2,1,0:T(8,128)(2,1)S(1)}, u32[]{:S(2)}, u32[]{:S(2)}) collective-permute-start(bf16[6,128,512]{2,1,0:T(8,128)(2,1)S(1)} %shard_map.96.refs_8_), channel_id=1, source_target_pairs={{0,4},{1,5},{2,6},{3,7},{4,0},{5,1},{6,2},{7,3},{8,12},{9,13},{10,... | collective-permute-start | bytes 2359304 | tf_op jit(solution)/shard_map/ppermute | solution.py:442
  66.7 5.8 %collective-permute-start.14 = (bf16[1,1,512,512]{3,2,1,0:T(8,128)(2,1)S(1)}, bf16[1,1,512,512]{3,2,1,0:T(8,128)(2,1)S(1)}, u32[]{:S(2)}, u32[]{:S(2)}) collective-permute-start(bf16[1,1,512,512]{3,2,1,0:T(8,128)(2,1)S(1)} %collective-permute-done.4.refs_16_), channel_id=1, source_target_pairs={{0,4},{1,5},{2,6},{3,7},{4,0},{5,1},{6,2},{7,3},{8,12},{9,13},{10,... | collective-permute-start | bytes 1572872 | tf_op jit(solution)/shard_map/ppermute | solution.py:442
  67.1 4.2 %collective-permute-start.12 = (bf16[3,128,512]{2,1,0:T(8,128)(2,1)}, bf16[3,128,512]{2,1,0:T(8,128)(2,1)S(1)}, u32[]{:S(2)}, u32[]{:S(2)}) collective-permute-start(bf16[3,128,512]{2,1,0:T(8,128)(2,1)} %collective-permute-done.9.refs_10_), channel_id=1, source_target_pairs={{0,4},{1,5},{2,6},{3,7},{4,0},{5,1},{6,2},{7,3},{8,12},{9,13},{10,... | collective-permute-start | bytes 1179656 | tf_op jit(solution)/shard_map/ppermute | solution.py:442
  71.3 2.1 %copy-start.17 = (bf16[3,128,512]{2,1,0:T(8,128)(2,1)}, bf16[3,128,512]{2,1,0:T(8,128)(2,1)S(1)}, u32[]{:S(2)}) copy-start(bf16[3,128,512]{2,1,0:T(8,128)(2,1)S(1)} %collective-permute-done.12.refs_13_) | copy-start | bytes 1179652
  72.5 1.1 copy-start.13
  72.5 0.9 copy-start.11
  73.6 1.0 copy-start.10
  92.1 2.6 %collective-permute-start.15 = (f32[12,128,128]{2,1,0:T(8,128)}, f32[12,128,128]{2,1,0:T(8,128)S(1)}, u32[]{:S(2)}, u32[]{:S(2)}) collective-permute-start(f32[12,128,128]{2,1,0:T(8,128)} %get-tuple-element.78), channel_id=1, source_target_pairs={{0,4},{1,5},{2,6},{3,7},{4,0},{5,1},{6,2},{7,3},{8,12},{9,13},{10,... | collective-permute-start | bytes 2359304 | tf_op jit(solution)/shard_map/ppermute | solution.py:442
  96.0 7.0 %collective-permute-start.16 = (bf16[2,3,128,128]{3,2,1,0:T(8,128)(2,1)S(1)}, bf16[2,3,128,128]{3,2,1,0:T(8,128)(2,1)S(1)}, u32[]{:S(2)}, u32[]{:S(2)}) collective-permute-start(bf16[2,3,128,128]{3,2,1,0:T(8,128)(2,1)S(1)} %pad_maximum_fusion.1), channel_id=1, source_target_pairs={{0,8},{1,9},{2,10},{3,11},{4,12},{5,13},{6,14},{7,15},{8,0},{9,1},... | collective-permute-start | bytes 589832 | tf_op jit(solution)/shard_map/ppermute | solution.py:442
  103.0 12.8 %collective-permute-start.17 = (bf16[2,3,128,128]{3,2,1,0:T(8,128)(2,1)S(1)}, bf16[2,3,128,128]{3,2,1,0:T(8,128)(2,1)S(1)}, u32[]{:S(2)}, u32[]{:S(2)}) collective-permute-start(bf16[2,3,128,128]{3,2,1,0:T(8,128)(2,1)S(1)} %fusion), channel_id=1, source_target_pairs={{0,16},{1,17},{2,18},{3,19},{4,20},{5,21},{6,22},{7,23},{8,24},{9,... | collective-permute-start | bytes 589832 | tf_op jit(solution)/shard_map/ppermute | solution.py:442
  116.0 15.8 %copy-start.5 = (bf16[2,3,128,128]{3,2,1,0:T(8,128)(2,1)}, bf16[2,3,128,128]{3,2,1,0:T(8,128)(2,1)S(1)}, u32[]{:S(2)}) copy-start(bf16[2,3,128,128]{3,2,1,0:T(8,128)(2,1)S(1)} %get-tuple-element.84.refs_0_) | copy-start | bytes 589828
  116.0 12.3 %collective-permute-start.20 = (bf16[2,3,128,128]{3,2,1,0:T(8,128)(2,1)S(1)}, bf16[2,3,128,128]{3,2,1,0:T(8,128)(2,1)S(1)}, u32[]{:S(2)}, u32[]{:S(2)}) collective-permute-start(bf16[2,3,128,128]{3,2,1,0:T(8,128)(2,1)S(1)} %get-tuple-element.84.refs_0_), channel_id=1, source_target_pairs={{0,3},{1,2},{2,1},{3,0},{4,7},{5,6},{6,5},{7,4},{8,11},{9,10},{10,... | collective-permute-start | bytes 589832 | tf_op jit(solution)/shard_map/ppermute | solution.py:442
  122.5 9.3 %collective-permute-start.19 = (bf16[2,3,128,128]{3,2,1,0:T(8,128)(2,1)S(1)}, bf16[2,3,128,128]{3,2,1,0:T(8,128)(2,1)S(1)}, u32[]{:S(2)}, u32[]{:S(2)}) collective-permute-start(bf16[2,3,128,128]{3,2,1,0:T(8,128)(2,1)S(1)} %get-tuple-element.84.refs_0_), channel_id=1, source_target_pairs={{0,2},{1,3},{2,0},{3,1},{4,6},{5,7},{6,4},{7,5},{8,10},{9,11},{10,... | collective-permute-start | bytes 589832 | tf_op jit(solution)/shard_map/ppermute | solution.py:442
  122.5 9.3 %collective-permute-start.18 = (bf16[2,3,128,128]{3,2,1,0:T(8,128)(2,1)S(1)}, bf16[2,3,128,128]{3,2,1,0:T(8,128)(2,1)S(1)}, u32[]{:S(2)}, u32[]{:S(2)}) collective-permute-start(bf16[2,3,128,128]{3,2,1,0:T(8,128)(2,1)S(1)} %get-tuple-element.84.refs_0_), channel_id=1, source_target_pairs={{0,1},{1,0},{2,3},{3,2},{4,5},{5,4},{6,7},{7,6},{8,9},{9,8},{10,11... | collective-permute-start | bytes 589832 | tf_op jit(solution)/shard_map/ppermute | solution.py:442
  128.2 3.5 %copy-start.6 = (bf16[2,3,128,128]{3,2,1,0:T(8,128)(2,1)}, bf16[2,3,128,128]{3,2,1,0:T(8,128)(2,1)S(1)}, u32[]{:S(2)}) copy-start(bf16[2,3,128,128]{3,2,1,0:T(8,128)(2,1)S(1)} %collective-permute-done.20.refs_3_) | copy-start | bytes 589828
  131.7 0.7 copy-start.7
  131.7 0.7 copy-start.8
  138.7 2.6 %collective-permute-start.21 = (f32[12,128,128]{2,1,0:T(8,128)}, f32[12,128,128]{2,1,0:T(8,128)S(1)}, u32[]{:S(2)}, u32[]{:S(2)}) collective-permute-start(f32[12,128,128]{2,1,0:T(8,128)} %get-tuple-element.81), channel_id=1, source_target_pairs={{0,4},{1,5},{2,6},{3,7},{4,0},{5,1},{6,2},{7,3},{8,12},{9,13},{10,... | collective-permute-start | bytes 2359304 | tf_op jit(solution)/shard_map/ppermute | solution.py:442
  142.7 5.1 %collective-permute-start.22 = (bf16[3,128,128]{2,1,0:T(8,128)(2,1)S(1)}, bf16[3,128,128]{2,1,0:T(8,128)(2,1)S(1)}, u32[]{:S(2)}, u32[]{:S(2)}) collective-permute-start(bf16[3,128,128]{2,1,0:T(8,128)(2,1)S(1)} %get-tuple-element.90), channel_id=1, source_target_pairs={{0,8},{1,9},{2,10},{3,11},{4,12},{5,13},{6,14},{7,15},{8,0},{9,1},... | collective-permute-start | bytes 294920 | tf_op jit(solution)/shard_map/ppermute | solution.py:442
  142.7 7.6 %collective-permute-start.24 = (bf16[3,128,128]{2,1,0:T(8,128)(2,1)S(1)}, bf16[3,128,128]{2,1,0:T(8,128)(2,1)S(1)}, u32[]{:S(2)}, u32[]{:S(2)}) collective-permute-start(bf16[3,128,128]{2,1,0:T(8,128)(2,1)S(1)} %get-tuple-element.91), channel_id=1, source_target_pairs={{0,24},{1,25},{2,26},{3,27},{4,28},{5,29},{6,30},{7,31},{8,16},{9,... | collective-permute-start | bytes 294920 | tf_op jit(solution)/shard_map/ppermute | solution.py:442
  144.6 10.4 %collective-permute-start.23 = (bf16[3,128,128]{2,1,0:T(8,128)(2,1)S(1)}, bf16[3,128,128]{2,1,0:T(8,128)(2,1)S(1)}, u32[]{:S(2)}, u32[]{:S(2)}) collective-permute-start(bf16[3,128,128]{2,1,0:T(8,128)(2,1)S(1)} %get-tuple-element.92), channel_id=1, source_target_pairs={{0,16},{1,17},{2,18},{3,19},{4,20},{5,21},{6,22},{7,23},{8,24},{9,... | collective-permute-start | bytes 294920 | tf_op jit(solution)/shard_map/ppermute | solution.py:442

commit v6 on v5

--- a/solution.py
+++ b/solution.py
@@ -152,32 +152,21 @@
         total[q] = total[q] + products[i * lay.side : (i + 1) * lay.side]
 
 
-def turn_own_kernel(lay, given, coarse, turned, mixed):
+def turn_own_kernel(lay, given, turned):
     for t in range(lay.blocks):
-        block = given[t, 0 : lay.pairs, :].T
-        turned[t] = block
-        mixed[t * lay.side : (t + 1) * lay.side, :] = block
-    row = lay.blocks * lay.side
-    for a in range(1, lay.points):
-        for at in range(lay.slots_dev):
-            mixed[row : row + lay.pairs, :] = coarse[a, at]
-            row += lay.pairs
-
-
-def turn_own(lay, joined, coarse):
+        turned[t] = given[t, 0 : lay.pairs, :].T
+
+
+def turn_own(lay, joined):
     vmem = pl.BlockSpec(memory_space=pltpu.VMEM)
-    rows = lay.blocks * lay.side + (lay.points - 1) * lay.slots_dev * lay.pairs
     return pl.pallas_call(
         functools.partial(turn_own_kernel, lay),
-        out_shape=(
-            jax.ShapeDtypeStruct((lay.blocks, lay.side, lay.pairs), jnp.bfloat16),
-            jax.ShapeDtypeStruct((rows, lay.pairs), jnp.bfloat16),
-        ),
-        in_specs=[vmem] * 2,
-        out_specs=(vmem,) * 2,
+        out_shape=jax.ShapeDtypeStruct((lay.blocks, lay.side, lay.pairs), jnp.bfloat16),
+        in_specs=[vmem],
+        out_specs=vmem,
         compiler_params=pltpu.CompilerParams(vmem_limit_bytes=16 * mib),
         cost_estimate=pl.CostEstimate(flops=1_000_000, bytes_accessed=5_000_000, transcendentals=0),
-    )(joined, coarse)
+    )(joined)
 
 
 def turn_both_kernel(lay, given, own, out):
@@ -198,44 +187,100 @@
     )(partner, own)
 
 
-def tiles_kernel(lay, slot_of, valid, sizes, group_input, entries, *refs):
+def project_kernel(lay, slot_of, valid, sizes, *refs):
+    refs = list(refs)
+    given_in = [refs.pop(0) for _ in range(lay.owners * lay.cols)]
+    given_coarse = [refs.pop(0) for _ in range(2 * lay.near)]
+    out, right, blocks, projected, sems, out_sems = refs
+    sets = []
+
+    def fetch(source, target, index):
+        sets[-1].append(pltpu.make_async_copy(source, target, sems.at[index]))
+        sets[-1][-1].start()
+
+    for owner in range(lay.owners):
+        sets.append([])
+        if owner == 0:
+            for i in range(2 * lay.near):
+                for a in range(lay.points):
+                    target = blocks.at[a, pl.ds(i * lay.slots_dev, lay.slots_dev)]
+                    fetch(given_coarse[i].at[a], target, i * lay.points + a)
+        for i in range(owner * lay.cols, (owner + 1) * lay.cols):
+            part = pl.ds(i * lay.blocks, lay.blocks)
+            source = given_in[i].at[:, pl.ds(0, lay.pairs)]
+            fetch(source, right.at[part], 2 * lay.near * lay.points + i)
+
+    for owner in range(lay.owners):
+        for copy in sets[owner]:
+            copy.wait()
+        found = sizes[1 + owner]
+
+        def store(i):
+            p = owner * lay.spread + i
+            return pltpu.make_async_copy(projected.at[p], out.at[p], out_sems.at[p])
+
+        def visit(step, carry):
+            for lane in range(2):
+                i = valid[owner * (lay.spread + 1) + jnp.minimum(2 * step + lane, found - 1)]
+                p = owner * lay.spread + i
+                for a in range(lay.points):
+                    projected[p, :, a * lay.side : (a + 1) * lay.side] = jnp.dot(
+                        blocks[a, slot_of[p]], right[p], preferred_element_type=jnp.float32
+                    ).astype(jnp.bfloat16)
+            return carry
+
+        lax.fori_loop(0, lax.div(found + 1, 2), visit, 0)
+        for i in range(lay.spread):
+
+            @pl.when(slot_of[owner * lay.spread + i] >= 0)
+            def _():
+                store(i).start()
+
+    for p in range(lay.inputs):
+
+        @pl.when(slot_of[p] >= 0)
+        def _():
+            pltpu.make_async_copy(projected.at[p], out.at[p], out_sems.at[p]).wait()
+
+
+def project(lay, plan, inputs, coarse):
+    smem = pl.BlockSpec(memory_space=pltpu.SMEM)
+    hbm = pl.BlockSpec(memory_space=pl.ANY)
+    shape = (lay.inputs, lay.pairs, lay.points * lay.side)
+    return pl.pallas_call(
+        functools.partial(project_kernel, lay),
+        out_shape=jax.ShapeDtypeStruct(shape, jnp.bfloat16),
+        in_specs=[smem] * 3 + [hbm] * (len(inputs) + len(coarse)),
+        out_specs=hbm,
+        scratch_shapes=[
+            pltpu.VMEM((lay.inputs, lay.pairs, lay.side), jnp.bfloat16),
+            pltpu.VMEM((lay.points, lay.slots, lay.pairs, lay.pairs), jnp.bfloat16),
+            pltpu.VMEM(shape, jnp.bfloat16),
+            pltpu.SemaphoreType.DMA((len(inputs) + len(coarse) * lay.points,)),
+            pltpu.SemaphoreType.DMA((lay.inputs,)),
+        ],
+        compiler_params=pltpu.CompilerParams(vmem_limit_bytes=lay.vmem),
+        cost_estimate=pl.CostEstimate(flops=2_000_000_000, bytes_accessed=25_000_000, transcendentals=0),
+    )(*plan[:3], *inputs, *coarse)
+
+
+def tiles_kernel(lay, slot_of, sizes, group_input, entries, *refs):
     lines = lay.line_steps()
     refs = list(refs)
     given_in = [refs.pop(0) for _ in range(lay.owners * lay.cols)]
     given_out = [refs.pop(0) for _ in range(2 * (1 + len(lines)))]
-    given_coarse = [refs.pop(0) for _ in range(2 * (2 * lay.near - 1))]
+    given_projected = refs.pop(0)
     own_sum, other_sum, tiles_out = refs[:3]
-    right, left, blocks, projected, rounded, tiles, total, sems, sum_sems, out_sems = refs[3:]
-    started, waited = [], []
+    left, projected, rounded, tiles, total, sems, sum_sems, in_sems, out_sems = refs[3:]
+    copies = []
 
     def fetch(source, target):
-        started.append(pltpu.make_async_copy(source, target, sems.at[len(started) + len(waited)]))
-        started[-1].start()
-
-    def arrive(count):
-        for copy in started[:count]:
-            copy.wait()
-        waited.extend(started[:count])
-        del started[:count]
-
-    def fetch_inputs(owner):
-        for i in range(owner * lay.cols, (owner + 1) * lay.cols):
-            part = pl.ds(i * lay.blocks, lay.blocks)
-            fetch(given_in[i].at[:, pl.ds(0, lay.pairs)], right.at[part])
-
-    for i in range(2 * lay.near):
-        first = given_coarse.pop(0)
-        for a in range(first.shape[0]):
-            fetch(first.at[a], blocks.at[a, pl.ds(i * lay.slots_dev, lay.slots_dev)])
-        if i < 2:
-            continue
-        rest = given_coarse.pop(0)
-        for a in range(1, lay.points):
-            for at in range(lay.slots_dev):
-                row = lay.blocks * lay.side + ((a - 1) * lay.slots_dev + at) * lay.pairs
-                fetch(rest.at[pl.ds(row, lay.pairs)], blocks.at[a, i * lay.slots_dev + at])
-    fetch_inputs(0)
-    for_projection = len(started)
+        copies.append(pltpu.make_async_copy(source, target, sems.at[len(copies)]))
+        copies[-1].start()
+
+    def load(p):
+        return pltpu.make_async_copy(given_projected.at[p], projected.at[p], in_sems.at[p])
+
     for k in range(2):
         held = given_out[k * (1 + len(lines)) :]
         for g in range(lay.owners):
@@ -243,39 +288,30 @@
             fetch(held[0].at[pl.ds(g * lay.blocks, lay.blocks)], left.at[pl.ds(spot, lay.blocks)])
         for i, d in enumerate(lines):
             spot = (k * lay.places + d) * lay.blocks
-            if d > lay.near:
-                fetch(held[1 + i], left.at[pl.ds(spot, lay.blocks)])
-            else:
-                for t in range(lay.blocks):
-                    fetch(held[1 + i].at[pl.ds(t * lay.side, lay.side)], left.at[spot + t])
+            fetch(held[1 + i], left.at[pl.ds(spot, lay.blocks)])
     for i, ref in enumerate(given_in):
         part = pl.ds(i * lay.blocks, lay.blocks)
         fetch(ref.at[:, pl.ds(lay.pairs, lay.side)], rounded.at[part])
-    for_tiles = len(started) - for_projection
-    for owner in range(1, lay.owners):
-        fetch_inputs(owner)
+    for p in range(lay.inputs):
+
+        @pl.when(slot_of[p] >= 0)
+        def _():
+            load(p).start()
+
     total[...] = jnp.zeros_like(total)
-    arrive(for_projection)
+    for copy in copies:
+        copy.wait()
     used = sizes[0]
 
     for owner in range(lay.owners):
-        found = sizes[1 + owner]
-
-        def visit(step, carry):
-            for lane in range(2):
-                i = valid[owner * (lay.spread + 1) + jnp.minimum(2 * step + lane, found - 1)]
-                p = owner * lay.spread + i
-                for a in range(lay.points):
-                    projected[i, :, a * lay.side : (a + 1) * lay.side] = jnp.dot(
-                        blocks[a, slot_of[p]], right[p], preferred_element_type=jnp.float32
-                    ).astype(jnp.bfloat16)
-            return carry
-
-        lax.fori_loop(0, lax.div(found + 1, 2), visit, 0)
-        arrive(for_tiles if owner == 0 else 0)
+        for p in range(owner * lay.spread, (owner + 1) * lay.spread):
+
+            @pl.when(slot_of[p] >= 0)
+            def _():
+                load(p).wait()
 
         def group_step(group, carry):
-            block = projected[group_input[group] - owner * lay.spread]
+            block = projected[group_input[group]]
             numbers = [entries[group * lay.unroll + i] for i in range(lay.unroll)]
             places = [jnp.minimum(lax.div(n, lay.points), lay.outputs - 1) for n in numbers]
             lefts = jnp.concatenate([left[q] for q in places], axis=0)
@@ -293,8 +329,6 @@
         first = 1 if owner == 0 else sizes[lay.owners + owner]
         last = used if owner == lay.owners - 1 else sizes[lay.owners + owner + 1]
         lax.fori_loop(first, last, group_step, 0)
-        if owner < lay.owners - 1:
-            arrive(lay.cols)
 
     span = chunk_groups * lay.unroll
 
@@ -328,33 +362,31 @@
     pltpu.make_async_copy(total.at[pl.ds(0, own)], own_sum, sems.at[0]).wait()
 
 
-def make_tiles(lay, plan, inputs, outputs, coarse):
+def make_tiles(lay, plan, inputs, outputs, projected):
     smem = pl.BlockSpec(memory_space=pltpu.SMEM)
     hbm = pl.BlockSpec(memory_space=pl.ANY)
     own = lay.places * lay.blocks
     sums = jax.ShapeDtypeStruct((own, lay.side, lay.width), jnp.float32)
-    n_copies = 2 * len(inputs) + 2 * lay.places * lay.blocks + lay.slots * lay.points
     tiles = (lay.groups * lay.unroll, lay.side, lay.side)
     return pl.pallas_call(
         functools.partial(tiles_kernel, lay),
         out_shape=(sums, sums, jax.ShapeDtypeStruct(tiles, jnp.bfloat16)),
-        in_specs=[smem] * 5 + [hbm] * (len(inputs) + len(outputs) + len(coarse)),
+        in_specs=[smem] * 4 + [hbm] * (len(inputs) + len(outputs) + 1),
         out_specs=(hbm,) * 3,
         scratch_shapes=[
-            pltpu.VMEM((lay.inputs, lay.pairs, lay.side), jnp.bfloat16),
             pltpu.VMEM((lay.outputs, lay.side, lay.pairs), jnp.bfloat16),
-            pltpu.VMEM((lay.points, lay.slots, lay.pairs, lay.pairs), jnp.bfloat16),
-            pltpu.VMEM((lay.spread, lay.pairs, lay.points * lay.side), jnp.bfloat16),
+            pltpu.VMEM(projected.shape, jnp.bfloat16),
             pltpu.VMEM((lay.inputs, lay.side, lay.width), jnp.bfloat16),
             pltpu.VMEM(tiles, jnp.bfloat16),
             pltpu.VMEM((lay.outputs + 1, lay.side, lay.width), jnp.float32),
-            pltpu.SemaphoreType.DMA((n_copies,)),
+            pltpu.SemaphoreType.DMA((len(inputs) + 2 * lay.places,)),
             pltpu.SemaphoreType.DMA((2,)),
+            pltpu.SemaphoreType.DMA((lay.inputs,)),
             pltpu.SemaphoreType.DMA((lay.groups // chunk_groups,)),
         ],
         compiler_params=pltpu.CompilerParams(vmem_limit_bytes=lay.vmem),
         cost_estimate=pl.CostEstimate(flops=4_000_000_000, bytes_accessed=30_000_000, transcendentals=0),
-    )(*plan, *inputs, *outputs, *coarse)
+    )(plan[0], *plan[2:], *inputs, *outputs, projected)
 
 
 def apply_kernel(lay, sizes, group_input, entries, tiles_in, *refs):
@@ -461,32 +493,32 @@
     digits = jnp.pad(digits, (0, blocks * depth * width - 2 * n_listed)).reshape(blocks, depth, width)
     joined = jnp.concatenate([intersections, start.astype(jnp.bfloat16), digits], axis=1)
 
+    near_coarse = [along(coarse, e) for e in range(1, near)]
+    partner = [along(joined, near)] if two_owners else []
     inputs = in_plane(joined)
-    partner = [along(joined, near)] if two_owners else []
-    late_coarse, late_joined = lax.optimization_barrier((coarse, joined))
-    near_coarse = [along(late_coarse[:1], e) for e in range(1, near)]
-    turned, mixed = turn_own(lay, late_joined, late_coarse)
-    held = (partner, inputs, near_coarse, turned, mixed)
-    partner, inputs, near_coarse, turned, mixed = lax.optimization_barrier(held)
+    inputs, partner, late_joined = lax.optimization_barrier((inputs, partner, joined))
     if two_owners:
         sent = partner[0][:, pairs + side :].reshape(-1)[: 2 * n_listed].astype(jnp.int32)
         listed = jnp.concatenate([listed, ((sent[:n_listed] << 8) + sent[n_listed:])[None]], axis=0)
     plan = make_plan(lay, ids, listed, fine_coarse, coarse_slot)
     for part in partner:
         inputs = inputs + in_plane(part)
-    lines = [along(mixed if d < near else turned, d) for d in lay.line_steps()]
+    turned = turn_own(lay, late_joined)
+    turned, near_coarse, plan = lax.optimization_barrier((turned, near_coarse, plan))
+    lines = [along(turned, d) for d in lay.line_steps()]
     for part in partner:
         turned = turn_both(lay, part, turned)
-    held = (inputs, turned, lines, near_coarse, plan, coarse)
-    inputs, turned, lines, near_coarse, plan, coarse = lax.optimization_barrier(held)
-    blocks_coarse = [coarse, to_core(coarse)]
-    lefts = [turned] + lines
-    lefts_core = [to_core(part) for part in lefts]
-    for e in range(1, near):
-        first_rows = near_coarse[e - 1]
-        blocks_coarse += [first_rows, lefts[e], to_core(first_rows), lefts_core[e]]
-    lefts = lefts + lefts_core
-    own_sum, other_sum, tiles = make_tiles(lay, plan, inputs, lefts, blocks_coarse)
+    far = lines[near - 1 :]
+    held = (inputs, near_coarse, far, coarse)
+    inputs, near_coarse, far, late_coarse = lax.optimization_barrier(held)
+    blocks_coarse = []
+    for part in [late_coarse] + near_coarse:
+        blocks_coarse += [part, to_core(part)]
+    projected = project(lay, plan, inputs, blocks_coarse)
+    late, projected = lax.optimization_barrier((lines[: near - 1], projected))
+    lefts = [turned] + late + far
+    lefts = lefts + [to_core(part) for part in lefts]
+    own_sum, other_sum, tiles = make_tiles(lay, plan, inputs, lefts, projected)
 
     def over_core(own_part, other_part):
         return (own_part + to_core(other_part)).reshape(lay.places, blocks, side, width)

time: 157 us -> 161 us (1.025)
  starting transfers between devices: 31.2 us -> 41 us
  waiting for transfers between devices: 78.4 us -> 70.8 us
  Pallas kernels: 30.1 us -> 34.6 us
  local copies, waits for them, and re-layouts: 6.02 us -> 2.23 us
    pallas_call x1 -> x2, Pallas kernels: 0.15 us -> 10 us  [the longest x1 9.88 us: project(): pl.pallas_call(functools.partial(project_kernel, lay), out_shape=jax.Shap...]
    ppermute x25, starting transfers between devices: 31.2 us -> 41 us  [move(): return lax.ppermute(array, axes, pairs_list)]
    ppermute x25, waiting for transfers between devices: 78.4 us -> 70.8 us  [move(): return lax.ppermute(array, axes, pairs_list)]
    pallas_call x1, Pallas kernels: 17.5 us -> 12.5 us  [make_tiles(): pl.pallas_call(functools.partial(tiles_kernel, lay), out_shape=(sums, sum...]
    unnamed x36 -> x26, local copies, waits for them, and re-layouts: 4.03 us -> 1.5 us
  transfers between devices with their start and end apart: 25 -> 25, of which waited for: 16 -> 17; matrix products, arithmetic and copies ran while one was open for 2% -> 2% of each run, Pallas kernels for 4% -> 10%
where the time goes in v6:
time: 161 us; the launch traced here: 159 us
  waiting for transfers between devices  70.8 us (44%)
  starting transfers between devices  41 us (25%)
  Pallas kernels  34.6 us (21%)
  other arithmetic  8.37 us (5%)
  local copies, waits for them, and re-layouts  2.23 us (1%)
    ppermute x25, waiting for transfers between devices, move(): return lax.ppermute(array, axes, pairs_list)  70.8 us
    ppermute x25, starting transfers between devices, move(): return lax.ppermute(array, axes, pairs_list)  41 us
    pallas_call x1, Pallas kernels, make_tiles(): pl.pallas_call(functools.partial(tiles_kernel, lay), out_shape=(sums, sum...  12.5 us
    pallas_call x1, Pallas kernels, project(): pl.pallas_call(functools.partial(project_kernel, lay), out_shape=jax.Shap...  9.88 us
    pallas_call x1, Pallas kernels, apply_tiles(): pl.pallas_call(functools.partial(apply_kernel, lay), out_shape=(sums, sum...  6.07 us
    pallas_call x1, Pallas kernels, make_plan(): pl.pallas_call(functools.partial(plan_kernel, lay), out_shape=tuple((jax....  5.85 us
  transfers between devices with their start and end apart: 25, of which 17 were waited for; matrix products, arithmetic and copies ran while one was open for 2% of the time, Pallas kernels for 10%

profile of v6, /device:TPU:0, one launch (start us, length us, event | category | flops | bytes accessed | tf_op | source)
XLA Modules:
  0.0 158.6 jit_solution(7777620772429976393)
XLA Ops:
  1.3 0.9 convert_element_type.34
  2.2 0.7 convert_bitcast_fusion.1
  3.0 1.0 pad_maximum_fusion.given.refs_0_
  4.1 4.1 %collective-permute-start.3 = (bf16[3,656,128]{2,1,0:T(8,128)(2,1)S(1)}, bf16[3,656,128]{2,1,0:T(8,128)(2,1)S(1)}, u32[]{:S(2)}, u32[]{:S(2)}) collective-permute-start(bf16[3,656,128]{2,1,0:T(8,128)(2,1)S(1)} %pad_maximum_fusion.given.refs_0_), channel_id=1, source_target_pairs={{0,16},{1,17},{2,18},{3,19},{4,20},{5,21},{6,22},{7,23},{8,24},{9,... | collective-permute-start | bytes 1511432 | tf_op jit(solution)/shard_map/ppermute | solution.py:474
  8.2 2.4 %collective-permute-start.2 = (bf16[3,656,128]{2,1,0:T(8,128)(2,1)S(1)}, bf16[3,656,128]{2,1,0:T(8,128)(2,1)S(1)}, u32[]{:S(2)}, u32[]{:S(2)}) collective-permute-start(bf16[3,656,128]{2,1,0:T(8,128)(2,1)S(1)} %pad_maximum_fusion.given.refs_0_), channel_id=1, source_target_pairs={{0,3},{1,2},{2,1},{3,0},{4,7},{5,6},{6,5},{7,4},{8,11},{9,10},{10,... | collective-permute-start | bytes 1511432 | tf_op jit(solution)/shard_map/ppermute | solution.py:474
  10.6 0.5 collective-permute-start.1
  11.1 0.5 collective-permute-start
  11.7 1.6 collective-permute-start.4
  13.2 0.6 pad_add_fusion.2.ids
  13.9 16.7 %collective-permute-done.3.given.refs_4_ = bf16[3,656,128]{2,1,0:T(8,128)(2,1)S(1)} collective-permute-done((bf16[3,656,128]{2,1,0:T(8,128)(2,1)S(1)}, bf16[3,656,128]{2,1,0:T(8,128)(2,1)S(1)}, u32[]{:S(2)}, u32[]{:S(2)}) %collective-permute-start.3) | collective-permute-done | bytes 503840 | tf_op jit(solution)/shard_map/ppermute | solution.py:474
  30.6 2.2 %collective-permute-done.1.refs_2_ = bf16[3,656,128]{2,1,0:T(8,128)(2,1)S(1)} collective-permute-done((bf16[3,656,128]{2,1,0:T(8,128)(2,1)S(1)}, bf16[3,656,128]{2,1,0:T(8,128)(2,1)S(1)}, u32[]{:S(2)}, u32[]{:S(2)}) %collective-permute-start.1) | collective-permute-done | bytes 503840 | tf_op jit(solution)/shard_map/ppermute | solution.py:474
  33.0 1.6 %collective-permute-start.7 = (bf16[3,656,128]{2,1,0:T(8,128)(2,1)S(1)}, bf16[3,656,128]{2,1,0:T(8,128)(2,1)}, u32[]{:S(2)}, u32[]{:S(2)}) collective-permute-start(bf16[3,656,128]{2,1,0:T(8,128)(2,1)S(1)} %collective-permute-done.3.given.refs_4_), channel_id=1, source_target_pairs={{0,3},{1,2},{2,1},{3,0},{4,7},{5,6},{6,5},{7,4},{8,11},{9,10},{10,... | collective-permute-start | bytes 1511432 | tf_op jit(solution)/shard_map/ppermute | solution.py:474
  34.6 1.3 collective-permute-start.6
  36.0 0.5 collective-permute-start.5
  36.6 1.3 pad_add_fusion.listed
  37.9 5.9 %shard_map.96 = (s32[24]{0:T(128)}, s32[26]{0:T(128)}, s32[4]{0:T(128)}, s32[72]{0:T(128)}, s32[288]{0:T(512)}) custom-call(s32[3]{0:T(128)} %pad_add_fusion.2.ids, s32[2,97]{1,0:T(2,128)} %pad_add_fusion.listed, s32[96]{0:T(128)} %fine.1, s32[8]{0:T(128)} %stored.1), custom_call_target="tpu_custom_call" | custom-call | bytes 20000000 | tf_op jit(solution)/shard_map/pallas_call | solution.py:137
  43.9 1.4 collective-permute-done.4.refs_10_
  45.3 2.4 %collective-permute-start.8 = (bf16[3,128,512]{2,1,0:T(8,128)(2,1)S(1)}, bf16[3,128,512]{2,1,0:T(8,128)(2,1)}, u32[]{:S(2)}, u32[]{:S(2)}) collective-permute-start(bf16[3,128,512]{2,1,0:T(8,128)(2,1)S(1)} %shard_map.95.own), channel_id=1, source_target_pairs={{0,24},{1,25},{2,26},{3,27},{4,28},{5,29},{6,30},{7,31},{8,16},{9,... | collective-permute-start | bytes 1179656 | tf_op jit(solution)/shard_map/ppermute | solution.py:474
  47.7 0.7 collective-permute-done.7.refs_7_
  48.4 9.8 %collective-permute-done.6.refs_6_ = bf16[3,656,128]{2,1,0:T(8,128)(2,1)} collective-permute-done((bf16[3,656,128]{2,1,0:T(8,128)(2,1)S(1)}, bf16[3,656,128]{2,1,0:T(8,128)(2,1)}, u32[]{:S(2)}, u32[]{:S(2)}) %collective-permute-start.6) | collective-permute-done | bytes 503840 | tf_op jit(solution)/shard_map/ppermute | solution.py:474
  58.2 0.8 collective-permute-done.8.refs_10_
  59.5 6.4 %collective-permute-start.9 = (bf16[3,128,512]{2,1,0:T(8,128)(2,1)S(1)}, bf16[3,128,512]{2,1,0:T(8,128)(2,1)}, u32[]{:S(2)}, u32[]{:S(2)}) collective-permute-start(bf16[3,128,512]{2,1,0:T(8,128)(2,1)S(1)} %shard_map.95.own), channel_id=1, source_target_pairs={{0,8},{1,9},{2,10},{3,11},{4,12},{5,13},{6,14},{7,15},{8,0},{9,1},... | collective-permute-start | bytes 1179656 | tf_op jit(solution)/shard_map/ppermute | solution.py:474
  66.2 0.5 collective-permute-start.14
  66.7 9.9 %shard_map.98.refs_14_ = bf16[24,512,256]{2,1,0:T(8,128)(2,1)} custom-call(s32[24]{0:T(128)} %get-tuple-element.45.slot_of, s32[26]{0:T(128)} %get-tuple-element.63.valid, s32[4]{0:T(128)} %get-tuple-element.46.sizes, bf16[3,656,128]{2,1,0:T(8,128)(2,1)} %copy-done, bf16[3,656,128]{2,1,0:T(8,128)(2,1)} %collective-permute-done.refs_1_, ...), custom_call_target="tpu_custom_call" | custom-call | flops 2000000000 | bytes 25000000 | tf_op jit(solution)/shard_map/pallas_call | solution.py:250
  76.7 1.9 %collective-permute-done.13.refs_12_ = bf16[3,128,512]{2,1,0:T(8,128)(2,1)S(1)} collective-permute-done((bf16[3,128,512]{2,1,0:T(8,128)(2,1)}, bf16[3,128,512]{2,1,0:T(8,128)(2,1)S(1)}, u32[]{:S(2)}, u32[]{:S(2)}) %collective-permute-start.13) | collective-permute-done | bytes 393248 | tf_op jit(solution)/shard_map/ppermute | solution.py:474
  78.6 0.8 copy-done.12
  79.4 12.5 %shard_map.99 = (f32[12,128,128]{2,1,0:T(8,128)}, f32[12,128,128]{2,1,0:T(8,128)}, bf16[288,128,128]{2,1,0:T(8,128)(2,1)}) custom-call(s32[24]{0:T(128)} %get-tuple-element.45.slot_of, s32[4]{0:T(128)} %get-tuple-element.46.sizes, s32[72]{0:T(128)} %get-tuple-element.47.group_input, s32[288]{0:T(512)} %get-tuple-element.48.entries, ...), custom_call_target="tpu_custom_call" | custom-call | flops 4000000000 | bytes 30000000 | tf_op jit(solution)/shard_map/pallas_call | solution.py:371
  91.9 3.4 %collective-permute-start.15 = (f32[12,128,128]{2,1,0:T(8,128)}, f32[12,128,128]{2,1,0:T(8,128)S(1)}, u32[]{:S(2)}, u32[]{:S(2)}) collective-permute-start(f32[12,128,128]{2,1,0:T(8,128)} %get-tuple-element.70), channel_id=1, source_target_pairs={{0,4},{1,5},{2,6},{3,7},{4,0},{5,1},{6,2},{7,3},{8,12},{9,13},{10,... | collective-permute-start | bytes 2359304 | tf_op jit(solution)/shard_map/ppermute | solution.py:474
  95.3 2.1 %collective-permute-done.15 = f32[12,128,128]{2,1,0:T(8,128)S(1)} collective-permute-done((f32[12,128,128]{2,1,0:T(8,128)}, f32[12,128,128]{2,1,0:T(8,128)S(1)}, u32[]{:S(2)}, u32[]{:S(2)}) %collective-permute-start.15) | collective-permute-done | bytes 786464 | tf_op jit(solution)/shard_map/ppermute | solution.py:474
  97.5 1.2 fusion.13
  99.0 7.0 %collective-permute-done.16 = bf16[2,3,128,128]{3,2,1,0:T(8,128)(2,1)S(1)} collective-permute-done((bf16[2,3,128,128]{3,2,1,0:T(8,128)(2,1)S(1)}, bf16[2,3,128,128]{3,2,1,0:T(8,128)(2,1)S(1)}, u32[]{:S(2)}, u32[]{:S(2)}) %collective-permute-start.16) | collective-permute-done | bytes 196640 | tf_op jit(solution)/shard_map/ppermute | solution.py:474
  106.1 5.0 %collective-permute-start.17 = (bf16[2,3,128,128]{3,2,1,0:T(8,128)(2,1)S(1)}, bf16[2,3,128,128]{3,2,1,0:T(8,128)(2,1)S(1)}, u32[]{:S(2)}, u32[]{:S(2)}) collective-permute-start(bf16[2,3,128,128]{3,2,1,0:T(8,128)(2,1)S(1)} %fusion), channel_id=1, source_target_pairs={{0,16},{1,17},{2,18},{3,19},{4,20},{5,21},{6,22},{7,23},{8,24},{9,... | collective-permute-start | bytes 589832 | tf_op jit(solution)/shard_map/ppermute | solution.py:474
  111.0 8.8 %collective-permute-done.17 = bf16[2,3,128,128]{3,2,1,0:T(8,128)(2,1)S(1)} collective-permute-done((bf16[2,3,128,128]{3,2,1,0:T(8,128)(2,1)S(1)}, bf16[2,3,128,128]{3,2,1,0:T(8,128)(2,1)S(1)}, u32[]{:S(2)}, u32[]{:S(2)}) %collective-permute-start.17) | collective-permute-done | bytes 196640 | tf_op jit(solution)/shard_map/ppermute | solution.py:474
  120.0 2.2 %collective-permute-start.19 = (bf16[2,3,128,128]{3,2,1,0:T(8,128)(2,1)S(1)}, bf16[2,3,128,128]{3,2,1,0:T(8,128)(2,1)S(1)}, u32[]{:S(2)}, u32[]{:S(2)}) collective-permute-start(bf16[2,3,128,128]{3,2,1,0:T(8,128)(2,1)S(1)} %get-tuple-element.76.refs_0_), channel_id=1, source_target_pairs={{0,2},{1,3},{2,0},{3,1},{4,6},{5,7},{6,4},{7,5},{8,10},{9,11},{10,... | collective-permute-start | bytes 589832 | tf_op jit(solution)/shard_map/ppermute | solution.py:474
  122.2 1.4 collective-permute-start.18
  123.6 5.2 %collective-permute-done.20.refs_3_ = bf16[2,3,128,128]{3,2,1,0:T(8,128)(2,1)S(1)} collective-permute-done((bf16[2,3,128,128]{3,2,1,0:T(8,128)(2,1)S(1)}, bf16[2,3,128,128]{3,2,1,0:T(8,128)(2,1)S(1)}, u32[]{:S(2)}, u32[]{:S(2)}) %collective-permute-start.20) | collective-permute-done | bytes 196640 | tf_op jit(solution)/shard_map/ppermute | solution.py:474
  128.7 2.4 %collective-permute-done.19.refs_2_ = bf16[2,3,128,128]{3,2,1,0:T(8,128)(2,1)S(1)} collective-permute-done((bf16[2,3,128,128]{3,2,1,0:T(8,128)(2,1)S(1)}, bf16[2,3,128,128]{3,2,1,0:T(8,128)(2,1)S(1)}, u32[]{:S(2)}, u32[]{:S(2)}) %collective-permute-start.19) | collective-permute-done | bytes 196640 | tf_op jit(solution)/shard_map/ppermute | solution.py:474
  131.1 0.7 collective-permute-done.18.refs_1_
  131.8 0.7 copy-done.10
  132.5 6.1 %shard_map.100 = (f32[12,128,128]{2,1,0:T(8,128)}, f32[12,128,128]{2,1,0:T(8,128)}) custom-call(s32[4]{0:T(128)} %get-tuple-element.46.sizes, s32[72]{0:T(128)} %get-tuple-element.47.group_input, s32[288]{0:T(512)} %get-tuple-element.48.entries, bf16[288,128,128]{2,1,0:T(8,128)(2,1)} %get-tuple-element.71.tiles_in, bf16[2,3,128,128]{3,2,1,0:T(8,128)(2,1)} %copy-done.5, ...), custom_call_target="tpu_custom_call" | custom-call | flops 400000000 | bytes 4000000 | tf_op jit(solution)/shard_map/pallas_call | solution.py:437
  138.7 2.5 %collective-permute-done.21 = f32[12,128,128]{2,1,0:T(8,128)S(1)} collective-permute-done((f32[12,128,128]{2,1,0:T(8,128)}, f32[12,128,128]{2,1,0:T(8,128)S(1)}, u32[]{:S(2)}, u32[]{:S(2)}) %collective-permute-start.21) | collective-permute-done | bytes 786464 | tf_op jit(solution)/shard_map/ppermute | solution.py:474
  141.1 1.2 fusion.11
  142.4 1.0 collective-permute-start.22
  143.4 4.7 %collective-permute-start.24 = (bf16[3,128,128]{2,1,0:T(8,128)(2,1)S(1)}, bf16[3,128,128]{2,1,0:T(8,128)(2,1)S(1)}, u32[]{:S(2)}, u32[]{:S(2)}) collective-permute-start(bf16[3,128,128]{2,1,0:T(8,128)(2,1)S(1)} %get-tuple-element.83), channel_id=1, source_target_pairs={{0,24},{1,25},{2,26},{3,27},{4,28},{5,29},{6,30},{7,31},{8,16},{9,... | collective-permute-start | bytes 294920 | tf_op jit(solution)/shard_map/ppermute | solution.py:474
  148.6 0.7 slice.79
  149.3 4.5 %collective-permute-done.24 = bf16[3,128,128]{2,1,0:T(8,128)(2,1)S(1)} collective-permute-done((bf16[3,128,128]{2,1,0:T(8,128)(2,1)S(1)}, bf16[3,128,128]{2,1,0:T(8,128)(2,1)S(1)}, u32[]{:S(2)}, u32[]{:S(2)}) %collective-permute-start.24) | collective-permute-done | bytes 98336 | tf_op jit(solution)/shard_map/ppermute | solution.py:474
  153.9 3.9 %collective-permute-done.23 = bf16[3,128,128]{2,1,0:T(8,128)(2,1)S(1)} collective-permute-done((bf16[3,128,128]{2,1,0:T(8,128)(2,1)S(1)}, bf16[3,128,128]{2,1,0:T(8,128)(2,1)S(1)}, u32[]{:S(2)}, u32[]{:S(2)}) %collective-permute-start.23) | collective-permute-done | bytes 98336 | tf_op jit(solution)/shard_map/ppermute | solution.py:474
  157.8 0.8 fusion.5
  (53 shorter events, 2.4 us)
Async XLA Ops:
  4.1 62.6 %copy-start = (bf16[3,656,128]{2,1,0:T(8,128)(2,1)}, bf16[3,656,128]{2,1,0:T(8,128)(2,1)S(1)}, u32[]{:S(2)}) copy-start(bf16[3,656,128]{2,1,0:T(8,128)(2,1)S(1)} %pad_maximum_fusion.given.refs_0_) | copy-start | bytes 1511428
  4.1 26.5 %collective-permute-start.3 = (bf16[3,656,128]{2,1,0:T(8,128)(2,1)S(1)}, bf16[3,656,128]{2,1,0:T(8,128)(2,1)S(1)}, u32[]{:S(2)}, u32[]{:S(2)}) collective-permute-start(bf16[3,656,128]{2,1,0:T(8,128)(2,1)S(1)} %pad_maximum_fusion.given.refs_0_), channel_id=1, source_target_pairs={{0,16},{1,17},{2,18},{3,19},{4,20},{5,21},{6,22},{7,23},{8,24},{9,... | collective-permute-start | bytes 1511432 | tf_op jit(solution)/shard_map/ppermute | solution.py:474
  8.2 22.4 %collective-permute-start.2 = (bf16[3,656,128]{2,1,0:T(8,128)(2,1)S(1)}, bf16[3,656,128]{2,1,0:T(8,128)(2,1)S(1)}, u32[]{:S(2)}, u32[]{:S(2)}) collective-permute-start(bf16[3,656,128]{2,1,0:T(8,128)(2,1)S(1)} %pad_maximum_fusion.given.refs_0_), channel_id=1, source_target_pairs={{0,3},{1,2},{2,1},{3,0},{4,7},{5,6},{6,5},{7,4},{8,11},{9,10},{10,... | collective-permute-start | bytes 1511432 | tf_op jit(solution)/shard_map/ppermute | solution.py:474
  10.6 22.2 %collective-permute-start.1 = (bf16[3,656,128]{2,1,0:T(8,128)(2,1)S(1)}, bf16[3,656,128]{2,1,0:T(8,128)(2,1)S(1)}, u32[]{:S(2)}, u32[]{:S(2)}) collective-permute-start(bf16[3,656,128]{2,1,0:T(8,128)(2,1)S(1)} %pad_maximum_fusion.given.refs_0_), channel_id=1, source_target_pairs={{0,2},{1,3},{2,0},{3,1},{4,6},{5,7},{6,4},{7,5},{8,10},{9,11},{10,... | collective-permute-start | bytes 1511432 | tf_op jit(solution)/shard_map/ppermute | solution.py:474
  11.1 21.9 %collective-permute-start = (bf16[3,656,128]{2,1,0:T(8,128)(2,1)S(1)}, bf16[3,656,128]{2,1,0:T(8,128)(2,1)}, u32[]{:S(2)}, u32[]{:S(2)}) collective-permute-start(bf16[3,656,128]{2,1,0:T(8,128)(2,1)S(1)} %pad_maximum_fusion.given.refs_0_), channel_id=1, source_target_pairs={{0,1},{1,0},{2,3},{3,2},{4,5},{5,4},{6,7},{7,6},{8,9},{9,8},{10,11... | collective-permute-start | bytes 1511432 | tf_op jit(solution)/shard_map/ppermute | solution.py:474
  11.7 33.6 %collective-permute-start.4 = (bf16[2,1,512,512]{3,2,1,0:T(8,128)(2,1)}, bf16[2,1,512,512]{3,2,1,0:T(8,128)(2,1)S(1)}, u32[]{:S(2)}, u32[]{:S(2)}) collective-permute-start(bf16[2,1,512,512]{3,2,1,0:T(8,128)(2,1)} %refs_8_), channel_id=1, source_target_pairs={{0,8},{1,9},{2,10},{3,11},{4,12},{5,13},{6,14},{7,15},{8,0},{9,1},... | collective-permute-start | bytes 3145736 | tf_op jit(solution)/shard_map/ppermute | solution.py:474
  30.6 36.1 %copy-start.1 = (bf16[3,656,128]{2,1,0:T(8,128)(2,1)}, bf16[3,656,128]{2,1,0:T(8,128)(2,1)S(1)}, u32[]{:S(2)}) copy-start(bf16[3,656,128]{2,1,0:T(8,128)(2,1)S(1)} %collective-permute-done.3.given.refs_4_) | copy-start | bytes 1511428
  30.6 36.1 %copy-start.6 = (bf16[3,656,128]{2,1,0:T(8,128)(2,1)}, bf16[3,656,128]{2,1,0:T(8,128)(2,1)S(1)}, u32[]{:S(2)}) copy-start(bf16[3,656,128]{2,1,0:T(8,128)(2,1)S(1)} %collective-permute-done.2.refs_3_) | copy-start | bytes 1511428
  32.8 26.7 %copy-start.7 = (bf16[3,656,128]{2,1,0:T(8,128)(2,1)}, bf16[3,656,128]{2,1,0:T(8,128)(2,1)S(1)}, u32[]{:S(2)}) copy-start(bf16[3,656,128]{2,1,0:T(8,128)(2,1)S(1)} %collective-permute-done.1.refs_2_) | copy-start | bytes 1511428
  33.0 15.4 %collective-permute-start.7 = (bf16[3,656,128]{2,1,0:T(8,128)(2,1)S(1)}, bf16[3,656,128]{2,1,0:T(8,128)(2,1)}, u32[]{:S(2)}, u32[]{:S(2)}) collective-permute-start(bf16[3,656,128]{2,1,0:T(8,128)(2,1)S(1)} %collective-permute-done.3.given.refs_4_), channel_id=1, source_target_pairs={{0,3},{1,2},{2,1},{3,0},{4,7},{5,6},{6,5},{7,4},{8,11},{9,10},{10,... | collective-permute-start | bytes 1511432 | tf_op jit(solution)/shard_map/ppermute | solution.py:474
  34.6 23.6 %collective-permute-start.6 = (bf16[3,656,128]{2,1,0:T(8,128)(2,1)S(1)}, bf16[3,656,128]{2,1,0:T(8,128)(2,1)}, u32[]{:S(2)}, u32[]{:S(2)}) collective-permute-start(bf16[3,656,128]{2,1,0:T(8,128)(2,1)S(1)} %collective-permute-done.3.given.refs_4_), channel_id=1, source_target_pairs={{0,2},{1,3},{2,0},{3,1},{4,6},{5,7},{6,4},{7,5},{8,10},{9,11},{10,... | collective-permute-start | bytes 1511432 | tf_op jit(solution)/shard_map/ppermute | solution.py:474
  36.0 22.2 %collective-permute-start.5 = (bf16[3,656,128]{2,1,0:T(8,128)(2,1)S(1)}, bf16[3,656,128]{2,1,0:T(8,128)(2,1)}, u32[]{:S(2)}, u32[]{:S(2)}) collective-permute-start(bf16[3,656,128]{2,1,0:T(8,128)(2,1)S(1)} %collective-permute-done.3.given.refs_4_), channel_id=1, source_target_pairs={{0,1},{1,0},{2,3},{3,2},{4,5},{5,4},{6,7},{7,6},{8,9},{9,8},{10,11... | collective-permute-start | bytes 1511432 | tf_op jit(solution)/shard_map/ppermute | solution.py:474
  45.3 21.4 %copy-start.4 = (bf16[2,1,512,512]{3,2,1,0:T(8,128)(2,1)}, bf16[2,1,512,512]{3,2,1,0:T(8,128)(2,1)S(1)}, u32[]{:S(2)}) copy-start(bf16[2,1,512,512]{3,2,1,0:T(8,128)(2,1)S(1)} %collective-permute-done.4.refs_10_) | copy-start | bytes 3145732
  45.3 13.7 %collective-permute-start.8 = (bf16[3,128,512]{2,1,0:T(8,128)(2,1)S(1)}, bf16[3,128,512]{2,1,0:T(8,128)(2,1)}, u32[]{:S(2)}, u32[]{:S(2)}) collective-permute-start(bf16[3,128,512]{2,1,0:T(8,128)(2,1)S(1)} %shard_map.95.own), channel_id=1, source_target_pairs={{0,24},{1,25},{2,26},{3,27},{4,28},{5,29},{6,30},{7,31},{8,16},{9,... | collective-permute-start | bytes 1179656 | tf_op jit(solution)/shard_map/ppermute | solution.py:474
  59.0 7.7 %collective-permute-start.10 = (bf16[2,1,512,512]{3,2,1,0:T(8,128)(2,1)}, bf16[2,1,512,512]{3,2,1,0:T(8,128)(2,1)}, u32[]{:S(2)}, u32[]{:S(2)}) collective-permute-start(bf16[2,1,512,512]{3,2,1,0:T(8,128)(2,1)} %refs_8_), channel_id=1, source_target_pairs={{0,4},{1,5},{2,6},{3,7},{4,0},{5,1},{6,2},{7,3},{8,12},{9,13},{10,... | collective-permute-start | bytes 3145736 | tf_op jit(solution)/shard_map/ppermute | solution.py:474
  59.1 7.5 %collective-permute-start.11 = (bf16[2,1,512,512]{3,2,1,0:T(8,128)(2,1)S(1)}, bf16[2,1,512,512]{3,2,1,0:T(8,128)(2,1)}, u32[]{:S(2)}, u32[]{:S(2)}) collective-permute-start(bf16[2,1,512,512]{3,2,1,0:T(8,128)(2,1)S(1)} %collective-permute-done.4.refs_10_), channel_id=1, source_target_pairs={{0,4},{1,5},{2,6},{3,7},{4,0},{5,1},{6,2},{7,3},{8,12},{9,13},{10,... | collective-permute-start | bytes 3145736 | tf_op jit(solution)/shard_map/ppermute | solution.py:474
  59.5 17.1 %collective-permute-start.9 = (bf16[3,128,512]{2,1,0:T(8,128)(2,1)S(1)}, bf16[3,128,512]{2,1,0:T(8,128)(2,1)}, u32[]{:S(2)}, u32[]{:S(2)}) collective-permute-start(bf16[3,128,512]{2,1,0:T(8,128)(2,1)S(1)} %shard_map.95.own), channel_id=1, source_target_pairs={{0,8},{1,9},{2,10},{3,11},{4,12},{5,13},{6,14},{7,15},{8,0},{9,1},... | collective-permute-start | bytes 1179656 | tf_op jit(solution)/shard_map/ppermute | solution.py:474
  66.1 12.6 %copy-start.2 = (bf16[6,128,512]{2,1,0:T(8,128)(2,1)}, bf16[6,128,512]{2,1,0:T(8,128)(2,1)S(1)}, u32[]{:S(2)}) copy-start(bf16[6,128,512]{2,1,0:T(8,128)(2,1)S(1)} %shard_map.97.refs_8_) | copy-start | bytes 2359300
  66.1 10.6 %collective-permute-start.12 = (bf16[6,128,512]{2,1,0:T(8,128)(2,1)S(1)}, bf16[6,128,512]{2,1,0:T(8,128)(2,1)}, u32[]{:S(2)}, u32[]{:S(2)}) collective-permute-start(bf16[6,128,512]{2,1,0:T(8,128)(2,1)S(1)} %shard_map.97.refs_8_), channel_id=1, source_target_pairs={{0,4},{1,5},{2,6},{3,7},{4,0},{5,1},{6,2},{7,3},{8,12},{9,13},{10,... | collective-permute-start | bytes 2359304 | tf_op jit(solution)/shard_map/ppermute | solution.py:474
  66.2 10.5 %collective-permute-start.14 = (bf16[3,128,512]{2,1,0:T(8,128)(2,1)}, bf16[3,128,512]{2,1,0:T(8,128)(2,1)}, u32[]{:S(2)}, u32[]{:S(2)}) collective-permute-start(bf16[3,128,512]{2,1,0:T(8,128)(2,1)} %collective-permute-done.8.refs_10_), channel_id=1, source_target_pairs={{0,4},{1,5},{2,6},{3,7},{4,0},{5,1},{6,2},{7,3},{8,12},{9,13},{10,... | collective-permute-start | bytes 1179656 | tf_op jit(solution)/shard_map/ppermute | solution.py:474
  76.6 22.2 %copy-start.3 = (f32[384,128]{1,0:T(8,128)S(1)}, f32[384,128]{1,0:T(8,128)}, u32[]{:S(2)}) copy-start(f32[384,128]{1,0:T(8,128)} %param.8) | copy-start | bytes 589828
  76.6 22.2 %copy-start.11 = (f32[384]{0:T(512)S(1)}, f32[384]{0:T(512)}, u32[]{:S(2)}) copy-start(f32[384]{0:T(512)} %param.9) | copy-start | bytes 4612
  76.6 2.0 %collective-permute-start.13 = (bf16[3,128,512]{2,1,0:T(8,128)(2,1)}, bf16[3,128,512]{2,1,0:T(8,128)(2,1)S(1)}, u32[]{:S(2)}, u32[]{:S(2)}) collective-permute-start(bf16[3,128,512]{2,1,0:T(8,128)(2,1)} %collective-permute-done.9.refs_9_), channel_id=1, source_target_pairs={{0,4},{1,5},{2,6},{3,7},{4,0},{5,1},{6,2},{7,3},{8,12},{9,13},{10,... | collective-permute-start | bytes 1179656 | tf_op jit(solution)/shard_map/ppermute | solution.py:474
  78.6 0.8 copy-start.12
  91.9 5.6 %collective-permute-start.15 = (f32[12,128,128]{2,1,0:T(8,128)}, f32[12,128,128]{2,1,0:T(8,128)S(1)}, u32[]{:S(2)}, u32[]{:S(2)}) collective-permute-start(f32[12,128,128]{2,1,0:T(8,128)} %get-tuple-element.70), channel_id=1, source_target_pairs={{0,4},{1,5},{2,6},{3,7},{4,0},{5,1},{6,2},{7,3},{8,12},{9,13},{10,... | collective-permute-start | bytes 2359304 | tf_op jit(solution)/shard_map/ppermute | solution.py:474
  98.8 7.2 %collective-permute-start.16 = (bf16[2,3,128,128]{3,2,1,0:T(8,128)(2,1)S(1)}, bf16[2,3,128,128]{3,2,1,0:T(8,128)(2,1)S(1)}, u32[]{:S(2)}, u32[]{:S(2)}) collective-permute-start(bf16[2,3,128,128]{3,2,1,0:T(8,128)(2,1)S(1)} %pad_maximum_fusion.1), channel_id=1, source_target_pairs={{0,8},{1,9},{2,10},{3,11},{4,12},{5,13},{6,14},{7,15},{8,0},{9,1},... | collective-permute-start | bytes 589832 | tf_op jit(solution)/shard_map/ppermute | solution.py:474
  106.1 13.8 %collective-permute-start.17 = (bf16[2,3,128,128]{3,2,1,0:T(8,128)(2,1)S(1)}, bf16[2,3,128,128]{3,2,1,0:T(8,128)(2,1)S(1)}, u32[]{:S(2)}, u32[]{:S(2)}) collective-permute-start(bf16[2,3,128,128]{3,2,1,0:T(8,128)(2,1)S(1)} %fusion), channel_id=1, source_target_pairs={{0,16},{1,17},{2,18},{3,19},{4,20},{5,21},{6,22},{7,23},{8,24},{9,... | collective-permute-start | bytes 589832 | tf_op jit(solution)/shard_map/ppermute | solution.py:474
  119.9 11.9 %copy-start.5 = (bf16[2,3,128,128]{3,2,1,0:T(8,128)(2,1)}, bf16[2,3,128,128]{3,2,1,0:T(8,128)(2,1)S(1)}, u32[]{:S(2)}) copy-start(bf16[2,3,128,128]{3,2,1,0:T(8,128)(2,1)S(1)} %get-tuple-element.76.refs_0_) | copy-start | bytes 589828
  119.9 8.8 %collective-permute-start.20 = (bf16[2,3,128,128]{3,2,1,0:T(8,128)(2,1)S(1)}, bf16[2,3,128,128]{3,2,1,0:T(8,128)(2,1)S(1)}, u32[]{:S(2)}, u32[]{:S(2)}) collective-permute-start(bf16[2,3,128,128]{3,2,1,0:T(8,128)(2,1)S(1)} %get-tuple-element.76.refs_0_), channel_id=1, source_target_pairs={{0,3},{1,2},{2,1},{3,0},{4,7},{5,6},{6,5},{7,4},{8,11},{9,10},{10,... | collective-permute-start | bytes 589832 | tf_op jit(solution)/shard_map/ppermute | solution.py:474
  120.0 11.1 %collective-permute-start.19 = (bf16[2,3,128,128]{3,2,1,0:T(8,128)(2,1)S(1)}, bf16[2,3,128,128]{3,2,1,0:T(8,128)(2,1)S(1)}, u32[]{:S(2)}, u32[]{:S(2)}) collective-permute-start(bf16[2,3,128,128]{3,2,1,0:T(8,128)(2,1)S(1)} %get-tuple-element.76.refs_0_), channel_id=1, source_target_pairs={{0,2},{1,3},{2,0},{3,1},{4,6},{5,7},{6,4},{7,5},{8,10},{9,11},{10,... | collective-permute-start | bytes 589832 | tf_op jit(solution)/shard_map/ppermute | solution.py:474
  122.2 9.7 %collective-permute-start.18 = (bf16[2,3,128,128]{3,2,1,0:T(8,128)(2,1)S(1)}, bf16[2,3,128,128]{3,2,1,0:T(8,128)(2,1)S(1)}, u32[]{:S(2)}, u32[]{:S(2)}) collective-permute-start(bf16[2,3,128,128]{3,2,1,0:T(8,128)(2,1)S(1)} %get-tuple-element.76.refs_0_), channel_id=1, source_target_pairs={{0,1},{1,0},{2,3},{3,2},{4,5},{5,4},{6,7},{7,6},{8,9},{9,8},{10,11... | collective-permute-start | bytes 589832 | tf_op jit(solution)/shard_map/ppermute | solution.py:474
  128.7 3.1 %copy-start.8 = (bf16[2,3,128,128]{3,2,1,0:T(8,128)(2,1)}, bf16[2,3,128,128]{3,2,1,0:T(8,128)(2,1)S(1)}, u32[]{:S(2)}) copy-start(bf16[2,3,128,128]{3,2,1,0:T(8,128)(2,1)S(1)} %collective-permute-done.20.refs_3_) | copy-start | bytes 589828
  131.1 0.7 copy-start.9
  131.8 0.7 copy-start.10
  138.6 2.6 %collective-permute-start.21 = (f32[12,128,128]{2,1,0:T(8,128)}, f32[12,128,128]{2,1,0:T(8,128)S(1)}, u32[]{:S(2)}, u32[]{:S(2)}) collective-permute-start(f32[12,128,128]{2,1,0:T(8,128)} %get-tuple-element.73), channel_id=1, source_target_pairs={{0,4},{1,5},{2,6},{3,7},{4,0},{5,1},{6,2},{7,3},{8,12},{9,13},{10,... | collective-permute-start | bytes 2359304 | tf_op jit(solution)/shard_map/ppermute | solution.py:474
  142.4 6.9 %collective-permute-start.22 = (bf16[3,128,128]{2,1,0:T(8,128)(2,1)S(1)}, bf16[3,128,128]{2,1,0:T(8,128)(2,1)S(1)}, u32[]{:S(2)}, u32[]{:S(2)}) collective-permute-start(bf16[3,128,128]{2,1,0:T(8,128)(2,1)S(1)} %get-tuple-element.82), channel_id=1, source_target_pairs={{0,8},{1,9},{2,10},{3,11},{4,12},{5,13},{6,14},{7,15},{8,0},{9,1},... | collective-permute-start | bytes 294920 | tf_op jit(solution)/shard_map/ppermute | solution.py:474
  143.4 10.4 %collective-permute-start.24 = (bf16[3,128,128]{2,1,0:T(8,128)(2,1)S(1)}, bf16[3,128,128]{2,1,0:T(8,128)(2,1)S(1)}, u32[]{:S(2)}, u32[]{:S(2)}) collective-permute-start(bf16[3,128,128]{2,1,0:T(8,128)(2,1)S(1)} %get-tuple-element.83), channel_id=1, source_target_pairs={{0,24},{1,25},{2,26},{3,27},{4,28},{5,29},{6,30},{7,31},{8,16},{9,... | collective-permute-start | bytes 294920 | tf_op jit(solution)/shard_map/ppermute | solution.py:474
  148.2 9.6 %collective-permute-start.23 = (bf16[3,128,128]{2,1,0:T(8,128)(2,1)S(1)}, bf16[3,128,128]{2,1,0:T(8,128)(2,1)S(1)}, u32[]{:S(2)}, u32[]{:S(2)}) collective-permute-start(bf16[3,128,128]{2,1,0:T(8,128)(2,1)S(1)} %get-tuple-element.84), channel_id=1, source_target_pairs={{0,16},{1,17},{2,18},{3,19},{4,20},{5,21},{6,22},{7,23},{8,24},{9,... | collective-permute-start | bytes 294920 | tf_op jit(solution)/shard_map/ppermute | solution.py:474

commit v7 on v6

--- a/solution.py
+++ b/solution.py
@@ -187,80 +187,72 @@
     )(partner, own)
 
 
-def project_kernel(lay, slot_of, valid, sizes, *refs):
+def project_kernel(lay, owner, slot_of, valid, sizes, *refs):
     refs = list(refs)
-    given_in = [refs.pop(0) for _ in range(lay.owners * lay.cols)]
+    given_in = [refs.pop(0) for _ in range(lay.cols)]
     given_coarse = [refs.pop(0) for _ in range(2 * lay.near)]
     out, right, blocks, projected, sems, out_sems = refs
-    sets = []
-
-    def fetch(source, target, index):
-        sets[-1].append(pltpu.make_async_copy(source, target, sems.at[index]))
-        sets[-1][-1].start()
-
-    for owner in range(lay.owners):
-        sets.append([])
-        if owner == 0:
-            for i in range(2 * lay.near):
-                for a in range(lay.points):
-                    target = blocks.at[a, pl.ds(i * lay.slots_dev, lay.slots_dev)]
-                    fetch(given_coarse[i].at[a], target, i * lay.points + a)
-        for i in range(owner * lay.cols, (owner + 1) * lay.cols):
-            part = pl.ds(i * lay.blocks, lay.blocks)
-            source = given_in[i].at[:, pl.ds(0, lay.pairs)]
-            fetch(source, right.at[part], 2 * lay.near * lay.points + i)
-
-    for owner in range(lay.owners):
-        for copy in sets[owner]:
-            copy.wait()
-        found = sizes[1 + owner]
-
-        def store(i):
-            p = owner * lay.spread + i
-            return pltpu.make_async_copy(projected.at[p], out.at[p], out_sems.at[p])
-
-        def visit(step, carry):
-            for lane in range(2):
-                i = valid[owner * (lay.spread + 1) + jnp.minimum(2 * step + lane, found - 1)]
-                p = owner * lay.spread + i
-                for a in range(lay.points):
-                    projected[p, :, a * lay.side : (a + 1) * lay.side] = jnp.dot(
-                        blocks[a, slot_of[p]], right[p], preferred_element_type=jnp.float32
-                    ).astype(jnp.bfloat16)
-            return carry
-
-        lax.fori_loop(0, lax.div(found + 1, 2), visit, 0)
-        for i in range(lay.spread):
-
-            @pl.when(slot_of[owner * lay.spread + i] >= 0)
-            def _():
-                store(i).start()
-
-    for p in range(lay.inputs):
-
-        @pl.when(slot_of[p] >= 0)
-        def _():
-            pltpu.make_async_copy(projected.at[p], out.at[p], out_sems.at[p]).wait()
-
-
-def project(lay, plan, inputs, coarse):
+    copies = []
+
+    def fetch(source, target):
+        copies.append(pltpu.make_async_copy(source, target, sems.at[len(copies)]))
+        copies[-1].start()
+
+    for i in range(2 * lay.near):
+        for a in range(lay.points):
+            fetch(given_coarse[i].at[a], blocks.at[a, pl.ds(i * lay.slots_dev, lay.slots_dev)])
+    for i in range(lay.cols):
+        fetch(given_in[i].at[:, pl.ds(0, lay.pairs)], right.at[pl.ds(i * lay.blocks, lay.blocks)])
+    for copy in copies:
+        copy.wait()
+    found = sizes[1 + owner]
+
+    def visit(step, carry):
+        for lane in range(2):
+            i = valid[owner * (lay.spread + 1) + jnp.minimum(2 * step + lane, found - 1)]
+            slot = slot_of[owner * lay.spread + i]
+            for a in range(lay.points):
+                projected[i, :, a * lay.side : (a + 1) * lay.side] = jnp.dot(
+                    blocks[a, slot], right[i], preferred_element_type=jnp.float32
+                ).astype(jnp.bfloat16)
+        return carry
+
+    lax.fori_loop(0, lax.div(found + 1, 2), visit, 0)
+
+    def store(i):
+        return pltpu.make_async_copy(projected.at[i], out.at[i], out_sems.at[i])
+
+    for i in range(lay.spread):
+
+        @pl.when(slot_of[owner * lay.spread + i] >= 0)
+        def _():
+            store(i).start()
+
+    for i in range(lay.spread):
+
+        @pl.when(slot_of[owner * lay.spread + i] >= 0)
+        def _():
+            store(i).wait()
+
+
+def project(lay, owner, plan, inputs, coarse):
     smem = pl.BlockSpec(memory_space=pltpu.SMEM)
     hbm = pl.BlockSpec(memory_space=pl.ANY)
-    shape = (lay.inputs, lay.pairs, lay.points * lay.side)
+    shape = (lay.spread, lay.pairs, lay.points * lay.side)
     return pl.pallas_call(
-        functools.partial(project_kernel, lay),
+        functools.partial(project_kernel, lay, owner),
         out_shape=jax.ShapeDtypeStruct(shape, jnp.bfloat16),
         in_specs=[smem] * 3 + [hbm] * (len(inputs) + len(coarse)),
         out_specs=hbm,
         scratch_shapes=[
-            pltpu.VMEM((lay.inputs, lay.pairs, lay.side), jnp.bfloat16),
+            pltpu.VMEM((lay.spread, lay.pairs, lay.side), jnp.bfloat16),
             pltpu.VMEM((lay.points, lay.slots, lay.pairs, lay.pairs), jnp.bfloat16),
             pltpu.VMEM(shape, jnp.bfloat16),
             pltpu.SemaphoreType.DMA((len(inputs) + len(coarse) * lay.points,)),
-            pltpu.SemaphoreType.DMA((lay.inputs,)),
+            pltpu.SemaphoreType.DMA((lay.spread,)),
         ],
         compiler_params=pltpu.CompilerParams(vmem_limit_bytes=lay.vmem),
-        cost_estimate=pl.CostEstimate(flops=2_000_000_000, bytes_accessed=25_000_000, transcendentals=0),
+        cost_estimate=pl.CostEstimate(flops=1_000_000_000, bytes_accessed=16_000_000, transcendentals=0),
     )(*plan[:3], *inputs, *coarse)
 
 
@@ -269,7 +261,7 @@
     refs = list(refs)
     given_in = [refs.pop(0) for _ in range(lay.owners * lay.cols)]
     given_out = [refs.pop(0) for _ in range(2 * (1 + len(lines)))]
-    given_projected = refs.pop(0)
+    given_projected = [refs.pop(0) for _ in range(lay.owners)]
     own_sum, other_sum, tiles_out = refs[:3]
     left, projected, rounded, tiles, total, sems, sum_sems, in_sems, out_sems = refs[3:]
     copies = []
@@ -279,7 +271,8 @@
         copies[-1].start()
 
     def load(p):
-        return pltpu.make_async_copy(given_projected.at[p], projected.at[p], in_sems.at[p])
+        source = given_projected[p // lay.spread].at[p % lay.spread]
+        return pltpu.make_async_copy(source, projected.at[p], in_sems.at[p])
 
     for k in range(2):
         held = given_out[k * (1 + len(lines)) :]
@@ -371,11 +364,11 @@
     return pl.pallas_call(
         functools.partial(tiles_kernel, lay),
         out_shape=(sums, sums, jax.ShapeDtypeStruct(tiles, jnp.bfloat16)),
-        in_specs=[smem] * 4 + [hbm] * (len(inputs) + len(outputs) + 1),
+        in_specs=[smem] * 4 + [hbm] * (len(inputs) + len(outputs) + len(projected)),
         out_specs=(hbm,) * 3,
         scratch_shapes=[
             pltpu.VMEM((lay.outputs, lay.side, lay.pairs), jnp.bfloat16),
-            pltpu.VMEM(projected.shape, jnp.bfloat16),
+            pltpu.VMEM((lay.inputs, lay.pairs, lay.points * lay.side), jnp.bfloat16),
             pltpu.VMEM((lay.inputs, lay.side, lay.width), jnp.bfloat16),
             pltpu.VMEM(tiles, jnp.bfloat16),
             pltpu.VMEM((lay.outputs + 1, lay.side, lay.width), jnp.float32),
@@ -386,7 +379,7 @@
         ],
         compiler_params=pltpu.CompilerParams(vmem_limit_bytes=lay.vmem),
         cost_estimate=pl.CostEstimate(flops=4_000_000_000, bytes_accessed=30_000_000, transcendentals=0),
-    )(plan[0], *plan[2:], *inputs, *outputs, projected)
+    )(plan[0], *plan[2:], *inputs, *outputs, *projected)
 
 
 def apply_kernel(lay, sizes, group_input, entries, tiles_in, *refs):
@@ -505,18 +498,18 @@
         inputs = inputs + in_plane(part)
     turned = turn_own(lay, late_joined)
     turned, near_coarse, plan = lax.optimization_barrier((turned, near_coarse, plan))
+    blocks_coarse = []
+    for part in [coarse] + near_coarse:
+        blocks_coarse += [part, to_core(part)]
+    turned, blocks_coarse = lax.optimization_barrier((turned, blocks_coarse))
     lines = [along(turned, d) for d in lay.line_steps()]
     for part in partner:
         turned = turn_both(lay, part, turned)
-    far = lines[near - 1 :]
-    held = (inputs, near_coarse, far, coarse)
-    inputs, near_coarse, far, late_coarse = lax.optimization_barrier(held)
-    blocks_coarse = []
-    for part in [late_coarse] + near_coarse:
-        blocks_coarse += [part, to_core(part)]
-    projected = project(lay, plan, inputs, blocks_coarse)
-    late, projected = lax.optimization_barrier((lines[: near - 1], projected))
-    lefts = [turned] + late + far
+    projected = [
+        project(lay, g, plan, inputs[g * cols : (g + 1) * cols], blocks_coarse) for g in range(lay.owners)
+    ]
+    lines, turned, projected = lax.optimization_barrier((lines, turned, projected))
+    lefts = [turned] + lines
     lefts = lefts + [to_core(part) for part in lefts]
     own_sum, other_sum, tiles = make_tiles(lay, plan, inputs, lefts, projected)
 

time: 161 us -> 163 us (1.012); the launches traced: 159 us -> 163 us
  waiting for transfers between devices: 70.8 us -> 78.3 us
  starting transfers between devices: 41 us -> 34.7 us
  Pallas kernels: 34.6 us -> 36.7 us
    ppermute x25, waiting for transfers between devices: 70.8 us -> 78.3 us  [move(): return lax.ppermute(array, axes, pairs_list)]
    ppermute x25, starting transfers between devices: 41 us -> 34.7 us  [move(): return lax.ppermute(array, axes, pairs_list)]
    pallas_call x1 -> x2, Pallas kernels: 9.88 us -> 13.5 us  [project(): pl.pallas_call(functools.partial(project_kernel, lay, owner), out_shape=j...]
  transfers between devices with their start and end apart: 25 -> 25, of which waited for: 17 -> 18; matrix products, arithmetic and copies ran while one was open for 2% -> 2% of each run, Pallas kernels for 10% -> 12%
where the time goes in v7:
time: 163 us
  waiting for transfers between devices  78.3 us (48%)
  Pallas kernels  36.7 us (23%)
  starting transfers between devices  34.7 us (21%)
  other arithmetic  8.3 us (5%)
  local copies, waits for them, and re-layouts  3.16 us (2%)
    ppermute x25, waiting for transfers between devices, move(): return lax.ppermute(array, axes, pairs_list)  78.3 us
    ppermute x25, starting transfers between devices, move(): return lax.ppermute(array, axes, pairs_list)  34.7 us
    pallas_call x2, Pallas kernels, project(): pl.pallas_call(functools.partial(project_kernel, lay, owner), out_shape=j...  13.5 us
    pallas_call x1, Pallas kernels, make_tiles(): pl.pallas_call(functools.partial(tiles_kernel, lay), out_shape=(sums, sum...  11.1 us
    pallas_call x1, Pallas kernels, make_plan(): pl.pallas_call(functools.partial(plan_kernel, lay), out_shape=tuple((jax....  6.07 us
    pallas_call x1, Pallas kernels, apply_tiles(): pl.pallas_call(functools.partial(apply_kernel, lay), out_shape=(sums, sum...  5.7 us
  transfers between devices with their start and end apart: 25, of which 18 were waited for; matrix products, arithmetic and copies ran while one was open for 2% of the time, Pallas kernels for 12%

profile of v7, /device:TPU:0, one launch (start us, length us, event | category | flops | bytes accessed | tf_op | source)
XLA Modules:
  0.0 162.7 jit_solution(18065975502284268764)
XLA Ops:
  1.3 0.9 convert_element_type.34
  2.2 0.7 convert_bitcast_fusion.1
  3.0 1.0 pad_maximum_fusion.given.refs_0_
  4.1 4.1 %collective-permute-start.3 = (bf16[3,656,128]{2,1,0:T(8,128)(2,1)S(1)}, bf16[3,656,128]{2,1,0:T(8,128)(2,1)S(1)}, u32[]{:S(2)}, u32[]{:S(2)}) collective-permute-start(bf16[3,656,128]{2,1,0:T(8,128)(2,1)S(1)} %pad_maximum_fusion.given.refs_0_), channel_id=1, source_target_pairs={{0,16},{1,17},{2,18},{3,19},{4,20},{5,21},{6,22},{7,23},{8,24},{9,... | collective-permute-start | bytes 1511432 | tf_op jit(solution)/shard_map/ppermute | solution.py:467
  8.2 2.4 %collective-permute-start.2 = (bf16[3,656,128]{2,1,0:T(8,128)(2,1)S(1)}, bf16[3,656,128]{2,1,0:T(8,128)(2,1)S(1)}, u32[]{:S(2)}, u32[]{:S(2)}) collective-permute-start(bf16[3,656,128]{2,1,0:T(8,128)(2,1)S(1)} %pad_maximum_fusion.given.refs_0_), channel_id=1, source_target_pairs={{0,3},{1,2},{2,1},{3,0},{4,7},{5,6},{6,5},{7,4},{8,11},{9,10},{10,... | collective-permute-start | bytes 1511432 | tf_op jit(solution)/shard_map/ppermute | solution.py:467
  10.6 0.5 collective-permute-start.1
  11.1 0.5 collective-permute-start
  11.7 1.6 collective-permute-start.4
  13.2 0.6 pad_add_fusion.2.ids
  13.8 16.7 %collective-permute-done.3.given.refs_0_.refs_4_ = bf16[3,656,128]{2,1,0:T(8,128)(2,1)S(1)} collective-permute-done((bf16[3,656,128]{2,1,0:T(8,128)(2,1)S(1)}, bf16[3,656,128]{2,1,0:T(8,128)(2,1)S(1)}, u32[]{:S(2)}, u32[]{:S(2)}) %collective-permute-start.3) | collective-permute-done | bytes 503840 | tf_op jit(solution)/shard_map/ppermute | solution.py:467
  30.6 2.2 %collective-permute-done.1.refs_2_ = bf16[3,656,128]{2,1,0:T(8,128)(2,1)S(1)} collective-permute-done((bf16[3,656,128]{2,1,0:T(8,128)(2,1)S(1)}, bf16[3,656,128]{2,1,0:T(8,128)(2,1)S(1)}, u32[]{:S(2)}, u32[]{:S(2)}) %collective-permute-start.1) | collective-permute-done | bytes 503840 | tf_op jit(solution)/shard_map/ppermute | solution.py:467
  33.1 1.3 pad_add_fusion.listed
  34.4 6.1 %shard_map.96 = (s32[24]{0:T(128)}, s32[26]{0:T(128)}, s32[4]{0:T(128)}, s32[72]{0:T(128)}, s32[288]{0:T(512)}) custom-call(s32[3]{0:T(128)} %pad_add_fusion.2.ids, s32[2,97]{1,0:T(2,128)} %pad_add_fusion.listed, s32[96]{0:T(128)} %fine.1, s32[8]{0:T(128)} %stored.1), custom_call_target="tpu_custom_call" | custom-call | bytes 20000000 | tf_op jit(solution)/shard_map/pallas_call | solution.py:137
  40.6 4.7 %collective-permute-done.4.refs_6_ = bf16[2,1,512,512]{3,2,1,0:T(8,128)(2,1)S(1)} collective-permute-done((bf16[2,1,512,512]{3,2,1,0:T(8,128)(2,1)}, bf16[2,1,512,512]{3,2,1,0:T(8,128)(2,1)S(1)}, u32[]{:S(2)}, u32[]{:S(2)}) %collective-permute-start.4) | collective-permute-done | bytes 1048608 | tf_op jit(solution)/shard_map/ppermute | solution.py:467
  45.3 2.5 %collective-permute-start.7 = (bf16[3,656,128]{2,1,0:T(8,128)(2,1)S(1)}, bf16[3,656,128]{2,1,0:T(8,128)(2,1)}, u32[]{:S(2)}, u32[]{:S(2)}) collective-permute-start(bf16[3,656,128]{2,1,0:T(8,128)(2,1)S(1)} %collective-permute-done.3.given.refs_0_.refs_4_), channel_id=1, source_target_pairs={{0,3},{1,2},{2,1},{3,0},{4,7},{5,6},{6,5},{7,4},{8,11},{9,10},{10,... | collective-permute-start | bytes 1511432 | tf_op jit(solution)/shard_map/ppermute | solution.py:467
  47.8 0.5 collective-permute-start.6
  48.3 0.7 collective-permute-start.5
  49.0 2.3 %collective-permute-start.11 = (bf16[3,128,512]{2,1,0:T(8,128)(2,1)S(1)}, bf16[3,128,512]{2,1,0:T(8,128)(2,1)}, u32[]{:S(2)}, u32[]{:S(2)}) collective-permute-start(bf16[3,128,512]{2,1,0:T(8,128)(2,1)S(1)} %shard_map.95.own), channel_id=1, source_target_pairs={{0,24},{1,25},{2,26},{3,27},{4,28},{5,29},{6,30},{7,31},{8,16},{9,... | collective-permute-start | bytes 1179656 | tf_op jit(solution)/shard_map/ppermute | solution.py:467
  51.5 6.8 %shard_map.98.refs_14_ = bf16[12,512,256]{2,1,0:T(8,128)(2,1)} custom-call(s32[24]{0:T(128)} %get-tuple-element.42.slot_of, s32[26]{0:T(128)} %get-tuple-element.53.valid, s32[4]{0:T(128)} %get-tuple-element.43.sizes, bf16[3,656,128]{2,1,0:T(8,128)(2,1)} %copy-done, bf16[3,656,128]{2,1,0:T(8,128)(2,1)} %collective-permute-done.refs_1_, ...), custom_call_target="tpu_custom_call" | custom-call | flops 1000000000 | bytes 16000000 | tf_op jit(solution)/shard_map/pallas_call | solution.py:242
  58.3 2.3 %collective-permute-done.7.refs_3_.refs_7_ = bf16[3,656,128]{2,1,0:T(8,128)(2,1)} collective-permute-done((bf16[3,656,128]{2,1,0:T(8,128)(2,1)S(1)}, bf16[3,656,128]{2,1,0:T(8,128)(2,1)}, u32[]{:S(2)}, u32[]{:S(2)}) %collective-permute-start.7) | collective-permute-done | bytes 503840 | tf_op jit(solution)/shard_map/ppermute | solution.py:467
  60.6 10.4 %collective-permute-done.6.refs_2_.refs_6_ = bf16[3,656,128]{2,1,0:T(8,128)(2,1)} collective-permute-done((bf16[3,656,128]{2,1,0:T(8,128)(2,1)S(1)}, bf16[3,656,128]{2,1,0:T(8,128)(2,1)}, u32[]{:S(2)}, u32[]{:S(2)}) %collective-permute-start.6) | collective-permute-done | bytes 503840 | tf_op jit(solution)/shard_map/ppermute | solution.py:467
  71.0 0.7 collective-permute-done.5.refs_1_.refs_5_
  71.7 6.7 %shard_map.99.refs_15_ = bf16[12,512,256]{2,1,0:T(8,128)(2,1)} custom-call(s32[24]{0:T(128)} %get-tuple-element.42.slot_of, s32[26]{0:T(128)} %get-tuple-element.53.valid, s32[4]{0:T(128)} %get-tuple-element.43.sizes, bf16[3,656,128]{2,1,0:T(8,128)(2,1)} %copy-done.1, bf16[3,656,128]{2,1,0:T(8,128)(2,1)} %collective-permute-done.5.refs_1_.refs_5_, ...), custom_call_target="tpu_custom_call" | custom-call | flops 1000000000 | bytes 16000000 | tf_op jit(solution)/shard_map/pallas_call | solution.py:242
  79.1 2.5 %collective-permute-done.13.refs_12_ = bf16[3,128,512]{2,1,0:T(8,128)(2,1)S(1)} collective-permute-done((bf16[3,128,512]{2,1,0:T(8,128)(2,1)}, bf16[3,128,512]{2,1,0:T(8,128)(2,1)S(1)}, u32[]{:S(2)}, u32[]{:S(2)}) %collective-permute-start.13) | collective-permute-done | bytes 393248 | tf_op jit(solution)/shard_map/ppermute | solution.py:467
  81.6 0.6 collective-permute-done.14.refs_13_
  82.3 0.6 copy-done.15
  83.0 0.9 copy-done.13
  83.9 11.1 %shard_map.100 = (f32[12,128,128]{2,1,0:T(8,128)}, f32[12,128,128]{2,1,0:T(8,128)}, bf16[288,128,128]{2,1,0:T(8,128)(2,1)}) custom-call(s32[24]{0:T(128)} %get-tuple-element.42.slot_of, s32[4]{0:T(128)} %get-tuple-element.43.sizes, s32[72]{0:T(128)} %get-tuple-element.44.group_input, s32[288]{0:T(512)} %get-tuple-element.45.entries, ...), custom_call_target="tpu_custom_call" | custom-call | flops 4000000000 | bytes 30000000 | tf_op jit(solution)/shard_map/pallas_call | solution.py:364
  95.0 1.8 %collective-permute-start.15 = (f32[12,128,128]{2,1,0:T(8,128)}, f32[12,128,128]{2,1,0:T(8,128)S(1)}, u32[]{:S(2)}, u32[]{:S(2)}) collective-permute-start(f32[12,128,128]{2,1,0:T(8,128)} %get-tuple-element.64), channel_id=1, source_target_pairs={{0,4},{1,5},{2,6},{3,7},{4,0},{5,1},{6,2},{7,3},{8,12},{9,13},{10,... | collective-permute-start | bytes 2359304 | tf_op jit(solution)/shard_map/ppermute | solution.py:467
  96.9 2.1 %collective-permute-done.15 = f32[12,128,128]{2,1,0:T(8,128)S(1)} collective-permute-done((f32[12,128,128]{2,1,0:T(8,128)}, f32[12,128,128]{2,1,0:T(8,128)S(1)}, u32[]{:S(2)}, u32[]{:S(2)}) %collective-permute-start.15) | collective-permute-done | bytes 786464 | tf_op jit(solution)/shard_map/ppermute | solution.py:467
  99.0 1.2 fusion.13
  100.5 7.0 %collective-permute-done.16 = bf16[2,3,128,128]{3,2,1,0:T(8,128)(2,1)S(1)} collective-permute-done((bf16[2,3,128,128]{3,2,1,0:T(8,128)(2,1)S(1)}, bf16[2,3,128,128]{3,2,1,0:T(8,128)(2,1)S(1)}, u32[]{:S(2)}, u32[]{:S(2)}) %collective-permute-start.16) | collective-permute-done | bytes 196640 | tf_op jit(solution)/shard_map/ppermute | solution.py:467
  107.6 3.6 %collective-permute-start.17 = (bf16[2,3,128,128]{3,2,1,0:T(8,128)(2,1)S(1)}, bf16[2,3,128,128]{3,2,1,0:T(8,128)(2,1)S(1)}, u32[]{:S(2)}, u32[]{:S(2)}) collective-permute-start(bf16[2,3,128,128]{3,2,1,0:T(8,128)(2,1)S(1)} %fusion), channel_id=1, source_target_pairs={{0,16},{1,17},{2,18},{3,19},{4,20},{5,21},{6,22},{7,23},{8,24},{9,... | collective-permute-start | bytes 589832 | tf_op jit(solution)/shard_map/ppermute | solution.py:467
  111.2 8.9 %collective-permute-done.17 = bf16[2,3,128,128]{3,2,1,0:T(8,128)(2,1)S(1)} collective-permute-done((bf16[2,3,128,128]{3,2,1,0:T(8,128)(2,1)S(1)}, bf16[2,3,128,128]{3,2,1,0:T(8,128)(2,1)S(1)}, u32[]{:S(2)}, u32[]{:S(2)}) %collective-permute-start.17) | collective-permute-done | bytes 196640 | tf_op jit(solution)/shard_map/ppermute | solution.py:467
  120.2 2.9 %collective-permute-start.20 = (bf16[2,3,128,128]{3,2,1,0:T(8,128)(2,1)S(1)}, bf16[2,3,128,128]{3,2,1,0:T(8,128)(2,1)S(1)}, u32[]{:S(2)}, u32[]{:S(2)}) collective-permute-start(bf16[2,3,128,128]{3,2,1,0:T(8,128)(2,1)S(1)} %get-tuple-element.70.refs_0_), channel_id=1, source_target_pairs={{0,3},{1,2},{2,1},{3,0},{4,7},{5,6},{6,5},{7,4},{8,11},{9,10},{10,... | collective-permute-start | bytes 589832 | tf_op jit(solution)/shard_map/ppermute | solution.py:467
  123.1 5.1 %collective-permute-start.19 = (bf16[2,3,128,128]{3,2,1,0:T(8,128)(2,1)S(1)}, bf16[2,3,128,128]{3,2,1,0:T(8,128)(2,1)S(1)}, u32[]{:S(2)}, u32[]{:S(2)}) collective-permute-start(bf16[2,3,128,128]{3,2,1,0:T(8,128)(2,1)S(1)} %get-tuple-element.70.refs_0_), channel_id=1, source_target_pairs={{0,2},{1,3},{2,0},{3,1},{4,6},{5,7},{6,4},{7,5},{8,10},{9,11},{10,... | collective-permute-start | bytes 589832 | tf_op jit(solution)/shard_map/ppermute | solution.py:467
  128.2 1.4 collective-permute-start.18
  129.6 7.1 %collective-permute-done.19.refs_2_ = bf16[2,3,128,128]{3,2,1,0:T(8,128)(2,1)S(1)} collective-permute-done((bf16[2,3,128,128]{3,2,1,0:T(8,128)(2,1)S(1)}, bf16[2,3,128,128]{3,2,1,0:T(8,128)(2,1)S(1)}, u32[]{:S(2)}, u32[]{:S(2)}) %collective-permute-start.19) | collective-permute-done | bytes 196640 | tf_op jit(solution)/shard_map/ppermute | solution.py:467
  136.8 1.9 %collective-permute-done.18.refs_1_ = bf16[2,3,128,128]{3,2,1,0:T(8,128)(2,1)S(1)} collective-permute-done((bf16[2,3,128,128]{3,2,1,0:T(8,128)(2,1)S(1)}, bf16[2,3,128,128]{3,2,1,0:T(8,128)(2,1)S(1)}, u32[]{:S(2)}, u32[]{:S(2)}) %collective-permute-start.18) | collective-permute-done | bytes 196640 | tf_op jit(solution)/shard_map/ppermute | solution.py:467
  138.7 0.7 copy-done.11
  139.3 5.7 %shard_map.101 = (f32[12,128,128]{2,1,0:T(8,128)}, f32[12,128,128]{2,1,0:T(8,128)}) custom-call(s32[4]{0:T(128)} %get-tuple-element.43.sizes, s32[72]{0:T(128)} %get-tuple-element.44.group_input, s32[288]{0:T(512)} %get-tuple-element.45.entries, bf16[288,128,128]{2,1,0:T(8,128)(2,1)} %get-tuple-element.65.tiles_in, bf16[2,3,128,128]{3,2,1,0:T(8,128)(2,1)} %copy-done.6, ...), custom_call_target="tpu_custom_call" | custom-call | flops 400000000 | bytes 4000000 | tf_op jit(solution)/shard_map/pallas_call | solution.py:430
  145.1 2.5 %collective-permute-done.21 = f32[12,128,128]{2,1,0:T(8,128)S(1)} collective-permute-done((f32[12,128,128]{2,1,0:T(8,128)}, f32[12,128,128]{2,1,0:T(8,128)S(1)}, u32[]{:S(2)}, u32[]{:S(2)}) %collective-permute-start.21) | collective-permute-done | bytes 786464 | tf_op jit(solution)/shard_map/ppermute | solution.py:467
  147.6 1.2 fusion.11
  149.0 3.3 %collective-permute-start.24 = (bf16[3,128,128]{2,1,0:T(8,128)(2,1)S(1)}, bf16[3,128,128]{2,1,0:T(8,128)(2,1)S(1)}, u32[]{:S(2)}, u32[]{:S(2)}) collective-permute-start(bf16[3,128,128]{2,1,0:T(8,128)(2,1)S(1)} %get-tuple-element.77), channel_id=1, source_target_pairs={{0,24},{1,25},{2,26},{3,27},{4,28},{5,29},{6,30},{7,31},{8,16},{9,... | collective-permute-start | bytes 294920 | tf_op jit(solution)/shard_map/ppermute | solution.py:467
  152.8 0.7 slice.79
  153.8 4.2 %collective-permute-done.24 = bf16[3,128,128]{2,1,0:T(8,128)(2,1)S(1)} collective-permute-done((bf16[3,128,128]{2,1,0:T(8,128)(2,1)S(1)}, bf16[3,128,128]{2,1,0:T(8,128)(2,1)S(1)}, u32[]{:S(2)}, u32[]{:S(2)}) %collective-permute-start.24) | collective-permute-done | bytes 98336 | tf_op jit(solution)/shard_map/ppermute | solution.py:467
  158.0 3.9 %collective-permute-done.23 = bf16[3,128,128]{2,1,0:T(8,128)(2,1)S(1)} collective-permute-done((bf16[3,128,128]{2,1,0:T(8,128)(2,1)S(1)}, bf16[3,128,128]{2,1,0:T(8,128)(2,1)S(1)}, u32[]{:S(2)}, u32[]{:S(2)}) %collective-permute-start.23) | collective-permute-done | bytes 98336 | tf_op jit(solution)/shard_map/ppermute | solution.py:467
  161.9 0.8 fusion.5
  (60 shorter events, 2.9 us)
Async XLA Ops:
  4.1 47.4 %copy-start = (bf16[3,656,128]{2,1,0:T(8,128)(2,1)}, bf16[3,656,128]{2,1,0:T(8,128)(2,1)S(1)}, u32[]{:S(2)}) copy-start(bf16[3,656,128]{2,1,0:T(8,128)(2,1)S(1)} %pad_maximum_fusion.given.refs_0_) | copy-start | bytes 1511428
  4.1 26.5 %collective-permute-start.3 = (bf16[3,656,128]{2,1,0:T(8,128)(2,1)S(1)}, bf16[3,656,128]{2,1,0:T(8,128)(2,1)S(1)}, u32[]{:S(2)}, u32[]{:S(2)}) collective-permute-start(bf16[3,656,128]{2,1,0:T(8,128)(2,1)S(1)} %pad_maximum_fusion.given.refs_0_), channel_id=1, source_target_pairs={{0,16},{1,17},{2,18},{3,19},{4,20},{5,21},{6,22},{7,23},{8,24},{9,... | collective-permute-start | bytes 1511432 | tf_op jit(solution)/shard_map/ppermute | solution.py:467
  8.2 22.4 %collective-permute-start.2 = (bf16[3,656,128]{2,1,0:T(8,128)(2,1)S(1)}, bf16[3,656,128]{2,1,0:T(8,128)(2,1)S(1)}, u32[]{:S(2)}, u32[]{:S(2)}) collective-permute-start(bf16[3,656,128]{2,1,0:T(8,128)(2,1)S(1)} %pad_maximum_fusion.given.refs_0_), channel_id=1, source_target_pairs={{0,3},{1,2},{2,1},{3,0},{4,7},{5,6},{6,5},{7,4},{8,11},{9,10},{10,... | collective-permute-start | bytes 1511432 | tf_op jit(solution)/shard_map/ppermute | solution.py:467
  10.6 22.2 %collective-permute-start.1 = (bf16[3,656,128]{2,1,0:T(8,128)(2,1)S(1)}, bf16[3,656,128]{2,1,0:T(8,128)(2,1)S(1)}, u32[]{:S(2)}, u32[]{:S(2)}) collective-permute-start(bf16[3,656,128]{2,1,0:T(8,128)(2,1)S(1)} %pad_maximum_fusion.given.refs_0_), channel_id=1, source_target_pairs={{0,2},{1,3},{2,0},{3,1},{4,6},{5,7},{6,4},{7,5},{8,10},{9,11},{10,... | collective-permute-start | bytes 1511432 | tf_op jit(solution)/shard_map/ppermute | solution.py:467
  11.1 21.9 %collective-permute-start = (bf16[3,656,128]{2,1,0:T(8,128)(2,1)S(1)}, bf16[3,656,128]{2,1,0:T(8,128)(2,1)}, u32[]{:S(2)}, u32[]{:S(2)}) collective-permute-start(bf16[3,656,128]{2,1,0:T(8,128)(2,1)S(1)} %pad_maximum_fusion.given.refs_0_), channel_id=1, source_target_pairs={{0,1},{1,0},{2,3},{3,2},{4,5},{5,4},{6,7},{7,6},{8,9},{9,8},{10,11... | collective-permute-start | bytes 1511432 | tf_op jit(solution)/shard_map/ppermute | solution.py:467
  11.7 33.6 %collective-permute-start.4 = (bf16[2,1,512,512]{3,2,1,0:T(8,128)(2,1)}, bf16[2,1,512,512]{3,2,1,0:T(8,128)(2,1)S(1)}, u32[]{:S(2)}, u32[]{:S(2)}) collective-permute-start(bf16[2,1,512,512]{3,2,1,0:T(8,128)(2,1)} %refs_4_.1), channel_id=1, source_target_pairs={{0,8},{1,9},{2,10},{3,11},{4,12},{5,13},{6,14},{7,15},{8,0},{9,1},... | collective-permute-start | bytes 3145736 | tf_op jit(solution)/shard_map/ppermute | solution.py:467
  30.6 27.7 %copy-start.1 = (bf16[3,656,128]{2,1,0:T(8,128)(2,1)}, bf16[3,656,128]{2,1,0:T(8,128)(2,1)S(1)}, u32[]{:S(2)}) copy-start(bf16[3,656,128]{2,1,0:T(8,128)(2,1)S(1)} %collective-permute-done.3.given.refs_0_.refs_4_) | copy-start | bytes 1511428
  30.6 18.4 %collective-permute-start.8 = (bf16[2,1,512,512]{3,2,1,0:T(8,128)(2,1)}, bf16[2,1,512,512]{3,2,1,0:T(8,128)(2,1)}, u32[]{:S(2)}, u32[]{:S(2)}) collective-permute-start(bf16[2,1,512,512]{3,2,1,0:T(8,128)(2,1)} %refs_4_.1), channel_id=1, source_target_pairs={{0,4},{1,5},{2,6},{3,7},{4,0},{5,1},{6,2},{7,3},{8,12},{9,13},{10,... | collective-permute-start | bytes 3145736 | tf_op jit(solution)/shard_map/ppermute | solution.py:467
  30.6 20.9 %copy-start.7 = (bf16[3,656,128]{2,1,0:T(8,128)(2,1)}, bf16[3,656,128]{2,1,0:T(8,128)(2,1)S(1)}, u32[]{:S(2)}) copy-start(bf16[3,656,128]{2,1,0:T(8,128)(2,1)S(1)} %collective-permute-done.2.refs_3_) | copy-start | bytes 1511428
  32.8 18.5 %copy-start.8 = (bf16[3,656,128]{2,1,0:T(8,128)(2,1)}, bf16[3,656,128]{2,1,0:T(8,128)(2,1)S(1)}, u32[]{:S(2)}) copy-start(bf16[3,656,128]{2,1,0:T(8,128)(2,1)S(1)} %collective-permute-done.1.refs_2_) | copy-start | bytes 1511428
  45.3 6.2 %copy-start.3 = (bf16[2,1,512,512]{3,2,1,0:T(8,128)(2,1)}, bf16[2,1,512,512]{3,2,1,0:T(8,128)(2,1)S(1)}, u32[]{:S(2)}) copy-start(bf16[2,1,512,512]{3,2,1,0:T(8,128)(2,1)S(1)} %collective-permute-done.4.refs_6_) | copy-start | bytes 3145732
  45.3 3.7 %collective-permute-start.9 = (bf16[2,1,512,512]{3,2,1,0:T(8,128)(2,1)S(1)}, bf16[2,1,512,512]{3,2,1,0:T(8,128)(2,1)S(1)}, u32[]{:S(2)}, u32[]{:S(2)}) collective-permute-start(bf16[2,1,512,512]{3,2,1,0:T(8,128)(2,1)S(1)} %collective-permute-done.4.refs_6_), channel_id=1, source_target_pairs={{0,4},{1,5},{2,6},{3,7},{4,0},{5,1},{6,2},{7,3},{8,12},{9,13},{10,... | collective-permute-start | bytes 3145736 | tf_op jit(solution)/shard_map/ppermute | solution.py:467
  45.3 15.3 %collective-permute-start.7 = (bf16[3,656,128]{2,1,0:T(8,128)(2,1)S(1)}, bf16[3,656,128]{2,1,0:T(8,128)(2,1)}, u32[]{:S(2)}, u32[]{:S(2)}) collective-permute-start(bf16[3,656,128]{2,1,0:T(8,128)(2,1)S(1)} %collective-permute-done.3.given.refs_0_.refs_4_), channel_id=1, source_target_pairs={{0,3},{1,2},{2,1},{3,0},{4,7},{5,6},{6,5},{7,4},{8,11},{9,10},{10,... | collective-permute-start | bytes 1511432 | tf_op jit(solution)/shard_map/ppermute | solution.py:467
  47.8 23.2 %collective-permute-start.6 = (bf16[3,656,128]{2,1,0:T(8,128)(2,1)S(1)}, bf16[3,656,128]{2,1,0:T(8,128)(2,1)}, u32[]{:S(2)}, u32[]{:S(2)}) collective-permute-start(bf16[3,656,128]{2,1,0:T(8,128)(2,1)S(1)} %collective-permute-done.3.given.refs_0_.refs_4_), channel_id=1, source_target_pairs={{0,2},{1,3},{2,0},{3,1},{4,6},{5,7},{6,4},{7,5},{8,10},{9,11},{10,... | collective-permute-start | bytes 1511432 | tf_op jit(solution)/shard_map/ppermute | solution.py:467
  48.3 23.4 %collective-permute-start.5 = (bf16[3,656,128]{2,1,0:T(8,128)(2,1)S(1)}, bf16[3,656,128]{2,1,0:T(8,128)(2,1)}, u32[]{:S(2)}, u32[]{:S(2)}) collective-permute-start(bf16[3,656,128]{2,1,0:T(8,128)(2,1)S(1)} %collective-permute-done.3.given.refs_0_.refs_4_), channel_id=1, source_target_pairs={{0,1},{1,0},{2,3},{3,2},{4,5},{5,4},{6,7},{7,6},{8,9},{9,8},{10,11... | collective-permute-start | bytes 1511432 | tf_op jit(solution)/shard_map/ppermute | solution.py:467
  49.0 2.3 %copy-start.4 = (bf16[2,1,512,512]{3,2,1,0:T(8,128)(2,1)}, bf16[2,1,512,512]{3,2,1,0:T(8,128)(2,1)S(1)}, u32[]{:S(2)}) copy-start(bf16[2,1,512,512]{3,2,1,0:T(8,128)(2,1)S(1)} %collective-permute-done.9.refs_7_) | copy-start | bytes 3145732
  49.0 29.5 %collective-permute-start.11 = (bf16[3,128,512]{2,1,0:T(8,128)(2,1)S(1)}, bf16[3,128,512]{2,1,0:T(8,128)(2,1)}, u32[]{:S(2)}, u32[]{:S(2)}) collective-permute-start(bf16[3,128,512]{2,1,0:T(8,128)(2,1)S(1)} %shard_map.95.own), channel_id=1, source_target_pairs={{0,24},{1,25},{2,26},{3,27},{4,28},{5,29},{6,30},{7,31},{8,16},{9,... | collective-permute-start | bytes 1179656 | tf_op jit(solution)/shard_map/ppermute | solution.py:467
  51.3 27.1 %collective-permute-start.10 = (bf16[3,128,512]{2,1,0:T(8,128)(2,1)S(1)}, bf16[3,128,512]{2,1,0:T(8,128)(2,1)}, u32[]{:S(2)}, u32[]{:S(2)}) collective-permute-start(bf16[3,128,512]{2,1,0:T(8,128)(2,1)S(1)} %shard_map.95.own), channel_id=1, source_target_pairs={{0,8},{1,9},{2,10},{3,11},{4,12},{5,13},{6,14},{7,15},{8,0},{9,1},... | collective-permute-start | bytes 1179656 | tf_op jit(solution)/shard_map/ppermute | solution.py:467
  51.5 26.9 %copy-start.2 = (bf16[6,128,512]{2,1,0:T(8,128)(2,1)}, bf16[6,128,512]{2,1,0:T(8,128)(2,1)S(1)}, u32[]{:S(2)}) copy-start(bf16[6,128,512]{2,1,0:T(8,128)(2,1)S(1)} %shard_map.97.refs_8_) | copy-start | bytes 2359300
  78.5 3.7 %collective-permute-start.12 = (bf16[6,128,512]{2,1,0:T(8,128)(2,1)S(1)}, bf16[6,128,512]{2,1,0:T(8,128)(2,1)S(1)}, u32[]{:S(2)}, u32[]{:S(2)}) collective-permute-start(bf16[6,128,512]{2,1,0:T(8,128)(2,1)S(1)} %shard_map.97.refs_8_), channel_id=1, source_target_pairs={{0,4},{1,5},{2,6},{3,7},{4,0},{5,1},{6,2},{7,3},{8,12},{9,13},{10,... | collective-permute-start | bytes 2359304 | tf_op jit(solution)/shard_map/ppermute | solution.py:467
  78.5 3.0 %collective-permute-start.13 = (bf16[3,128,512]{2,1,0:T(8,128)(2,1)}, bf16[3,128,512]{2,1,0:T(8,128)(2,1)S(1)}, u32[]{:S(2)}, u32[]{:S(2)}) collective-permute-start(bf16[3,128,512]{2,1,0:T(8,128)(2,1)} %collective-permute-done.10.refs_9_), channel_id=1, source_target_pairs={{0,4},{1,5},{2,6},{3,7},{4,0},{5,1},{6,2},{7,3},{8,12},{9,13},{10,... | collective-permute-start | bytes 1179656 | tf_op jit(solution)/shard_map/ppermute | solution.py:467
  79.0 3.1 %collective-permute-start.14 = (bf16[3,128,512]{2,1,0:T(8,128)(2,1)}, bf16[3,128,512]{2,1,0:T(8,128)(2,1)S(1)}, u32[]{:S(2)}, u32[]{:S(2)}) collective-permute-start(bf16[3,128,512]{2,1,0:T(8,128)(2,1)} %collective-permute-done.11.refs_10_), channel_id=1, source_target_pairs={{0,4},{1,5},{2,6},{3,7},{4,0},{5,1},{6,2},{7,3},{8,12},{9,13},{10,... | collective-permute-start | bytes 1179656 | tf_op jit(solution)/shard_map/ppermute | solution.py:467
  81.6 0.8 copy-start.14
  82.1 0.8 copy-start.15
  83.0 0.9 copy-start.13
  95.0 5.4 %copy-start.5 = (f32[384,128]{1,0:T(8,128)S(1)}, f32[384,128]{1,0:T(8,128)}, u32[]{:S(2)}) copy-start(f32[384,128]{1,0:T(8,128)} %param.8) | copy-start | bytes 589828
  95.0 5.4 %copy-start.12 = (f32[384]{0:T(512)S(1)}, f32[384]{0:T(512)}, u32[]{:S(2)}) copy-start(f32[384]{0:T(512)} %param.9) | copy-start | bytes 4612
  95.0 4.0 %collective-permute-start.15 = (f32[12,128,128]{2,1,0:T(8,128)}, f32[12,128,128]{2,1,0:T(8,128)S(1)}, u32[]{:S(2)}, u32[]{:S(2)}) collective-permute-start(f32[12,128,128]{2,1,0:T(8,128)} %get-tuple-element.64), channel_id=1, source_target_pairs={{0,4},{1,5},{2,6},{3,7},{4,0},{5,1},{6,2},{7,3},{8,12},{9,13},{10,... | collective-permute-start | bytes 2359304 | tf_op jit(solution)/shard_map/ppermute | solution.py:467
  100.3 7.2 %collective-permute-start.16 = (bf16[2,3,128,128]{3,2,1,0:T(8,128)(2,1)S(1)}, bf16[2,3,128,128]{3,2,1,0:T(8,128)(2,1)S(1)}, u32[]{:S(2)}, u32[]{:S(2)}) collective-permute-start(bf16[2,3,128,128]{3,2,1,0:T(8,128)(2,1)S(1)} %pad_maximum_fusion.1), channel_id=1, source_target_pairs={{0,8},{1,9},{2,10},{3,11},{4,12},{5,13},{6,14},{7,15},{8,0},{9,1},... | collective-permute-start | bytes 589832 | tf_op jit(solution)/shard_map/ppermute | solution.py:467
  107.6 12.5 %collective-permute-start.17 = (bf16[2,3,128,128]{3,2,1,0:T(8,128)(2,1)S(1)}, bf16[2,3,128,128]{3,2,1,0:T(8,128)(2,1)S(1)}, u32[]{:S(2)}, u32[]{:S(2)}) collective-permute-start(bf16[2,3,128,128]{3,2,1,0:T(8,128)(2,1)S(1)} %fusion), channel_id=1, source_target_pairs={{0,16},{1,17},{2,18},{3,19},{4,20},{5,21},{6,22},{7,23},{8,24},{9,... | collective-permute-start | bytes 589832 | tf_op jit(solution)/shard_map/ppermute | solution.py:467
  120.2 18.4 %copy-start.6 = (bf16[2,3,128,128]{3,2,1,0:T(8,128)(2,1)}, bf16[2,3,128,128]{3,2,1,0:T(8,128)(2,1)S(1)}, u32[]{:S(2)}) copy-start(bf16[2,3,128,128]{3,2,1,0:T(8,128)(2,1)S(1)} %get-tuple-element.70.refs_0_) | copy-start | bytes 589828
  120.2 9.4 %collective-permute-start.20 = (bf16[2,3,128,128]{3,2,1,0:T(8,128)(2,1)S(1)}, bf16[2,3,128,128]{3,2,1,0:T(8,128)(2,1)S(1)}, u32[]{:S(2)}, u32[]{:S(2)}) collective-permute-start(bf16[2,3,128,128]{3,2,1,0:T(8,128)(2,1)S(1)} %get-tuple-element.70.refs_0_), channel_id=1, source_target_pairs={{0,3},{1,2},{2,1},{3,0},{4,7},{5,6},{6,5},{7,4},{8,11},{9,10},{10,... | collective-permute-start | bytes 589832 | tf_op jit(solution)/shard_map/ppermute | solution.py:467
  123.1 13.7 %collective-permute-start.19 = (bf16[2,3,128,128]{3,2,1,0:T(8,128)(2,1)S(1)}, bf16[2,3,128,128]{3,2,1,0:T(8,128)(2,1)S(1)}, u32[]{:S(2)}, u32[]{:S(2)}) collective-permute-start(bf16[2,3,128,128]{3,2,1,0:T(8,128)(2,1)S(1)} %get-tuple-element.70.refs_0_), channel_id=1, source_target_pairs={{0,2},{1,3},{2,0},{3,1},{4,6},{5,7},{6,4},{7,5},{8,10},{9,11},{10,... | collective-permute-start | bytes 589832 | tf_op jit(solution)/shard_map/ppermute | solution.py:467
  128.2 10.4 %collective-permute-start.18 = (bf16[2,3,128,128]{3,2,1,0:T(8,128)(2,1)S(1)}, bf16[2,3,128,128]{3,2,1,0:T(8,128)(2,1)S(1)}, u32[]{:S(2)}, u32[]{:S(2)}) collective-permute-start(bf16[2,3,128,128]{3,2,1,0:T(8,128)(2,1)S(1)} %get-tuple-element.70.refs_0_), channel_id=1, source_target_pairs={{0,1},{1,0},{2,3},{3,2},{4,5},{5,4},{6,7},{7,6},{8,9},{9,8},{10,11... | collective-permute-start | bytes 589832 | tf_op jit(solution)/shard_map/ppermute | solution.py:467
  129.6 9.0 %copy-start.9 = (bf16[2,3,128,128]{3,2,1,0:T(8,128)(2,1)}, bf16[2,3,128,128]{3,2,1,0:T(8,128)(2,1)S(1)}, u32[]{:S(2)}) copy-start(bf16[2,3,128,128]{3,2,1,0:T(8,128)(2,1)S(1)} %collective-permute-done.20.refs_3_) | copy-start | bytes 589828
  136.8 1.9 %copy-start.10 = (bf16[2,3,128,128]{3,2,1,0:T(8,128)(2,1)}, bf16[2,3,128,128]{3,2,1,0:T(8,128)(2,1)S(1)}, u32[]{:S(2)}) copy-start(bf16[2,3,128,128]{3,2,1,0:T(8,128)(2,1)S(1)} %collective-permute-done.19.refs_2_) | copy-start | bytes 589828
  138.6 0.7 copy-start.11
  145.0 2.6 %collective-permute-start.21 = (f32[12,128,128]{2,1,0:T(8,128)}, f32[12,128,128]{2,1,0:T(8,128)S(1)}, u32[]{:S(2)}, u32[]{:S(2)}) collective-permute-start(f32[12,128,128]{2,1,0:T(8,128)} %get-tuple-element.67), channel_id=1, source_target_pairs={{0,4},{1,5},{2,6},{3,7},{4,0},{5,1},{6,2},{7,3},{8,12},{9,13},{10,... | collective-permute-start | bytes 2359304 | tf_op jit(solution)/shard_map/ppermute | solution.py:467
  148.9 4.9 %collective-permute-start.22 = (bf16[3,128,128]{2,1,0:T(8,128)(2,1)S(1)}, bf16[3,128,128]{2,1,0:T(8,128)(2,1)S(1)}, u32[]{:S(2)}, u32[]{:S(2)}) collective-permute-start(bf16[3,128,128]{2,1,0:T(8,128)(2,1)S(1)} %get-tuple-element.76), channel_id=1, source_target_pairs={{0,8},{1,9},{2,10},{3,11},{4,12},{5,13},{6,14},{7,15},{8,0},{9,1},... | collective-permute-start | bytes 294920 | tf_op jit(solution)/shard_map/ppermute | solution.py:467
  149.0 9.0 %collective-permute-start.24 = (bf16[3,128,128]{2,1,0:T(8,128)(2,1)S(1)}, bf16[3,128,128]{2,1,0:T(8,128)(2,1)S(1)}, u32[]{:S(2)}, u32[]{:S(2)}) collective-permute-start(bf16[3,128,128]{2,1,0:T(8,128)(2,1)S(1)} %get-tuple-element.77), channel_id=1, source_target_pairs={{0,24},{1,25},{2,26},{3,27},{4,28},{5,29},{6,30},{7,31},{8,16},{9,... | collective-permute-start | bytes 294920 | tf_op jit(solution)/shard_map/ppermute | solution.py:467
  152.3 9.6 %collective-permute-start.23 = (bf16[3,128,128]{2,1,0:T(8,128)(2,1)S(1)}, bf16[3,128,128]{2,1,0:T(8,128)(2,1)S(1)}, u32[]{:S(2)}, u32[]{:S(2)}) collective-permute-start(bf16[3,128,128]{2,1,0:T(8,128)(2,1)S(1)} %get-tuple-element.78), channel_id=1, source_target_pairs={{0,16},{1,17},{2,18},{3,19},{4,20},{5,21},{6,22},{7,23},{8,24},{9,... | collective-permute-start | bytes 294920 | tf_op jit(solution)/shard_map/ppermute | solution.py:467

commit v8 on v7

--- a/solution.py
+++ b/solution.py
@@ -497,6 +497,7 @@
     for part in partner:
         inputs = inputs + in_plane(part)
     turned = turn_own(lay, late_joined)
+    inputs[-1], near_coarse = lax.optimization_barrier((inputs[-1], near_coarse))
     turned, near_coarse, plan = lax.optimization_barrier((turned, near_coarse, plan))
     blocks_coarse = []
     for part in [coarse] + near_coarse:

time: 163 us -> 155 us (0.951)
  starting transfers between devices: 34.7 us -> 26.1 us
  waiting for transfers between devices: 78.3 us -> 71.5 us
  Pallas kernels: 36.7 us -> 43 us
    ppermute x25, starting transfers between devices: 34.7 us -> 26.1 us  [move(): return lax.ppermute(array, axes, pairs_list)]
    ppermute x25, waiting for transfers between devices: 78.3 us -> 71.5 us  [move(): return lax.ppermute(array, axes, pairs_list)]
    pallas_call x1, Pallas kernels: 11.1 us -> 14.9 us  [make_tiles(): pl.pallas_call(functools.partial(tiles_kernel, lay), out_shape=(sums, sum...]
    pallas_call x2, Pallas kernels: 13.5 us -> 15.3 us  [project(): pl.pallas_call(functools.partial(project_kernel, lay, owner), out_shape=j...]
  transfers between devices with their start and end apart: 25 -> 25, of which waited for: 18 -> 20; matrix products, arithmetic and copies ran while one was open for 2% -> 2% of each run, Pallas kernels for 12% -> 14%
where the time goes in v8:
time: 155 us; the launch traced here: 154 us
  waiting for transfers between devices  71.5 us (46%)
  Pallas kernels  43 us (28%)
  starting transfers between devices  26.1 us (17%)
  other arithmetic  8.3 us (5%)
  local copies, waits for them, and re-layouts  3.16 us (2%)
  between operations  1.56 us (1%)
    ppermute x25, waiting for transfers between devices, move(): return lax.ppermute(array, axes, pairs_list)  71.5 us
    ppermute x25, starting transfers between devices, move(): return lax.ppermute(array, axes, pairs_list)  26.1 us
    pallas_call x2, Pallas kernels, project(): pl.pallas_call(functools.partial(project_kernel, lay, owner), out_shape=j...  15.3 us
    pallas_call x1, Pallas kernels, make_tiles(): pl.pallas_call(functools.partial(tiles_kernel, lay), out_shape=(sums, sum...  14.9 us
    pallas_call x1, Pallas kernels, apply_tiles(): pl.pallas_call(functools.partial(apply_kernel, lay), out_shape=(sums, sum...  7.17 us
    pallas_call x1, Pallas kernels, make_plan(): pl.pallas_call(functools.partial(plan_kernel, lay), out_shape=tuple((jax....  5.41 us
  transfers between devices with their start and end apart: 25, of which 20 were waited for; matrix products, arithmetic and copies ran while one was open for 2% of the time, Pallas kernels for 14%

profile of v8, /device:TPU:0, one launch (start us, length us, event | category | flops | bytes accessed | tf_op | source)
XLA Modules:
  0.0 153.6 jit_solution(8330202169448117809)
XLA Ops:
  1.3 0.9 convert_element_type.34
  2.2 0.7 convert_bitcast_fusion.1
  3.0 1.0 pad_maximum_fusion.given.refs_0_
  4.1 4.1 %collective-permute-start.3 = (bf16[3,656,128]{2,1,0:T(8,128)(2,1)S(1)}, bf16[3,656,128]{2,1,0:T(8,128)(2,1)S(1)}, u32[]{:S(2)}, u32[]{:S(2)}) collective-permute-start(bf16[3,656,128]{2,1,0:T(8,128)(2,1)S(1)} %pad_maximum_fusion.given.refs_0_), channel_id=1, source_target_pairs={{0,16},{1,17},{2,18},{3,19},{4,20},{5,21},{6,22},{7,23},{8,24},{9,... | collective-permute-start | bytes 1511432 | tf_op jit(solution)/shard_map/ppermute | solution.py:467
  8.2 2.4 %collective-permute-start.2 = (bf16[3,656,128]{2,1,0:T(8,128)(2,1)S(1)}, bf16[3,656,128]{2,1,0:T(8,128)(2,1)S(1)}, u32[]{:S(2)}, u32[]{:S(2)}) collective-permute-start(bf16[3,656,128]{2,1,0:T(8,128)(2,1)S(1)} %pad_maximum_fusion.given.refs_0_), channel_id=1, source_target_pairs={{0,3},{1,2},{2,1},{3,0},{4,7},{5,6},{6,5},{7,4},{8,11},{9,10},{10,... | collective-permute-start | bytes 1511432 | tf_op jit(solution)/shard_map/ppermute | solution.py:467
  11.1 0.5 collective-permute-start
  11.7 1.6 %collective-permute-start.5 = (bf16[2,1,512,512]{3,2,1,0:T(8,128)(2,1)}, bf16[2,1,512,512]{3,2,1,0:T(8,128)(2,1)S(1)}, u32[]{:S(2)}, u32[]{:S(2)}) collective-permute-start(bf16[2,1,512,512]{3,2,1,0:T(8,128)(2,1)} %refs_4_.1), channel_id=1, source_target_pairs={{0,8},{1,9},{2,10},{3,11},{4,12},{5,13},{6,14},{7,15},{8,0},{9,1},... | collective-permute-start | bytes 3145736 | tf_op jit(solution)/shard_map/ppermute | solution.py:467
  13.2 0.6 pad_add_fusion.2.ids
  13.8 16.7 %collective-permute-done.3.given.refs_0_.refs_4_ = bf16[3,656,128]{2,1,0:T(8,128)(2,1)S(1)} collective-permute-done((bf16[3,656,128]{2,1,0:T(8,128)(2,1)S(1)}, bf16[3,656,128]{2,1,0:T(8,128)(2,1)S(1)}, u32[]{:S(2)}, u32[]{:S(2)}) %collective-permute-start.3) | collective-permute-done | bytes 503840 | tf_op jit(solution)/shard_map/ppermute | solution.py:467
  30.6 2.2 %collective-permute-done.1.refs_2_ = bf16[3,656,128]{2,1,0:T(8,128)(2,1)S(1)} collective-permute-done((bf16[3,656,128]{2,1,0:T(8,128)(2,1)S(1)}, bf16[3,656,128]{2,1,0:T(8,128)(2,1)S(1)}, u32[]{:S(2)}, u32[]{:S(2)}) %collective-permute-start.1) | collective-permute-done | bytes 503840 | tf_op jit(solution)/shard_map/ppermute | solution.py:467
  33.0 1.6 %collective-permute-start.4 = (bf16[3,656,128]{2,1,0:T(8,128)(2,1)S(1)}, bf16[3,656,128]{2,1,0:T(8,128)(2,1)}, u32[]{:S(2)}, u32[]{:S(2)}) collective-permute-start(bf16[3,656,128]{2,1,0:T(8,128)(2,1)S(1)} %collective-permute-done.3.given.refs_0_.refs_4_), channel_id=1, source_target_pairs={{0,3},{1,2},{2,1},{3,0},{4,7},{5,6},{6,5},{7,4},{8,11},{9,10},{10,... | collective-permute-start | bytes 1511432 | tf_op jit(solution)/shard_map/ppermute | solution.py:467
  34.7 1.3 pad_add_fusion.listed
  36.0 5.4 %shard_map.96 = (s32[24]{0:T(128)}, s32[26]{0:T(128)}, s32[4]{0:T(128)}, s32[72]{0:T(128)}, s32[288]{0:T(512)}) custom-call(s32[3]{0:T(128)} %pad_add_fusion.2.ids, s32[2,97]{1,0:T(2,128)} %pad_add_fusion.listed, s32[96]{0:T(128)} %fine.1, s32[8]{0:T(128)} %stored.1), custom_call_target="tpu_custom_call" | custom-call | bytes 20000000 | tf_op jit(solution)/shard_map/pallas_call | solution.py:137
  41.6 5.8 %collective-permute-done.4.refs_3_.refs_7_ = bf16[3,656,128]{2,1,0:T(8,128)(2,1)} collective-permute-done((bf16[3,656,128]{2,1,0:T(8,128)(2,1)S(1)}, bf16[3,656,128]{2,1,0:T(8,128)(2,1)}, u32[]{:S(2)}, u32[]{:S(2)}) %collective-permute-start.4) | collective-permute-done | bytes 503840 | tf_op jit(solution)/shard_map/ppermute | solution.py:467
  47.4 1.5 collective-permute-start.7
  49.1 1.0 collective-permute-done.9.refs_7_
  50.1 2.2 %collective-permute-start.11 = (bf16[3,128,512]{2,1,0:T(8,128)(2,1)S(1)}, bf16[3,128,512]{2,1,0:T(8,128)(2,1)}, u32[]{:S(2)}, u32[]{:S(2)}) collective-permute-start(bf16[3,128,512]{2,1,0:T(8,128)(2,1)S(1)} %shard_map.95.own), channel_id=1, source_target_pairs={{0,24},{1,25},{2,26},{3,27},{4,28},{5,29},{6,30},{7,31},{8,16},{9,... | collective-permute-start | bytes 1179656 | tf_op jit(solution)/shard_map/ppermute | solution.py:467
  52.8 7.6 %shard_map.98.refs_14_ = bf16[12,512,256]{2,1,0:T(8,128)(2,1)} custom-call(s32[24]{0:T(128)} %get-tuple-element.45.slot_of, s32[26]{0:T(128)} %get-tuple-element.57.valid, s32[4]{0:T(128)} %get-tuple-element.46.sizes, bf16[3,656,128]{2,1,0:T(8,128)(2,1)} %copy-done, bf16[3,656,128]{2,1,0:T(8,128)(2,1)} %collective-permute-done.refs_1_, ...), custom_call_target="tpu_custom_call" | custom-call | flops 1000000000 | bytes 16000000 | tf_op jit(solution)/shard_map/pallas_call | solution.py:242
  60.4 1.0 collective-permute-done.7.refs_2_.refs_6_
  61.4 1.1 collective-permute-done.6.refs_1_.refs_5_
  62.6 7.6 %shard_map.99.refs_15_ = bf16[12,512,256]{2,1,0:T(8,128)(2,1)} custom-call(s32[24]{0:T(128)} %get-tuple-element.45.slot_of, s32[26]{0:T(128)} %get-tuple-element.57.valid, s32[4]{0:T(128)} %get-tuple-element.46.sizes, bf16[3,656,128]{2,1,0:T(8,128)(2,1)} %copy-done.1, bf16[3,656,128]{2,1,0:T(8,128)(2,1)} %collective-permute-done.6.refs_1_.refs_5_, ...), custom_call_target="tpu_custom_call" | custom-call | flops 1000000000 | bytes 16000000 | tf_op jit(solution)/shard_map/pallas_call | solution.py:242
  70.2 1.2 collective-permute-done.10.refs_9_
  71.5 0.5 collective-permute-start.13
  72.0 2.2 %collective-permute-done.13.refs_12_ = bf16[3,128,512]{2,1,0:T(8,128)(2,1)S(1)} collective-permute-done((bf16[3,128,512]{2,1,0:T(8,128)(2,1)}, bf16[3,128,512]{2,1,0:T(8,128)(2,1)S(1)}, u32[]{:S(2)}, u32[]{:S(2)}) %collective-permute-start.13) | collective-permute-done | bytes 393248 | tf_op jit(solution)/shard_map/ppermute | solution.py:467
  74.1 0.9 collective-permute-done.14.refs_13_
  75.1 0.8 copy-done.15
  75.9 0.9 copy-done.13
  76.8 14.9 %shard_map.100 = (f32[12,128,128]{2,1,0:T(8,128)}, f32[12,128,128]{2,1,0:T(8,128)}, bf16[288,128,128]{2,1,0:T(8,128)(2,1)}) custom-call(s32[24]{0:T(128)} %get-tuple-element.45.slot_of, s32[4]{0:T(128)} %get-tuple-element.46.sizes, s32[72]{0:T(128)} %get-tuple-element.47.group_input, s32[288]{0:T(512)} %get-tuple-element.48.entries, ...), custom_call_target="tpu_custom_call" | custom-call | flops 4000000000 | bytes 30000000 | tf_op jit(solution)/shard_map/pallas_call | solution.py:364
  91.8 2.5 %collective-permute-done.15 = f32[12,128,128]{2,1,0:T(8,128)S(1)} collective-permute-done((f32[12,128,128]{2,1,0:T(8,128)}, f32[12,128,128]{2,1,0:T(8,128)S(1)}, u32[]{:S(2)}, u32[]{:S(2)}) %collective-permute-start.15) | collective-permute-done | bytes 786464 | tf_op jit(solution)/shard_map/ppermute | solution.py:467
  94.3 1.2 fusion.13
  95.6 0.8 collective-permute-start.16
  96.5 6.0 %collective-permute-done.16 = bf16[2,3,128,128]{3,2,1,0:T(8,128)(2,1)S(1)} collective-permute-done((bf16[2,3,128,128]{3,2,1,0:T(8,128)(2,1)S(1)}, bf16[2,3,128,128]{3,2,1,0:T(8,128)(2,1)S(1)}, u32[]{:S(2)}, u32[]{:S(2)}) %collective-permute-start.16) | collective-permute-done | bytes 196640 | tf_op jit(solution)/shard_map/ppermute | solution.py:467
  102.7 11.2 %collective-permute-done.17 = bf16[2,3,128,128]{3,2,1,0:T(8,128)(2,1)S(1)} collective-permute-done((bf16[2,3,128,128]{3,2,1,0:T(8,128)(2,1)S(1)}, bf16[2,3,128,128]{3,2,1,0:T(8,128)(2,1)S(1)}, u32[]{:S(2)}, u32[]{:S(2)}) %collective-permute-start.17) | collective-permute-done | bytes 196640 | tf_op jit(solution)/shard_map/ppermute | solution.py:467
  114.0 3.6 %collective-permute-start.20 = (bf16[2,3,128,128]{3,2,1,0:T(8,128)(2,1)S(1)}, bf16[2,3,128,128]{3,2,1,0:T(8,128)(2,1)S(1)}, u32[]{:S(2)}, u32[]{:S(2)}) collective-permute-start(bf16[2,3,128,128]{3,2,1,0:T(8,128)(2,1)S(1)} %get-tuple-element.74.refs_0_), channel_id=1, source_target_pairs={{0,3},{1,2},{2,1},{3,0},{4,7},{5,6},{6,5},{7,4},{8,11},{9,10},{10,... | collective-permute-start | bytes 589832 | tf_op jit(solution)/shard_map/ppermute | solution.py:467
  117.7 2.4 %collective-permute-start.19 = (bf16[2,3,128,128]{3,2,1,0:T(8,128)(2,1)S(1)}, bf16[2,3,128,128]{3,2,1,0:T(8,128)(2,1)S(1)}, u32[]{:S(2)}, u32[]{:S(2)}) collective-permute-start(bf16[2,3,128,128]{3,2,1,0:T(8,128)(2,1)S(1)} %get-tuple-element.74.refs_0_), channel_id=1, source_target_pairs={{0,2},{1,3},{2,0},{3,1},{4,6},{5,7},{6,4},{7,5},{8,10},{9,11},{10,... | collective-permute-start | bytes 589832 | tf_op jit(solution)/shard_map/ppermute | solution.py:467
  120.0 2.3 %collective-permute-done.20.refs_3_ = bf16[2,3,128,128]{3,2,1,0:T(8,128)(2,1)S(1)} collective-permute-done((bf16[2,3,128,128]{3,2,1,0:T(8,128)(2,1)S(1)}, bf16[2,3,128,128]{3,2,1,0:T(8,128)(2,1)S(1)}, u32[]{:S(2)}, u32[]{:S(2)}) %collective-permute-start.20) | collective-permute-done | bytes 196640 | tf_op jit(solution)/shard_map/ppermute | solution.py:467
  122.4 5.3 %collective-permute-done.19.refs_2_ = bf16[2,3,128,128]{3,2,1,0:T(8,128)(2,1)S(1)} collective-permute-done((bf16[2,3,128,128]{3,2,1,0:T(8,128)(2,1)S(1)}, bf16[2,3,128,128]{3,2,1,0:T(8,128)(2,1)S(1)}, u32[]{:S(2)}, u32[]{:S(2)}) %collective-permute-start.19) | collective-permute-done | bytes 196640 | tf_op jit(solution)/shard_map/ppermute | solution.py:467
  127.7 1.1 collective-permute-done.18.refs_1_
  128.7 0.7 copy-done.11
  129.4 7.2 %shard_map.101 = (f32[12,128,128]{2,1,0:T(8,128)}, f32[12,128,128]{2,1,0:T(8,128)}) custom-call(s32[4]{0:T(128)} %get-tuple-element.46.sizes, s32[72]{0:T(128)} %get-tuple-element.47.group_input, s32[288]{0:T(512)} %get-tuple-element.48.entries, bf16[288,128,128]{2,1,0:T(8,128)(2,1)} %get-tuple-element.69.tiles_in, bf16[2,3,128,128]{3,2,1,0:T(8,128)(2,1)} %copy-done.6, ...), custom_call_target="tpu_custom_call" | custom-call | flops 400000000 | bytes 4000000 | tf_op jit(solution)/shard_map/pallas_call | solution.py:430
  136.7 2.5 %collective-permute-done.21 = f32[12,128,128]{2,1,0:T(8,128)S(1)} collective-permute-done((f32[12,128,128]{2,1,0:T(8,128)}, f32[12,128,128]{2,1,0:T(8,128)S(1)}, u32[]{:S(2)}, u32[]{:S(2)}) %collective-permute-start.21) | collective-permute-done | bytes 786464 | tf_op jit(solution)/shard_map/ppermute | solution.py:467
  139.1 1.2 fusion.11
  140.6 3.4 %collective-permute-start.23 = (bf16[3,128,128]{2,1,0:T(8,128)(2,1)S(1)}, bf16[3,128,128]{2,1,0:T(8,128)(2,1)S(1)}, u32[]{:S(2)}, u32[]{:S(2)}) collective-permute-start(bf16[3,128,128]{2,1,0:T(8,128)(2,1)S(1)} %get-tuple-element.82), channel_id=1, source_target_pairs={{0,16},{1,17},{2,18},{3,19},{4,20},{5,21},{6,22},{7,23},{8,24},{9,... | collective-permute-start | bytes 294920 | tf_op jit(solution)/shard_map/ppermute | solution.py:467
  144.0 0.7 slice.79
  144.7 2.1 %collective-permute-done.22 = bf16[3,128,128]{2,1,0:T(8,128)(2,1)S(1)} collective-permute-done((bf16[3,128,128]{2,1,0:T(8,128)(2,1)S(1)}, bf16[3,128,128]{2,1,0:T(8,128)(2,1)S(1)}, u32[]{:S(2)}, u32[]{:S(2)}) %collective-permute-start.22) | collective-permute-done | bytes 98336 | tf_op jit(solution)/shard_map/ppermute | solution.py:467
  146.7 1.4 collective-permute-done.24
  148.1 4.7 %collective-permute-done.23 = bf16[3,128,128]{2,1,0:T(8,128)(2,1)S(1)} collective-permute-done((bf16[3,128,128]{2,1,0:T(8,128)(2,1)S(1)}, bf16[3,128,128]{2,1,0:T(8,128)(2,1)S(1)}, u32[]{:S(2)}, u32[]{:S(2)}) %collective-permute-start.23) | collective-permute-done | bytes 98336 | tf_op jit(solution)/shard_map/ppermute | solution.py:467
  152.8 0.8 fusion.5
  (60 shorter events, 2.4 us)
Async XLA Ops:
  4.1 48.7 %copy-start = (bf16[3,656,128]{2,1,0:T(8,128)(2,1)}, bf16[3,656,128]{2,1,0:T(8,128)(2,1)S(1)}, u32[]{:S(2)}) copy-start(bf16[3,656,128]{2,1,0:T(8,128)(2,1)S(1)} %pad_maximum_fusion.given.refs_0_) | copy-start | bytes 1511428
  4.1 26.5 %collective-permute-start.3 = (bf16[3,656,128]{2,1,0:T(8,128)(2,1)S(1)}, bf16[3,656,128]{2,1,0:T(8,128)(2,1)S(1)}, u32[]{:S(2)}, u32[]{:S(2)}) collective-permute-start(bf16[3,656,128]{2,1,0:T(8,128)(2,1)S(1)} %pad_maximum_fusion.given.refs_0_), channel_id=1, source_target_pairs={{0,16},{1,17},{2,18},{3,19},{4,20},{5,21},{6,22},{7,23},{8,24},{9,... | collective-permute-start | bytes 1511432 | tf_op jit(solution)/shard_map/ppermute | solution.py:467
  8.2 22.4 %collective-permute-start.2 = (bf16[3,656,128]{2,1,0:T(8,128)(2,1)S(1)}, bf16[3,656,128]{2,1,0:T(8,128)(2,1)S(1)}, u32[]{:S(2)}, u32[]{:S(2)}) collective-permute-start(bf16[3,656,128]{2,1,0:T(8,128)(2,1)S(1)} %pad_maximum_fusion.given.refs_0_), channel_id=1, source_target_pairs={{0,3},{1,2},{2,1},{3,0},{4,7},{5,6},{6,5},{7,4},{8,11},{9,10},{10,... | collective-permute-start | bytes 1511432 | tf_op jit(solution)/shard_map/ppermute | solution.py:467
  10.6 22.2 %collective-permute-start.1 = (bf16[3,656,128]{2,1,0:T(8,128)(2,1)S(1)}, bf16[3,656,128]{2,1,0:T(8,128)(2,1)S(1)}, u32[]{:S(2)}, u32[]{:S(2)}) collective-permute-start(bf16[3,656,128]{2,1,0:T(8,128)(2,1)S(1)} %pad_maximum_fusion.given.refs_0_), channel_id=1, source_target_pairs={{0,2},{1,3},{2,0},{3,1},{4,6},{5,7},{6,4},{7,5},{8,10},{9,11},{10,... | collective-permute-start | bytes 1511432 | tf_op jit(solution)/shard_map/ppermute | solution.py:467
  11.1 21.9 %collective-permute-start = (bf16[3,656,128]{2,1,0:T(8,128)(2,1)S(1)}, bf16[3,656,128]{2,1,0:T(8,128)(2,1)}, u32[]{:S(2)}, u32[]{:S(2)}) collective-permute-start(bf16[3,656,128]{2,1,0:T(8,128)(2,1)S(1)} %pad_maximum_fusion.given.refs_0_), channel_id=1, source_target_pairs={{0,1},{1,0},{2,3},{3,2},{4,5},{5,4},{6,7},{7,6},{8,9},{9,8},{10,11... | collective-permute-start | bytes 1511432 | tf_op jit(solution)/shard_map/ppermute | solution.py:467
  11.7 35.7 %collective-permute-start.5 = (bf16[2,1,512,512]{3,2,1,0:T(8,128)(2,1)}, bf16[2,1,512,512]{3,2,1,0:T(8,128)(2,1)S(1)}, u32[]{:S(2)}, u32[]{:S(2)}) collective-permute-start(bf16[2,1,512,512]{3,2,1,0:T(8,128)(2,1)} %refs_4_.1), channel_id=1, source_target_pairs={{0,8},{1,9},{2,10},{3,11},{4,12},{5,13},{6,14},{7,15},{8,0},{9,1},... | collective-permute-start | bytes 3145736 | tf_op jit(solution)/shard_map/ppermute | solution.py:467
  30.6 29.9 %copy-start.1 = (bf16[3,656,128]{2,1,0:T(8,128)(2,1)}, bf16[3,656,128]{2,1,0:T(8,128)(2,1)S(1)}, u32[]{:S(2)}) copy-start(bf16[3,656,128]{2,1,0:T(8,128)(2,1)S(1)} %collective-permute-done.3.given.refs_0_.refs_4_) | copy-start | bytes 1511428
  30.6 18.5 %collective-permute-start.8 = (bf16[2,1,512,512]{3,2,1,0:T(8,128)(2,1)}, bf16[2,1,512,512]{3,2,1,0:T(8,128)(2,1)}, u32[]{:S(2)}, u32[]{:S(2)}) collective-permute-start(bf16[2,1,512,512]{3,2,1,0:T(8,128)(2,1)} %refs_4_.1), channel_id=1, source_target_pairs={{0,4},{1,5},{2,6},{3,7},{4,0},{5,1},{6,2},{7,3},{8,12},{9,13},{10,... | collective-permute-start | bytes 3145736 | tf_op jit(solution)/shard_map/ppermute | solution.py:467
  30.6 22.2 %copy-start.7 = (bf16[3,656,128]{2,1,0:T(8,128)(2,1)}, bf16[3,656,128]{2,1,0:T(8,128)(2,1)S(1)}, u32[]{:S(2)}) copy-start(bf16[3,656,128]{2,1,0:T(8,128)(2,1)S(1)} %collective-permute-done.2.refs_3_) | copy-start | bytes 1511428
  32.8 19.5 %copy-start.8 = (bf16[3,656,128]{2,1,0:T(8,128)(2,1)}, bf16[3,656,128]{2,1,0:T(8,128)(2,1)S(1)}, u32[]{:S(2)}) copy-start(bf16[3,656,128]{2,1,0:T(8,128)(2,1)S(1)} %collective-permute-done.1.refs_2_) | copy-start | bytes 1511428
  33.0 14.4 %collective-permute-start.4 = (bf16[3,656,128]{2,1,0:T(8,128)(2,1)S(1)}, bf16[3,656,128]{2,1,0:T(8,128)(2,1)}, u32[]{:S(2)}, u32[]{:S(2)}) collective-permute-start(bf16[3,656,128]{2,1,0:T(8,128)(2,1)S(1)} %collective-permute-done.3.given.refs_0_.refs_4_), channel_id=1, source_target_pairs={{0,3},{1,2},{2,1},{3,0},{4,7},{5,6},{6,5},{7,4},{8,11},{9,10},{10,... | collective-permute-start | bytes 1511432 | tf_op jit(solution)/shard_map/ppermute | solution.py:467
  47.4 5.4 %copy-start.3 = (bf16[2,1,512,512]{3,2,1,0:T(8,128)(2,1)}, bf16[2,1,512,512]{3,2,1,0:T(8,128)(2,1)S(1)}, u32[]{:S(2)}) copy-start(bf16[2,1,512,512]{3,2,1,0:T(8,128)(2,1)S(1)} %collective-permute-done.5.refs_6_) | copy-start | bytes 3145732
  47.4 2.7 %collective-permute-start.9 = (bf16[2,1,512,512]{3,2,1,0:T(8,128)(2,1)S(1)}, bf16[2,1,512,512]{3,2,1,0:T(8,128)(2,1)S(1)}, u32[]{:S(2)}, u32[]{:S(2)}) collective-permute-start(bf16[2,1,512,512]{3,2,1,0:T(8,128)(2,1)S(1)} %collective-permute-done.5.refs_6_), channel_id=1, source_target_pairs={{0,4},{1,5},{2,6},{3,7},{4,0},{5,1},{6,2},{7,3},{8,12},{9,13},{10,... | collective-permute-start | bytes 3145736 | tf_op jit(solution)/shard_map/ppermute | solution.py:467
  47.4 14.0 %collective-permute-start.7 = (bf16[3,656,128]{2,1,0:T(8,128)(2,1)S(1)}, bf16[3,656,128]{2,1,0:T(8,128)(2,1)}, u32[]{:S(2)}, u32[]{:S(2)}) collective-permute-start(bf16[3,656,128]{2,1,0:T(8,128)(2,1)S(1)} %collective-permute-done.3.given.refs_0_.refs_4_), channel_id=1, source_target_pairs={{0,2},{1,3},{2,0},{3,1},{4,6},{5,7},{6,4},{7,5},{8,10},{9,11},{10,... | collective-permute-start | bytes 1511432 | tf_op jit(solution)/shard_map/ppermute | solution.py:467
  48.9 13.7 %collective-permute-start.6 = (bf16[3,656,128]{2,1,0:T(8,128)(2,1)S(1)}, bf16[3,656,128]{2,1,0:T(8,128)(2,1)}, u32[]{:S(2)}, u32[]{:S(2)}) collective-permute-start(bf16[3,656,128]{2,1,0:T(8,128)(2,1)S(1)} %collective-permute-done.3.given.refs_0_.refs_4_), channel_id=1, source_target_pairs={{0,1},{1,0},{2,3},{3,2},{4,5},{5,4},{6,7},{7,6},{8,9},{9,8},{10,11... | collective-permute-start | bytes 1511432 | tf_op jit(solution)/shard_map/ppermute | solution.py:467
  50.1 2.2 %copy-start.4 = (bf16[2,1,512,512]{3,2,1,0:T(8,128)(2,1)}, bf16[2,1,512,512]{3,2,1,0:T(8,128)(2,1)S(1)}, u32[]{:S(2)}) copy-start(bf16[2,1,512,512]{3,2,1,0:T(8,128)(2,1)S(1)} %collective-permute-done.9.refs_7_) | copy-start | bytes 3145732
  50.1 20.1 %collective-permute-start.11 = (bf16[3,128,512]{2,1,0:T(8,128)(2,1)S(1)}, bf16[3,128,512]{2,1,0:T(8,128)(2,1)}, u32[]{:S(2)}, u32[]{:S(2)}) collective-permute-start(bf16[3,128,512]{2,1,0:T(8,128)(2,1)S(1)} %shard_map.95.own), channel_id=1, source_target_pairs={{0,24},{1,25},{2,26},{3,27},{4,28},{5,29},{6,30},{7,31},{8,16},{9,... | collective-permute-start | bytes 1179656 | tf_op jit(solution)/shard_map/ppermute | solution.py:467
  52.3 19.2 %collective-permute-start.10 = (bf16[3,128,512]{2,1,0:T(8,128)(2,1)S(1)}, bf16[3,128,512]{2,1,0:T(8,128)(2,1)}, u32[]{:S(2)}, u32[]{:S(2)}) collective-permute-start(bf16[3,128,512]{2,1,0:T(8,128)(2,1)S(1)} %shard_map.95.own), channel_id=1, source_target_pairs={{0,8},{1,9},{2,10},{3,11},{4,12},{5,13},{6,14},{7,15},{8,0},{9,1},... | collective-permute-start | bytes 1179656 | tf_op jit(solution)/shard_map/ppermute | solution.py:467
  52.8 18.6 %copy-start.2 = (bf16[6,128,512]{2,1,0:T(8,128)(2,1)}, bf16[6,128,512]{2,1,0:T(8,128)(2,1)S(1)}, u32[]{:S(2)}) copy-start(bf16[6,128,512]{2,1,0:T(8,128)(2,1)S(1)} %shard_map.97.refs_8_) | copy-start | bytes 2359300
  71.4 3.6 %collective-permute-start.12 = (bf16[6,128,512]{2,1,0:T(8,128)(2,1)S(1)}, bf16[6,128,512]{2,1,0:T(8,128)(2,1)S(1)}, u32[]{:S(2)}, u32[]{:S(2)}) collective-permute-start(bf16[6,128,512]{2,1,0:T(8,128)(2,1)S(1)} %shard_map.97.refs_8_), channel_id=1, source_target_pairs={{0,4},{1,5},{2,6},{3,7},{4,0},{5,1},{6,2},{7,3},{8,12},{9,13},{10,... | collective-permute-start | bytes 2359304 | tf_op jit(solution)/shard_map/ppermute | solution.py:467
  71.5 2.7 %collective-permute-start.13 = (bf16[3,128,512]{2,1,0:T(8,128)(2,1)}, bf16[3,128,512]{2,1,0:T(8,128)(2,1)S(1)}, u32[]{:S(2)}, u32[]{:S(2)}) collective-permute-start(bf16[3,128,512]{2,1,0:T(8,128)(2,1)} %collective-permute-done.10.refs_9_), channel_id=1, source_target_pairs={{0,4},{1,5},{2,6},{3,7},{4,0},{5,1},{6,2},{7,3},{8,12},{9,13},{10,... | collective-permute-start | bytes 1179656 | tf_op jit(solution)/shard_map/ppermute | solution.py:467
  72.0 3.1 %collective-permute-start.14 = (bf16[3,128,512]{2,1,0:T(8,128)(2,1)}, bf16[3,128,512]{2,1,0:T(8,128)(2,1)S(1)}, u32[]{:S(2)}, u32[]{:S(2)}) collective-permute-start(bf16[3,128,512]{2,1,0:T(8,128)(2,1)} %collective-permute-done.11.refs_10_), channel_id=1, source_target_pairs={{0,4},{1,5},{2,6},{3,7},{4,0},{5,1},{6,2},{7,3},{8,12},{9,13},{10,... | collective-permute-start | bytes 1179656 | tf_op jit(solution)/shard_map/ppermute | solution.py:467
  74.1 0.9 copy-start.14
  75.1 0.8 copy-start.15
  75.9 0.9 copy-start.13
  91.7 4.7 %copy-start.5 = (f32[384,128]{1,0:T(8,128)S(1)}, f32[384,128]{1,0:T(8,128)}, u32[]{:S(2)}) copy-start(f32[384,128]{1,0:T(8,128)} %param.8) | copy-start | bytes 589828
  91.7 4.7 %copy-start.12 = (f32[384]{0:T(512)S(1)}, f32[384]{0:T(512)}, u32[]{:S(2)}) copy-start(f32[384]{0:T(512)} %param.9) | copy-start | bytes 4612
  91.7 2.6 %collective-permute-start.15 = (f32[12,128,128]{2,1,0:T(8,128)}, f32[12,128,128]{2,1,0:T(8,128)S(1)}, u32[]{:S(2)}, u32[]{:S(2)}) collective-permute-start(f32[12,128,128]{2,1,0:T(8,128)} %get-tuple-element.68), channel_id=1, source_target_pairs={{0,4},{1,5},{2,6},{3,7},{4,0},{5,1},{6,2},{7,3},{8,12},{9,13},{10,... | collective-permute-start | bytes 2359304 | tf_op jit(solution)/shard_map/ppermute | solution.py:467
  95.6 7.0 %collective-permute-start.16 = (bf16[2,3,128,128]{3,2,1,0:T(8,128)(2,1)S(1)}, bf16[2,3,128,128]{3,2,1,0:T(8,128)(2,1)S(1)}, u32[]{:S(2)}, u32[]{:S(2)}) collective-permute-start(bf16[2,3,128,128]{3,2,1,0:T(8,128)(2,1)S(1)} %pad_maximum_fusion.1), channel_id=1, source_target_pairs={{0,8},{1,9},{2,10},{3,11},{4,12},{5,13},{6,14},{7,15},{8,0},{9,1},... | collective-permute-start | bytes 589832 | tf_op jit(solution)/shard_map/ppermute | solution.py:467
  102.6 11.3 %collective-permute-start.17 = (bf16[2,3,128,128]{3,2,1,0:T(8,128)(2,1)S(1)}, bf16[2,3,128,128]{3,2,1,0:T(8,128)(2,1)S(1)}, u32[]{:S(2)}, u32[]{:S(2)}) collective-permute-start(bf16[2,3,128,128]{3,2,1,0:T(8,128)(2,1)S(1)} %fusion), channel_id=1, source_target_pairs={{0,16},{1,17},{2,18},{3,19},{4,20},{5,21},{6,22},{7,23},{8,24},{9,... | collective-permute-start | bytes 589832 | tf_op jit(solution)/shard_map/ppermute | solution.py:467
  114.0 14.7 %copy-start.6 = (bf16[2,3,128,128]{3,2,1,0:T(8,128)(2,1)}, bf16[2,3,128,128]{3,2,1,0:T(8,128)(2,1)S(1)}, u32[]{:S(2)}) copy-start(bf16[2,3,128,128]{3,2,1,0:T(8,128)(2,1)S(1)} %get-tuple-element.74.refs_0_) | copy-start | bytes 589828
  114.0 8.3 %collective-permute-start.20 = (bf16[2,3,128,128]{3,2,1,0:T(8,128)(2,1)S(1)}, bf16[2,3,128,128]{3,2,1,0:T(8,128)(2,1)S(1)}, u32[]{:S(2)}, u32[]{:S(2)}) collective-permute-start(bf16[2,3,128,128]{3,2,1,0:T(8,128)(2,1)S(1)} %get-tuple-element.74.refs_0_), channel_id=1, source_target_pairs={{0,3},{1,2},{2,1},{3,0},{4,7},{5,6},{6,5},{7,4},{8,11},{9,10},{10,... | collective-permute-start | bytes 589832 | tf_op jit(solution)/shard_map/ppermute | solution.py:467
  117.7 10.0 %collective-permute-start.19 = (bf16[2,3,128,128]{3,2,1,0:T(8,128)(2,1)S(1)}, bf16[2,3,128,128]{3,2,1,0:T(8,128)(2,1)S(1)}, u32[]{:S(2)}, u32[]{:S(2)}) collective-permute-start(bf16[2,3,128,128]{3,2,1,0:T(8,128)(2,1)S(1)} %get-tuple-element.74.refs_0_), channel_id=1, source_target_pairs={{0,2},{1,3},{2,0},{3,1},{4,6},{5,7},{6,4},{7,5},{8,10},{9,11},{10,... | collective-permute-start | bytes 589832 | tf_op jit(solution)/shard_map/ppermute | solution.py:467
  120.0 8.7 %collective-permute-start.18 = (bf16[2,3,128,128]{3,2,1,0:T(8,128)(2,1)S(1)}, bf16[2,3,128,128]{3,2,1,0:T(8,128)(2,1)S(1)}, u32[]{:S(2)}, u32[]{:S(2)}) collective-permute-start(bf16[2,3,128,128]{3,2,1,0:T(8,128)(2,1)S(1)} %get-tuple-element.74.refs_0_), channel_id=1, source_target_pairs={{0,1},{1,0},{2,3},{3,2},{4,5},{5,4},{6,7},{7,6},{8,9},{9,8},{10,11... | collective-permute-start | bytes 589832 | tf_op jit(solution)/shard_map/ppermute | solution.py:467
  122.4 6.4 %copy-start.9 = (bf16[2,3,128,128]{3,2,1,0:T(8,128)(2,1)}, bf16[2,3,128,128]{3,2,1,0:T(8,128)(2,1)S(1)}, u32[]{:S(2)}) copy-start(bf16[2,3,128,128]{3,2,1,0:T(8,128)(2,1)S(1)} %collective-permute-done.20.refs_3_) | copy-start | bytes 589828
  127.7 1.1 copy-start.10
  128.7 0.7 copy-start.11
  136.6 2.6 %collective-permute-start.21 = (f32[12,128,128]{2,1,0:T(8,128)}, f32[12,128,128]{2,1,0:T(8,128)S(1)}, u32[]{:S(2)}, u32[]{:S(2)}) collective-permute-start(f32[12,128,128]{2,1,0:T(8,128)} %get-tuple-element.71), channel_id=1, source_target_pairs={{0,4},{1,5},{2,6},{3,7},{4,0},{5,1},{6,2},{7,3},{8,12},{9,13},{10,... | collective-permute-start | bytes 2359304 | tf_op jit(solution)/shard_map/ppermute | solution.py:467
  140.4 6.3 %collective-permute-start.22 = (bf16[3,128,128]{2,1,0:T(8,128)(2,1)S(1)}, bf16[3,128,128]{2,1,0:T(8,128)(2,1)S(1)}, u32[]{:S(2)}, u32[]{:S(2)}) collective-permute-start(bf16[3,128,128]{2,1,0:T(8,128)(2,1)S(1)} %get-tuple-element.80), channel_id=1, source_target_pairs={{0,8},{1,9},{2,10},{3,11},{4,12},{5,13},{6,14},{7,15},{8,0},{9,1},... | collective-permute-start | bytes 294920 | tf_op jit(solution)/shard_map/ppermute | solution.py:467
  140.5 7.6 %collective-permute-start.24 = (bf16[3,128,128]{2,1,0:T(8,128)(2,1)S(1)}, bf16[3,128,128]{2,1,0:T(8,128)(2,1)S(1)}, u32[]{:S(2)}, u32[]{:S(2)}) collective-permute-start(bf16[3,128,128]{2,1,0:T(8,128)(2,1)S(1)} %get-tuple-element.81), channel_id=1, source_target_pairs={{0,24},{1,25},{2,26},{3,27},{4,28},{5,29},{6,30},{7,31},{8,16},{9,... | collective-permute-start | bytes 294920 | tf_op jit(solution)/shard_map/ppermute | solution.py:467
  140.6 12.2 %collective-permute-start.23 = (bf16[3,128,128]{2,1,0:T(8,128)(2,1)S(1)}, bf16[3,128,128]{2,1,0:T(8,128)(2,1)S(1)}, u32[]{:S(2)}, u32[]{:S(2)}) collective-permute-start(bf16[3,128,128]{2,1,0:T(8,128)(2,1)S(1)} %get-tuple-element.82), channel_id=1, source_target_pairs={{0,16},{1,17},{2,18},{3,19},{4,20},{5,21},{6,22},{7,23},{8,24},{9,... | collective-permute-start | bytes 294920 | tf_op jit(solution)/shard_map/ppermute | solution.py:467

commit v9 on v7

--- a/solution.py
+++ b/solution.py
@@ -263,7 +263,7 @@
     given_out = [refs.pop(0) for _ in range(2 * (1 + len(lines)))]
     given_projected = [refs.pop(0) for _ in range(lay.owners)]
     own_sum, other_sum, tiles_out = refs[:3]
-    left, projected, rounded, tiles, total, sems, sum_sems, in_sems, out_sems = refs[3:]
+    left, projected, rounded, tiles, total, sent, sems, sum_sems, in_sems, out_sems = refs[3:]
     copies = []
 
     def fetch(source, target):
@@ -336,7 +336,7 @@
             store(chunk).start()
 
     add_products(lay, used - 1, group_input, entries, tiles, rounded, total)
-    give_sums(lay, total, own_sum, other_sum, sum_sems)
+    give_sums(lay, total, sent, own_sum, other_sum, sum_sems)
     for chunk in range(lay.groups // chunk_groups):
 
         @pl.when(used > chunk * chunk_groups)
@@ -344,15 +344,15 @@
             store(chunk).wait()
 
 
-def give_sums(lay, total, own_sum, other_sum, sems):
+def give_sums(lay, total, sent, own_sum, other_sum, sems):
     own = lay.places * lay.blocks
-    for copy in (
-        pltpu.make_async_copy(total.at[pl.ds(own, own)], other_sum, sems.at[1]),
-        pltpu.make_async_copy(total.at[pl.ds(0, own)], own_sum, sems.at[0]),
-    ):
-        copy.start()
-    pltpu.make_async_copy(total.at[pl.ds(own, own)], other_sum, sems.at[1]).wait()
-    pltpu.make_async_copy(total.at[pl.ds(0, own)], own_sum, sems.at[0]).wait()
+    for_own = pltpu.make_async_copy(total.at[pl.ds(0, own)], own_sum, sems.at[0])
+    for_own.start()
+    sent[...] = total[own : 2 * own].astype(jnp.bfloat16)
+    for_other = pltpu.make_async_copy(sent, other_sum, sems.at[1])
+    for_other.start()
+    for_own.wait()
+    for_other.wait()
 
 
 def make_tiles(lay, plan, inputs, outputs, projected):
@@ -360,10 +360,11 @@
     hbm = pl.BlockSpec(memory_space=pl.ANY)
     own = lay.places * lay.blocks
     sums = jax.ShapeDtypeStruct((own, lay.side, lay.width), jnp.float32)
+    sent = jax.ShapeDtypeStruct((own, lay.side, lay.width), jnp.bfloat16)
     tiles = (lay.groups * lay.unroll, lay.side, lay.side)
     return pl.pallas_call(
         functools.partial(tiles_kernel, lay),
-        out_shape=(sums, sums, jax.ShapeDtypeStruct(tiles, jnp.bfloat16)),
+        out_shape=(sums, sent, jax.ShapeDtypeStruct(tiles, jnp.bfloat16)),
         in_specs=[smem] * 4 + [hbm] * (len(inputs) + len(outputs) + len(projected)),
         out_specs=(hbm,) * 3,
         scratch_shapes=[
@@ -372,6 +373,7 @@
             pltpu.VMEM((lay.inputs, lay.side, lay.width), jnp.bfloat16),
             pltpu.VMEM(tiles, jnp.bfloat16),
             pltpu.VMEM((lay.outputs + 1, lay.side, lay.width), jnp.float32),
+            pltpu.VMEM((own, lay.side, lay.width), jnp.bfloat16),
             pltpu.SemaphoreType.DMA((len(inputs) + 2 * lay.places,)),
             pltpu.SemaphoreType.DMA((2,)),
             pltpu.SemaphoreType.DMA((lay.inputs,)),
@@ -385,7 +387,7 @@
 def apply_kernel(lay, sizes, group_input, entries, tiles_in, *refs):
     given_vec = refs[: lay.cols]
     own_sum, other_sum = refs[lay.cols : lay.cols + 2]
-    rounded, tiles, total, sems, sum_sems, out_sems = refs[lay.cols + 2 :]
+    rounded, tiles, total, sent, sems, sum_sems, out_sems = refs[lay.cols + 2 :]
     used = sizes[0]
     span = chunk_groups * lay.unroll
 
@@ -419,7 +421,7 @@
         return carry
 
     lax.fori_loop(1, used, group_step, 0)
-    give_sums(lay, total, own_sum, other_sum, sum_sems)
+    give_sums(lay, total, sent, own_sum, other_sum, sum_sems)
 
 
 def apply_tiles(lay, plan, tiles, rounded):
@@ -427,15 +429,17 @@
     hbm = pl.BlockSpec(memory_space=pl.ANY)
     own = lay.places * lay.blocks
     sums = jax.ShapeDtypeStruct((own, lay.side, lay.width), jnp.float32)
+    sent = jax.ShapeDtypeStruct((own, lay.side, lay.width), jnp.bfloat16)
     return pl.pallas_call(
         functools.partial(apply_kernel, lay),
-        out_shape=(sums, sums),
+        out_shape=(sums, sent),
         in_specs=[smem] * 3 + [hbm] * (1 + len(rounded)),
         out_specs=(hbm, hbm),
         scratch_shapes=[
             pltpu.VMEM((lay.inputs, lay.side, lay.width), jnp.bfloat16),
             pltpu.VMEM(tiles.shape, jnp.bfloat16),
             pltpu.VMEM((lay.outputs + 1, lay.side, lay.width), jnp.float32),
+            pltpu.VMEM((own, lay.side, lay.width), jnp.bfloat16),
             pltpu.SemaphoreType.DMA((len(rounded) * lay.owners,)),
             pltpu.SemaphoreType.DMA((2,)),
             pltpu.SemaphoreType.DMA((lay.groups // chunk_groups,)),
@@ -486,10 +490,11 @@
     digits = jnp.pad(digits, (0, blocks * depth * width - 2 * n_listed)).reshape(blocks, depth, width)
     joined = jnp.concatenate([intersections, start.astype(jnp.bfloat16), digits], axis=1)
 
+    inputs = in_plane(joined)
+    partner = [along(joined, near)] if two_owners else []
     near_coarse = [along(coarse, e) for e in range(1, near)]
-    partner = [along(joined, near)] if two_owners else []
-    inputs = in_plane(joined)
-    inputs, partner, late_joined = lax.optimization_barrier((inputs, partner, joined))
+    held = (partner, inputs, near_coarse, joined)
+    partner, inputs, near_coarse, late_joined = lax.optimization_barrier(held)
     if two_owners:
         sent = partner[0][:, pairs + side :].reshape(-1)[: 2 * n_listed].astype(jnp.int32)
         listed = jnp.concatenate([listed, ((sent[:n_listed] << 8) + sent[n_listed:])[None]], axis=0)
@@ -497,7 +502,6 @@
     for part in partner:
         inputs = inputs + in_plane(part)
     turned = turn_own(lay, late_joined)
-    turned, near_coarse, plan = lax.optimization_barrier((turned, near_coarse, plan))
     blocks_coarse = []
     for part in [coarse] + near_coarse:
         blocks_coarse += [part, to_core(part)]
@@ -514,7 +518,7 @@
     own_sum, other_sum, tiles = make_tiles(lay, plan, inputs, lefts, projected)
 
     def over_core(own_part, other_part):
-        return (own_part + to_core(other_part)).reshape(lay.places, blocks, side, width)
+        return (own_part + to_core(other_part).astype(jnp.float32)).reshape(lay.places, blocks, side, width)
 
     def shifted_part(field):
         return energy * field - spectrum_center * field

time: 163 us -> 154 us (0.945)
  waiting for transfers between devices: 78.3 us -> 67.9 us
  Pallas kernels: 36.7 us -> 39.2 us
    ppermute x25, waiting for transfers between devices: 78.3 us -> 67.9 us  [move(): return lax.ppermute(array, axes, pairs_list)]
  transfers between devices with their start and end apart: 25 -> 25, of which waited for: 18 -> 18; matrix products, arithmetic and copies ran while one was open for 2% -> 4% of each run, Pallas kernels for 12% -> 13%
where the time goes in v9:
time: 154 us; the launch traced here: 155 us
  waiting for transfers between devices  67.9 us (44%)
  Pallas kernels  39.2 us (25%)
  starting transfers between devices  35.5 us (23%)
  other arithmetic  8.44 us (5%)
  local copies, waits for them, and re-layouts  2.59 us (2%)
  between operations  1.59 us (1%)
    ppermute x25, waiting for transfers between devices, move(): return lax.ppermute(array, axes, pairs_list)  67.9 us
    ppermute x25, starting transfers between devices, move(): return lax.ppermute(array, axes, pairs_list)  35.5 us
    pallas_call x2, Pallas kernels, project(): pl.pallas_call(functools.partial(project_kernel, lay, owner), out_shape=j...  14.4 us
    pallas_call x1, Pallas kernels, make_tiles(): pl.pallas_call(functools.partial(tiles_kernel, lay), out_shape=(sums, sen...  12.4 us
    pallas_call x1, Pallas kernels, make_plan(): pl.pallas_call(functools.partial(plan_kernel, lay), out_shape=tuple((jax....  6.21 us
    pallas_call x1, Pallas kernels, apply_tiles(): pl.pallas_call(functools.partial(apply_kernel, lay), out_shape=(sums, sen...  5.92 us
  transfers between devices with their start and end apart: 25, of which 18 were waited for; matrix products, arithmetic and copies ran while one was open for 4% of the time, Pallas kernels for 13%

profile of v9, /device:TPU:0, one launch (start us, length us, event | category | flops | bytes accessed | tf_op | source)
XLA Modules:
  0.0 155.3 jit_solution(13893033319053137925)
XLA Ops:
  0.6 3.1 %collective-permute-start.4 = (bf16[2,1,512,512]{3,2,1,0:T(8,128)(2,1)}, bf16[2,1,512,512]{3,2,1,0:T(8,128)(2,1)S(1)}, u32[]{:S(2)}, u32[]{:S(2)}) collective-permute-start(bf16[2,1,512,512]{3,2,1,0:T(8,128)(2,1)} %refs_4_.1), channel_id=1, source_target_pairs={{0,8},{1,9},{2,10},{3,11},{4,12},{5,13},{6,14},{7,15},{8,0},{9,1},... | collective-permute-start | bytes 3145736 | tf_op jit(solution)/shard_map/ppermute | solution.py:471
  4.4 0.9 convert_element_type.40
  5.3 0.7 convert_bitcast_fusion.1
  6.1 1.0 pad_maximum_fusion.given.refs_0_
  7.2 2.5 %collective-permute-start.3 = (bf16[3,656,128]{2,1,0:T(8,128)(2,1)S(1)}, bf16[3,656,128]{2,1,0:T(8,128)(2,1)S(1)}, u32[]{:S(2)}, u32[]{:S(2)}) collective-permute-start(bf16[3,656,128]{2,1,0:T(8,128)(2,1)S(1)} %pad_maximum_fusion.given.refs_0_), channel_id=1, source_target_pairs={{0,3},{1,2},{2,1},{3,0},{4,7},{5,6},{6,5},{7,4},{8,11},{9,10},{10,... | collective-permute-start | bytes 1511432 | tf_op jit(solution)/shard_map/ppermute | solution.py:471
  9.7 0.5 collective-permute-start.2
  10.2 0.5 collective-permute-start.1
  10.7 2.6 %collective-permute-start = (bf16[3,656,128]{2,1,0:T(8,128)(2,1)S(1)}, bf16[3,656,128]{2,1,0:T(8,128)(2,1)S(1)}, u32[]{:S(2)}, u32[]{:S(2)}) collective-permute-start(bf16[3,656,128]{2,1,0:T(8,128)(2,1)S(1)} %pad_maximum_fusion.given.refs_0_), channel_id=1, source_target_pairs={{0,16},{1,17},{2,18},{3,19},{4,20},{5,21},{6,22},{7,23},{8,24},{9,... | collective-permute-start | bytes 1511432 | tf_op jit(solution)/shard_map/ppermute | solution.py:471
  13.3 9.3 %collective-permute-done.3.refs_3_ = bf16[3,656,128]{2,1,0:T(8,128)(2,1)S(1)} collective-permute-done((bf16[3,656,128]{2,1,0:T(8,128)(2,1)S(1)}, bf16[3,656,128]{2,1,0:T(8,128)(2,1)S(1)}, u32[]{:S(2)}, u32[]{:S(2)}) %collective-permute-start.3) | collective-permute-done | bytes 503840 | tf_op jit(solution)/shard_map/ppermute | solution.py:471
  22.6 9.3 %collective-permute-done.2.refs_2_ = bf16[3,656,128]{2,1,0:T(8,128)(2,1)S(1)} collective-permute-done((bf16[3,656,128]{2,1,0:T(8,128)(2,1)S(1)}, bf16[3,656,128]{2,1,0:T(8,128)(2,1)S(1)}, u32[]{:S(2)}, u32[]{:S(2)}) %collective-permute-start.2) | collective-permute-done | bytes 503840 | tf_op jit(solution)/shard_map/ppermute | solution.py:471
  32.0 5.2 %collective-permute-done.given.refs_0_.refs_4_ = bf16[3,656,128]{2,1,0:T(8,128)(2,1)S(1)} collective-permute-done((bf16[3,656,128]{2,1,0:T(8,128)(2,1)S(1)}, bf16[3,656,128]{2,1,0:T(8,128)(2,1)S(1)}, u32[]{:S(2)}, u32[]{:S(2)}) %collective-permute-start) | collective-permute-done | bytes 503840 | tf_op jit(solution)/shard_map/ppermute | solution.py:471
  37.1 0.7 collective-permute-done.4.refs_6_
  37.9 0.7 pad_add_fusion.1.ids
  38.6 2.6 %collective-permute-start.7 = (bf16[3,656,128]{2,1,0:T(8,128)(2,1)S(1)}, bf16[3,656,128]{2,1,0:T(8,128)(2,1)}, u32[]{:S(2)}, u32[]{:S(2)}) collective-permute-start(bf16[3,656,128]{2,1,0:T(8,128)(2,1)S(1)} %collective-permute-done.given.refs_0_.refs_4_), channel_id=1, source_target_pairs={{0,3},{1,2},{2,1},{3,0},{4,7},{5,6},{6,5},{7,4},{8,11},{9,10},{10,... | collective-permute-start | bytes 1511432 | tf_op jit(solution)/shard_map/ppermute | solution.py:471
  41.2 0.5 collective-permute-start.6
  41.7 0.4 collective-permute-start.5
  42.3 3.8 %collective-permute-start.11 = (bf16[3,128,512]{2,1,0:T(8,128)(2,1)S(1)}, bf16[3,128,512]{2,1,0:T(8,128)(2,1)}, u32[]{:S(2)}, u32[]{:S(2)}) collective-permute-start(bf16[3,128,512]{2,1,0:T(8,128)(2,1)S(1)} %shard_map.96.own), channel_id=1, source_target_pairs={{0,24},{1,25},{2,26},{3,27},{4,28},{5,29},{6,30},{7,31},{8,16},{9,... | collective-permute-start | bytes 1179656 | tf_op jit(solution)/shard_map/ppermute | solution.py:471
  46.2 1.3 pad_add_fusion.listed
  47.5 6.2 %shard_map.95 = (s32[24]{0:T(128)}, s32[26]{0:T(128)}, s32[4]{0:T(128)}, s32[72]{0:T(128)}, s32[288]{0:T(512)}) custom-call(s32[3]{0:T(128)} %pad_add_fusion.1.ids, s32[2,97]{1,0:T(2,128)} %pad_add_fusion.listed, s32[96]{0:T(128)} %fine.1, s32[8]{0:T(128)} %stored.1), custom_call_target="tpu_custom_call" | custom-call | bytes 20000000 | tf_op jit(solution)/shard_map/pallas_call | solution.py:137
  53.9 6.8 %shard_map.98.refs_14_ = bf16[12,512,256]{2,1,0:T(8,128)(2,1)} custom-call(s32[24]{0:T(128)} %get-tuple-element.30.slot_of, s32[26]{0:T(128)} %get-tuple-element.41.valid, s32[4]{0:T(128)} %get-tuple-element.31.sizes, bf16[3,656,128]{2,1,0:T(8,128)(2,1)} %copy-done, bf16[3,656,128]{2,1,0:T(8,128)(2,1)} %copy-done.8, bf16[3,656,128]{2,1,0:T(8,128)(2,1)} %copy-done.7, ...), custom_call_target="tpu_custom_call" | custom-call | flops 1000000000 | bytes 16000000 | tf_op jit(solution)/shard_map/pallas_call | solution.py:242
  60.7 3.5 %collective-permute-done.6.refs_2_.refs_6_ = bf16[3,656,128]{2,1,0:T(8,128)(2,1)} collective-permute-done((bf16[3,656,128]{2,1,0:T(8,128)(2,1)S(1)}, bf16[3,656,128]{2,1,0:T(8,128)(2,1)}, u32[]{:S(2)}, u32[]{:S(2)}) %collective-permute-start.6) | collective-permute-done | bytes 503840 | tf_op jit(solution)/shard_map/ppermute | solution.py:471
  64.5 7.6 %shard_map.99.refs_15_ = bf16[12,512,256]{2,1,0:T(8,128)(2,1)} custom-call(s32[24]{0:T(128)} %get-tuple-element.30.slot_of, s32[26]{0:T(128)} %get-tuple-element.41.valid, s32[4]{0:T(128)} %get-tuple-element.31.sizes, bf16[3,656,128]{2,1,0:T(8,128)(2,1)} %copy-done.1, bf16[3,656,128]{2,1,0:T(8,128)(2,1)} %collective-permute-done.5.refs_1_.refs_5_, ...), custom_call_target="tpu_custom_call" | custom-call | flops 1000000000 | bytes 16000000 | tf_op jit(solution)/shard_map/pallas_call | solution.py:242
  72.2 0.5 collective-permute-start.13
  72.8 2.5 %collective-permute-done.13.refs_12_ = bf16[3,128,512]{2,1,0:T(8,128)(2,1)S(1)} collective-permute-done((bf16[3,128,512]{2,1,0:T(8,128)(2,1)}, bf16[3,128,512]{2,1,0:T(8,128)(2,1)S(1)}, u32[]{:S(2)}, u32[]{:S(2)}) %collective-permute-start.13) | collective-permute-done | bytes 393248 | tf_op jit(solution)/shard_map/ppermute | solution.py:471
  75.2 0.6 collective-permute-done.14.refs_13_
  76.0 0.6 copy-done.15
  76.9 12.4 %shard_map.100 = (f32[12,128,128]{2,1,0:T(8,128)}, bf16[12,128,128]{2,1,0:T(8,128)(2,1)}, bf16[288,128,128]{2,1,0:T(8,128)(2,1)}) custom-call(s32[24]{0:T(128)} %get-tuple-element.30.slot_of, s32[4]{0:T(128)} %get-tuple-element.31.sizes, s32[72]{0:T(128)} %get-tuple-element.32.group_input, s32[288]{0:T(512)} %get-tuple-element.33.entries, ...), custom_call_target="tpu_custom_call" | custom-call | flops 4000000000 | bytes 30000000 | tf_op jit(solution)/shard_map/pallas_call | solution.py:365
  89.3 2.7 %collective-permute-start.15 = (bf16[12,128,128]{2,1,0:T(8,128)(2,1)}, bf16[12,128,128]{2,1,0:T(8,128)(2,1)S(1)}, u32[]{:S(2)}, u32[]{:S(2)}) collective-permute-start(bf16[12,128,128]{2,1,0:T(8,128)(2,1)} %get-tuple-element.52), channel_id=1, source_target_pairs={{0,4},{1,5},{2,6},{3,7},{4,0},{5,1},{6,2},{7,3},{8,12},{9,13},{10,... | collective-permute-start | bytes 1179656 | tf_op jit(solution)/shard_map/ppermute | solution.py:471
  92.0 1.6 %collective-permute-done.15 = bf16[12,128,128]{2,1,0:T(8,128)(2,1)S(1)} collective-permute-done((bf16[12,128,128]{2,1,0:T(8,128)(2,1)}, bf16[12,128,128]{2,1,0:T(8,128)(2,1)S(1)}, u32[]{:S(2)}, u32[]{:S(2)}) %collective-permute-start.15) | collective-permute-done | bytes 393248 | tf_op jit(solution)/shard_map/ppermute | solution.py:471
  93.6 1.3 fusion.13
  94.9 4.6 %collective-permute-start.16 = (bf16[2,3,128,128]{3,2,1,0:T(8,128)(2,1)S(1)}, bf16[2,3,128,128]{3,2,1,0:T(8,128)(2,1)S(1)}, u32[]{:S(2)}, u32[]{:S(2)}) collective-permute-start(bf16[2,3,128,128]{3,2,1,0:T(8,128)(2,1)S(1)} %pad_maximum_fusion.1), channel_id=1, source_target_pairs={{0,8},{1,9},{2,10},{3,11},{4,12},{5,13},{6,14},{7,15},{8,0},{9,1},... | collective-permute-start | bytes 589832 | tf_op jit(solution)/shard_map/ppermute | solution.py:471
  99.6 5.1 %collective-permute-done.16 = bf16[2,3,128,128]{3,2,1,0:T(8,128)(2,1)S(1)} collective-permute-done((bf16[2,3,128,128]{3,2,1,0:T(8,128)(2,1)S(1)}, bf16[2,3,128,128]{3,2,1,0:T(8,128)(2,1)S(1)}, u32[]{:S(2)}, u32[]{:S(2)}) %collective-permute-start.16) | collective-permute-done | bytes 196640 | tf_op jit(solution)/shard_map/ppermute | solution.py:471
  105.0 11.3 %collective-permute-done.17 = bf16[2,3,128,128]{3,2,1,0:T(8,128)(2,1)S(1)} collective-permute-done((bf16[2,3,128,128]{3,2,1,0:T(8,128)(2,1)S(1)}, bf16[2,3,128,128]{3,2,1,0:T(8,128)(2,1)S(1)}, u32[]{:S(2)}, u32[]{:S(2)}) %collective-permute-start.17) | collective-permute-done | bytes 196640 | tf_op jit(solution)/shard_map/ppermute | solution.py:471
  116.5 5.4 %collective-permute-start.20 = (bf16[2,3,128,128]{3,2,1,0:T(8,128)(2,1)S(1)}, bf16[2,3,128,128]{3,2,1,0:T(8,128)(2,1)S(1)}, u32[]{:S(2)}, u32[]{:S(2)}) collective-permute-start(bf16[2,3,128,128]{3,2,1,0:T(8,128)(2,1)S(1)} %get-tuple-element.58.refs_0_), channel_id=1, source_target_pairs={{0,3},{1,2},{2,1},{3,0},{4,7},{5,6},{6,5},{7,4},{8,11},{9,10},{10,... | collective-permute-start | bytes 589832 | tf_op jit(solution)/shard_map/ppermute | solution.py:471
  121.8 0.6 collective-permute-start.18
  122.5 5.1 %collective-permute-done.20.refs_3_ = bf16[2,3,128,128]{3,2,1,0:T(8,128)(2,1)S(1)} collective-permute-done((bf16[2,3,128,128]{3,2,1,0:T(8,128)(2,1)S(1)}, bf16[2,3,128,128]{3,2,1,0:T(8,128)(2,1)S(1)}, u32[]{:S(2)}, u32[]{:S(2)}) %collective-permute-start.20) | collective-permute-done | bytes 196640 | tf_op jit(solution)/shard_map/ppermute | solution.py:471
  127.6 3.5 %collective-permute-done.19.refs_2_ = bf16[2,3,128,128]{3,2,1,0:T(8,128)(2,1)S(1)} collective-permute-done((bf16[2,3,128,128]{3,2,1,0:T(8,128)(2,1)S(1)}, bf16[2,3,128,128]{3,2,1,0:T(8,128)(2,1)S(1)}, u32[]{:S(2)}, u32[]{:S(2)}) %collective-permute-start.19) | collective-permute-done | bytes 196640 | tf_op jit(solution)/shard_map/ppermute | solution.py:471
  131.2 0.6 copy-done.10
  131.9 5.9 %shard_map.101 = (f32[12,128,128]{2,1,0:T(8,128)}, bf16[12,128,128]{2,1,0:T(8,128)(2,1)}) custom-call(s32[4]{0:T(128)} %get-tuple-element.31.sizes, s32[72]{0:T(128)} %get-tuple-element.32.group_input, s32[288]{0:T(512)} %get-tuple-element.33.entries, bf16[288,128,128]{2,1,0:T(8,128)(2,1)} %get-tuple-element.53.tiles_in, bf16[2,3,128,128]{3,2,1,0:T(8,128)(2,1)} %copy-done.5, ...), custom_call_target="tpu_custom_call" | custom-call | flops 400000000 | bytes 4000000 | tf_op jit(solution)/shard_map/pallas_call | solution.py:433
  137.8 1.2 collective-permute-start.21
  139.0 1.6 %collective-permute-done.21 = bf16[12,128,128]{2,1,0:T(8,128)(2,1)S(1)} collective-permute-done((bf16[12,128,128]{2,1,0:T(8,128)(2,1)}, bf16[12,128,128]{2,1,0:T(8,128)(2,1)S(1)}, u32[]{:S(2)}, u32[]{:S(2)}) %collective-permute-start.21) | collective-permute-done | bytes 393248 | tf_op jit(solution)/shard_map/ppermute | solution.py:471
  140.5 1.3 fusion.11
  142.2 3.2 %collective-permute-start.23 = (bf16[3,128,128]{2,1,0:T(8,128)(2,1)S(1)}, bf16[3,128,128]{2,1,0:T(8,128)(2,1)S(1)}, u32[]{:S(2)}, u32[]{:S(2)}) collective-permute-start(bf16[3,128,128]{2,1,0:T(8,128)(2,1)S(1)} %get-tuple-element.66), channel_id=1, source_target_pairs={{0,16},{1,17},{2,18},{3,19},{4,20},{5,21},{6,22},{7,23},{8,24},{9,... | collective-permute-start | bytes 294920 | tf_op jit(solution)/shard_map/ppermute | solution.py:471
  145.4 0.7 slice.79
  146.1 2.6 %collective-permute-done.22 = bf16[3,128,128]{2,1,0:T(8,128)(2,1)S(1)} collective-permute-done((bf16[3,128,128]{2,1,0:T(8,128)(2,1)S(1)}, bf16[3,128,128]{2,1,0:T(8,128)(2,1)S(1)}, u32[]{:S(2)}, u32[]{:S(2)}) %collective-permute-start.22) | collective-permute-done | bytes 98336 | tf_op jit(solution)/shard_map/ppermute | solution.py:471
  148.6 0.9 collective-permute-done.24
  149.5 5.0 %collective-permute-done.23 = bf16[3,128,128]{2,1,0:T(8,128)(2,1)S(1)} collective-permute-done((bf16[3,128,128]{2,1,0:T(8,128)(2,1)S(1)}, bf16[3,128,128]{2,1,0:T(8,128)(2,1)S(1)}, u32[]{:S(2)}, u32[]{:S(2)}) %collective-permute-start.23) | collective-permute-done | bytes 98336 | tf_op jit(solution)/shard_map/ppermute | solution.py:471
  154.5 0.8 fusion.5
  (60 shorter events, 2.6 us)
Async XLA Ops:
  0.6 37.3 %collective-permute-start.4 = (bf16[2,1,512,512]{3,2,1,0:T(8,128)(2,1)}, bf16[2,1,512,512]{3,2,1,0:T(8,128)(2,1)S(1)}, u32[]{:S(2)}, u32[]{:S(2)}) collective-permute-start(bf16[2,1,512,512]{3,2,1,0:T(8,128)(2,1)} %refs_4_.1), channel_id=1, source_target_pairs={{0,8},{1,9},{2,10},{3,11},{4,12},{5,13},{6,14},{7,15},{8,0},{9,1},... | collective-permute-start | bytes 3145736 | tf_op jit(solution)/shard_map/ppermute | solution.py:471
  7.2 46.7 %copy-start = (bf16[3,656,128]{2,1,0:T(8,128)(2,1)}, bf16[3,656,128]{2,1,0:T(8,128)(2,1)S(1)}, u32[]{:S(2)}) copy-start(bf16[3,656,128]{2,1,0:T(8,128)(2,1)S(1)} %pad_maximum_fusion.given.refs_0_) | copy-start | bytes 1511428
  7.2 15.4 %collective-permute-start.3 = (bf16[3,656,128]{2,1,0:T(8,128)(2,1)S(1)}, bf16[3,656,128]{2,1,0:T(8,128)(2,1)S(1)}, u32[]{:S(2)}, u32[]{:S(2)}) collective-permute-start(bf16[3,656,128]{2,1,0:T(8,128)(2,1)S(1)} %pad_maximum_fusion.given.refs_0_), channel_id=1, source_target_pairs={{0,3},{1,2},{2,1},{3,0},{4,7},{5,6},{6,5},{7,4},{8,11},{9,10},{10,... | collective-permute-start | bytes 1511432 | tf_op jit(solution)/shard_map/ppermute | solution.py:471
  9.7 22.2 %collective-permute-start.2 = (bf16[3,656,128]{2,1,0:T(8,128)(2,1)S(1)}, bf16[3,656,128]{2,1,0:T(8,128)(2,1)S(1)}, u32[]{:S(2)}, u32[]{:S(2)}) collective-permute-start(bf16[3,656,128]{2,1,0:T(8,128)(2,1)S(1)} %pad_maximum_fusion.given.refs_0_), channel_id=1, source_target_pairs={{0,2},{1,3},{2,0},{3,1},{4,6},{5,7},{6,4},{7,5},{8,10},{9,11},{10,... | collective-permute-start | bytes 1511432 | tf_op jit(solution)/shard_map/ppermute | solution.py:471
  10.2 21.8 %collective-permute-start.1 = (bf16[3,656,128]{2,1,0:T(8,128)(2,1)S(1)}, bf16[3,656,128]{2,1,0:T(8,128)(2,1)S(1)}, u32[]{:S(2)}, u32[]{:S(2)}) collective-permute-start(bf16[3,656,128]{2,1,0:T(8,128)(2,1)S(1)} %pad_maximum_fusion.given.refs_0_), channel_id=1, source_target_pairs={{0,1},{1,0},{2,3},{3,2},{4,5},{5,4},{6,7},{7,6},{8,9},{9,8},{10,11... | collective-permute-start | bytes 1511432 | tf_op jit(solution)/shard_map/ppermute | solution.py:471
  10.7 26.4 %collective-permute-start = (bf16[3,656,128]{2,1,0:T(8,128)(2,1)S(1)}, bf16[3,656,128]{2,1,0:T(8,128)(2,1)S(1)}, u32[]{:S(2)}, u32[]{:S(2)}) collective-permute-start(bf16[3,656,128]{2,1,0:T(8,128)(2,1)S(1)} %pad_maximum_fusion.given.refs_0_), channel_id=1, source_target_pairs={{0,16},{1,17},{2,18},{3,19},{4,20},{5,21},{6,22},{7,23},{8,24},{9,... | collective-permute-start | bytes 1511432 | tf_op jit(solution)/shard_map/ppermute | solution.py:471
  22.6 19.5 %copy-start.6 = (bf16[3,656,128]{2,1,0:T(8,128)(2,1)}, bf16[3,656,128]{2,1,0:T(8,128)(2,1)S(1)}, u32[]{:S(2)}) copy-start(bf16[3,656,128]{2,1,0:T(8,128)(2,1)S(1)} %collective-permute-done.3.refs_3_) | copy-start | bytes 1511428
  22.6 19.7 %collective-permute-start.8 = (bf16[2,1,512,512]{3,2,1,0:T(8,128)(2,1)}, bf16[2,1,512,512]{3,2,1,0:T(8,128)(2,1)}, u32[]{:S(2)}, u32[]{:S(2)}) collective-permute-start(bf16[2,1,512,512]{3,2,1,0:T(8,128)(2,1)} %refs_4_.1), channel_id=1, source_target_pairs={{0,4},{1,5},{2,6},{3,7},{4,0},{5,1},{6,2},{7,3},{8,12},{9,13},{10,... | collective-permute-start | bytes 3145736 | tf_op jit(solution)/shard_map/ppermute | solution.py:471
  31.9 15.6 %copy-start.7 = (bf16[3,656,128]{2,1,0:T(8,128)(2,1)}, bf16[3,656,128]{2,1,0:T(8,128)(2,1)S(1)}, u32[]{:S(2)}) copy-start(bf16[3,656,128]{2,1,0:T(8,128)(2,1)S(1)} %collective-permute-done.2.refs_2_) | copy-start | bytes 1511428
  32.0 5.9 %copy-start.8 = (bf16[3,656,128]{2,1,0:T(8,128)(2,1)}, bf16[3,656,128]{2,1,0:T(8,128)(2,1)S(1)}, u32[]{:S(2)}) copy-start(bf16[3,656,128]{2,1,0:T(8,128)(2,1)S(1)} %collective-permute-done.1.refs_1_) | copy-start | bytes 1511428
  37.1 23.6 %copy-start.1 = (bf16[3,656,128]{2,1,0:T(8,128)(2,1)}, bf16[3,656,128]{2,1,0:T(8,128)(2,1)S(1)}, u32[]{:S(2)}) copy-start(bf16[3,656,128]{2,1,0:T(8,128)(2,1)S(1)} %collective-permute-done.given.refs_0_.refs_4_) | copy-start | bytes 1511428
  37.9 16.0 %copy-start.3 = (bf16[2,1,512,512]{3,2,1,0:T(8,128)(2,1)}, bf16[2,1,512,512]{3,2,1,0:T(8,128)(2,1)S(1)}, u32[]{:S(2)}) copy-start(bf16[2,1,512,512]{3,2,1,0:T(8,128)(2,1)S(1)} %collective-permute-done.4.refs_6_) | copy-start | bytes 3145732
  37.9 4.4 %collective-permute-start.9 = (bf16[2,1,512,512]{3,2,1,0:T(8,128)(2,1)S(1)}, bf16[2,1,512,512]{3,2,1,0:T(8,128)(2,1)}, u32[]{:S(2)}, u32[]{:S(2)}) collective-permute-start(bf16[2,1,512,512]{3,2,1,0:T(8,128)(2,1)S(1)} %collective-permute-done.4.refs_6_), channel_id=1, source_target_pairs={{0,4},{1,5},{2,6},{3,7},{4,0},{5,1},{6,2},{7,3},{8,12},{9,13},{10,... | collective-permute-start | bytes 3145736 | tf_op jit(solution)/shard_map/ppermute | solution.py:471
  38.6 22.1 %collective-permute-start.7 = (bf16[3,656,128]{2,1,0:T(8,128)(2,1)S(1)}, bf16[3,656,128]{2,1,0:T(8,128)(2,1)}, u32[]{:S(2)}, u32[]{:S(2)}) collective-permute-start(bf16[3,656,128]{2,1,0:T(8,128)(2,1)S(1)} %collective-permute-done.given.refs_0_.refs_4_), channel_id=1, source_target_pairs={{0,3},{1,2},{2,1},{3,0},{4,7},{5,6},{6,5},{7,4},{8,11},{9,10},{10,... | collective-permute-start | bytes 1511432 | tf_op jit(solution)/shard_map/ppermute | solution.py:471
  41.2 23.0 %collective-permute-start.6 = (bf16[3,656,128]{2,1,0:T(8,128)(2,1)S(1)}, bf16[3,656,128]{2,1,0:T(8,128)(2,1)}, u32[]{:S(2)}, u32[]{:S(2)}) collective-permute-start(bf16[3,656,128]{2,1,0:T(8,128)(2,1)S(1)} %collective-permute-done.given.refs_0_.refs_4_), channel_id=1, source_target_pairs={{0,2},{1,3},{2,0},{3,1},{4,6},{5,7},{6,4},{7,5},{8,10},{9,11},{10,... | collective-permute-start | bytes 1511432 | tf_op jit(solution)/shard_map/ppermute | solution.py:471
  41.7 22.8 %collective-permute-start.5 = (bf16[3,656,128]{2,1,0:T(8,128)(2,1)S(1)}, bf16[3,656,128]{2,1,0:T(8,128)(2,1)}, u32[]{:S(2)}, u32[]{:S(2)}) collective-permute-start(bf16[3,656,128]{2,1,0:T(8,128)(2,1)S(1)} %collective-permute-done.given.refs_0_.refs_4_), channel_id=1, source_target_pairs={{0,1},{1,0},{2,3},{3,2},{4,5},{5,4},{6,7},{7,6},{8,9},{9,8},{10,11... | collective-permute-start | bytes 1511432 | tf_op jit(solution)/shard_map/ppermute | solution.py:471
  42.3 29.8 %collective-permute-start.11 = (bf16[3,128,512]{2,1,0:T(8,128)(2,1)S(1)}, bf16[3,128,512]{2,1,0:T(8,128)(2,1)}, u32[]{:S(2)}, u32[]{:S(2)}) collective-permute-start(bf16[3,128,512]{2,1,0:T(8,128)(2,1)S(1)} %shard_map.96.own), channel_id=1, source_target_pairs={{0,24},{1,25},{2,26},{3,27},{4,28},{5,29},{6,30},{7,31},{8,16},{9,... | collective-permute-start | bytes 1179656 | tf_op jit(solution)/shard_map/ppermute | solution.py:471
  46.1 26.0 %collective-permute-start.10 = (bf16[3,128,512]{2,1,0:T(8,128)(2,1)S(1)}, bf16[3,128,512]{2,1,0:T(8,128)(2,1)}, u32[]{:S(2)}, u32[]{:S(2)}) collective-permute-start(bf16[3,128,512]{2,1,0:T(8,128)(2,1)S(1)} %shard_map.96.own), channel_id=1, source_target_pairs={{0,8},{1,9},{2,10},{3,11},{4,12},{5,13},{6,14},{7,15},{8,0},{9,1},... | collective-permute-start | bytes 1179656 | tf_op jit(solution)/shard_map/ppermute | solution.py:471
  53.9 18.2 %copy-start.2 = (bf16[6,128,512]{2,1,0:T(8,128)(2,1)}, bf16[6,128,512]{2,1,0:T(8,128)(2,1)S(1)}, u32[]{:S(2)}) copy-start(bf16[6,128,512]{2,1,0:T(8,128)(2,1)S(1)} %shard_map.97.refs_8_) | copy-start | bytes 2359300
  72.1 3.7 %collective-permute-start.12 = (bf16[6,128,512]{2,1,0:T(8,128)(2,1)S(1)}, bf16[6,128,512]{2,1,0:T(8,128)(2,1)S(1)}, u32[]{:S(2)}, u32[]{:S(2)}) collective-permute-start(bf16[6,128,512]{2,1,0:T(8,128)(2,1)S(1)} %shard_map.97.refs_8_), channel_id=1, source_target_pairs={{0,4},{1,5},{2,6},{3,7},{4,0},{5,1},{6,2},{7,3},{8,12},{9,13},{10,... | collective-permute-start | bytes 2359304 | tf_op jit(solution)/shard_map/ppermute | solution.py:471
  72.2 3.0 %collective-permute-start.13 = (bf16[3,128,512]{2,1,0:T(8,128)(2,1)}, bf16[3,128,512]{2,1,0:T(8,128)(2,1)S(1)}, u32[]{:S(2)}, u32[]{:S(2)}) collective-permute-start(bf16[3,128,512]{2,1,0:T(8,128)(2,1)} %collective-permute-done.10.refs_9_), channel_id=1, source_target_pairs={{0,4},{1,5},{2,6},{3,7},{4,0},{5,1},{6,2},{7,3},{8,12},{9,13},{10,... | collective-permute-start | bytes 1179656 | tf_op jit(solution)/shard_map/ppermute | solution.py:471
  72.7 3.1 %collective-permute-start.14 = (bf16[3,128,512]{2,1,0:T(8,128)(2,1)}, bf16[3,128,512]{2,1,0:T(8,128)(2,1)S(1)}, u32[]{:S(2)}, u32[]{:S(2)}) collective-permute-start(bf16[3,128,512]{2,1,0:T(8,128)(2,1)} %collective-permute-done.11.refs_10_), channel_id=1, source_target_pairs={{0,4},{1,5},{2,6},{3,7},{4,0},{5,1},{6,2},{7,3},{8,12},{9,13},{10,... | collective-permute-start | bytes 1179656 | tf_op jit(solution)/shard_map/ppermute | solution.py:471
  75.2 0.8 copy-start.14
  75.8 0.8 copy-start.15
  75.8 1.1 copy-start.13
  89.3 10.2 %copy-start.4 = (f32[384,128]{1,0:T(8,128)S(1)}, f32[384,128]{1,0:T(8,128)}, u32[]{:S(2)}) copy-start(f32[384,128]{1,0:T(8,128)} %param.8) | copy-start | bytes 589828
  89.3 10.2 %copy-start.12 = (f32[384]{0:T(512)S(1)}, f32[384]{0:T(512)}, u32[]{:S(2)}) copy-start(f32[384]{0:T(512)} %param.9) | copy-start | bytes 4612
  89.3 4.2 %collective-permute-start.15 = (bf16[12,128,128]{2,1,0:T(8,128)(2,1)}, bf16[12,128,128]{2,1,0:T(8,128)(2,1)S(1)}, u32[]{:S(2)}, u32[]{:S(2)}) collective-permute-start(bf16[12,128,128]{2,1,0:T(8,128)(2,1)} %get-tuple-element.52), channel_id=1, source_target_pairs={{0,4},{1,5},{2,6},{3,7},{4,0},{5,1},{6,2},{7,3},{8,12},{9,13},{10,... | collective-permute-start | bytes 1179656 | tf_op jit(solution)/shard_map/ppermute | solution.py:471
  94.9 9.8 %collective-permute-start.16 = (bf16[2,3,128,128]{3,2,1,0:T(8,128)(2,1)S(1)}, bf16[2,3,128,128]{3,2,1,0:T(8,128)(2,1)S(1)}, u32[]{:S(2)}, u32[]{:S(2)}) collective-permute-start(bf16[2,3,128,128]{3,2,1,0:T(8,128)(2,1)S(1)} %pad_maximum_fusion.1), channel_id=1, source_target_pairs={{0,8},{1,9},{2,10},{3,11},{4,12},{5,13},{6,14},{7,15},{8,0},{9,1},... | collective-permute-start | bytes 589832 | tf_op jit(solution)/shard_map/ppermute | solution.py:471
  104.7 11.6 %collective-permute-start.17 = (bf16[2,3,128,128]{3,2,1,0:T(8,128)(2,1)S(1)}, bf16[2,3,128,128]{3,2,1,0:T(8,128)(2,1)S(1)}, u32[]{:S(2)}, u32[]{:S(2)}) collective-permute-start(bf16[2,3,128,128]{3,2,1,0:T(8,128)(2,1)S(1)} %fusion), channel_id=1, source_target_pairs={{0,16},{1,17},{2,18},{3,19},{4,20},{5,21},{6,22},{7,23},{8,24},{9,... | collective-permute-start | bytes 589832 | tf_op jit(solution)/shard_map/ppermute | solution.py:471
  116.4 14.7 %copy-start.5 = (bf16[2,3,128,128]{3,2,1,0:T(8,128)(2,1)}, bf16[2,3,128,128]{3,2,1,0:T(8,128)(2,1)S(1)}, u32[]{:S(2)}) copy-start(bf16[2,3,128,128]{3,2,1,0:T(8,128)(2,1)S(1)} %get-tuple-element.58.refs_0_) | copy-start | bytes 589828
  116.5 11.1 %collective-permute-start.20 = (bf16[2,3,128,128]{3,2,1,0:T(8,128)(2,1)S(1)}, bf16[2,3,128,128]{3,2,1,0:T(8,128)(2,1)S(1)}, u32[]{:S(2)}, u32[]{:S(2)}) collective-permute-start(bf16[2,3,128,128]{3,2,1,0:T(8,128)(2,1)S(1)} %get-tuple-element.58.refs_0_), channel_id=1, source_target_pairs={{0,3},{1,2},{2,1},{3,0},{4,7},{5,6},{6,5},{7,4},{8,11},{9,10},{10,... | collective-permute-start | bytes 589832 | tf_op jit(solution)/shard_map/ppermute | solution.py:471
  121.8 9.3 %collective-permute-start.19 = (bf16[2,3,128,128]{3,2,1,0:T(8,128)(2,1)S(1)}, bf16[2,3,128,128]{3,2,1,0:T(8,128)(2,1)S(1)}, u32[]{:S(2)}, u32[]{:S(2)}) collective-permute-start(bf16[2,3,128,128]{3,2,1,0:T(8,128)(2,1)S(1)} %get-tuple-element.58.refs_0_), channel_id=1, source_target_pairs={{0,2},{1,3},{2,0},{3,1},{4,6},{5,7},{6,4},{7,5},{8,10},{9,11},{10,... | collective-permute-start | bytes 589832 | tf_op jit(solution)/shard_map/ppermute | solution.py:471
  121.8 9.3 %collective-permute-start.18 = (bf16[2,3,128,128]{3,2,1,0:T(8,128)(2,1)S(1)}, bf16[2,3,128,128]{3,2,1,0:T(8,128)(2,1)S(1)}, u32[]{:S(2)}, u32[]{:S(2)}) collective-permute-start(bf16[2,3,128,128]{3,2,1,0:T(8,128)(2,1)S(1)} %get-tuple-element.58.refs_0_), channel_id=1, source_target_pairs={{0,1},{1,0},{2,3},{3,2},{4,5},{5,4},{6,7},{7,6},{8,9},{9,8},{10,11... | collective-permute-start | bytes 589832 | tf_op jit(solution)/shard_map/ppermute | solution.py:471
  127.6 3.6 %copy-start.9 = (bf16[2,3,128,128]{3,2,1,0:T(8,128)(2,1)}, bf16[2,3,128,128]{3,2,1,0:T(8,128)(2,1)S(1)}, u32[]{:S(2)}) copy-start(bf16[2,3,128,128]{3,2,1,0:T(8,128)(2,1)S(1)} %collective-permute-done.20.refs_3_) | copy-start | bytes 589828
  131.1 0.7 copy-start.10
  131.1 0.7 copy-start.11
  137.8 2.7 %collective-permute-start.21 = (bf16[12,128,128]{2,1,0:T(8,128)(2,1)}, bf16[12,128,128]{2,1,0:T(8,128)(2,1)S(1)}, u32[]{:S(2)}, u32[]{:S(2)}) collective-permute-start(bf16[12,128,128]{2,1,0:T(8,128)(2,1)} %get-tuple-element.55), channel_id=1, source_target_pairs={{0,4},{1,5},{2,6},{3,7},{4,0},{5,1},{6,2},{7,3},{8,12},{9,13},{10,... | collective-permute-start | bytes 1179656 | tf_op jit(solution)/shard_map/ppermute | solution.py:471
  141.8 6.8 %collective-permute-start.22 = (bf16[3,128,128]{2,1,0:T(8,128)(2,1)S(1)}, bf16[3,128,128]{2,1,0:T(8,128)(2,1)S(1)}, u32[]{:S(2)}, u32[]{:S(2)}) collective-permute-start(bf16[3,128,128]{2,1,0:T(8,128)(2,1)S(1)} %get-tuple-element.64), channel_id=1, source_target_pairs={{0,8},{1,9},{2,10},{3,11},{4,12},{5,13},{6,14},{7,15},{8,0},{9,1},... | collective-permute-start | bytes 294920 | tf_op jit(solution)/shard_map/ppermute | solution.py:471
  141.9 7.6 %collective-permute-start.24 = (bf16[3,128,128]{2,1,0:T(8,128)(2,1)S(1)}, bf16[3,128,128]{2,1,0:T(8,128)(2,1)S(1)}, u32[]{:S(2)}, u32[]{:S(2)}) collective-permute-start(bf16[3,128,128]{2,1,0:T(8,128)(2,1)S(1)} %get-tuple-element.65), channel_id=1, source_target_pairs={{0,24},{1,25},{2,26},{3,27},{4,28},{5,29},{6,30},{7,31},{8,16},{9,... | collective-permute-start | bytes 294920 | tf_op jit(solution)/shard_map/ppermute | solution.py:471
  142.2 12.3 %collective-permute-start.23 = (bf16[3,128,128]{2,1,0:T(8,128)(2,1)S(1)}, bf16[3,128,128]{2,1,0:T(8,128)(2,1)S(1)}, u32[]{:S(2)}, u32[]{:S(2)}) collective-permute-start(bf16[3,128,128]{2,1,0:T(8,128)(2,1)S(1)} %get-tuple-element.66), channel_id=1, source_target_pairs={{0,16},{1,17},{2,18},{3,19},{4,20},{5,21},{6,22},{7,23},{8,24},{9,... | collective-permute-start | bytes 294920 | tf_op jit(solution)/shard_map/ppermute | solution.py:471

commit v10 on v9

--- a/solution.py
+++ b/solution.py
@@ -509,12 +509,13 @@
     lines = [along(turned, d) for d in lay.line_steps()]
     for part in partner:
         turned = turn_both(lay, part, turned)
-    projected = [
-        project(lay, g, plan, inputs[g * cols : (g + 1) * cols], blocks_coarse) for g in range(lay.owners)
-    ]
-    lines, turned, projected = lax.optimization_barrier((lines, turned, projected))
+    projected = [project(lay, 0, plan, inputs[:cols], blocks_coarse)]
+    held = (inputs, lines, turned, projected)
+    inputs, lines, turned, projected = lax.optimization_barrier(held)
     lefts = [turned] + lines
     lefts = lefts + [to_core(part) for part in lefts]
+    if two_owners:
+        projected.append(project(lay, 1, plan, inputs[cols:], blocks_coarse))
     own_sum, other_sum, tiles = make_tiles(lay, plan, inputs, lefts, projected)
 
     def over_core(own_part, other_part):

time: 154 us -> 152 us (0.987); the launches traced: 155 us -> 150 us
  waiting for transfers between devices: 67.9 us -> 62.5 us
  starting transfers between devices: 35.5 us -> 33.1 us
  Pallas kernels: 39.2 us -> 41.4 us
    ppermute x25, waiting for transfers between devices: 67.9 us -> 62.5 us  [move(): return lax.ppermute(array, axes, pairs_list)]
    ppermute x25, starting transfers between devices: 35.5 us -> 33.1 us  [move(): return lax.ppermute(array, axes, pairs_list)]
  transfers between devices with their start and end apart: 25 -> 25, of which waited for: 18 -> 16; matrix products, arithmetic and copies ran while one was open for 4% -> 4% of each run, Pallas kernels for 13% -> 14%
where the time goes in v10:
time: 152 us; the launch traced here: 150 us
  waiting for transfers between devices  62.5 us (41%)
  Pallas kernels  41.4 us (27%)
  starting transfers between devices  33.1 us (22%)
  other arithmetic  8.44 us (6%)
  local copies, waits for them, and re-layouts  2.62 us (2%)
  between operations  1.61 us (1%)
    ppermute x25, waiting for transfers between devices, move(): return lax.ppermute(array, axes, pairs_list)  62.5 us
    ppermute x25, starting transfers between devices, move(): return lax.ppermute(array, axes, pairs_list)  33.1 us
    pallas_call x1, Pallas kernels, make_tiles(): pl.pallas_call(functools.partial(tiles_kernel, lay), out_shape=(sums, sen...  13.8 us
    pallas_call x2, Pallas kernels, project(): pl.pallas_call(functools.partial(project_kernel, lay, owner), out_shape=j...  13.6 us
    pallas_call x1, Pallas kernels, make_plan(): pl.pallas_call(functools.partial(plan_kernel, lay), out_shape=tuple((jax....  7.11 us
    pallas_call x1, Pallas kernels, apply_tiles(): pl.pallas_call(functools.partial(apply_kernel, lay), out_shape=(sums, sen...  6.49 us
  transfers between devices with their start and end apart: 25, of which 16 were waited for; matrix products, arithmetic and copies ran while one was open for 4% of the time, Pallas kernels for 14%

profile of v10, /device:TPU:0, one launch (start us, length us, event | category | flops | bytes accessed | tf_op | source)
XLA Modules:
  0.0 149.7 jit_solution(15132960021841294038)
XLA Ops:
  0.6 3.1 %collective-permute-start.4 = (bf16[2,1,512,512]{3,2,1,0:T(8,128)(2,1)}, bf16[2,1,512,512]{3,2,1,0:T(8,128)(2,1)S(1)}, u32[]{:S(2)}, u32[]{:S(2)}) collective-permute-start(bf16[2,1,512,512]{3,2,1,0:T(8,128)(2,1)} %refs_4_.1), channel_id=1, source_target_pairs={{0,8},{1,9},{2,10},{3,11},{4,12},{5,13},{6,14},{7,15},{8,0},{9,1},... | collective-permute-start | bytes 3145736 | tf_op jit(solution)/shard_map/ppermute | solution.py:471
  4.4 0.9 convert_element_type.40
  5.3 0.7 convert_bitcast_fusion.1
  6.1 1.0 pad_maximum_fusion.given.refs_0_
  7.2 2.5 %collective-permute-start.3 = (bf16[3,656,128]{2,1,0:T(8,128)(2,1)S(1)}, bf16[3,656,128]{2,1,0:T(8,128)(2,1)S(1)}, u32[]{:S(2)}, u32[]{:S(2)}) collective-permute-start(bf16[3,656,128]{2,1,0:T(8,128)(2,1)S(1)} %pad_maximum_fusion.given.refs_0_), channel_id=1, source_target_pairs={{0,3},{1,2},{2,1},{3,0},{4,7},{5,6},{6,5},{7,4},{8,11},{9,10},{10,... | collective-permute-start | bytes 1511432 | tf_op jit(solution)/shard_map/ppermute | solution.py:471
  9.7 0.5 collective-permute-start.2
  10.2 0.5 collective-permute-start.1
  10.7 2.6 %collective-permute-start = (bf16[3,656,128]{2,1,0:T(8,128)(2,1)S(1)}, bf16[3,656,128]{2,1,0:T(8,128)(2,1)S(1)}, u32[]{:S(2)}, u32[]{:S(2)}) collective-permute-start(bf16[3,656,128]{2,1,0:T(8,128)(2,1)S(1)} %pad_maximum_fusion.given.refs_0_), channel_id=1, source_target_pairs={{0,16},{1,17},{2,18},{3,19},{4,20},{5,21},{6,22},{7,23},{8,24},{9,... | collective-permute-start | bytes 1511432 | tf_op jit(solution)/shard_map/ppermute | solution.py:471
  13.3 9.3 %collective-permute-done.3.refs_3_ = bf16[3,656,128]{2,1,0:T(8,128)(2,1)S(1)} collective-permute-done((bf16[3,656,128]{2,1,0:T(8,128)(2,1)S(1)}, bf16[3,656,128]{2,1,0:T(8,128)(2,1)S(1)}, u32[]{:S(2)}, u32[]{:S(2)}) %collective-permute-start.3) | collective-permute-done | bytes 503840 | tf_op jit(solution)/shard_map/ppermute | solution.py:471
  22.6 9.3 %collective-permute-done.2.refs_2_ = bf16[3,656,128]{2,1,0:T(8,128)(2,1)S(1)} collective-permute-done((bf16[3,656,128]{2,1,0:T(8,128)(2,1)S(1)}, bf16[3,656,128]{2,1,0:T(8,128)(2,1)S(1)}, u32[]{:S(2)}, u32[]{:S(2)}) %collective-permute-start.2) | collective-permute-done | bytes 503840 | tf_op jit(solution)/shard_map/ppermute | solution.py:471
  32.0 5.2 %collective-permute-done.given.refs_0_.refs_4_ = bf16[3,656,128]{2,1,0:T(8,128)(2,1)S(1)} collective-permute-done((bf16[3,656,128]{2,1,0:T(8,128)(2,1)S(1)}, bf16[3,656,128]{2,1,0:T(8,128)(2,1)S(1)}, u32[]{:S(2)}, u32[]{:S(2)}) %collective-permute-start) | collective-permute-done | bytes 503840 | tf_op jit(solution)/shard_map/ppermute | solution.py:471
  37.1 0.7 collective-permute-done.4.refs_6_
  37.9 0.7 pad_add_fusion.1.ids
  38.6 2.6 %collective-permute-start.7 = (bf16[3,656,128]{2,1,0:T(8,128)(2,1)S(1)}, bf16[3,656,128]{2,1,0:T(8,128)(2,1)}, u32[]{:S(2)}, u32[]{:S(2)}) collective-permute-start(bf16[3,656,128]{2,1,0:T(8,128)(2,1)S(1)} %collective-permute-done.given.refs_0_.refs_4_), channel_id=1, source_target_pairs={{0,3},{1,2},{2,1},{3,0},{4,7},{5,6},{6,5},{7,4},{8,11},{9,10},{10,... | collective-permute-start | bytes 1511432 | tf_op jit(solution)/shard_map/ppermute | solution.py:471
  41.2 0.5 collective-permute-start.6
  41.7 0.4 collective-permute-start.5
  42.3 3.8 %collective-permute-start.11 = (bf16[3,128,512]{2,1,0:T(8,128)(2,1)S(1)}, bf16[3,128,512]{2,1,0:T(8,128)(2,1)}, u32[]{:S(2)}, u32[]{:S(2)}) collective-permute-start(bf16[3,128,512]{2,1,0:T(8,128)(2,1)S(1)} %shard_map.96.own), channel_id=1, source_target_pairs={{0,24},{1,25},{2,26},{3,27},{4,28},{5,29},{6,30},{7,31},{8,16},{9,... | collective-permute-start | bytes 1179656 | tf_op jit(solution)/shard_map/ppermute | solution.py:471
  46.2 1.3 pad_add_fusion.listed
  47.5 7.1 %shard_map.95 = (s32[24]{0:T(128)}, s32[26]{0:T(128)}, s32[4]{0:T(128)}, s32[72]{0:T(128)}, s32[288]{0:T(512)}) custom-call(s32[3]{0:T(128)} %pad_add_fusion.1.ids, s32[2,97]{1,0:T(2,128)} %pad_add_fusion.listed, s32[96]{0:T(128)} %fine.1, s32[8]{0:T(128)} %stored.1), custom_call_target="tpu_custom_call" | custom-call | bytes 20000000 | tf_op jit(solution)/shard_map/pallas_call | solution.py:137
  54.8 6.8 %shard_map.98.refs_14_ = bf16[12,512,256]{2,1,0:T(8,128)(2,1)} custom-call(s32[24]{0:T(128)} %get-tuple-element.37.slot_of, s32[26]{0:T(128)} %get-tuple-element.48.valid, s32[4]{0:T(128)} %get-tuple-element.38.sizes, bf16[3,656,128]{2,1,0:T(8,128)(2,1)} %copy-done, bf16[3,656,128]{2,1,0:T(8,128)(2,1)} %copy-done.8, bf16[3,656,128]{2,1,0:T(8,128)(2,1)} %copy-done.7, ...), custom_call_target="tpu_custom_call" | custom-call | flops 1000000000 | bytes 16000000 | tf_op jit(solution)/shard_map/pallas_call | solution.py:242
  61.7 2.6 %collective-permute-done.6.refs_2_.refs_6_ = bf16[3,656,128]{2,1,0:T(8,128)(2,1)} collective-permute-done((bf16[3,656,128]{2,1,0:T(8,128)(2,1)S(1)}, bf16[3,656,128]{2,1,0:T(8,128)(2,1)}, u32[]{:S(2)}, u32[]{:S(2)}) %collective-permute-start.6) | collective-permute-done | bytes 503840 | tf_op jit(solution)/shard_map/ppermute | solution.py:471
  64.6 0.5 collective-permute-start.13
  65.2 6.8 %shard_map.99.refs_15_ = bf16[12,512,256]{2,1,0:T(8,128)(2,1)} custom-call(s32[24]{0:T(128)} %get-tuple-element.37.slot_of, s32[26]{0:T(128)} %get-tuple-element.48.valid, s32[4]{0:T(128)} %get-tuple-element.38.sizes, bf16[3,656,128]{2,1,0:T(8,128)(2,1)} %copy-done.1, bf16[3,656,128]{2,1,0:T(8,128)(2,1)} %collective-permute-done.5.refs_1_.refs_5_, ...), custom_call_target="tpu_custom_call" | custom-call | flops 1000000000 | bytes 16000000 | tf_op jit(solution)/shard_map/pallas_call | solution.py:242
  72.0 0.7 copy-done.14
  73.2 13.8 %shard_map.100 = (f32[12,128,128]{2,1,0:T(8,128)}, bf16[12,128,128]{2,1,0:T(8,128)(2,1)}, bf16[288,128,128]{2,1,0:T(8,128)(2,1)}) custom-call(s32[24]{0:T(128)} %get-tuple-element.37.slot_of, s32[4]{0:T(128)} %get-tuple-element.38.sizes, s32[72]{0:T(128)} %get-tuple-element.39.group_input, s32[288]{0:T(512)} %get-tuple-element.40.entries, ...), custom_call_target="tpu_custom_call" | custom-call | flops 4000000000 | bytes 30000000 | tf_op jit(solution)/shard_map/pallas_call | solution.py:365
  87.0 1.3 collective-permute-start.15
  88.3 1.6 %collective-permute-done.15 = bf16[12,128,128]{2,1,0:T(8,128)(2,1)S(1)} collective-permute-done((bf16[12,128,128]{2,1,0:T(8,128)(2,1)}, bf16[12,128,128]{2,1,0:T(8,128)(2,1)S(1)}, u32[]{:S(2)}, u32[]{:S(2)}) %collective-permute-start.15) | collective-permute-done | bytes 393248 | tf_op jit(solution)/shard_map/ppermute | solution.py:471
  89.9 1.3 fusion.13
  91.2 1.4 collective-permute-start.16
  92.7 5.8 %collective-permute-done.16 = bf16[2,3,128,128]{3,2,1,0:T(8,128)(2,1)S(1)} collective-permute-done((bf16[2,3,128,128]{3,2,1,0:T(8,128)(2,1)S(1)}, bf16[2,3,128,128]{3,2,1,0:T(8,128)(2,1)S(1)}, u32[]{:S(2)}, u32[]{:S(2)}) %collective-permute-start.16) | collective-permute-done | bytes 196640 | tf_op jit(solution)/shard_map/ppermute | solution.py:471
  98.5 1.9 %collective-permute-start.17 = (bf16[2,3,128,128]{3,2,1,0:T(8,128)(2,1)S(1)}, bf16[2,3,128,128]{3,2,1,0:T(8,128)(2,1)S(1)}, u32[]{:S(2)}, u32[]{:S(2)}) collective-permute-start(bf16[2,3,128,128]{3,2,1,0:T(8,128)(2,1)S(1)} %fusion), channel_id=1, source_target_pairs={{0,16},{1,17},{2,18},{3,19},{4,20},{5,21},{6,22},{7,23},{8,24},{9,... | collective-permute-start | bytes 589832 | tf_op jit(solution)/shard_map/ppermute | solution.py:471
  100.4 9.6 %collective-permute-done.17 = bf16[2,3,128,128]{3,2,1,0:T(8,128)(2,1)S(1)} collective-permute-done((bf16[2,3,128,128]{3,2,1,0:T(8,128)(2,1)S(1)}, bf16[2,3,128,128]{3,2,1,0:T(8,128)(2,1)S(1)}, u32[]{:S(2)}, u32[]{:S(2)}) %collective-permute-start.17) | collective-permute-done | bytes 196640 | tf_op jit(solution)/shard_map/ppermute | solution.py:471
  110.1 2.9 %collective-permute-start.20 = (bf16[2,3,128,128]{3,2,1,0:T(8,128)(2,1)S(1)}, bf16[2,3,128,128]{3,2,1,0:T(8,128)(2,1)S(1)}, u32[]{:S(2)}, u32[]{:S(2)}) collective-permute-start(bf16[2,3,128,128]{3,2,1,0:T(8,128)(2,1)S(1)} %get-tuple-element.72.refs_0_), channel_id=1, source_target_pairs={{0,3},{1,2},{2,1},{3,0},{4,7},{5,6},{6,5},{7,4},{8,11},{9,10},{10,... | collective-permute-start | bytes 589832 | tf_op jit(solution)/shard_map/ppermute | solution.py:471
  113.1 3.4 %collective-permute-start.19 = (bf16[2,3,128,128]{3,2,1,0:T(8,128)(2,1)S(1)}, bf16[2,3,128,128]{3,2,1,0:T(8,128)(2,1)S(1)}, u32[]{:S(2)}, u32[]{:S(2)}) collective-permute-start(bf16[2,3,128,128]{3,2,1,0:T(8,128)(2,1)S(1)} %get-tuple-element.72.refs_0_), channel_id=1, source_target_pairs={{0,2},{1,3},{2,0},{3,1},{4,6},{5,7},{6,4},{7,5},{8,10},{9,11},{10,... | collective-permute-start | bytes 589832 | tf_op jit(solution)/shard_map/ppermute | solution.py:471
  116.5 1.4 collective-permute-start.18
  117.9 6.2 %collective-permute-done.19.refs_2_ = bf16[2,3,128,128]{3,2,1,0:T(8,128)(2,1)S(1)} collective-permute-done((bf16[2,3,128,128]{3,2,1,0:T(8,128)(2,1)S(1)}, bf16[2,3,128,128]{3,2,1,0:T(8,128)(2,1)S(1)}, u32[]{:S(2)}, u32[]{:S(2)}) %collective-permute-start.19) | collective-permute-done | bytes 196640 | tf_op jit(solution)/shard_map/ppermute | solution.py:471
  124.1 1.9 %collective-permute-done.18.refs_1_ = bf16[2,3,128,128]{3,2,1,0:T(8,128)(2,1)S(1)} collective-permute-done((bf16[2,3,128,128]{3,2,1,0:T(8,128)(2,1)S(1)}, bf16[2,3,128,128]{3,2,1,0:T(8,128)(2,1)S(1)}, u32[]{:S(2)}, u32[]{:S(2)}) %collective-permute-start.18) | collective-permute-done | bytes 196640 | tf_op jit(solution)/shard_map/ppermute | solution.py:471
  126.0 0.7 copy-done.11
  126.6 6.5 %shard_map.101 = (f32[12,128,128]{2,1,0:T(8,128)}, bf16[12,128,128]{2,1,0:T(8,128)(2,1)}) custom-call(s32[4]{0:T(128)} %get-tuple-element.38.sizes, s32[72]{0:T(128)} %get-tuple-element.39.group_input, s32[288]{0:T(512)} %get-tuple-element.40.entries, bf16[288,128,128]{2,1,0:T(8,128)(2,1)} %get-tuple-element.67.tiles_in, bf16[2,3,128,128]{3,2,1,0:T(8,128)(2,1)} %copy-done.5, ...), custom_call_target="tpu_custom_call" | custom-call | flops 400000000 | bytes 4000000 | tf_op jit(solution)/shard_map/pallas_call | solution.py:433
  133.2 1.9 %collective-permute-done.21 = bf16[12,128,128]{2,1,0:T(8,128)(2,1)S(1)} collective-permute-done((bf16[12,128,128]{2,1,0:T(8,128)(2,1)}, bf16[12,128,128]{2,1,0:T(8,128)(2,1)S(1)}, u32[]{:S(2)}, u32[]{:S(2)}) %collective-permute-start.21) | collective-permute-done | bytes 393248 | tf_op jit(solution)/shard_map/ppermute | solution.py:471
  135.1 1.3 fusion.11
  136.5 1.6 %collective-permute-start.24 = (bf16[3,128,128]{2,1,0:T(8,128)(2,1)S(1)}, bf16[3,128,128]{2,1,0:T(8,128)(2,1)S(1)}, u32[]{:S(2)}, u32[]{:S(2)}) collective-permute-start(bf16[3,128,128]{2,1,0:T(8,128)(2,1)S(1)} %get-tuple-element.79), channel_id=1, source_target_pairs={{0,24},{1,25},{2,26},{3,27},{4,28},{5,29},{6,30},{7,31},{8,16},{9,... | collective-permute-start | bytes 294920 | tf_op jit(solution)/shard_map/ppermute | solution.py:471
  138.2 1.8 %collective-permute-start.23 = (bf16[3,128,128]{2,1,0:T(8,128)(2,1)S(1)}, bf16[3,128,128]{2,1,0:T(8,128)(2,1)S(1)}, u32[]{:S(2)}, u32[]{:S(2)}) collective-permute-start(bf16[3,128,128]{2,1,0:T(8,128)(2,1)S(1)} %get-tuple-element.80), channel_id=1, source_target_pairs={{0,16},{1,17},{2,18},{3,19},{4,20},{5,21},{6,22},{7,23},{8,24},{9,... | collective-permute-start | bytes 294920 | tf_op jit(solution)/shard_map/ppermute | solution.py:471
  140.0 0.7 slice.79
  140.7 2.0 %collective-permute-done.22 = bf16[3,128,128]{2,1,0:T(8,128)(2,1)S(1)} collective-permute-done((bf16[3,128,128]{2,1,0:T(8,128)(2,1)S(1)}, bf16[3,128,128]{2,1,0:T(8,128)(2,1)S(1)}, u32[]{:S(2)}, u32[]{:S(2)}) %collective-permute-start.22) | collective-permute-done | bytes 98336 | tf_op jit(solution)/shard_map/ppermute | solution.py:471
  142.7 1.4 collective-permute-done.24
  144.1 4.7 %collective-permute-done.23 = bf16[3,128,128]{2,1,0:T(8,128)(2,1)S(1)} collective-permute-done((bf16[3,128,128]{2,1,0:T(8,128)(2,1)S(1)}, bf16[3,128,128]{2,1,0:T(8,128)(2,1)S(1)}, u32[]{:S(2)}, u32[]{:S(2)}) %collective-permute-start.23) | collective-permute-done | bytes 98336 | tf_op jit(solution)/shard_map/ppermute | solution.py:471
  148.8 0.8 fusion.5
  (60 shorter events, 2.0 us)
Async XLA Ops:
  0.6 37.3 %collective-permute-start.4 = (bf16[2,1,512,512]{3,2,1,0:T(8,128)(2,1)}, bf16[2,1,512,512]{3,2,1,0:T(8,128)(2,1)S(1)}, u32[]{:S(2)}, u32[]{:S(2)}) collective-permute-start(bf16[2,1,512,512]{3,2,1,0:T(8,128)(2,1)} %refs_4_.1), channel_id=1, source_target_pairs={{0,8},{1,9},{2,10},{3,11},{4,12},{5,13},{6,14},{7,15},{8,0},{9,1},... | collective-permute-start | bytes 3145736 | tf_op jit(solution)/shard_map/ppermute | solution.py:471
  7.2 47.6 %copy-start = (bf16[3,656,128]{2,1,0:T(8,128)(2,1)}, bf16[3,656,128]{2,1,0:T(8,128)(2,1)S(1)}, u32[]{:S(2)}) copy-start(bf16[3,656,128]{2,1,0:T(8,128)(2,1)S(1)} %pad_maximum_fusion.given.refs_0_) | copy-start | bytes 1511428
  7.2 15.4 %collective-permute-start.3 = (bf16[3,656,128]{2,1,0:T(8,128)(2,1)S(1)}, bf16[3,656,128]{2,1,0:T(8,128)(2,1)S(1)}, u32[]{:S(2)}, u32[]{:S(2)}) collective-permute-start(bf16[3,656,128]{2,1,0:T(8,128)(2,1)S(1)} %pad_maximum_fusion.given.refs_0_), channel_id=1, source_target_pairs={{0,3},{1,2},{2,1},{3,0},{4,7},{5,6},{6,5},{7,4},{8,11},{9,10},{10,... | collective-permute-start | bytes 1511432 | tf_op jit(solution)/shard_map/ppermute | solution.py:471
  9.7 22.2 %collective-permute-start.2 = (bf16[3,656,128]{2,1,0:T(8,128)(2,1)S(1)}, bf16[3,656,128]{2,1,0:T(8,128)(2,1)S(1)}, u32[]{:S(2)}, u32[]{:S(2)}) collective-permute-start(bf16[3,656,128]{2,1,0:T(8,128)(2,1)S(1)} %pad_maximum_fusion.given.refs_0_), channel_id=1, source_target_pairs={{0,2},{1,3},{2,0},{3,1},{4,6},{5,7},{6,4},{7,5},{8,10},{9,11},{10,... | collective-permute-start | bytes 1511432 | tf_op jit(solution)/shard_map/ppermute | solution.py:471
  10.2 21.8 %collective-permute-start.1 = (bf16[3,656,128]{2,1,0:T(8,128)(2,1)S(1)}, bf16[3,656,128]{2,1,0:T(8,128)(2,1)S(1)}, u32[]{:S(2)}, u32[]{:S(2)}) collective-permute-start(bf16[3,656,128]{2,1,0:T(8,128)(2,1)S(1)} %pad_maximum_fusion.given.refs_0_), channel_id=1, source_target_pairs={{0,1},{1,0},{2,3},{3,2},{4,5},{5,4},{6,7},{7,6},{8,9},{9,8},{10,11... | collective-permute-start | bytes 1511432 | tf_op jit(solution)/shard_map/ppermute | solution.py:471
  10.7 26.4 %collective-permute-start = (bf16[3,656,128]{2,1,0:T(8,128)(2,1)S(1)}, bf16[3,656,128]{2,1,0:T(8,128)(2,1)S(1)}, u32[]{:S(2)}, u32[]{:S(2)}) collective-permute-start(bf16[3,656,128]{2,1,0:T(8,128)(2,1)S(1)} %pad_maximum_fusion.given.refs_0_), channel_id=1, source_target_pairs={{0,16},{1,17},{2,18},{3,19},{4,20},{5,21},{6,22},{7,23},{8,24},{9,... | collective-permute-start | bytes 1511432 | tf_op jit(solution)/shard_map/ppermute | solution.py:471
  22.6 19.5 %copy-start.6 = (bf16[3,656,128]{2,1,0:T(8,128)(2,1)}, bf16[3,656,128]{2,1,0:T(8,128)(2,1)S(1)}, u32[]{:S(2)}) copy-start(bf16[3,656,128]{2,1,0:T(8,128)(2,1)S(1)} %collective-permute-done.3.refs_3_) | copy-start | bytes 1511428
  22.6 19.7 %collective-permute-start.8 = (bf16[2,1,512,512]{3,2,1,0:T(8,128)(2,1)}, bf16[2,1,512,512]{3,2,1,0:T(8,128)(2,1)}, u32[]{:S(2)}, u32[]{:S(2)}) collective-permute-start(bf16[2,1,512,512]{3,2,1,0:T(8,128)(2,1)} %refs_4_.1), channel_id=1, source_target_pairs={{0,4},{1,5},{2,6},{3,7},{4,0},{5,1},{6,2},{7,3},{8,12},{9,13},{10,... | collective-permute-start | bytes 3145736 | tf_op jit(solution)/shard_map/ppermute | solution.py:471
  31.9 15.6 %copy-start.7 = (bf16[3,656,128]{2,1,0:T(8,128)(2,1)}, bf16[3,656,128]{2,1,0:T(8,128)(2,1)S(1)}, u32[]{:S(2)}) copy-start(bf16[3,656,128]{2,1,0:T(8,128)(2,1)S(1)} %collective-permute-done.2.refs_2_) | copy-start | bytes 1511428
  32.0 5.9 %copy-start.8 = (bf16[3,656,128]{2,1,0:T(8,128)(2,1)}, bf16[3,656,128]{2,1,0:T(8,128)(2,1)S(1)}, u32[]{:S(2)}) copy-start(bf16[3,656,128]{2,1,0:T(8,128)(2,1)S(1)} %collective-permute-done.1.refs_1_) | copy-start | bytes 1511428
  37.1 24.5 %copy-start.1 = (bf16[3,656,128]{2,1,0:T(8,128)(2,1)}, bf16[3,656,128]{2,1,0:T(8,128)(2,1)S(1)}, u32[]{:S(2)}) copy-start(bf16[3,656,128]{2,1,0:T(8,128)(2,1)S(1)} %collective-permute-done.given.refs_0_.refs_4_) | copy-start | bytes 1511428
  37.9 16.9 %copy-start.3 = (bf16[2,1,512,512]{3,2,1,0:T(8,128)(2,1)}, bf16[2,1,512,512]{3,2,1,0:T(8,128)(2,1)S(1)}, u32[]{:S(2)}) copy-start(bf16[2,1,512,512]{3,2,1,0:T(8,128)(2,1)S(1)} %collective-permute-done.4.refs_6_) | copy-start | bytes 3145732
  37.9 4.4 %collective-permute-start.9 = (bf16[2,1,512,512]{3,2,1,0:T(8,128)(2,1)S(1)}, bf16[2,1,512,512]{3,2,1,0:T(8,128)(2,1)}, u32[]{:S(2)}, u32[]{:S(2)}) collective-permute-start(bf16[2,1,512,512]{3,2,1,0:T(8,128)(2,1)S(1)} %collective-permute-done.4.refs_6_), channel_id=1, source_target_pairs={{0,4},{1,5},{2,6},{3,7},{4,0},{5,1},{6,2},{7,3},{8,12},{9,13},{10,... | collective-permute-start | bytes 3145736 | tf_op jit(solution)/shard_map/ppermute | solution.py:471
  38.6 23.0 %collective-permute-start.7 = (bf16[3,656,128]{2,1,0:T(8,128)(2,1)S(1)}, bf16[3,656,128]{2,1,0:T(8,128)(2,1)}, u32[]{:S(2)}, u32[]{:S(2)}) collective-permute-start(bf16[3,656,128]{2,1,0:T(8,128)(2,1)S(1)} %collective-permute-done.given.refs_0_.refs_4_), channel_id=1, source_target_pairs={{0,3},{1,2},{2,1},{3,0},{4,7},{5,6},{6,5},{7,4},{8,11},{9,10},{10,... | collective-permute-start | bytes 1511432 | tf_op jit(solution)/shard_map/ppermute | solution.py:471
  41.2 23.0 %collective-permute-start.6 = (bf16[3,656,128]{2,1,0:T(8,128)(2,1)S(1)}, bf16[3,656,128]{2,1,0:T(8,128)(2,1)}, u32[]{:S(2)}, u32[]{:S(2)}) collective-permute-start(bf16[3,656,128]{2,1,0:T(8,128)(2,1)S(1)} %collective-permute-done.given.refs_0_.refs_4_), channel_id=1, source_target_pairs={{0,2},{1,3},{2,0},{3,1},{4,6},{5,7},{6,4},{7,5},{8,10},{9,11},{10,... | collective-permute-start | bytes 1511432 | tf_op jit(solution)/shard_map/ppermute | solution.py:471
  41.7 22.8 %collective-permute-start.5 = (bf16[3,656,128]{2,1,0:T(8,128)(2,1)S(1)}, bf16[3,656,128]{2,1,0:T(8,128)(2,1)}, u32[]{:S(2)}, u32[]{:S(2)}) collective-permute-start(bf16[3,656,128]{2,1,0:T(8,128)(2,1)S(1)} %collective-permute-done.given.refs_0_.refs_4_), channel_id=1, source_target_pairs={{0,1},{1,0},{2,3},{3,2},{4,5},{5,4},{6,7},{7,6},{8,9},{9,8},{10,11... | collective-permute-start | bytes 1511432 | tf_op jit(solution)/shard_map/ppermute | solution.py:471
  42.3 22.2 %collective-permute-start.11 = (bf16[3,128,512]{2,1,0:T(8,128)(2,1)S(1)}, bf16[3,128,512]{2,1,0:T(8,128)(2,1)}, u32[]{:S(2)}, u32[]{:S(2)}) collective-permute-start(bf16[3,128,512]{2,1,0:T(8,128)(2,1)S(1)} %shard_map.96.own), channel_id=1, source_target_pairs={{0,24},{1,25},{2,26},{3,27},{4,28},{5,29},{6,30},{7,31},{8,16},{9,... | collective-permute-start | bytes 1179656 | tf_op jit(solution)/shard_map/ppermute | solution.py:471
  46.1 18.4 %collective-permute-start.10 = (bf16[3,128,512]{2,1,0:T(8,128)(2,1)S(1)}, bf16[3,128,512]{2,1,0:T(8,128)(2,1)}, u32[]{:S(2)}, u32[]{:S(2)}) collective-permute-start(bf16[3,128,512]{2,1,0:T(8,128)(2,1)S(1)} %shard_map.96.own), channel_id=1, source_target_pairs={{0,8},{1,9},{2,10},{3,11},{4,12},{5,13},{6,14},{7,15},{8,0},{9,1},... | collective-permute-start | bytes 1179656 | tf_op jit(solution)/shard_map/ppermute | solution.py:471
  54.8 9.7 %copy-start.2 = (bf16[6,128,512]{2,1,0:T(8,128)(2,1)}, bf16[6,128,512]{2,1,0:T(8,128)(2,1)S(1)}, u32[]{:S(2)}) copy-start(bf16[6,128,512]{2,1,0:T(8,128)(2,1)S(1)} %shard_map.97.refs_8_) | copy-start | bytes 2359300
  64.5 7.5 %collective-permute-start.12 = (bf16[6,128,512]{2,1,0:T(8,128)(2,1)S(1)}, bf16[6,128,512]{2,1,0:T(8,128)(2,1)S(1)}, u32[]{:S(2)}, u32[]{:S(2)}) collective-permute-start(bf16[6,128,512]{2,1,0:T(8,128)(2,1)S(1)} %shard_map.97.refs_8_), channel_id=1, source_target_pairs={{0,4},{1,5},{2,6},{3,7},{4,0},{5,1},{6,2},{7,3},{8,12},{9,13},{10,... | collective-permute-start | bytes 2359304 | tf_op jit(solution)/shard_map/ppermute | solution.py:471
  64.6 7.4 %collective-permute-start.13 = (bf16[3,128,512]{2,1,0:T(8,128)(2,1)}, bf16[3,128,512]{2,1,0:T(8,128)(2,1)S(1)}, u32[]{:S(2)}, u32[]{:S(2)}) collective-permute-start(bf16[3,128,512]{2,1,0:T(8,128)(2,1)} %collective-permute-done.10.refs_9_), channel_id=1, source_target_pairs={{0,4},{1,5},{2,6},{3,7},{4,0},{5,1},{6,2},{7,3},{8,12},{9,13},{10,... | collective-permute-start | bytes 1179656 | tf_op jit(solution)/shard_map/ppermute | solution.py:471
  65.1 6.9 %collective-permute-start.14 = (bf16[3,128,512]{2,1,0:T(8,128)(2,1)}, bf16[3,128,512]{2,1,0:T(8,128)(2,1)S(1)}, u32[]{:S(2)}, u32[]{:S(2)}) collective-permute-start(bf16[3,128,512]{2,1,0:T(8,128)(2,1)} %collective-permute-done.11.refs_10_), channel_id=1, source_target_pairs={{0,4},{1,5},{2,6},{3,7},{4,0},{5,1},{6,2},{7,3},{8,12},{9,13},{10,... | collective-permute-start | bytes 1179656 | tf_op jit(solution)/shard_map/ppermute | solution.py:471
  72.0 0.8 copy-start.14
  72.0 0.9 copy-start.15
  72.0 1.2 copy-start.13
  87.0 5.5 %copy-start.4 = (f32[384,128]{1,0:T(8,128)S(1)}, f32[384,128]{1,0:T(8,128)}, u32[]{:S(2)}) copy-start(f32[384,128]{1,0:T(8,128)} %param.8) | copy-start | bytes 589828
  87.0 5.5 %copy-start.12 = (f32[384]{0:T(512)S(1)}, f32[384]{0:T(512)}, u32[]{:S(2)}) copy-start(f32[384]{0:T(512)} %param.9) | copy-start | bytes 4612
  87.0 2.8 %collective-permute-start.15 = (bf16[12,128,128]{2,1,0:T(8,128)(2,1)}, bf16[12,128,128]{2,1,0:T(8,128)(2,1)S(1)}, u32[]{:S(2)}, u32[]{:S(2)}) collective-permute-start(bf16[12,128,128]{2,1,0:T(8,128)(2,1)} %get-tuple-element.66), channel_id=1, source_target_pairs={{0,4},{1,5},{2,6},{3,7},{4,0},{5,1},{6,2},{7,3},{8,12},{9,13},{10,... | collective-permute-start | bytes 1179656 | tf_op jit(solution)/shard_map/ppermute | solution.py:471
  91.2 7.2 %collective-permute-start.16 = (bf16[2,3,128,128]{3,2,1,0:T(8,128)(2,1)S(1)}, bf16[2,3,128,128]{3,2,1,0:T(8,128)(2,1)S(1)}, u32[]{:S(2)}, u32[]{:S(2)}) collective-permute-start(bf16[2,3,128,128]{3,2,1,0:T(8,128)(2,1)S(1)} %pad_maximum_fusion.1), channel_id=1, source_target_pairs={{0,8},{1,9},{2,10},{3,11},{4,12},{5,13},{6,14},{7,15},{8,0},{9,1},... | collective-permute-start | bytes 589832 | tf_op jit(solution)/shard_map/ppermute | solution.py:471
  98.5 11.5 %collective-permute-start.17 = (bf16[2,3,128,128]{3,2,1,0:T(8,128)(2,1)S(1)}, bf16[2,3,128,128]{3,2,1,0:T(8,128)(2,1)S(1)}, u32[]{:S(2)}, u32[]{:S(2)}) collective-permute-start(bf16[2,3,128,128]{3,2,1,0:T(8,128)(2,1)S(1)} %fusion), channel_id=1, source_target_pairs={{0,16},{1,17},{2,18},{3,19},{4,20},{5,21},{6,22},{7,23},{8,24},{9,... | collective-permute-start | bytes 589832 | tf_op jit(solution)/shard_map/ppermute | solution.py:471
  110.1 15.9 %copy-start.5 = (bf16[2,3,128,128]{3,2,1,0:T(8,128)(2,1)}, bf16[2,3,128,128]{3,2,1,0:T(8,128)(2,1)S(1)}, u32[]{:S(2)}) copy-start(bf16[2,3,128,128]{3,2,1,0:T(8,128)(2,1)S(1)} %get-tuple-element.72.refs_0_) | copy-start | bytes 589828
  110.1 7.8 %collective-permute-start.20 = (bf16[2,3,128,128]{3,2,1,0:T(8,128)(2,1)S(1)}, bf16[2,3,128,128]{3,2,1,0:T(8,128)(2,1)S(1)}, u32[]{:S(2)}, u32[]{:S(2)}) collective-permute-start(bf16[2,3,128,128]{3,2,1,0:T(8,128)(2,1)S(1)} %get-tuple-element.72.refs_0_), channel_id=1, source_target_pairs={{0,3},{1,2},{2,1},{3,0},{4,7},{5,6},{6,5},{7,4},{8,11},{9,10},{10,... | collective-permute-start | bytes 589832 | tf_op jit(solution)/shard_map/ppermute | solution.py:471
  113.1 11.0 %collective-permute-start.19 = (bf16[2,3,128,128]{3,2,1,0:T(8,128)(2,1)S(1)}, bf16[2,3,128,128]{3,2,1,0:T(8,128)(2,1)S(1)}, u32[]{:S(2)}, u32[]{:S(2)}) collective-permute-start(bf16[2,3,128,128]{3,2,1,0:T(8,128)(2,1)S(1)} %get-tuple-element.72.refs_0_), channel_id=1, source_target_pairs={{0,2},{1,3},{2,0},{3,1},{4,6},{5,7},{6,4},{7,5},{8,10},{9,11},{10,... | collective-permute-start | bytes 589832 | tf_op jit(solution)/shard_map/ppermute | solution.py:471
  116.5 9.5 %collective-permute-start.18 = (bf16[2,3,128,128]{3,2,1,0:T(8,128)(2,1)S(1)}, bf16[2,3,128,128]{3,2,1,0:T(8,128)(2,1)S(1)}, u32[]{:S(2)}, u32[]{:S(2)}) collective-permute-start(bf16[2,3,128,128]{3,2,1,0:T(8,128)(2,1)S(1)} %get-tuple-element.72.refs_0_), channel_id=1, source_target_pairs={{0,1},{1,0},{2,3},{3,2},{4,5},{5,4},{6,7},{7,6},{8,9},{9,8},{10,11... | collective-permute-start | bytes 589832 | tf_op jit(solution)/shard_map/ppermute | solution.py:471
  117.9 8.1 %copy-start.9 = (bf16[2,3,128,128]{3,2,1,0:T(8,128)(2,1)}, bf16[2,3,128,128]{3,2,1,0:T(8,128)(2,1)S(1)}, u32[]{:S(2)}) copy-start(bf16[2,3,128,128]{3,2,1,0:T(8,128)(2,1)S(1)} %collective-permute-done.20.refs_3_) | copy-start | bytes 589828
  124.1 1.9 %copy-start.10 = (bf16[2,3,128,128]{3,2,1,0:T(8,128)(2,1)}, bf16[2,3,128,128]{3,2,1,0:T(8,128)(2,1)S(1)}, u32[]{:S(2)}) copy-start(bf16[2,3,128,128]{3,2,1,0:T(8,128)(2,1)S(1)} %collective-permute-done.19.refs_2_) | copy-start | bytes 589828
  126.0 0.7 copy-start.11
  133.1 2.0 %collective-permute-start.21 = (bf16[12,128,128]{2,1,0:T(8,128)(2,1)}, bf16[12,128,128]{2,1,0:T(8,128)(2,1)S(1)}, u32[]{:S(2)}, u32[]{:S(2)}) collective-permute-start(bf16[12,128,128]{2,1,0:T(8,128)(2,1)} %get-tuple-element.69), channel_id=1, source_target_pairs={{0,4},{1,5},{2,6},{3,7},{4,0},{5,1},{6,2},{7,3},{8,12},{9,13},{10,... | collective-permute-start | bytes 1179656 | tf_op jit(solution)/shard_map/ppermute | solution.py:471
  136.4 6.3 %collective-permute-start.22 = (bf16[3,128,128]{2,1,0:T(8,128)(2,1)S(1)}, bf16[3,128,128]{2,1,0:T(8,128)(2,1)S(1)}, u32[]{:S(2)}, u32[]{:S(2)}) collective-permute-start(bf16[3,128,128]{2,1,0:T(8,128)(2,1)S(1)} %get-tuple-element.78), channel_id=1, source_target_pairs={{0,8},{1,9},{2,10},{3,11},{4,12},{5,13},{6,14},{7,15},{8,0},{9,1},... | collective-permute-start | bytes 294920 | tf_op jit(solution)/shard_map/ppermute | solution.py:471
  136.5 7.6 %collective-permute-start.24 = (bf16[3,128,128]{2,1,0:T(8,128)(2,1)S(1)}, bf16[3,128,128]{2,1,0:T(8,128)(2,1)S(1)}, u32[]{:S(2)}, u32[]{:S(2)}) collective-permute-start(bf16[3,128,128]{2,1,0:T(8,128)(2,1)S(1)} %get-tuple-element.79), channel_id=1, source_target_pairs={{0,24},{1,25},{2,26},{3,27},{4,28},{5,29},{6,30},{7,31},{8,16},{9,... | collective-permute-start | bytes 294920 | tf_op jit(solution)/shard_map/ppermute | solution.py:471
  138.2 10.7 %collective-permute-start.23 = (bf16[3,128,128]{2,1,0:T(8,128)(2,1)S(1)}, bf16[3,128,128]{2,1,0:T(8,128)(2,1)S(1)}, u32[]{:S(2)}, u32[]{:S(2)}) collective-permute-start(bf16[3,128,128]{2,1,0:T(8,128)(2,1)S(1)} %get-tuple-element.80), channel_id=1, source_target_pairs={{0,16},{1,17},{2,18},{3,19},{4,20},{5,21},{6,22},{7,23},{8,24},{9,... | collective-permute-start | bytes 294920 | tf_op jit(solution)/shard_map/ppermute | solution.py:471

commit v11 on v10

--- a/solution.py
+++ b/solution.py
@@ -28,6 +28,7 @@
         self.slots = 2 * self.near * slots_dev
         self.unroll = unroll
         self.vmem = 60 * mib
+        self.vmem_sums = (50 if unroll > 1 else 60) * mib
         most = self.owners * tile_max + self.inputs * (unroll - 1) + unroll
         self.groups = -(-most // (unroll * chunk_groups)) * chunk_groups
 
@@ -263,7 +264,7 @@
     given_out = [refs.pop(0) for _ in range(2 * (1 + len(lines)))]
     given_projected = [refs.pop(0) for _ in range(lay.owners)]
     own_sum, other_sum, tiles_out = refs[:3]
-    left, projected, rounded, tiles, total, sent, sems, sum_sems, in_sems, out_sems = refs[3:]
+    left, projected, rounded, tiles, total, sems, in_sems, out_sems = refs[3:]
     copies = []
 
     def fetch(source, target):
@@ -336,7 +337,7 @@
             store(chunk).start()
 
     add_products(lay, used - 1, group_input, entries, tiles, rounded, total)
-    give_sums(lay, total, sent, own_sum, other_sum, sum_sems)
+    give_sums(lay, total, own_sum, other_sum)
     for chunk in range(lay.groups // chunk_groups):
 
         @pl.when(used > chunk * chunk_groups)
@@ -344,20 +345,16 @@
             store(chunk).wait()
 
 
-def give_sums(lay, total, sent, own_sum, other_sum, sems):
+def give_sums(lay, total, own_sum, other_sum):
     own = lay.places * lay.blocks
-    for_own = pltpu.make_async_copy(total.at[pl.ds(0, own)], own_sum, sems.at[0])
-    for_own.start()
-    sent[...] = total[own : 2 * own].astype(jnp.bfloat16)
-    for_other = pltpu.make_async_copy(sent, other_sum, sems.at[1])
-    for_other.start()
-    for_own.wait()
-    for_other.wait()
+    own_sum[...] = total[0:own]
+    other_sum[...] = total[own : 2 * own].astype(jnp.bfloat16)
 
 
 def make_tiles(lay, plan, inputs, outputs, projected):
     smem = pl.BlockSpec(memory_space=pltpu.SMEM)
     hbm = pl.BlockSpec(memory_space=pl.ANY)
+    vmem = pl.BlockSpec(memory_space=pltpu.VMEM)
     own = lay.places * lay.blocks
     sums = jax.ShapeDtypeStruct((own, lay.side, lay.width), jnp.float32)
     sent = jax.ShapeDtypeStruct((own, lay.side, lay.width), jnp.bfloat16)
@@ -366,20 +363,18 @@
         functools.partial(tiles_kernel, lay),
         out_shape=(sums, sent, jax.ShapeDtypeStruct(tiles, jnp.bfloat16)),
         in_specs=[smem] * 4 + [hbm] * (len(inputs) + len(outputs) + len(projected)),
-        out_specs=(hbm,) * 3,
+        out_specs=(vmem, vmem, hbm),
         scratch_shapes=[
             pltpu.VMEM((lay.outputs, lay.side, lay.pairs), jnp.bfloat16),
             pltpu.VMEM((lay.inputs, lay.pairs, lay.points * lay.side), jnp.bfloat16),
             pltpu.VMEM((lay.inputs, lay.side, lay.width), jnp.bfloat16),
             pltpu.VMEM(tiles, jnp.bfloat16),
             pltpu.VMEM((lay.outputs + 1, lay.side, lay.width), jnp.float32),
-            pltpu.VMEM((own, lay.side, lay.width), jnp.bfloat16),
             pltpu.SemaphoreType.DMA((len(inputs) + 2 * lay.places,)),
-            pltpu.SemaphoreType.DMA((2,)),
             pltpu.SemaphoreType.DMA((lay.inputs,)),
             pltpu.SemaphoreType.DMA((lay.groups // chunk_groups,)),
         ],
-        compiler_params=pltpu.CompilerParams(vmem_limit_bytes=lay.vmem),
+        compiler_params=pltpu.CompilerParams(vmem_limit_bytes=lay.vmem_sums),
         cost_estimate=pl.CostEstimate(flops=4_000_000_000, bytes_accessed=30_000_000, transcendentals=0),
     )(plan[0], *plan[2:], *inputs, *outputs, *projected)
 
@@ -387,7 +382,7 @@
 def apply_kernel(lay, sizes, group_input, entries, tiles_in, *refs):
     given_vec = refs[: lay.cols]
     own_sum, other_sum = refs[lay.cols : lay.cols + 2]
-    rounded, tiles, total, sent, sems, sum_sems, out_sems = refs[lay.cols + 2 :]
+    rounded, tiles, total, sems, out_sems = refs[lay.cols + 2 :]
     used = sizes[0]
     span = chunk_groups * lay.unroll
 
@@ -421,12 +416,13 @@
         return carry
 
     lax.fori_loop(1, used, group_step, 0)
-    give_sums(lay, total, sent, own_sum, other_sum, sum_sems)
+    give_sums(lay, total, own_sum, other_sum)
 
 
 def apply_tiles(lay, plan, tiles, rounded):
     smem = pl.BlockSpec(memory_space=pltpu.SMEM)
     hbm = pl.BlockSpec(memory_space=pl.ANY)
+    vmem = pl.BlockSpec(memory_space=pltpu.VMEM)
     own = lay.places * lay.blocks
     sums = jax.ShapeDtypeStruct((own, lay.side, lay.width), jnp.float32)
     sent = jax.ShapeDtypeStruct((own, lay.side, lay.width), jnp.bfloat16)
@@ -434,17 +430,15 @@
         functools.partial(apply_kernel, lay),
         out_shape=(sums, sent),
         in_specs=[smem] * 3 + [hbm] * (1 + len(rounded)),
-        out_specs=(hbm, hbm),
+        out_specs=(vmem, vmem),
         scratch_shapes=[
             pltpu.VMEM((lay.inputs, lay.side, lay.width), jnp.bfloat16),
             pltpu.VMEM(tiles.shape, jnp.bfloat16),
             pltpu.VMEM((lay.outputs + 1, lay.side, lay.width), jnp.float32),
-            pltpu.VMEM((own, lay.side, lay.width), jnp.bfloat16),
             pltpu.SemaphoreType.DMA((len(rounded) * lay.owners,)),
-            pltpu.SemaphoreType.DMA((2,)),
             pltpu.SemaphoreType.DMA((lay.groups // chunk_groups,)),
         ],
-        compiler_params=pltpu.CompilerParams(vmem_limit_bytes=lay.vmem),
+        compiler_params=pltpu.CompilerParams(vmem_limit_bytes=lay.vmem_sums),
         cost_estimate=pl.CostEstimate(flops=400_000_000, bytes_accessed=4_000_000, transcendentals=0),
     )(*plan[2:], tiles, *rounded)
 

time: 152 us -> 148 us (0.974)
  starting transfers between devices: 33.1 us -> 36.8 us
  Pallas kernels: 41.4 us -> 38.5 us
  local copies, waits for them, and re-layouts: 2.62 us -> 0.8 us
  waiting for transfers between devices: 62.5 us -> 60.9 us
    ppermute x25, starting transfers between devices: 33.1 us -> 36.8 us  [move(): return lax.ppermute(array, axes, pairs_list)]
    pallas_call x1, Pallas kernels: 6.49 us -> 4.61 us  [apply_tiles(): pl.pallas_call(functools.partial(apply_kernel, lay), out_shape=(sums, sen...]
    unnamed x32, local copies, waits for them, and re-layouts: 1.89 us -> 0.07 us
    ppermute x25, waiting for transfers between devices: 62.5 us -> 60.9 us  [move(): return lax.ppermute(array, axes, pairs_list)]
  transfers between devices with their start and end apart: 25 -> 25, of which waited for: 16 -> 16; matrix products, arithmetic and copies ran while one was open for 4% -> 4% of each run, Pallas kernels for 14% -> 15%
where the time goes in v11:
time: 148 us; the launch traced here: 146 us
  waiting for transfers between devices  60.9 us (41%)
  Pallas kernels  38.5 us (26%)
  starting transfers between devices  36.8 us (25%)
  other arithmetic  7.3 us (5%)
  between operations  1.69 us (1%)
    ppermute x25, waiting for transfers between devices, move(): return lax.ppermute(array, axes, pairs_list)  60.9 us
    ppermute x25, starting transfers between devices, move(): return lax.ppermute(array, axes, pairs_list)  36.8 us
    pallas_call x2, Pallas kernels, project(): pl.pallas_call(functools.partial(project_kernel, lay, owner), out_shape=j...  14.4 us
    pallas_call x1, Pallas kernels, make_tiles(): pl.pallas_call(functools.partial(tiles_kernel, lay), out_shape=(sums, sen...  12.4 us
    pallas_call x1, Pallas kernels, make_plan(): pl.pallas_call(functools.partial(plan_kernel, lay), out_shape=tuple((jax....  6.77 us
    pallas_call x1, Pallas kernels, apply_tiles(): pl.pallas_call(functools.partial(apply_kernel, lay), out_shape=(sums, sen...  4.61 us
  transfers between devices with their start and end apart: 25, of which 16 were waited for; matrix products, arithmetic and copies ran while one was open for 4% of the time, Pallas kernels for 15%

profile of v11, /device:TPU:0, one launch (start us, length us, event | category | flops | bytes accessed | tf_op | source)
XLA Modules:
  0.0 146.0 jit_solution(16386705861607510029)
XLA Ops:
  0.6 3.1 %collective-permute-start.4 = (bf16[2,1,512,512]{3,2,1,0:T(8,128)(2,1)}, bf16[2,1,512,512]{3,2,1,0:T(8,128)(2,1)}, u32[]{:S(2)}, u32[]{:S(2)}) collective-permute-start(bf16[2,1,512,512]{3,2,1,0:T(8,128)(2,1)} %refs_4_.1), channel_id=1, source_target_pairs={{0,8},{1,9},{2,10},{3,11},{4,12},{5,13},{6,14},{7,15},{8,0},{9,1},... | collective-permute-start | bytes 3145736 | tf_op jit(solution)/shard_map/ppermute | solution.py:465
  4.4 0.9 convert_element_type.40
  5.3 0.7 convert_bitcast_fusion.1
  6.1 1.0 pad_maximum_fusion.given.refs_0_
  7.2 2.5 %collective-permute-start.3 = (bf16[3,656,128]{2,1,0:T(8,128)(2,1)S(1)}, bf16[3,656,128]{2,1,0:T(8,128)(2,1)S(1)}, u32[]{:S(2)}, u32[]{:S(2)}) collective-permute-start(bf16[3,656,128]{2,1,0:T(8,128)(2,1)S(1)} %pad_maximum_fusion.given.refs_0_), channel_id=1, source_target_pairs={{0,3},{1,2},{2,1},{3,0},{4,7},{5,6},{6,5},{7,4},{8,11},{9,10},{10,... | collective-permute-start | bytes 1511432 | tf_op jit(solution)/shard_map/ppermute | solution.py:465
  9.7 0.5 collective-permute-start.2
  10.2 0.5 collective-permute-start.1
  10.7 2.6 %collective-permute-start = (bf16[3,656,128]{2,1,0:T(8,128)(2,1)S(1)}, bf16[3,656,128]{2,1,0:T(8,128)(2,1)S(1)}, u32[]{:S(2)}, u32[]{:S(2)}) collective-permute-start(bf16[3,656,128]{2,1,0:T(8,128)(2,1)S(1)} %pad_maximum_fusion.given.refs_0_), channel_id=1, source_target_pairs={{0,16},{1,17},{2,18},{3,19},{4,20},{5,21},{6,22},{7,23},{8,24},{9,... | collective-permute-start | bytes 1511432 | tf_op jit(solution)/shard_map/ppermute | solution.py:465
  13.3 9.3 %collective-permute-done.3.refs_3_ = bf16[3,656,128]{2,1,0:T(8,128)(2,1)S(1)} collective-permute-done((bf16[3,656,128]{2,1,0:T(8,128)(2,1)S(1)}, bf16[3,656,128]{2,1,0:T(8,128)(2,1)S(1)}, u32[]{:S(2)}, u32[]{:S(2)}) %collective-permute-start.3) | collective-permute-done | bytes 503840 | tf_op jit(solution)/shard_map/ppermute | solution.py:465
  22.6 9.3 %collective-permute-done.2.refs_2_ = bf16[3,656,128]{2,1,0:T(8,128)(2,1)S(1)} collective-permute-done((bf16[3,656,128]{2,1,0:T(8,128)(2,1)S(1)}, bf16[3,656,128]{2,1,0:T(8,128)(2,1)S(1)}, u32[]{:S(2)}, u32[]{:S(2)}) %collective-permute-start.2) | collective-permute-done | bytes 503840 | tf_op jit(solution)/shard_map/ppermute | solution.py:465
  32.0 5.2 %collective-permute-done.given.refs_0_.refs_4_ = bf16[3,656,128]{2,1,0:T(8,128)(2,1)S(1)} collective-permute-done((bf16[3,656,128]{2,1,0:T(8,128)(2,1)S(1)}, bf16[3,656,128]{2,1,0:T(8,128)(2,1)S(1)}, u32[]{:S(2)}, u32[]{:S(2)}) %collective-permute-start) | collective-permute-done | bytes 503840 | tf_op jit(solution)/shard_map/ppermute | solution.py:465
  37.1 0.8 collective-permute-done.4.refs_6_
  38.0 0.7 pad_add_fusion.1.ids
  38.7 2.6 %collective-permute-start.7 = (bf16[3,656,128]{2,1,0:T(8,128)(2,1)S(1)}, bf16[3,656,128]{2,1,0:T(8,128)(2,1)}, u32[]{:S(2)}, u32[]{:S(2)}) collective-permute-start(bf16[3,656,128]{2,1,0:T(8,128)(2,1)S(1)} %collective-permute-done.given.refs_0_.refs_4_), channel_id=1, source_target_pairs={{0,3},{1,2},{2,1},{3,0},{4,7},{5,6},{6,5},{7,4},{8,11},{9,10},{10,... | collective-permute-start | bytes 1511432 | tf_op jit(solution)/shard_map/ppermute | solution.py:465
  41.3 0.5 collective-permute-start.6
  41.8 0.4 collective-permute-start.5
  42.1 0.2 shard_map.96.own
  42.3 3.8 %collective-permute-start.11 = (bf16[3,128,512]{2,1,0:T(8,128)(2,1)S(1)}, bf16[3,128,512]{2,1,0:T(8,128)(2,1)}, u32[]{:S(2)}, u32[]{:S(2)}) collective-permute-start(bf16[3,128,512]{2,1,0:T(8,128)(2,1)S(1)} %shard_map.96.own), channel_id=1, source_target_pairs={{0,24},{1,25},{2,26},{3,27},{4,28},{5,29},{6,30},{7,31},{8,16},{9,... | collective-permute-start | bytes 1179656 | tf_op jit(solution)/shard_map/ppermute | solution.py:465
  46.2 1.3 pad_add_fusion.listed
  47.5 6.8 %shard_map.95 = (s32[24]{0:T(128)}, s32[26]{0:T(128)}, s32[4]{0:T(128)}, s32[72]{0:T(128)}, s32[288]{0:T(512)}) custom-call(s32[3]{0:T(128)} %pad_add_fusion.1.ids, s32[2,97]{1,0:T(2,128)} %pad_add_fusion.listed, s32[96]{0:T(128)} %fine.1, s32[8]{0:T(128)} %stored.1), custom_call_target="tpu_custom_call" | custom-call | bytes 20000000 | tf_op jit(solution)/shard_map/pallas_call | solution.py:138
  54.3 0.2 shard_map.97.refs_8_
  54.5 7.6 %shard_map.98.refs_14_ = bf16[12,512,256]{2,1,0:T(8,128)(2,1)} custom-call(s32[24]{0:T(128)} %get-tuple-element.37.slot_of, s32[26]{0:T(128)} %get-tuple-element.48.valid, s32[4]{0:T(128)} %get-tuple-element.38.sizes, bf16[3,656,128]{2,1,0:T(8,128)(2,1)} %copy-done, bf16[3,656,128]{2,1,0:T(8,128)(2,1)} %copy-done.8, bf16[3,656,128]{2,1,0:T(8,128)(2,1)} %copy-done.6, ...), custom_call_target="tpu_custom_call" | custom-call | flops 1000000000 | bytes 16000000 | tf_op jit(solution)/shard_map/pallas_call | solution.py:243
  62.2 2.1 %collective-permute-done.6.refs_2_.refs_6_ = bf16[3,656,128]{2,1,0:T(8,128)(2,1)} collective-permute-done((bf16[3,656,128]{2,1,0:T(8,128)(2,1)S(1)}, bf16[3,656,128]{2,1,0:T(8,128)(2,1)}, u32[]{:S(2)}, u32[]{:S(2)}) %collective-permute-start.6) | collective-permute-done | bytes 503840 | tf_op jit(solution)/shard_map/ppermute | solution.py:465
  64.3 0.3 collective-permute-done.5.refs_1_.refs_5_
  64.7 0.5 collective-permute-start.13
  65.3 6.8 %shard_map.99.refs_15_ = bf16[12,512,256]{2,1,0:T(8,128)(2,1)} custom-call(s32[24]{0:T(128)} %get-tuple-element.37.slot_of, s32[26]{0:T(128)} %get-tuple-element.48.valid, s32[4]{0:T(128)} %get-tuple-element.38.sizes, bf16[3,656,128]{2,1,0:T(8,128)(2,1)} %copy-done.2, bf16[3,656,128]{2,1,0:T(8,128)(2,1)} %collective-permute-done.5.refs_1_.refs_5_, ...), custom_call_target="tpu_custom_call" | custom-call | flops 1000000000 | bytes 16000000 | tf_op jit(solution)/shard_map/pallas_call | solution.py:243
  72.2 12.4 %shard_map.100 = (f32[12,128,128]{2,1,0:T(8,128)}, bf16[12,128,128]{2,1,0:T(8,128)(2,1)S(1)}, bf16[288,128,128]{2,1,0:T(8,128)(2,1)}) custom-call(s32[24]{0:T(128)S(1)} %copy-done.12, s32[4]{0:T(128)S(1)} %copy-done.10, s32[72]{0:T(128)S(1)} %copy-done.13, s32[288]{0:T(512)S(1)} %copy-done.11, bf16[3,656,128]{2,1,0:T(8,128)(2,1)S(1)} %copy-done.1, ...), custom_call_target="tpu_custom_call" | custom-call | flops 4000000000 | bytes 30000000 | tf_op jit(solution)/shard_map/pallas_call | solution.py:362
  84.7 1.7 %collective-permute-done.15 = bf16[12,128,128]{2,1,0:T(8,128)(2,1)S(1)} collective-permute-done((bf16[12,128,128]{2,1,0:T(8,128)(2,1)S(1)}, bf16[12,128,128]{2,1,0:T(8,128)(2,1)S(1)}, u32[]{:S(2)}, u32[]{:S(2)}) %collective-permute-start.15) | collective-permute-done | bytes 393248 | tf_op jit(solution)/shard_map/ppermute | solution.py:465
  86.4 1.3 fusion.13
  87.7 3.2 %collective-permute-start.16 = (bf16[2,3,128,128]{3,2,1,0:T(8,128)(2,1)S(1)}, bf16[2,3,128,128]{3,2,1,0:T(8,128)(2,1)S(1)}, u32[]{:S(2)}, u32[]{:S(2)}) collective-permute-start(bf16[2,3,128,128]{3,2,1,0:T(8,128)(2,1)S(1)} %pad_maximum_fusion.1), channel_id=1, source_target_pairs={{0,8},{1,9},{2,10},{3,11},{4,12},{5,13},{6,14},{7,15},{8,0},{9,1},... | collective-permute-start | bytes 589832 | tf_op jit(solution)/shard_map/ppermute | solution.py:465
  90.9 0.1 fusion.6
  91.0 5.3 %collective-permute-done.16 = bf16[2,3,128,128]{3,2,1,0:T(8,128)(2,1)S(1)} collective-permute-done((bf16[2,3,128,128]{3,2,1,0:T(8,128)(2,1)S(1)}, bf16[2,3,128,128]{3,2,1,0:T(8,128)(2,1)S(1)}, u32[]{:S(2)}, u32[]{:S(2)}) %collective-permute-start.16) | collective-permute-done | bytes 196640 | tf_op jit(solution)/shard_map/ppermute | solution.py:465
  96.4 1.7 %collective-permute-start.17 = (bf16[2,3,128,128]{3,2,1,0:T(8,128)(2,1)S(1)}, bf16[2,3,128,128]{3,2,1,0:T(8,128)(2,1)S(1)}, u32[]{:S(2)}, u32[]{:S(2)}) collective-permute-start(bf16[2,3,128,128]{3,2,1,0:T(8,128)(2,1)S(1)} %fusion), channel_id=1, source_target_pairs={{0,16},{1,17},{2,18},{3,19},{4,20},{5,21},{6,22},{7,23},{8,24},{9,... | collective-permute-start | bytes 589832 | tf_op jit(solution)/shard_map/ppermute | solution.py:465
  98.1 10.1 %collective-permute-done.17 = bf16[2,3,128,128]{3,2,1,0:T(8,128)(2,1)S(1)} collective-permute-done((bf16[2,3,128,128]{3,2,1,0:T(8,128)(2,1)S(1)}, bf16[2,3,128,128]{3,2,1,0:T(8,128)(2,1)S(1)}, u32[]{:S(2)}, u32[]{:S(2)}) %collective-permute-start.17) | collective-permute-done | bytes 196640 | tf_op jit(solution)/shard_map/ppermute | solution.py:465
  108.2 6.9 %collective-permute-start.20 = (bf16[2,3,128,128]{3,2,1,0:T(8,128)(2,1)S(1)}, bf16[2,3,128,128]{3,2,1,0:T(8,128)(2,1)S(1)}, u32[]{:S(2)}, u32[]{:S(2)}) collective-permute-start(bf16[2,3,128,128]{3,2,1,0:T(8,128)(2,1)S(1)} %get-tuple-element.72.refs_0_), channel_id=1, source_target_pairs={{0,3},{1,2},{2,1},{3,0},{4,7},{5,6},{6,5},{7,4},{8,11},{9,10},{10,... | collective-permute-start | bytes 589832 | tf_op jit(solution)/shard_map/ppermute | solution.py:465
  115.1 4.1 %collective-permute-start.19 = (bf16[2,3,128,128]{3,2,1,0:T(8,128)(2,1)S(1)}, bf16[2,3,128,128]{3,2,1,0:T(8,128)(2,1)S(1)}, u32[]{:S(2)}, u32[]{:S(2)}) collective-permute-start(bf16[2,3,128,128]{3,2,1,0:T(8,128)(2,1)S(1)} %get-tuple-element.72.refs_0_), channel_id=1, source_target_pairs={{0,2},{1,3},{2,0},{3,1},{4,6},{5,7},{6,4},{7,5},{8,10},{9,11},{10,... | collective-permute-start | bytes 589832 | tf_op jit(solution)/shard_map/ppermute | solution.py:465
  119.3 5.8 %collective-permute-done.19.refs_2_ = bf16[2,3,128,128]{3,2,1,0:T(8,128)(2,1)S(1)} collective-permute-done((bf16[2,3,128,128]{3,2,1,0:T(8,128)(2,1)S(1)}, bf16[2,3,128,128]{3,2,1,0:T(8,128)(2,1)S(1)}, u32[]{:S(2)}, u32[]{:S(2)}) %collective-permute-start.19) | collective-permute-done | bytes 196640 | tf_op jit(solution)/shard_map/ppermute | solution.py:465
  125.1 1.0 collective-permute-done.18.refs_1_
  126.1 4.6 %shard_map.101 = (f32[12,128,128]{2,1,0:T(8,128)S(1)}, bf16[12,128,128]{2,1,0:T(8,128)(2,1)S(1)}) custom-call(s32[4]{0:T(128)S(1)} %copy-done.10, s32[72]{0:T(128)S(1)} %copy-done.13, s32[288]{0:T(512)S(1)} %copy-done.11, bf16[288,128,128]{2,1,0:T(8,128)(2,1)} %get-tuple-element.67.tiles_in, bf16[2,3,128,128]{3,2,1,0:T(8,128)(2,1)S(1)} %get-tuple-element.72.refs_0_, ...), custom_call_target="tpu_custom_call" | custom-call | flops 400000000 | bytes 4000000 | tf_op jit(solution)/shard_map/pallas_call | solution.py:429
  130.8 1.7 %collective-permute-done.21 = bf16[12,128,128]{2,1,0:T(8,128)(2,1)S(1)} collective-permute-done((bf16[12,128,128]{2,1,0:T(8,128)(2,1)S(1)}, bf16[12,128,128]{2,1,0:T(8,128)(2,1)S(1)}, u32[]{:S(2)}, u32[]{:S(2)}) %collective-permute-start.21) | collective-permute-done | bytes 393248 | tf_op jit(solution)/shard_map/ppermute | solution.py:465
  132.5 0.1 fusion.11
  132.8 2.5 %collective-permute-start.24 = (bf16[3,128,128]{2,1,0:T(8,128)(2,1)S(1)}, bf16[3,128,128]{2,1,0:T(8,128)(2,1)S(1)}, u32[]{:S(2)}, u32[]{:S(2)}) collective-permute-start(bf16[3,128,128]{2,1,0:T(8,128)(2,1)S(1)} %get-tuple-element.79), channel_id=1, source_target_pairs={{0,24},{1,25},{2,26},{3,27},{4,28},{5,29},{6,30},{7,31},{8,16},{9,... | collective-permute-start | bytes 294920 | tf_op jit(solution)/shard_map/ppermute | solution.py:465
  135.3 1.0 collective-permute-start.23
  136.3 0.7 slice.79
  137.0 0.7 collective-permute-done.22
  137.6 3.4 %collective-permute-done.24 = bf16[3,128,128]{2,1,0:T(8,128)(2,1)S(1)} collective-permute-done((bf16[3,128,128]{2,1,0:T(8,128)(2,1)S(1)}, bf16[3,128,128]{2,1,0:T(8,128)(2,1)S(1)}, u32[]{:S(2)}, u32[]{:S(2)}) %collective-permute-start.24) | collective-permute-done | bytes 98336 | tf_op jit(solution)/shard_map/ppermute | solution.py:465
  141.0 4.2 %collective-permute-done.23 = bf16[3,128,128]{2,1,0:T(8,128)(2,1)S(1)} collective-permute-done((bf16[3,128,128]{2,1,0:T(8,128)(2,1)S(1)}, bf16[3,128,128]{2,1,0:T(8,128)(2,1)S(1)}, u32[]{:S(2)}, u32[]{:S(2)}) %collective-permute-start.23) | collective-permute-done | bytes 98336 | tf_op jit(solution)/shard_map/ppermute | solution.py:465
  145.2 0.8 fusion.5
  (60 shorter events, 0.9 us)
Async XLA Ops:
  0.6 37.4 %collective-permute-start.4 = (bf16[2,1,512,512]{3,2,1,0:T(8,128)(2,1)}, bf16[2,1,512,512]{3,2,1,0:T(8,128)(2,1)}, u32[]{:S(2)}, u32[]{:S(2)}) collective-permute-start(bf16[2,1,512,512]{3,2,1,0:T(8,128)(2,1)} %refs_4_.1), channel_id=1, source_target_pairs={{0,8},{1,9},{2,10},{3,11},{4,12},{5,13},{6,14},{7,15},{8,0},{9,1},... | collective-permute-start | bytes 3145736 | tf_op jit(solution)/shard_map/ppermute | solution.py:465
  7.2 47.3 %copy-start = (bf16[3,656,128]{2,1,0:T(8,128)(2,1)}, bf16[3,656,128]{2,1,0:T(8,128)(2,1)S(1)}, u32[]{:S(2)}) copy-start(bf16[3,656,128]{2,1,0:T(8,128)(2,1)S(1)} %pad_maximum_fusion.given.refs_0_) | copy-start | bytes 1511428
  7.2 15.4 %collective-permute-start.3 = (bf16[3,656,128]{2,1,0:T(8,128)(2,1)S(1)}, bf16[3,656,128]{2,1,0:T(8,128)(2,1)S(1)}, u32[]{:S(2)}, u32[]{:S(2)}) collective-permute-start(bf16[3,656,128]{2,1,0:T(8,128)(2,1)S(1)} %pad_maximum_fusion.given.refs_0_), channel_id=1, source_target_pairs={{0,3},{1,2},{2,1},{3,0},{4,7},{5,6},{6,5},{7,4},{8,11},{9,10},{10,... | collective-permute-start | bytes 1511432 | tf_op jit(solution)/shard_map/ppermute | solution.py:465
  9.7 22.2 %collective-permute-start.2 = (bf16[3,656,128]{2,1,0:T(8,128)(2,1)S(1)}, bf16[3,656,128]{2,1,0:T(8,128)(2,1)S(1)}, u32[]{:S(2)}, u32[]{:S(2)}) collective-permute-start(bf16[3,656,128]{2,1,0:T(8,128)(2,1)S(1)} %pad_maximum_fusion.given.refs_0_), channel_id=1, source_target_pairs={{0,2},{1,3},{2,0},{3,1},{4,6},{5,7},{6,4},{7,5},{8,10},{9,11},{10,... | collective-permute-start | bytes 1511432 | tf_op jit(solution)/shard_map/ppermute | solution.py:465
  10.2 21.8 %collective-permute-start.1 = (bf16[3,656,128]{2,1,0:T(8,128)(2,1)S(1)}, bf16[3,656,128]{2,1,0:T(8,128)(2,1)S(1)}, u32[]{:S(2)}, u32[]{:S(2)}) collective-permute-start(bf16[3,656,128]{2,1,0:T(8,128)(2,1)S(1)} %pad_maximum_fusion.given.refs_0_), channel_id=1, source_target_pairs={{0,1},{1,0},{2,3},{3,2},{4,5},{5,4},{6,7},{7,6},{8,9},{9,8},{10,11... | collective-permute-start | bytes 1511432 | tf_op jit(solution)/shard_map/ppermute | solution.py:465
  10.7 26.4 %collective-permute-start = (bf16[3,656,128]{2,1,0:T(8,128)(2,1)S(1)}, bf16[3,656,128]{2,1,0:T(8,128)(2,1)S(1)}, u32[]{:S(2)}, u32[]{:S(2)}) collective-permute-start(bf16[3,656,128]{2,1,0:T(8,128)(2,1)S(1)} %pad_maximum_fusion.given.refs_0_), channel_id=1, source_target_pairs={{0,16},{1,17},{2,18},{3,19},{4,20},{5,21},{6,22},{7,23},{8,24},{9,... | collective-permute-start | bytes 1511432 | tf_op jit(solution)/shard_map/ppermute | solution.py:465
  22.6 31.9 %copy-start.4 = (bf16[3,656,128]{2,1,0:T(8,128)(2,1)}, bf16[3,656,128]{2,1,0:T(8,128)(2,1)S(1)}, u32[]{:S(2)}) copy-start(bf16[3,656,128]{2,1,0:T(8,128)(2,1)S(1)} %collective-permute-done.3.refs_3_) | copy-start | bytes 1511428
  22.6 19.7 %collective-permute-start.8 = (bf16[2,1,512,512]{3,2,1,0:T(8,128)(2,1)}, bf16[2,1,512,512]{3,2,1,0:T(8,128)(2,1)}, u32[]{:S(2)}, u32[]{:S(2)}) collective-permute-start(bf16[2,1,512,512]{3,2,1,0:T(8,128)(2,1)} %refs_4_.1), channel_id=1, source_target_pairs={{0,4},{1,5},{2,6},{3,7},{4,0},{5,1},{6,2},{7,3},{8,12},{9,13},{10,... | collective-permute-start | bytes 3145736 | tf_op jit(solution)/shard_map/ppermute | solution.py:465
  31.9 22.6 %copy-start.6 = (bf16[3,656,128]{2,1,0:T(8,128)(2,1)}, bf16[3,656,128]{2,1,0:T(8,128)(2,1)S(1)}, u32[]{:S(2)}) copy-start(bf16[3,656,128]{2,1,0:T(8,128)(2,1)S(1)} %collective-permute-done.2.refs_2_) | copy-start | bytes 1511428
  32.0 10.2 %copy-start.8 = (bf16[3,656,128]{2,1,0:T(8,128)(2,1)}, bf16[3,656,128]{2,1,0:T(8,128)(2,1)S(1)}, u32[]{:S(2)}) copy-start(bf16[3,656,128]{2,1,0:T(8,128)(2,1)S(1)} %collective-permute-done.1.refs_1_) | copy-start | bytes 1511428
  37.1 25.0 %copy-start.2 = (bf16[3,656,128]{2,1,0:T(8,128)(2,1)}, bf16[3,656,128]{2,1,0:T(8,128)(2,1)S(1)}, u32[]{:S(2)}) copy-start(bf16[3,656,128]{2,1,0:T(8,128)(2,1)S(1)} %collective-permute-done.given.refs_0_.refs_4_) | copy-start | bytes 1511428
  38.0 4.3 %collective-permute-start.9 = (bf16[2,1,512,512]{3,2,1,0:T(8,128)(2,1)}, bf16[2,1,512,512]{3,2,1,0:T(8,128)(2,1)}, u32[]{:S(2)}, u32[]{:S(2)}) collective-permute-start(bf16[2,1,512,512]{3,2,1,0:T(8,128)(2,1)} %collective-permute-done.4.refs_6_), channel_id=1, source_target_pairs={{0,4},{1,5},{2,6},{3,7},{4,0},{5,1},{6,2},{7,3},{8,12},{9,13},{10,... | collective-permute-start | bytes 3145736 | tf_op jit(solution)/shard_map/ppermute | solution.py:465
  38.7 23.6 %collective-permute-start.7 = (bf16[3,656,128]{2,1,0:T(8,128)(2,1)S(1)}, bf16[3,656,128]{2,1,0:T(8,128)(2,1)}, u32[]{:S(2)}, u32[]{:S(2)}) collective-permute-start(bf16[3,656,128]{2,1,0:T(8,128)(2,1)S(1)} %collective-permute-done.given.refs_0_.refs_4_), channel_id=1, source_target_pairs={{0,3},{1,2},{2,1},{3,0},{4,7},{5,6},{6,5},{7,4},{8,11},{9,10},{10,... | collective-permute-start | bytes 1511432 | tf_op jit(solution)/shard_map/ppermute | solution.py:465
  41.3 23.1 %collective-permute-start.6 = (bf16[3,656,128]{2,1,0:T(8,128)(2,1)S(1)}, bf16[3,656,128]{2,1,0:T(8,128)(2,1)}, u32[]{:S(2)}, u32[]{:S(2)}) collective-permute-start(bf16[3,656,128]{2,1,0:T(8,128)(2,1)S(1)} %collective-permute-done.given.refs_0_.refs_4_), channel_id=1, source_target_pairs={{0,2},{1,3},{2,0},{3,1},{4,6},{5,7},{6,4},{7,5},{8,10},{9,11},{10,... | collective-permute-start | bytes 1511432 | tf_op jit(solution)/shard_map/ppermute | solution.py:465
  41.8 22.8 %collective-permute-start.5 = (bf16[3,656,128]{2,1,0:T(8,128)(2,1)S(1)}, bf16[3,656,128]{2,1,0:T(8,128)(2,1)}, u32[]{:S(2)}, u32[]{:S(2)}) collective-permute-start(bf16[3,656,128]{2,1,0:T(8,128)(2,1)S(1)} %collective-permute-done.given.refs_0_.refs_4_), channel_id=1, source_target_pairs={{0,1},{1,0},{2,3},{3,2},{4,5},{5,4},{6,7},{7,6},{8,9},{9,8},{10,11... | collective-permute-start | bytes 1511432 | tf_op jit(solution)/shard_map/ppermute | solution.py:465
  42.3 22.3 %collective-permute-start.11 = (bf16[3,128,512]{2,1,0:T(8,128)(2,1)S(1)}, bf16[3,128,512]{2,1,0:T(8,128)(2,1)}, u32[]{:S(2)}, u32[]{:S(2)}) collective-permute-start(bf16[3,128,512]{2,1,0:T(8,128)(2,1)S(1)} %shard_map.96.own), channel_id=1, source_target_pairs={{0,24},{1,25},{2,26},{3,27},{4,28},{5,29},{6,30},{7,31},{8,16},{9,... | collective-permute-start | bytes 1179656 | tf_op jit(solution)/shard_map/ppermute | solution.py:465
  46.2 18.5 %collective-permute-start.10 = (bf16[3,128,512]{2,1,0:T(8,128)(2,1)S(1)}, bf16[3,128,512]{2,1,0:T(8,128)(2,1)}, u32[]{:S(2)}, u32[]{:S(2)}) collective-permute-start(bf16[3,128,512]{2,1,0:T(8,128)(2,1)S(1)} %shard_map.96.own), channel_id=1, source_target_pairs={{0,8},{1,9},{2,10},{3,11},{4,12},{5,13},{6,14},{7,15},{8,0},{9,1},... | collective-permute-start | bytes 1179656 | tf_op jit(solution)/shard_map/ppermute | solution.py:465
  54.5 10.2 %copy-start.3 = (bf16[6,128,512]{2,1,0:T(8,128)(2,1)}, bf16[6,128,512]{2,1,0:T(8,128)(2,1)S(1)}, u32[]{:S(2)}) copy-start(bf16[6,128,512]{2,1,0:T(8,128)(2,1)S(1)} %shard_map.97.refs_8_) | copy-start | bytes 2359300
  62.1 9.9 %copy-start.1 = (bf16[3,656,128]{2,1,0:T(8,128)(2,1)S(1)}, bf16[3,656,128]{2,1,0:T(8,128)(2,1)}, u32[]{:S(2)}) copy-start(bf16[3,656,128]{2,1,0:T(8,128)(2,1)} %copy-done) | copy-start | bytes 1511428
  62.1 9.9 %copy-start.5 = (bf16[3,656,128]{2,1,0:T(8,128)(2,1)S(1)}, bf16[3,656,128]{2,1,0:T(8,128)(2,1)}, u32[]{:S(2)}) copy-start(bf16[3,656,128]{2,1,0:T(8,128)(2,1)} %copy-done.4) | copy-start | bytes 1511428
  62.2 9.9 %copy-start.7 = (bf16[3,656,128]{2,1,0:T(8,128)(2,1)S(1)}, bf16[3,656,128]{2,1,0:T(8,128)(2,1)}, u32[]{:S(2)}) copy-start(bf16[3,656,128]{2,1,0:T(8,128)(2,1)} %copy-done.6) | copy-start | bytes 1511428
  62.2 9.9 %copy-start.9 = (bf16[3,656,128]{2,1,0:T(8,128)(2,1)S(1)}, bf16[3,656,128]{2,1,0:T(8,128)(2,1)}, u32[]{:S(2)}) copy-start(bf16[3,656,128]{2,1,0:T(8,128)(2,1)} %copy-done.8) | copy-start | bytes 1511428
  62.2 9.9 %copy-start.10 = (s32[4]{0:T(128)S(1)}, s32[4]{0:T(128)}, u32[]{:S(2)}) copy-start(s32[4]{0:T(128)} %get-tuple-element.38.sizes) | copy-start | bytes 52
  62.2 9.9 %copy-start.11 = (s32[288]{0:T(512)S(1)}, s32[288]{0:T(512)}, u32[]{:S(2)}) copy-start(s32[288]{0:T(512)} %get-tuple-element.40.entries) | copy-start | bytes 3460
  62.2 9.9 %copy-start.12 = (s32[24]{0:T(128)S(1)}, s32[24]{0:T(128)}, u32[]{:S(2)}) copy-start(s32[24]{0:T(128)} %get-tuple-element.37.slot_of) | copy-start | bytes 292
  62.2 9.9 %copy-start.13 = (s32[72]{0:T(128)S(1)}, s32[72]{0:T(128)}, u32[]{:S(2)}) copy-start(s32[72]{0:T(128)} %get-tuple-element.39.group_input) | copy-start | bytes 868
  64.6 7.4 %collective-permute-start.12 = (bf16[6,128,512]{2,1,0:T(8,128)(2,1)S(1)}, bf16[6,128,512]{2,1,0:T(8,128)(2,1)}, u32[]{:S(2)}, u32[]{:S(2)}) collective-permute-start(bf16[6,128,512]{2,1,0:T(8,128)(2,1)S(1)} %shard_map.97.refs_8_), channel_id=1, source_target_pairs={{0,4},{1,5},{2,6},{3,7},{4,0},{5,1},{6,2},{7,3},{8,12},{9,13},{10,... | collective-permute-start | bytes 2359304 | tf_op jit(solution)/shard_map/ppermute | solution.py:465
  64.7 7.3 %collective-permute-start.13 = (bf16[3,128,512]{2,1,0:T(8,128)(2,1)}, bf16[3,128,512]{2,1,0:T(8,128)(2,1)S(1)}, u32[]{:S(2)}, u32[]{:S(2)}) collective-permute-start(bf16[3,128,512]{2,1,0:T(8,128)(2,1)} %collective-permute-done.10.refs_9_), channel_id=1, source_target_pairs={{0,4},{1,5},{2,6},{3,7},{4,0},{5,1},{6,2},{7,3},{8,12},{9,13},{10,... | collective-permute-start | bytes 1179656 | tf_op jit(solution)/shard_map/ppermute | solution.py:465
  65.2 6.9 %collective-permute-start.14 = (bf16[3,128,512]{2,1,0:T(8,128)(2,1)}, bf16[3,128,512]{2,1,0:T(8,128)(2,1)S(1)}, u32[]{:S(2)}, u32[]{:S(2)}) collective-permute-start(bf16[3,128,512]{2,1,0:T(8,128)(2,1)} %collective-permute-done.11.refs_10_), channel_id=1, source_target_pairs={{0,4},{1,5},{2,6},{3,7},{4,0},{5,1},{6,2},{7,3},{8,12},{9,13},{10,... | collective-permute-start | bytes 1179656 | tf_op jit(solution)/shard_map/ppermute | solution.py:465
  84.6 6.3 %copy-start.14 = (f32[384,128]{1,0:T(8,128)S(1)}, f32[384,128]{1,0:T(8,128)}, u32[]{:S(2)}) copy-start(f32[384,128]{1,0:T(8,128)} %param.8) | copy-start | bytes 589828
  84.6 6.3 %copy-start.15 = (f32[384]{0:T(512)S(1)}, f32[384]{0:T(512)}, u32[]{:S(2)}) copy-start(f32[384]{0:T(512)} %param.9) | copy-start | bytes 4612
  84.6 1.8 %collective-permute-start.15 = (bf16[12,128,128]{2,1,0:T(8,128)(2,1)S(1)}, bf16[12,128,128]{2,1,0:T(8,128)(2,1)S(1)}, u32[]{:S(2)}, u32[]{:S(2)}) collective-permute-start(bf16[12,128,128]{2,1,0:T(8,128)(2,1)S(1)} %get-tuple-element.66), channel_id=1, source_target_pairs={{0,4},{1,5},{2,6},{3,7},{4,0},{5,1},{6,2},{7,3},{8,12},{9,13},{10,... | collective-permute-start | bytes 1179656 | tf_op jit(solution)/shard_map/ppermute | solution.py:465
  87.7 8.6 %collective-permute-start.16 = (bf16[2,3,128,128]{3,2,1,0:T(8,128)(2,1)S(1)}, bf16[2,3,128,128]{3,2,1,0:T(8,128)(2,1)S(1)}, u32[]{:S(2)}, u32[]{:S(2)}) collective-permute-start(bf16[2,3,128,128]{3,2,1,0:T(8,128)(2,1)S(1)} %pad_maximum_fusion.1), channel_id=1, source_target_pairs={{0,8},{1,9},{2,10},{3,11},{4,12},{5,13},{6,14},{7,15},{8,0},{9,1},... | collective-permute-start | bytes 589832 | tf_op jit(solution)/shard_map/ppermute | solution.py:465
  96.4 11.8 %collective-permute-start.17 = (bf16[2,3,128,128]{3,2,1,0:T(8,128)(2,1)S(1)}, bf16[2,3,128,128]{3,2,1,0:T(8,128)(2,1)S(1)}, u32[]{:S(2)}, u32[]{:S(2)}) collective-permute-start(bf16[2,3,128,128]{3,2,1,0:T(8,128)(2,1)S(1)} %fusion), channel_id=1, source_target_pairs={{0,16},{1,17},{2,18},{3,19},{4,20},{5,21},{6,22},{7,23},{8,24},{9,... | collective-permute-start | bytes 589832 | tf_op jit(solution)/shard_map/ppermute | solution.py:465
  108.2 11.1 %collective-permute-start.20 = (bf16[2,3,128,128]{3,2,1,0:T(8,128)(2,1)S(1)}, bf16[2,3,128,128]{3,2,1,0:T(8,128)(2,1)S(1)}, u32[]{:S(2)}, u32[]{:S(2)}) collective-permute-start(bf16[2,3,128,128]{3,2,1,0:T(8,128)(2,1)S(1)} %get-tuple-element.72.refs_0_), channel_id=1, source_target_pairs={{0,3},{1,2},{2,1},{3,0},{4,7},{5,6},{6,5},{7,4},{8,11},{9,10},{10,... | collective-permute-start | bytes 589832 | tf_op jit(solution)/shard_map/ppermute | solution.py:465
  115.1 10.0 %collective-permute-start.19 = (bf16[2,3,128,128]{3,2,1,0:T(8,128)(2,1)S(1)}, bf16[2,3,128,128]{3,2,1,0:T(8,128)(2,1)S(1)}, u32[]{:S(2)}, u32[]{:S(2)}) collective-permute-start(bf16[2,3,128,128]{3,2,1,0:T(8,128)(2,1)S(1)} %get-tuple-element.72.refs_0_), channel_id=1, source_target_pairs={{0,2},{1,3},{2,0},{3,1},{4,6},{5,7},{6,4},{7,5},{8,10},{9,11},{10,... | collective-permute-start | bytes 589832 | tf_op jit(solution)/shard_map/ppermute | solution.py:465
  119.3 6.9 %collective-permute-start.18 = (bf16[2,3,128,128]{3,2,1,0:T(8,128)(2,1)S(1)}, bf16[2,3,128,128]{3,2,1,0:T(8,128)(2,1)S(1)}, u32[]{:S(2)}, u32[]{:S(2)}) collective-permute-start(bf16[2,3,128,128]{3,2,1,0:T(8,128)(2,1)S(1)} %get-tuple-element.72.refs_0_), channel_id=1, source_target_pairs={{0,1},{1,0},{2,3},{3,2},{4,5},{5,4},{6,7},{7,6},{8,9},{9,8},{10,11... | collective-permute-start | bytes 589832 | tf_op jit(solution)/shard_map/ppermute | solution.py:465
  130.8 1.8 %collective-permute-start.21 = (bf16[12,128,128]{2,1,0:T(8,128)(2,1)S(1)}, bf16[12,128,128]{2,1,0:T(8,128)(2,1)S(1)}, u32[]{:S(2)}, u32[]{:S(2)}) collective-permute-start(bf16[12,128,128]{2,1,0:T(8,128)(2,1)S(1)} %get-tuple-element.69), channel_id=1, source_target_pairs={{0,4},{1,5},{2,6},{3,7},{4,0},{5,1},{6,2},{7,3},{8,12},{9,13},{10,... | collective-permute-start | bytes 1179656 | tf_op jit(solution)/shard_map/ppermute | solution.py:465
  132.7 4.9 %collective-permute-start.22 = (bf16[3,128,128]{2,1,0:T(8,128)(2,1)S(1)}, bf16[3,128,128]{2,1,0:T(8,128)(2,1)S(1)}, u32[]{:S(2)}, u32[]{:S(2)}) collective-permute-start(bf16[3,128,128]{2,1,0:T(8,128)(2,1)S(1)} %get-tuple-element.78), channel_id=1, source_target_pairs={{0,8},{1,9},{2,10},{3,11},{4,12},{5,13},{6,14},{7,15},{8,0},{9,1},... | collective-permute-start | bytes 294920 | tf_op jit(solution)/shard_map/ppermute | solution.py:465
  132.8 8.2 %collective-permute-start.24 = (bf16[3,128,128]{2,1,0:T(8,128)(2,1)S(1)}, bf16[3,128,128]{2,1,0:T(8,128)(2,1)S(1)}, u32[]{:S(2)}, u32[]{:S(2)}) collective-permute-start(bf16[3,128,128]{2,1,0:T(8,128)(2,1)S(1)} %get-tuple-element.79), channel_id=1, source_target_pairs={{0,24},{1,25},{2,26},{3,27},{4,28},{5,29},{6,30},{7,31},{8,16},{9,... | collective-permute-start | bytes 294920 | tf_op jit(solution)/shard_map/ppermute | solution.py:465
  135.3 9.9 %collective-permute-start.23 = (bf16[3,128,128]{2,1,0:T(8,128)(2,1)S(1)}, bf16[3,128,128]{2,1,0:T(8,128)(2,1)S(1)}, u32[]{:S(2)}, u32[]{:S(2)}) collective-permute-start(bf16[3,128,128]{2,1,0:T(8,128)(2,1)S(1)} %get-tuple-element.80), channel_id=1, source_target_pairs={{0,16},{1,17},{2,18},{3,19},{4,20},{5,21},{6,22},{7,23},{8,24},{9,... | collective-permute-start | bytes 294920 | tf_op jit(solution)/shard_map/ppermute | solution.py:465

commit v12 on v11

--- a/solution.py
+++ b/solution.py
@@ -29,7 +29,7 @@
         self.unroll = unroll
         self.vmem = 60 * mib
         self.vmem_sums = (50 if unroll > 1 else 60) * mib
-        most = self.owners * tile_max + self.inputs * (unroll - 1) + unroll
+        most = self.owners * tile_max + self.inputs * (unroll - 1) + (3 + self.owners) * unroll
         self.groups = -(-most // (unroll * chunk_groups)) * chunk_groups
 
     def line_steps(self):
@@ -76,6 +76,7 @@
         lax.fori_loop(0, listed[owner, lay.tile_max], count, 0)
 
     group_input[0] = 0
+    group_input[1] = 0
 
     def place_groups(p, start):
         used = jnp.where(slot_of[p] >= 0, fill[p], 0)
@@ -89,11 +90,13 @@
         lax.fori_loop(start, end, name, 0)
         return end
 
-    total = 1
+    total = 2
     for owner in range(lay.owners):
         if owner > 0:
             sizes[lay.owners + owner] = total
         total = lax.fori_loop(owner * lay.spread, (owner + 1) * lay.spread, place_groups, total)
+        group_input[total] = owner * lay.spread
+        total = total + lax.rem(total, 2)
     sizes[0] = total
 
     def clear(i, carry):
@@ -304,7 +307,7 @@
             def _():
                 load(p).wait()
 
-        def group_step(group, carry):
+        def make_group(group):
             block = projected[group_input[group]]
             numbers = [entries[group * lay.unroll + i] for i in range(lay.unroll)]
             places = [jnp.minimum(lax.div(n, lay.points), lay.outputs - 1) for n in numbers]
@@ -317,12 +320,17 @@
                     at_b = mine[:, b * lay.side : (b + 1) * lay.side]
                     tile = jnp.where(lax.rem(numbers[i], lay.points) == b, at_b, tile)
                 tiles[group * lay.unroll + i] = tile.astype(jnp.bfloat16)
-            add_products(lay, group - 1, group_input, entries, tiles, rounded, total)
+
+        def pair_step(pair, carry):
+            for lane in range(2):
+                add_products(lay, 2 * pair - 2 + lane, group_input, entries, tiles, rounded, total)
+            for lane in range(2):
+                make_group(2 * pair + lane)
             return carry
 
-        first = 1 if owner == 0 else sizes[lay.owners + owner]
+        first = 1 if owner == 0 else lax.div(sizes[lay.owners + owner], 2)
         last = used if owner == lay.owners - 1 else sizes[lay.owners + owner + 1]
-        lax.fori_loop(first, last, group_step, 0)
+        lax.fori_loop(first, lax.div(last, 2), pair_step, 0)
 
     span = chunk_groups * lay.unroll
 
@@ -336,7 +344,8 @@
         def _():
             store(chunk).start()
 
-    add_products(lay, used - 1, group_input, entries, tiles, rounded, total)
+    for lane in range(2):
+        add_products(lay, used - 2 + lane, group_input, entries, tiles, rounded, total)
     give_sums(lay, total, own_sum, other_sum)
     for chunk in range(lay.groups // chunk_groups):
 
@@ -411,11 +420,12 @@
         def _():
             load(chunk).wait()
 
-    def group_step(group, carry):
-        add_products(lay, group, group_input, entries, tiles, rounded, total)
+    def pair_step(pair, carry):
+        for lane in range(2):
+            add_products(lay, 2 * pair + lane, group_input, entries, tiles, rounded, total)
         return carry
 
-    lax.fori_loop(1, used, group_step, 0)
+    lax.fori_loop(1, lax.div(used, 2), pair_step, 0)
     give_sums(lay, total, own_sum, other_sum)
 
 

time: 148 us -> 140 us (0.946); the launches traced: 146 us -> 140 us
  Pallas kernels: 38.5 us -> 31.7 us
  waiting for transfers between devices: 60.9 us -> 67.4 us
  starting transfers between devices: 36.8 us -> 30.9 us
    ppermute x25, waiting for transfers between devices: 60.9 us -> 67.4 us  [move(): return lax.ppermute(array, axes, pairs_list)]
    ppermute x25, starting transfers between devices: 36.8 us -> 30.9 us  [move(): return lax.ppermute(array, axes, pairs_list)]
    pallas_call x1, Pallas kernels: 12.4 us -> 8.99 us  [make_tiles(): pl.pallas_call(functools.partial(tiles_kernel, lay), out_shape=(sums, sen...]
    pallas_call x1, Pallas kernels: 6.77 us -> 4.36 us  [make_plan(): pl.pallas_call(functools.partial(plan_kernel, lay), out_shape=tuple((jax....]
  transfers between devices with their start and end apart: 25 -> 25, of which waited for: 16 -> 16; matrix products, arithmetic and copies ran while one was open for 4% -> 4% of each run, Pallas kernels for 15% -> 14%
where the time goes in v12:
time: 140 us
  waiting for transfers between devices  67.4 us (48%)
  Pallas kernels  31.7 us (23%)
  starting transfers between devices  30.9 us (22%)
  other arithmetic  7.3 us (5%)
  between operations  1.71 us (1%)
    ppermute x25, waiting for transfers between devices, move(): return lax.ppermute(array, axes, pairs_list)  67.4 us
    ppermute x25, starting transfers between devices, move(): return lax.ppermute(array, axes, pairs_list)  30.9 us
    pallas_call x2, Pallas kernels, project(): pl.pallas_call(functools.partial(project_kernel, lay, owner), out_shape=j...  14.4 us
    pallas_call x1, Pallas kernels, make_tiles(): pl.pallas_call(functools.partial(tiles_kernel, lay), out_shape=(sums, sen...  8.99 us
    pallas_call x1, Pallas kernels, make_plan(): pl.pallas_call(functools.partial(plan_kernel, lay), out_shape=tuple((jax....  4.36 us
    pallas_call x1, Pallas kernels, apply_tiles(): pl.pallas_call(functools.partial(apply_kernel, lay), out_shape=(sums, sen...  3.58 us
  transfers between devices with their start and end apart: 25, of which 16 were waited for; matrix products, arithmetic and copies ran while one was open for 4% of the time, Pallas kernels for 14%

profile of v12, /device:TPU:0, one launch (start us, length us, event | category | flops | bytes accessed | tf_op | source)
XLA Modules:
  0.0 139.8 jit_solution(14197094630422975678)
XLA Ops:
  0.6 3.1 %collective-permute-start.4 = (bf16[2,1,512,512]{3,2,1,0:T(8,128)(2,1)}, bf16[2,1,512,512]{3,2,1,0:T(8,128)(2,1)}, u32[]{:S(2)}, u32[]{:S(2)}) collective-permute-start(bf16[2,1,512,512]{3,2,1,0:T(8,128)(2,1)} %refs_4_.1), channel_id=1, source_target_pairs={{0,8},{1,9},{2,10},{3,11},{4,12},{5,13},{6,14},{7,15},{8,0},{9,1},... | collective-permute-start | bytes 3145736 | tf_op jit(solution)/shard_map/ppermute | solution.py:475
  4.4 0.9 convert_element_type.40
  5.3 0.7 convert_bitcast_fusion.1
  6.1 1.0 pad_maximum_fusion.given.refs_0_
  7.2 2.5 %collective-permute-start.3 = (bf16[3,656,128]{2,1,0:T(8,128)(2,1)S(1)}, bf16[3,656,128]{2,1,0:T(8,128)(2,1)S(1)}, u32[]{:S(2)}, u32[]{:S(2)}) collective-permute-start(bf16[3,656,128]{2,1,0:T(8,128)(2,1)S(1)} %pad_maximum_fusion.given.refs_0_), channel_id=1, source_target_pairs={{0,3},{1,2},{2,1},{3,0},{4,7},{5,6},{6,5},{7,4},{8,11},{9,10},{10,... | collective-permute-start | bytes 1511432 | tf_op jit(solution)/shard_map/ppermute | solution.py:475
  9.7 0.5 collective-permute-start.2
  10.2 0.5 collective-permute-start.1
  10.7 2.6 %collective-permute-start = (bf16[3,656,128]{2,1,0:T(8,128)(2,1)S(1)}, bf16[3,656,128]{2,1,0:T(8,128)(2,1)S(1)}, u32[]{:S(2)}, u32[]{:S(2)}) collective-permute-start(bf16[3,656,128]{2,1,0:T(8,128)(2,1)S(1)} %pad_maximum_fusion.given.refs_0_), channel_id=1, source_target_pairs={{0,16},{1,17},{2,18},{3,19},{4,20},{5,21},{6,22},{7,23},{8,24},{9,... | collective-permute-start | bytes 1511432 | tf_op jit(solution)/shard_map/ppermute | solution.py:475
  13.3 9.3 %collective-permute-done.3.refs_3_ = bf16[3,656,128]{2,1,0:T(8,128)(2,1)S(1)} collective-permute-done((bf16[3,656,128]{2,1,0:T(8,128)(2,1)S(1)}, bf16[3,656,128]{2,1,0:T(8,128)(2,1)S(1)}, u32[]{:S(2)}, u32[]{:S(2)}) %collective-permute-start.3) | collective-permute-done | bytes 503840 | tf_op jit(solution)/shard_map/ppermute | solution.py:475
  22.6 9.3 %collective-permute-done.2.refs_2_ = bf16[3,656,128]{2,1,0:T(8,128)(2,1)S(1)} collective-permute-done((bf16[3,656,128]{2,1,0:T(8,128)(2,1)S(1)}, bf16[3,656,128]{2,1,0:T(8,128)(2,1)S(1)}, u32[]{:S(2)}, u32[]{:S(2)}) %collective-permute-start.2) | collective-permute-done | bytes 503840 | tf_op jit(solution)/shard_map/ppermute | solution.py:475
  32.0 5.2 %collective-permute-done.given.refs_0_.refs_4_ = bf16[3,656,128]{2,1,0:T(8,128)(2,1)S(1)} collective-permute-done((bf16[3,656,128]{2,1,0:T(8,128)(2,1)S(1)}, bf16[3,656,128]{2,1,0:T(8,128)(2,1)S(1)}, u32[]{:S(2)}, u32[]{:S(2)}) %collective-permute-start) | collective-permute-done | bytes 503840 | tf_op jit(solution)/shard_map/ppermute | solution.py:475
  37.1 0.8 collective-permute-done.4.refs_6_
  38.0 0.7 pad_add_fusion.1.ids
  38.7 2.6 %collective-permute-start.7 = (bf16[3,656,128]{2,1,0:T(8,128)(2,1)S(1)}, bf16[3,656,128]{2,1,0:T(8,128)(2,1)}, u32[]{:S(2)}, u32[]{:S(2)}) collective-permute-start(bf16[3,656,128]{2,1,0:T(8,128)(2,1)S(1)} %collective-permute-done.given.refs_0_.refs_4_), channel_id=1, source_target_pairs={{0,3},{1,2},{2,1},{3,0},{4,7},{5,6},{6,5},{7,4},{8,11},{9,10},{10,... | collective-permute-start | bytes 1511432 | tf_op jit(solution)/shard_map/ppermute | solution.py:475
  41.3 0.5 collective-permute-start.6
  41.8 0.4 collective-permute-start.5
  42.1 0.2 shard_map.96.own
  42.3 3.8 %collective-permute-start.11 = (bf16[3,128,512]{2,1,0:T(8,128)(2,1)S(1)}, bf16[3,128,512]{2,1,0:T(8,128)(2,1)}, u32[]{:S(2)}, u32[]{:S(2)}) collective-permute-start(bf16[3,128,512]{2,1,0:T(8,128)(2,1)S(1)} %shard_map.96.own), channel_id=1, source_target_pairs={{0,24},{1,25},{2,26},{3,27},{4,28},{5,29},{6,30},{7,31},{8,16},{9,... | collective-permute-start | bytes 1179656 | tf_op jit(solution)/shard_map/ppermute | solution.py:475
  46.2 1.3 pad_add_fusion.listed
  47.5 4.4 %shard_map.95 = (s32[24]{0:T(128)}, s32[26]{0:T(128)}, s32[4]{0:T(128)}, s32[72]{0:T(128)}, s32[288]{0:T(512)}) custom-call(s32[3]{0:T(128)} %pad_add_fusion.1.ids, s32[2,97]{1,0:T(2,128)} %pad_add_fusion.listed, s32[96]{0:T(128)} %fine.1, s32[8]{0:T(128)} %stored.1), custom_call_target="tpu_custom_call" | custom-call | bytes 20000000 | tf_op jit(solution)/shard_map/pallas_call | solution.py:141
  51.9 0.2 shard_map.97.refs_8_
  52.1 6.8 %shard_map.98.refs_14_ = bf16[12,512,256]{2,1,0:T(8,128)(2,1)} custom-call(s32[24]{0:T(128)} %get-tuple-element.37.slot_of, s32[26]{0:T(128)} %get-tuple-element.48.valid, s32[4]{0:T(128)} %get-tuple-element.38.sizes, bf16[3,656,128]{2,1,0:T(8,128)(2,1)} %copy-done, bf16[3,656,128]{2,1,0:T(8,128)(2,1)} %copy-done.8, bf16[3,656,128]{2,1,0:T(8,128)(2,1)} %copy-done.6, ...), custom_call_target="tpu_custom_call" | custom-call | flops 1000000000 | bytes 16000000 | tf_op jit(solution)/shard_map/pallas_call | solution.py:246
  59.0 5.3 %collective-permute-done.6.refs_2_.refs_6_ = bf16[3,656,128]{2,1,0:T(8,128)(2,1)} collective-permute-done((bf16[3,656,128]{2,1,0:T(8,128)(2,1)S(1)}, bf16[3,656,128]{2,1,0:T(8,128)(2,1)}, u32[]{:S(2)}, u32[]{:S(2)}) %collective-permute-start.6) | collective-permute-done | bytes 503840 | tf_op jit(solution)/shard_map/ppermute | solution.py:475
  64.3 0.3 collective-permute-done.5.refs_1_.refs_5_
  64.6 0.2 collective-permute-start.12
  64.9 0.3 collective-permute-start.13
  65.2 0.2 collective-permute-start.14
  65.4 7.6 %shard_map.99.refs_15_ = bf16[12,512,256]{2,1,0:T(8,128)(2,1)} custom-call(s32[24]{0:T(128)} %get-tuple-element.37.slot_of, s32[26]{0:T(128)} %get-tuple-element.48.valid, s32[4]{0:T(128)} %get-tuple-element.38.sizes, bf16[3,656,128]{2,1,0:T(8,128)(2,1)} %copy-done.2, bf16[3,656,128]{2,1,0:T(8,128)(2,1)} %collective-permute-done.5.refs_1_.refs_5_, ...), custom_call_target="tpu_custom_call" | custom-call | flops 1000000000 | bytes 16000000 | tf_op jit(solution)/shard_map/pallas_call | solution.py:246
  73.1 9.0 %shard_map.100 = (f32[12,128,128]{2,1,0:T(8,128)}, bf16[12,128,128]{2,1,0:T(8,128)(2,1)S(1)}, bf16[288,128,128]{2,1,0:T(8,128)(2,1)}) custom-call(s32[24]{0:T(128)S(1)} %copy-done.12, s32[4]{0:T(128)S(1)} %copy-done.10, s32[72]{0:T(128)S(1)} %copy-done.13, s32[288]{0:T(512)S(1)} %copy-done.11, bf16[3,656,128]{2,1,0:T(8,128)(2,1)S(1)} %copy-done.1, ...), custom_call_target="tpu_custom_call" | custom-call | flops 4000000000 | bytes 30000000 | tf_op jit(solution)/shard_map/pallas_call | solution.py:371
  82.1 4.8 %collective-permute-start.15 = (bf16[12,128,128]{2,1,0:T(8,128)(2,1)S(1)}, bf16[12,128,128]{2,1,0:T(8,128)(2,1)S(1)}, u32[]{:S(2)}, u32[]{:S(2)}) collective-permute-start(bf16[12,128,128]{2,1,0:T(8,128)(2,1)S(1)} %get-tuple-element.66), channel_id=1, source_target_pairs={{0,4},{1,5},{2,6},{3,7},{4,0},{5,1},{6,2},{7,3},{8,12},{9,13},{10,... | collective-permute-start | bytes 1179656 | tf_op jit(solution)/shard_map/ppermute | solution.py:475
  86.9 1.3 collective-permute-done.15
  88.3 1.3 fusion.13
  89.8 7.0 %collective-permute-done.16 = bf16[2,3,128,128]{3,2,1,0:T(8,128)(2,1)S(1)} collective-permute-done((bf16[2,3,128,128]{3,2,1,0:T(8,128)(2,1)S(1)}, bf16[2,3,128,128]{3,2,1,0:T(8,128)(2,1)S(1)}, u32[]{:S(2)}, u32[]{:S(2)}) %collective-permute-start.16) | collective-permute-done | bytes 196640 | tf_op jit(solution)/shard_map/ppermute | solution.py:475
  97.0 11.4 %collective-permute-done.17 = bf16[2,3,128,128]{3,2,1,0:T(8,128)(2,1)S(1)} collective-permute-done((bf16[2,3,128,128]{3,2,1,0:T(8,128)(2,1)S(1)}, bf16[2,3,128,128]{3,2,1,0:T(8,128)(2,1)S(1)}, u32[]{:S(2)}, u32[]{:S(2)}) %collective-permute-start.17) | collective-permute-done | bytes 196640 | tf_op jit(solution)/shard_map/ppermute | solution.py:475
  108.6 0.9 collective-permute-start.19
  109.5 2.6 %collective-permute-start.18 = (bf16[2,3,128,128]{3,2,1,0:T(8,128)(2,1)S(1)}, bf16[2,3,128,128]{3,2,1,0:T(8,128)(2,1)S(1)}, u32[]{:S(2)}, u32[]{:S(2)}) collective-permute-start(bf16[2,3,128,128]{3,2,1,0:T(8,128)(2,1)S(1)} %get-tuple-element.72.refs_0_), channel_id=1, source_target_pairs={{0,1},{1,0},{2,3},{3,2},{4,5},{5,4},{6,7},{7,6},{8,9},{9,8},{10,11... | collective-permute-start | bytes 589832 | tf_op jit(solution)/shard_map/ppermute | solution.py:475
  112.1 5.2 %collective-permute-done.20.refs_3_ = bf16[2,3,128,128]{3,2,1,0:T(8,128)(2,1)S(1)} collective-permute-done((bf16[2,3,128,128]{3,2,1,0:T(8,128)(2,1)S(1)}, bf16[2,3,128,128]{3,2,1,0:T(8,128)(2,1)S(1)}, u32[]{:S(2)}, u32[]{:S(2)}) %collective-permute-start.20) | collective-permute-done | bytes 196640 | tf_op jit(solution)/shard_map/ppermute | solution.py:475
  117.3 2.4 %collective-permute-done.19.refs_2_ = bf16[2,3,128,128]{3,2,1,0:T(8,128)(2,1)S(1)} collective-permute-done((bf16[2,3,128,128]{3,2,1,0:T(8,128)(2,1)S(1)}, bf16[2,3,128,128]{3,2,1,0:T(8,128)(2,1)S(1)}, u32[]{:S(2)}, u32[]{:S(2)}) %collective-permute-start.19) | collective-permute-done | bytes 196640 | tf_op jit(solution)/shard_map/ppermute | solution.py:475
  119.7 3.6 %shard_map.101 = (f32[12,128,128]{2,1,0:T(8,128)S(1)}, bf16[12,128,128]{2,1,0:T(8,128)(2,1)S(1)}) custom-call(s32[4]{0:T(128)S(1)} %copy-done.10, s32[72]{0:T(128)S(1)} %copy-done.13, s32[288]{0:T(512)S(1)} %copy-done.11, bf16[288,128,128]{2,1,0:T(8,128)(2,1)} %get-tuple-element.67.tiles_in, bf16[2,3,128,128]{3,2,1,0:T(8,128)(2,1)S(1)} %get-tuple-element.72.refs_0_, ...), custom_call_target="tpu_custom_call" | custom-call | flops 400000000 | bytes 4000000 | tf_op jit(solution)/shard_map/pallas_call | solution.py:439
  123.3 1.6 %collective-permute-start.21 = (bf16[12,128,128]{2,1,0:T(8,128)(2,1)S(1)}, bf16[12,128,128]{2,1,0:T(8,128)(2,1)S(1)}, u32[]{:S(2)}, u32[]{:S(2)}) collective-permute-start(bf16[12,128,128]{2,1,0:T(8,128)(2,1)S(1)} %get-tuple-element.69), channel_id=1, source_target_pairs={{0,4},{1,5},{2,6},{3,7},{4,0},{5,1},{6,2},{7,3},{8,12},{9,13},{10,... | collective-permute-start | bytes 1179656 | tf_op jit(solution)/shard_map/ppermute | solution.py:475
  124.9 1.3 collective-permute-done.21
  126.5 1.5 %collective-permute-start.24 = (bf16[3,128,128]{2,1,0:T(8,128)(2,1)S(1)}, bf16[3,128,128]{2,1,0:T(8,128)(2,1)S(1)}, u32[]{:S(2)}, u32[]{:S(2)}) collective-permute-start(bf16[3,128,128]{2,1,0:T(8,128)(2,1)S(1)} %get-tuple-element.79), channel_id=1, source_target_pairs={{0,24},{1,25},{2,26},{3,27},{4,28},{5,29},{6,30},{7,31},{8,16},{9,... | collective-permute-start | bytes 294920 | tf_op jit(solution)/shard_map/ppermute | solution.py:475
  128.0 2.0 %collective-permute-start.23 = (bf16[3,128,128]{2,1,0:T(8,128)(2,1)S(1)}, bf16[3,128,128]{2,1,0:T(8,128)(2,1)S(1)}, u32[]{:S(2)}, u32[]{:S(2)}) collective-permute-start(bf16[3,128,128]{2,1,0:T(8,128)(2,1)S(1)} %get-tuple-element.80), channel_id=1, source_target_pairs={{0,16},{1,17},{2,18},{3,19},{4,20},{5,21},{6,22},{7,23},{8,24},{9,... | collective-permute-start | bytes 294920 | tf_op jit(solution)/shard_map/ppermute | solution.py:475
  130.0 0.7 slice.79
  130.7 2.6 %collective-permute-done.22 = bf16[3,128,128]{2,1,0:T(8,128)(2,1)S(1)} collective-permute-done((bf16[3,128,128]{2,1,0:T(8,128)(2,1)S(1)}, bf16[3,128,128]{2,1,0:T(8,128)(2,1)S(1)}, u32[]{:S(2)}, u32[]{:S(2)}) %collective-permute-start.22) | collective-permute-done | bytes 98336 | tf_op jit(solution)/shard_map/ppermute | solution.py:475
  133.2 0.9 collective-permute-done.24
  134.1 5.0 %collective-permute-done.23 = bf16[3,128,128]{2,1,0:T(8,128)(2,1)S(1)} collective-permute-done((bf16[3,128,128]{2,1,0:T(8,128)(2,1)S(1)}, bf16[3,128,128]{2,1,0:T(8,128)(2,1)S(1)}, u32[]{:S(2)}, u32[]{:S(2)}) %collective-permute-start.23) | collective-permute-done | bytes 98336 | tf_op jit(solution)/shard_map/ppermute | solution.py:475
  139.0 0.8 fusion.5
  (60 shorter events, 1.1 us)
Async XLA Ops:
  0.6 37.4 %collective-permute-start.4 = (bf16[2,1,512,512]{3,2,1,0:T(8,128)(2,1)}, bf16[2,1,512,512]{3,2,1,0:T(8,128)(2,1)}, u32[]{:S(2)}, u32[]{:S(2)}) collective-permute-start(bf16[2,1,512,512]{3,2,1,0:T(8,128)(2,1)} %refs_4_.1), channel_id=1, source_target_pairs={{0,8},{1,9},{2,10},{3,11},{4,12},{5,13},{6,14},{7,15},{8,0},{9,1},... | collective-permute-start | bytes 3145736 | tf_op jit(solution)/shard_map/ppermute | solution.py:475
  7.2 44.9 %copy-start = (bf16[3,656,128]{2,1,0:T(8,128)(2,1)}, bf16[3,656,128]{2,1,0:T(8,128)(2,1)S(1)}, u32[]{:S(2)}) copy-start(bf16[3,656,128]{2,1,0:T(8,128)(2,1)S(1)} %pad_maximum_fusion.given.refs_0_) | copy-start | bytes 1511428
  7.2 15.4 %collective-permute-start.3 = (bf16[3,656,128]{2,1,0:T(8,128)(2,1)S(1)}, bf16[3,656,128]{2,1,0:T(8,128)(2,1)S(1)}, u32[]{:S(2)}, u32[]{:S(2)}) collective-permute-start(bf16[3,656,128]{2,1,0:T(8,128)(2,1)S(1)} %pad_maximum_fusion.given.refs_0_), channel_id=1, source_target_pairs={{0,3},{1,2},{2,1},{3,0},{4,7},{5,6},{6,5},{7,4},{8,11},{9,10},{10,... | collective-permute-start | bytes 1511432 | tf_op jit(solution)/shard_map/ppermute | solution.py:475
  9.7 22.2 %collective-permute-start.2 = (bf16[3,656,128]{2,1,0:T(8,128)(2,1)S(1)}, bf16[3,656,128]{2,1,0:T(8,128)(2,1)S(1)}, u32[]{:S(2)}, u32[]{:S(2)}) collective-permute-start(bf16[3,656,128]{2,1,0:T(8,128)(2,1)S(1)} %pad_maximum_fusion.given.refs_0_), channel_id=1, source_target_pairs={{0,2},{1,3},{2,0},{3,1},{4,6},{5,7},{6,4},{7,5},{8,10},{9,11},{10,... | collective-permute-start | bytes 1511432 | tf_op jit(solution)/shard_map/ppermute | solution.py:475
  10.2 21.8 %collective-permute-start.1 = (bf16[3,656,128]{2,1,0:T(8,128)(2,1)S(1)}, bf16[3,656,128]{2,1,0:T(8,128)(2,1)S(1)}, u32[]{:S(2)}, u32[]{:S(2)}) collective-permute-start(bf16[3,656,128]{2,1,0:T(8,128)(2,1)S(1)} %pad_maximum_fusion.given.refs_0_), channel_id=1, source_target_pairs={{0,1},{1,0},{2,3},{3,2},{4,5},{5,4},{6,7},{7,6},{8,9},{9,8},{10,11... | collective-permute-start | bytes 1511432 | tf_op jit(solution)/shard_map/ppermute | solution.py:475
  10.7 26.4 %collective-permute-start = (bf16[3,656,128]{2,1,0:T(8,128)(2,1)S(1)}, bf16[3,656,128]{2,1,0:T(8,128)(2,1)S(1)}, u32[]{:S(2)}, u32[]{:S(2)}) collective-permute-start(bf16[3,656,128]{2,1,0:T(8,128)(2,1)S(1)} %pad_maximum_fusion.given.refs_0_), channel_id=1, source_target_pairs={{0,16},{1,17},{2,18},{3,19},{4,20},{5,21},{6,22},{7,23},{8,24},{9,... | collective-permute-start | bytes 1511432 | tf_op jit(solution)/shard_map/ppermute | solution.py:475
  22.6 29.5 %copy-start.4 = (bf16[3,656,128]{2,1,0:T(8,128)(2,1)}, bf16[3,656,128]{2,1,0:T(8,128)(2,1)S(1)}, u32[]{:S(2)}) copy-start(bf16[3,656,128]{2,1,0:T(8,128)(2,1)S(1)} %collective-permute-done.3.refs_3_) | copy-start | bytes 1511428
  22.6 19.7 %collective-permute-start.8 = (bf16[2,1,512,512]{3,2,1,0:T(8,128)(2,1)}, bf16[2,1,512,512]{3,2,1,0:T(8,128)(2,1)}, u32[]{:S(2)}, u32[]{:S(2)}) collective-permute-start(bf16[2,1,512,512]{3,2,1,0:T(8,128)(2,1)} %refs_4_.1), channel_id=1, source_target_pairs={{0,4},{1,5},{2,6},{3,7},{4,0},{5,1},{6,2},{7,3},{8,12},{9,13},{10,... | collective-permute-start | bytes 3145736 | tf_op jit(solution)/shard_map/ppermute | solution.py:475
  31.9 20.2 %copy-start.6 = (bf16[3,656,128]{2,1,0:T(8,128)(2,1)}, bf16[3,656,128]{2,1,0:T(8,128)(2,1)S(1)}, u32[]{:S(2)}) copy-start(bf16[3,656,128]{2,1,0:T(8,128)(2,1)S(1)} %collective-permute-done.2.refs_2_) | copy-start | bytes 1511428
  32.0 10.2 %copy-start.8 = (bf16[3,656,128]{2,1,0:T(8,128)(2,1)}, bf16[3,656,128]{2,1,0:T(8,128)(2,1)S(1)}, u32[]{:S(2)}) copy-start(bf16[3,656,128]{2,1,0:T(8,128)(2,1)S(1)} %collective-permute-done.1.refs_1_) | copy-start | bytes 1511428
  37.1 21.8 %copy-start.2 = (bf16[3,656,128]{2,1,0:T(8,128)(2,1)}, bf16[3,656,128]{2,1,0:T(8,128)(2,1)S(1)}, u32[]{:S(2)}) copy-start(bf16[3,656,128]{2,1,0:T(8,128)(2,1)S(1)} %collective-permute-done.given.refs_0_.refs_4_) | copy-start | bytes 1511428
  38.0 4.3 %collective-permute-start.9 = (bf16[2,1,512,512]{3,2,1,0:T(8,128)(2,1)}, bf16[2,1,512,512]{3,2,1,0:T(8,128)(2,1)}, u32[]{:S(2)}, u32[]{:S(2)}) collective-permute-start(bf16[2,1,512,512]{3,2,1,0:T(8,128)(2,1)} %collective-permute-done.4.refs_6_), channel_id=1, source_target_pairs={{0,4},{1,5},{2,6},{3,7},{4,0},{5,1},{6,2},{7,3},{8,12},{9,13},{10,... | collective-permute-start | bytes 3145736 | tf_op jit(solution)/shard_map/ppermute | solution.py:475
  38.7 20.4 %collective-permute-start.7 = (bf16[3,656,128]{2,1,0:T(8,128)(2,1)S(1)}, bf16[3,656,128]{2,1,0:T(8,128)(2,1)}, u32[]{:S(2)}, u32[]{:S(2)}) collective-permute-start(bf16[3,656,128]{2,1,0:T(8,128)(2,1)S(1)} %collective-permute-done.given.refs_0_.refs_4_), channel_id=1, source_target_pairs={{0,3},{1,2},{2,1},{3,0},{4,7},{5,6},{6,5},{7,4},{8,11},{9,10},{10,... | collective-permute-start | bytes 1511432 | tf_op jit(solution)/shard_map/ppermute | solution.py:475
  41.3 23.1 %collective-permute-start.6 = (bf16[3,656,128]{2,1,0:T(8,128)(2,1)S(1)}, bf16[3,656,128]{2,1,0:T(8,128)(2,1)}, u32[]{:S(2)}, u32[]{:S(2)}) collective-permute-start(bf16[3,656,128]{2,1,0:T(8,128)(2,1)S(1)} %collective-permute-done.given.refs_0_.refs_4_), channel_id=1, source_target_pairs={{0,2},{1,3},{2,0},{3,1},{4,6},{5,7},{6,4},{7,5},{8,10},{9,11},{10,... | collective-permute-start | bytes 1511432 | tf_op jit(solution)/shard_map/ppermute | solution.py:475
  41.8 22.8 %collective-permute-start.5 = (bf16[3,656,128]{2,1,0:T(8,128)(2,1)S(1)}, bf16[3,656,128]{2,1,0:T(8,128)(2,1)}, u32[]{:S(2)}, u32[]{:S(2)}) collective-permute-start(bf16[3,656,128]{2,1,0:T(8,128)(2,1)S(1)} %collective-permute-done.given.refs_0_.refs_4_), channel_id=1, source_target_pairs={{0,1},{1,0},{2,3},{3,2},{4,5},{5,4},{6,7},{7,6},{8,9},{9,8},{10,11... | collective-permute-start | bytes 1511432 | tf_op jit(solution)/shard_map/ppermute | solution.py:475
  42.3 22.3 %collective-permute-start.11 = (bf16[3,128,512]{2,1,0:T(8,128)(2,1)S(1)}, bf16[3,128,512]{2,1,0:T(8,128)(2,1)}, u32[]{:S(2)}, u32[]{:S(2)}) collective-permute-start(bf16[3,128,512]{2,1,0:T(8,128)(2,1)S(1)} %shard_map.96.own), channel_id=1, source_target_pairs={{0,24},{1,25},{2,26},{3,27},{4,28},{5,29},{6,30},{7,31},{8,16},{9,... | collective-permute-start | bytes 1179656 | tf_op jit(solution)/shard_map/ppermute | solution.py:475
  46.2 18.5 %collective-permute-start.10 = (bf16[3,128,512]{2,1,0:T(8,128)(2,1)S(1)}, bf16[3,128,512]{2,1,0:T(8,128)(2,1)}, u32[]{:S(2)}, u32[]{:S(2)}) collective-permute-start(bf16[3,128,512]{2,1,0:T(8,128)(2,1)S(1)} %shard_map.96.own), channel_id=1, source_target_pairs={{0,8},{1,9},{2,10},{3,11},{4,12},{5,13},{6,14},{7,15},{8,0},{9,1},... | collective-permute-start | bytes 1179656 | tf_op jit(solution)/shard_map/ppermute | solution.py:475
  52.1 12.6 %copy-start.3 = (bf16[6,128,512]{2,1,0:T(8,128)(2,1)}, bf16[6,128,512]{2,1,0:T(8,128)(2,1)S(1)}, u32[]{:S(2)}) copy-start(bf16[6,128,512]{2,1,0:T(8,128)(2,1)S(1)} %shard_map.97.refs_8_) | copy-start | bytes 2359300
  58.9 14.1 %copy-start.1 = (bf16[3,656,128]{2,1,0:T(8,128)(2,1)S(1)}, bf16[3,656,128]{2,1,0:T(8,128)(2,1)}, u32[]{:S(2)}) copy-start(bf16[3,656,128]{2,1,0:T(8,128)(2,1)} %copy-done) | copy-start | bytes 1511428
  58.9 14.1 %copy-start.5 = (bf16[3,656,128]{2,1,0:T(8,128)(2,1)S(1)}, bf16[3,656,128]{2,1,0:T(8,128)(2,1)}, u32[]{:S(2)}) copy-start(bf16[3,656,128]{2,1,0:T(8,128)(2,1)} %copy-done.4) | copy-start | bytes 1511428
  58.9 14.1 %copy-start.7 = (bf16[3,656,128]{2,1,0:T(8,128)(2,1)S(1)}, bf16[3,656,128]{2,1,0:T(8,128)(2,1)}, u32[]{:S(2)}) copy-start(bf16[3,656,128]{2,1,0:T(8,128)(2,1)} %copy-done.6) | copy-start | bytes 1511428
  58.9 14.1 %copy-start.9 = (bf16[3,656,128]{2,1,0:T(8,128)(2,1)S(1)}, bf16[3,656,128]{2,1,0:T(8,128)(2,1)}, u32[]{:S(2)}) copy-start(bf16[3,656,128]{2,1,0:T(8,128)(2,1)} %copy-done.8) | copy-start | bytes 1511428
  59.0 14.1 %copy-start.10 = (s32[4]{0:T(128)S(1)}, s32[4]{0:T(128)}, u32[]{:S(2)}) copy-start(s32[4]{0:T(128)} %get-tuple-element.38.sizes) | copy-start | bytes 52
  59.0 14.1 %copy-start.11 = (s32[288]{0:T(512)S(1)}, s32[288]{0:T(512)}, u32[]{:S(2)}) copy-start(s32[288]{0:T(512)} %get-tuple-element.40.entries) | copy-start | bytes 3460
  59.0 14.1 %copy-start.12 = (s32[24]{0:T(128)S(1)}, s32[24]{0:T(128)}, u32[]{:S(2)}) copy-start(s32[24]{0:T(128)} %get-tuple-element.37.slot_of) | copy-start | bytes 292
  59.0 14.1 %copy-start.13 = (s32[72]{0:T(128)S(1)}, s32[72]{0:T(128)}, u32[]{:S(2)}) copy-start(s32[72]{0:T(128)} %get-tuple-element.39.group_input) | copy-start | bytes 868
  64.6 8.4 %collective-permute-start.12 = (bf16[6,128,512]{2,1,0:T(8,128)(2,1)S(1)}, bf16[6,128,512]{2,1,0:T(8,128)(2,1)}, u32[]{:S(2)}, u32[]{:S(2)}) collective-permute-start(bf16[6,128,512]{2,1,0:T(8,128)(2,1)S(1)} %shard_map.97.refs_8_), channel_id=1, source_target_pairs={{0,4},{1,5},{2,6},{3,7},{4,0},{5,1},{6,2},{7,3},{8,12},{9,13},{10,... | collective-permute-start | bytes 2359304 | tf_op jit(solution)/shard_map/ppermute | solution.py:475
  64.9 8.1 %collective-permute-start.13 = (bf16[3,128,512]{2,1,0:T(8,128)(2,1)}, bf16[3,128,512]{2,1,0:T(8,128)(2,1)S(1)}, u32[]{:S(2)}, u32[]{:S(2)}) collective-permute-start(bf16[3,128,512]{2,1,0:T(8,128)(2,1)} %collective-permute-done.10.refs_9_), channel_id=1, source_target_pairs={{0,4},{1,5},{2,6},{3,7},{4,0},{5,1},{6,2},{7,3},{8,12},{9,13},{10,... | collective-permute-start | bytes 1179656 | tf_op jit(solution)/shard_map/ppermute | solution.py:475
  65.2 7.8 %collective-permute-start.14 = (bf16[3,128,512]{2,1,0:T(8,128)(2,1)}, bf16[3,128,512]{2,1,0:T(8,128)(2,1)S(1)}, u32[]{:S(2)}, u32[]{:S(2)}) collective-permute-start(bf16[3,128,512]{2,1,0:T(8,128)(2,1)} %collective-permute-done.11.refs_10_), channel_id=1, source_target_pairs={{0,4},{1,5},{2,6},{3,7},{4,0},{5,1},{6,2},{7,3},{8,12},{9,13},{10,... | collective-permute-start | bytes 1179656 | tf_op jit(solution)/shard_map/ppermute | solution.py:475
  82.1 7.6 %copy-start.14 = (f32[384,128]{1,0:T(8,128)S(1)}, f32[384,128]{1,0:T(8,128)}, u32[]{:S(2)}) copy-start(f32[384,128]{1,0:T(8,128)} %param.8) | copy-start | bytes 589828
  82.1 7.6 %copy-start.15 = (f32[384]{0:T(512)S(1)}, f32[384]{0:T(512)}, u32[]{:S(2)}) copy-start(f32[384]{0:T(512)} %param.9) | copy-start | bytes 4612
  82.1 6.2 %collective-permute-start.15 = (bf16[12,128,128]{2,1,0:T(8,128)(2,1)S(1)}, bf16[12,128,128]{2,1,0:T(8,128)(2,1)S(1)}, u32[]{:S(2)}, u32[]{:S(2)}) collective-permute-start(bf16[12,128,128]{2,1,0:T(8,128)(2,1)S(1)} %get-tuple-element.66), channel_id=1, source_target_pairs={{0,4},{1,5},{2,6},{3,7},{4,0},{5,1},{6,2},{7,3},{8,12},{9,13},{10,... | collective-permute-start | bytes 1179656 | tf_op jit(solution)/shard_map/ppermute | solution.py:475
  89.6 7.2 %collective-permute-start.16 = (bf16[2,3,128,128]{3,2,1,0:T(8,128)(2,1)S(1)}, bf16[2,3,128,128]{3,2,1,0:T(8,128)(2,1)S(1)}, u32[]{:S(2)}, u32[]{:S(2)}) collective-permute-start(bf16[2,3,128,128]{3,2,1,0:T(8,128)(2,1)S(1)} %pad_maximum_fusion.1), channel_id=1, source_target_pairs={{0,8},{1,9},{2,10},{3,11},{4,12},{5,13},{6,14},{7,15},{8,0},{9,1},... | collective-permute-start | bytes 589832 | tf_op jit(solution)/shard_map/ppermute | solution.py:475
  96.9 11.5 %collective-permute-start.17 = (bf16[2,3,128,128]{3,2,1,0:T(8,128)(2,1)S(1)}, bf16[2,3,128,128]{3,2,1,0:T(8,128)(2,1)S(1)}, u32[]{:S(2)}, u32[]{:S(2)}) collective-permute-start(bf16[2,3,128,128]{3,2,1,0:T(8,128)(2,1)S(1)} %fusion), channel_id=1, source_target_pairs={{0,16},{1,17},{2,18},{3,19},{4,20},{5,21},{6,22},{7,23},{8,24},{9,... | collective-permute-start | bytes 589832 | tf_op jit(solution)/shard_map/ppermute | solution.py:475
  108.5 8.8 %collective-permute-start.20 = (bf16[2,3,128,128]{3,2,1,0:T(8,128)(2,1)S(1)}, bf16[2,3,128,128]{3,2,1,0:T(8,128)(2,1)S(1)}, u32[]{:S(2)}, u32[]{:S(2)}) collective-permute-start(bf16[2,3,128,128]{3,2,1,0:T(8,128)(2,1)S(1)} %get-tuple-element.72.refs_0_), channel_id=1, source_target_pairs={{0,3},{1,2},{2,1},{3,0},{4,7},{5,6},{6,5},{7,4},{8,11},{9,10},{10,... | collective-permute-start | bytes 589832 | tf_op jit(solution)/shard_map/ppermute | solution.py:475
  108.6 11.1 %collective-permute-start.19 = (bf16[2,3,128,128]{3,2,1,0:T(8,128)(2,1)S(1)}, bf16[2,3,128,128]{3,2,1,0:T(8,128)(2,1)S(1)}, u32[]{:S(2)}, u32[]{:S(2)}) collective-permute-start(bf16[2,3,128,128]{3,2,1,0:T(8,128)(2,1)S(1)} %get-tuple-element.72.refs_0_), channel_id=1, source_target_pairs={{0,2},{1,3},{2,0},{3,1},{4,6},{5,7},{6,4},{7,5},{8,10},{9,11},{10,... | collective-permute-start | bytes 589832 | tf_op jit(solution)/shard_map/ppermute | solution.py:475
  109.5 10.2 %collective-permute-start.18 = (bf16[2,3,128,128]{3,2,1,0:T(8,128)(2,1)S(1)}, bf16[2,3,128,128]{3,2,1,0:T(8,128)(2,1)S(1)}, u32[]{:S(2)}, u32[]{:S(2)}) collective-permute-start(bf16[2,3,128,128]{3,2,1,0:T(8,128)(2,1)S(1)} %get-tuple-element.72.refs_0_), channel_id=1, source_target_pairs={{0,1},{1,0},{2,3},{3,2},{4,5},{5,4},{6,7},{7,6},{8,9},{9,8},{10,11... | collective-permute-start | bytes 589832 | tf_op jit(solution)/shard_map/ppermute | solution.py:475
  123.3 2.9 %collective-permute-start.21 = (bf16[12,128,128]{2,1,0:T(8,128)(2,1)S(1)}, bf16[12,128,128]{2,1,0:T(8,128)(2,1)S(1)}, u32[]{:S(2)}, u32[]{:S(2)}) collective-permute-start(bf16[12,128,128]{2,1,0:T(8,128)(2,1)S(1)} %get-tuple-element.69), channel_id=1, source_target_pairs={{0,4},{1,5},{2,6},{3,7},{4,0},{5,1},{6,2},{7,3},{8,12},{9,13},{10,... | collective-permute-start | bytes 1179656 | tf_op jit(solution)/shard_map/ppermute | solution.py:475
  126.4 6.8 %collective-permute-start.22 = (bf16[3,128,128]{2,1,0:T(8,128)(2,1)S(1)}, bf16[3,128,128]{2,1,0:T(8,128)(2,1)S(1)}, u32[]{:S(2)}, u32[]{:S(2)}) collective-permute-start(bf16[3,128,128]{2,1,0:T(8,128)(2,1)S(1)} %get-tuple-element.78), channel_id=1, source_target_pairs={{0,8},{1,9},{2,10},{3,11},{4,12},{5,13},{6,14},{7,15},{8,0},{9,1},... | collective-permute-start | bytes 294920 | tf_op jit(solution)/shard_map/ppermute | solution.py:475
  126.5 7.6 %collective-permute-start.24 = (bf16[3,128,128]{2,1,0:T(8,128)(2,1)S(1)}, bf16[3,128,128]{2,1,0:T(8,128)(2,1)S(1)}, u32[]{:S(2)}, u32[]{:S(2)}) collective-permute-start(bf16[3,128,128]{2,1,0:T(8,128)(2,1)S(1)} %get-tuple-element.79), channel_id=1, source_target_pairs={{0,24},{1,25},{2,26},{3,27},{4,28},{5,29},{6,30},{7,31},{8,16},{9,... | collective-permute-start | bytes 294920 | tf_op jit(solution)/shard_map/ppermute | solution.py:475
  128.0 11.0 %collective-permute-start.23 = (bf16[3,128,128]{2,1,0:T(8,128)(2,1)S(1)}, bf16[3,128,128]{2,1,0:T(8,128)(2,1)S(1)}, u32[]{:S(2)}, u32[]{:S(2)}) collective-permute-start(bf16[3,128,128]{2,1,0:T(8,128)(2,1)S(1)} %get-tuple-element.80), channel_id=1, source_target_pairs={{0,16},{1,17},{2,18},{3,19},{4,20},{5,21},{6,22},{7,23},{8,24},{9,... | collective-permute-start | bytes 294920 | tf_op jit(solution)/shard_map/ppermute | solution.py:475

commit v13 on v11

--- a/solution.py
+++ b/solution.py
@@ -11,6 +11,7 @@
 spectrum_half = 3.0
 axes = ("row", "col")
 chunk_groups = 8
+batch = 4
 mib = 1 << 20
 
 
@@ -29,7 +30,7 @@
         self.unroll = unroll
         self.vmem = 60 * mib
         self.vmem_sums = (50 if unroll > 1 else 60) * mib
-        most = self.owners * tile_max + self.inputs * (unroll - 1) + unroll
+        most = self.owners * tile_max + self.inputs * (unroll - 1) + (2 * batch + self.owners * (batch - 1)) * unroll
         self.groups = -(-most // (unroll * chunk_groups)) * chunk_groups
 
     def line_steps(self):
@@ -75,7 +76,8 @@
 
         lax.fori_loop(0, listed[owner, lay.tile_max], count, 0)
 
-    group_input[0] = 0
+    for lane in range(batch):
+        group_input[lane] = 0
 
     def place_groups(p, start):
         used = jnp.where(slot_of[p] >= 0, fill[p], 0)
@@ -89,11 +91,14 @@
         lax.fori_loop(start, end, name, 0)
         return end
 
-    total = 1
+    total = batch
     for owner in range(lay.owners):
         if owner > 0:
             sizes[lay.owners + owner] = total
         total = lax.fori_loop(owner * lay.spread, (owner + 1) * lay.spread, place_groups, total)
+        for lane in range(batch - 1):
+            group_input[total + lane] = owner * lay.spread
+        total = lax.div(total + batch - 1, batch) * batch
     sizes[0] = total
 
     def clear(i, carry):
@@ -304,7 +309,7 @@
             def _():
                 load(p).wait()
 
-        def group_step(group, carry):
+        def make_group(group):
             block = projected[group_input[group]]
             numbers = [entries[group * lay.unroll + i] for i in range(lay.unroll)]
             places = [jnp.minimum(lax.div(n, lay.points), lay.outputs - 1) for n in numbers]
@@ -317,12 +322,17 @@
                     at_b = mine[:, b * lay.side : (b + 1) * lay.side]
                     tile = jnp.where(lax.rem(numbers[i], lay.points) == b, at_b, tile)
                 tiles[group * lay.unroll + i] = tile.astype(jnp.bfloat16)
-            add_products(lay, group - 1, group_input, entries, tiles, rounded, total)
+
+        def batch_step(step, carry):
+            for lane in range(batch):
+                add_products(lay, batch * (step - 1) + lane, group_input, entries, tiles, rounded, total)
+            for lane in range(batch):
+                make_group(batch * step + lane)
             return carry
 
-        first = 1 if owner == 0 else sizes[lay.owners + owner]
+        first = 1 if owner == 0 else lax.div(sizes[lay.owners + owner], batch)
         last = used if owner == lay.owners - 1 else sizes[lay.owners + owner + 1]
-        lax.fori_loop(first, last, group_step, 0)
+        lax.fori_loop(first, lax.div(last, batch), batch_step, 0)
 
     span = chunk_groups * lay.unroll
 
@@ -336,7 +346,8 @@
         def _():
             store(chunk).start()
 
-    add_products(lay, used - 1, group_input, entries, tiles, rounded, total)
+    for lane in range(batch):
+        add_products(lay, used - batch + lane, group_input, entries, tiles, rounded, total)
     give_sums(lay, total, own_sum, other_sum)
     for chunk in range(lay.groups // chunk_groups):
 
@@ -411,11 +422,12 @@
         def _():
             load(chunk).wait()
 
-    def group_step(group, carry):
-        add_products(lay, group, group_input, entries, tiles, rounded, total)
+    def batch_step(step, carry):
+        for lane in range(batch):
+            add_products(lay, batch * step + lane, group_input, entries, tiles, rounded, total)
         return carry
 
-    lax.fori_loop(1, used, group_step, 0)
+    lax.fori_loop(1, lax.div(used, batch), batch_step, 0)
     give_sums(lay, total, own_sum, other_sum)
 
 

time: 148 us -> 139 us (0.939); the launches traced: 146 us -> 139 us
  starting transfers between devices: 36.8 us -> 26.7 us
  Pallas kernels: 38.5 us -> 42.3 us
    ppermute x25, starting transfers between devices: 36.8 us -> 26.7 us  [move(): return lax.ppermute(array, axes, pairs_list)]
    pallas_call x1, Pallas kernels: 6.77 us -> 11 us  [make_plan(): pl.pallas_call(functools.partial(plan_kernel, lay), out_shape=tuple((jax....]
  transfers between devices with their start and end apart: 25 -> 25, of which waited for: 16 -> 14; matrix products, arithmetic and copies ran while one was open for 4% -> 4% of each run, Pallas kernels for 15% -> 18%
where the time goes in v13:
time: 139 us
  waiting for transfers between devices  60.3 us (43%)
  Pallas kernels  42.3 us (30%)
  starting transfers between devices  26.7 us (19%)
  other arithmetic  7.23 us (5%)
  between operations  1.75 us (1%)
    ppermute x25, waiting for transfers between devices, move(): return lax.ppermute(array, axes, pairs_list)  60.3 us
    ppermute x25, starting transfers between devices, move(): return lax.ppermute(array, axes, pairs_list)  26.7 us
    pallas_call x2, Pallas kernels, project(): pl.pallas_call(functools.partial(project_kernel, lay, owner), out_shape=j...  13.7 us
    pallas_call x1, Pallas kernels, make_tiles(): pl.pallas_call(functools.partial(tiles_kernel, lay), out_shape=(sums, sen...  12.3 us
    pallas_call x1, Pallas kernels, make_plan(): pl.pallas_call(functools.partial(plan_kernel, lay), out_shape=tuple((jax....  11 us
    pallas_call x1, Pallas kernels, apply_tiles(): pl.pallas_call(functools.partial(apply_kernel, lay), out_shape=(sums, sen...  4.97 us
  transfers between devices with their start and end apart: 25, of which 14 were waited for; matrix products, arithmetic and copies ran while one was open for 4% of the time, Pallas kernels for 18%

profile of v13, /device:TPU:0, one launch (start us, length us, event | category | flops | bytes accessed | tf_op | source)
XLA Modules:
  0.0 139.1 jit_solution(16180997141875880009)
XLA Ops:
  0.6 3.1 %collective-permute-start.4 = (bf16[2,1,512,512]{3,2,1,0:T(8,128)(2,1)}, bf16[2,1,512,512]{3,2,1,0:T(8,128)(2,1)}, u32[]{:S(2)}, u32[]{:S(2)}) collective-permute-start(bf16[2,1,512,512]{3,2,1,0:T(8,128)(2,1)} %refs_4_.1), channel_id=1, source_target_pairs={{0,8},{1,9},{2,10},{3,11},{4,12},{5,13},{6,14},{7,15},{8,0},{9,1},... | collective-permute-start | bytes 3145736 | tf_op jit(solution)/shard_map/ppermute | solution.py:477
  4.4 0.9 convert_element_type.40
  5.3 0.7 convert_bitcast_fusion.1
  6.1 1.0 pad_maximum_fusion.given.refs_0_
  7.2 2.5 %collective-permute-start.3 = (bf16[3,656,128]{2,1,0:T(8,128)(2,1)S(1)}, bf16[3,656,128]{2,1,0:T(8,128)(2,1)S(1)}, u32[]{:S(2)}, u32[]{:S(2)}) collective-permute-start(bf16[3,656,128]{2,1,0:T(8,128)(2,1)S(1)} %pad_maximum_fusion.given.refs_0_), channel_id=1, source_target_pairs={{0,3},{1,2},{2,1},{3,0},{4,7},{5,6},{6,5},{7,4},{8,11},{9,10},{10,... | collective-permute-start | bytes 1511432 | tf_op jit(solution)/shard_map/ppermute | solution.py:477
  9.7 0.5 collective-permute-start.2
  10.2 0.5 collective-permute-start.1
  10.7 2.6 %collective-permute-start = (bf16[3,656,128]{2,1,0:T(8,128)(2,1)S(1)}, bf16[3,656,128]{2,1,0:T(8,128)(2,1)S(1)}, u32[]{:S(2)}, u32[]{:S(2)}) collective-permute-start(bf16[3,656,128]{2,1,0:T(8,128)(2,1)S(1)} %pad_maximum_fusion.given.refs_0_), channel_id=1, source_target_pairs={{0,16},{1,17},{2,18},{3,19},{4,20},{5,21},{6,22},{7,23},{8,24},{9,... | collective-permute-start | bytes 1511432 | tf_op jit(solution)/shard_map/ppermute | solution.py:477
  13.3 9.3 %collective-permute-done.3.refs_3_ = bf16[3,656,128]{2,1,0:T(8,128)(2,1)S(1)} collective-permute-done((bf16[3,656,128]{2,1,0:T(8,128)(2,1)S(1)}, bf16[3,656,128]{2,1,0:T(8,128)(2,1)S(1)}, u32[]{:S(2)}, u32[]{:S(2)}) %collective-permute-start.3) | collective-permute-done | bytes 503840 | tf_op jit(solution)/shard_map/ppermute | solution.py:477
  22.6 9.3 %collective-permute-done.2.refs_2_ = bf16[3,656,128]{2,1,0:T(8,128)(2,1)S(1)} collective-permute-done((bf16[3,656,128]{2,1,0:T(8,128)(2,1)S(1)}, bf16[3,656,128]{2,1,0:T(8,128)(2,1)S(1)}, u32[]{:S(2)}, u32[]{:S(2)}) %collective-permute-start.2) | collective-permute-done | bytes 503840 | tf_op jit(solution)/shard_map/ppermute | solution.py:477
  31.9 0.1 collective-permute-done.1.refs_1_
  32.0 5.2 %collective-permute-done.given.refs_0_.refs_4_ = bf16[3,656,128]{2,1,0:T(8,128)(2,1)S(1)} collective-permute-done((bf16[3,656,128]{2,1,0:T(8,128)(2,1)S(1)}, bf16[3,656,128]{2,1,0:T(8,128)(2,1)S(1)}, u32[]{:S(2)}, u32[]{:S(2)}) %collective-permute-start) | collective-permute-done | bytes 503840 | tf_op jit(solution)/shard_map/ppermute | solution.py:477
  37.1 0.8 collective-permute-done.4.refs_6_
  38.0 0.6 pad_add_fusion.1.ids
  38.6 2.6 %collective-permute-start.7 = (bf16[3,656,128]{2,1,0:T(8,128)(2,1)S(1)}, bf16[3,656,128]{2,1,0:T(8,128)(2,1)}, u32[]{:S(2)}, u32[]{:S(2)}) collective-permute-start(bf16[3,656,128]{2,1,0:T(8,128)(2,1)S(1)} %collective-permute-done.given.refs_0_.refs_4_), channel_id=1, source_target_pairs={{0,3},{1,2},{2,1},{3,0},{4,7},{5,6},{6,5},{7,4},{8,11},{9,10},{10,... | collective-permute-start | bytes 1511432 | tf_op jit(solution)/shard_map/ppermute | solution.py:477
  41.2 0.5 collective-permute-start.6
  41.7 0.4 collective-permute-start.5
  42.1 0.2 shard_map.96.own
  42.3 3.8 %collective-permute-start.11 = (bf16[3,128,512]{2,1,0:T(8,128)(2,1)S(1)}, bf16[3,128,512]{2,1,0:T(8,128)(2,1)}, u32[]{:S(2)}, u32[]{:S(2)}) collective-permute-start(bf16[3,128,512]{2,1,0:T(8,128)(2,1)S(1)} %shard_map.96.own), channel_id=1, source_target_pairs={{0,24},{1,25},{2,26},{3,27},{4,28},{5,29},{6,30},{7,31},{8,16},{9,... | collective-permute-start | bytes 1179656 | tf_op jit(solution)/shard_map/ppermute | solution.py:477
  46.2 1.3 pad_add_fusion.listed
  47.4 11.0 %shard_map.95 = (s32[24]{0:T(128)}, s32[26]{0:T(128)}, s32[4]{0:T(128)}, s32[80]{0:T(128)}, s32[320]{0:T(512)}) custom-call(s32[3]{0:T(128)} %pad_add_fusion.1.ids, s32[2,97]{1,0:T(2,128)} %pad_add_fusion.listed, s32[96]{0:T(128)} %fine.1, s32[8]{0:T(128)} %stored.1), custom_call_target="tpu_custom_call" | custom-call | bytes 20000000 | tf_op jit(solution)/shard_map/pallas_call | solution.py:143
  58.5 0.2 shard_map.97.refs_8_
  58.7 6.8 %shard_map.98.refs_14_ = bf16[12,512,256]{2,1,0:T(8,128)(2,1)} custom-call(s32[24]{0:T(128)} %get-tuple-element.37.slot_of, s32[26]{0:T(128)} %get-tuple-element.48.valid, s32[4]{0:T(128)} %get-tuple-element.38.sizes, bf16[3,656,128]{2,1,0:T(8,128)(2,1)} %copy-done, bf16[3,656,128]{2,1,0:T(8,128)(2,1)} %copy-done.8, bf16[3,656,128]{2,1,0:T(8,128)(2,1)} %copy-done.6, ...), custom_call_target="tpu_custom_call" | custom-call | flops 1000000000 | bytes 16000000 | tf_op jit(solution)/shard_map/pallas_call | solution.py:248
  65.8 0.5 collective-permute-start.13
  66.3 6.8 %shard_map.99.refs_15_ = bf16[12,512,256]{2,1,0:T(8,128)(2,1)} custom-call(s32[24]{0:T(128)} %get-tuple-element.37.slot_of, s32[26]{0:T(128)} %get-tuple-element.48.valid, s32[4]{0:T(128)} %get-tuple-element.38.sizes, bf16[3,656,128]{2,1,0:T(8,128)(2,1)} %copy-done.2, bf16[3,656,128]{2,1,0:T(8,128)(2,1)} %collective-permute-done.5.refs_1_.refs_5_, ...), custom_call_target="tpu_custom_call" | custom-call | flops 1000000000 | bytes 16000000 | tf_op jit(solution)/shard_map/pallas_call | solution.py:248
  73.3 12.3 %shard_map.100 = (f32[12,128,128]{2,1,0:T(8,128)}, bf16[12,128,128]{2,1,0:T(8,128)(2,1)S(1)}, bf16[320,128,128]{2,1,0:T(8,128)(2,1)}) custom-call(s32[24]{0:T(128)S(1)} %copy-done.12, s32[4]{0:T(128)S(1)} %copy-done.10, s32[80]{0:T(128)S(1)} %copy-done.13, s32[320]{0:T(512)S(1)} %copy-done.11, bf16[3,656,128]{2,1,0:T(8,128)(2,1)S(1)} %copy-done.1, ...), custom_call_target="tpu_custom_call" | custom-call | flops 4000000000 | bytes 30000000 | tf_op jit(solution)/shard_map/pallas_call | solution.py:373
  85.7 0.5 collective-permute-start.15
  86.2 1.3 collective-permute-done.15
  87.5 1.3 fusion.13
  88.9 0.1 fusion.6
  89.1 7.0 %collective-permute-done.16 = bf16[2,3,128,128]{3,2,1,0:T(8,128)(2,1)S(1)} collective-permute-done((bf16[2,3,128,128]{3,2,1,0:T(8,128)(2,1)S(1)}, bf16[2,3,128,128]{3,2,1,0:T(8,128)(2,1)S(1)}, u32[]{:S(2)}, u32[]{:S(2)}) %collective-permute-start.16) | collective-permute-done | bytes 196640 | tf_op jit(solution)/shard_map/ppermute | solution.py:477
  96.1 1.8 %collective-permute-start.17 = (bf16[2,3,128,128]{3,2,1,0:T(8,128)(2,1)S(1)}, bf16[2,3,128,128]{3,2,1,0:T(8,128)(2,1)S(1)}, u32[]{:S(2)}, u32[]{:S(2)}) collective-permute-start(bf16[2,3,128,128]{3,2,1,0:T(8,128)(2,1)S(1)} %fusion), channel_id=1, source_target_pairs={{0,16},{1,17},{2,18},{3,19},{4,20},{5,21},{6,22},{7,23},{8,24},{9,... | collective-permute-start | bytes 589832 | tf_op jit(solution)/shard_map/ppermute | solution.py:477
  97.9 9.7 %collective-permute-done.17 = bf16[2,3,128,128]{3,2,1,0:T(8,128)(2,1)S(1)} collective-permute-done((bf16[2,3,128,128]{3,2,1,0:T(8,128)(2,1)S(1)}, bf16[2,3,128,128]{3,2,1,0:T(8,128)(2,1)S(1)}, u32[]{:S(2)}, u32[]{:S(2)}) %collective-permute-start.17) | collective-permute-done | bytes 196640 | tf_op jit(solution)/shard_map/ppermute | solution.py:477
  107.6 0.1 fusion.12
  107.8 1.5 %collective-permute-start.19 = (bf16[2,3,128,128]{3,2,1,0:T(8,128)(2,1)S(1)}, bf16[2,3,128,128]{3,2,1,0:T(8,128)(2,1)S(1)}, u32[]{:S(2)}, u32[]{:S(2)}) collective-permute-start(bf16[2,3,128,128]{3,2,1,0:T(8,128)(2,1)S(1)} %get-tuple-element.72.refs_0_), channel_id=1, source_target_pairs={{0,2},{1,3},{2,0},{3,1},{4,6},{5,7},{6,4},{7,5},{8,10},{9,11},{10,... | collective-permute-start | bytes 589832 | tf_op jit(solution)/shard_map/ppermute | solution.py:477
  109.3 2.0 %collective-permute-start.18 = (bf16[2,3,128,128]{3,2,1,0:T(8,128)(2,1)S(1)}, bf16[2,3,128,128]{3,2,1,0:T(8,128)(2,1)S(1)}, u32[]{:S(2)}, u32[]{:S(2)}) collective-permute-start(bf16[2,3,128,128]{3,2,1,0:T(8,128)(2,1)S(1)} %get-tuple-element.72.refs_0_), channel_id=1, source_target_pairs={{0,1},{1,0},{2,3},{3,2},{4,5},{5,4},{6,7},{7,6},{8,9},{9,8},{10,11... | collective-permute-start | bytes 589832 | tf_op jit(solution)/shard_map/ppermute | solution.py:477
  111.3 5.2 %collective-permute-done.20.refs_3_ = bf16[2,3,128,128]{3,2,1,0:T(8,128)(2,1)S(1)} collective-permute-done((bf16[2,3,128,128]{3,2,1,0:T(8,128)(2,1)S(1)}, bf16[2,3,128,128]{3,2,1,0:T(8,128)(2,1)S(1)}, u32[]{:S(2)}, u32[]{:S(2)}) %collective-permute-start.20) | collective-permute-done | bytes 196640 | tf_op jit(solution)/shard_map/ppermute | solution.py:477
  116.5 2.4 %collective-permute-done.19.refs_2_ = bf16[2,3,128,128]{3,2,1,0:T(8,128)(2,1)S(1)} collective-permute-done((bf16[2,3,128,128]{3,2,1,0:T(8,128)(2,1)S(1)}, bf16[2,3,128,128]{3,2,1,0:T(8,128)(2,1)S(1)}, u32[]{:S(2)}, u32[]{:S(2)}) %collective-permute-start.19) | collective-permute-done | bytes 196640 | tf_op jit(solution)/shard_map/ppermute | solution.py:477
  118.9 5.0 %shard_map.101 = (f32[12,128,128]{2,1,0:T(8,128)S(1)}, bf16[12,128,128]{2,1,0:T(8,128)(2,1)S(1)}) custom-call(s32[4]{0:T(128)S(1)} %copy-done.10, s32[80]{0:T(128)S(1)} %copy-done.13, s32[320]{0:T(512)S(1)} %copy-done.11, bf16[320,128,128]{2,1,0:T(8,128)(2,1)} %get-tuple-element.67.tiles_in, bf16[2,3,128,128]{3,2,1,0:T(8,128)(2,1)S(1)} %get-tuple-element.72.refs_0_, ...), custom_call_target="tpu_custom_call" | custom-call | flops 400000000 | bytes 4000000 | tf_op jit(solution)/shard_map/pallas_call | solution.py:441
  124.0 1.7 %collective-permute-done.21 = bf16[12,128,128]{2,1,0:T(8,128)(2,1)S(1)} collective-permute-done((bf16[12,128,128]{2,1,0:T(8,128)(2,1)S(1)}, bf16[12,128,128]{2,1,0:T(8,128)(2,1)S(1)}, u32[]{:S(2)}, u32[]{:S(2)}) %collective-permute-start.21) | collective-permute-done | bytes 393248 | tf_op jit(solution)/shard_map/ppermute | solution.py:477
  125.7 0.1 fusion.11
  125.9 1.3 collective-permute-start.24
  127.3 2.1 %collective-permute-start.23 = (bf16[3,128,128]{2,1,0:T(8,128)(2,1)S(1)}, bf16[3,128,128]{2,1,0:T(8,128)(2,1)S(1)}, u32[]{:S(2)}, u32[]{:S(2)}) collective-permute-start(bf16[3,128,128]{2,1,0:T(8,128)(2,1)S(1)} %get-tuple-element.80), channel_id=1, source_target_pairs={{0,16},{1,17},{2,18},{3,19},{4,20},{5,21},{6,22},{7,23},{8,24},{9,... | collective-permute-start | bytes 294920 | tf_op jit(solution)/shard_map/ppermute | solution.py:477
  129.4 0.7 slice.79
  130.1 2.1 %collective-permute-done.22 = bf16[3,128,128]{2,1,0:T(8,128)(2,1)S(1)} collective-permute-done((bf16[3,128,128]{2,1,0:T(8,128)(2,1)S(1)}, bf16[3,128,128]{2,1,0:T(8,128)(2,1)S(1)}, u32[]{:S(2)}, u32[]{:S(2)}) %collective-permute-start.22) | collective-permute-done | bytes 98336 | tf_op jit(solution)/shard_map/ppermute | solution.py:477
  132.2 1.4 collective-permute-done.24
  133.5 4.7 %collective-permute-done.23 = bf16[3,128,128]{2,1,0:T(8,128)(2,1)S(1)} collective-permute-done((bf16[3,128,128]{2,1,0:T(8,128)(2,1)S(1)}, bf16[3,128,128]{2,1,0:T(8,128)(2,1)S(1)}, u32[]{:S(2)}, u32[]{:S(2)}) %collective-permute-start.23) | collective-permute-done | bytes 98336 | tf_op jit(solution)/shard_map/ppermute | solution.py:477
  138.2 0.8 fusion.5
  (60 shorter events, 0.8 us)
Async XLA Ops:
  0.6 37.4 %collective-permute-start.4 = (bf16[2,1,512,512]{3,2,1,0:T(8,128)(2,1)}, bf16[2,1,512,512]{3,2,1,0:T(8,128)(2,1)}, u32[]{:S(2)}, u32[]{:S(2)}) collective-permute-start(bf16[2,1,512,512]{3,2,1,0:T(8,128)(2,1)} %refs_4_.1), channel_id=1, source_target_pairs={{0,8},{1,9},{2,10},{3,11},{4,12},{5,13},{6,14},{7,15},{8,0},{9,1},... | collective-permute-start | bytes 3145736 | tf_op jit(solution)/shard_map/ppermute | solution.py:477
  7.2 51.5 %copy-start = (bf16[3,656,128]{2,1,0:T(8,128)(2,1)}, bf16[3,656,128]{2,1,0:T(8,128)(2,1)S(1)}, u32[]{:S(2)}) copy-start(bf16[3,656,128]{2,1,0:T(8,128)(2,1)S(1)} %pad_maximum_fusion.given.refs_0_) | copy-start | bytes 1511428
  7.2 15.4 %collective-permute-start.3 = (bf16[3,656,128]{2,1,0:T(8,128)(2,1)S(1)}, bf16[3,656,128]{2,1,0:T(8,128)(2,1)S(1)}, u32[]{:S(2)}, u32[]{:S(2)}) collective-permute-start(bf16[3,656,128]{2,1,0:T(8,128)(2,1)S(1)} %pad_maximum_fusion.given.refs_0_), channel_id=1, source_target_pairs={{0,3},{1,2},{2,1},{3,0},{4,7},{5,6},{6,5},{7,4},{8,11},{9,10},{10,... | collective-permute-start | bytes 1511432 | tf_op jit(solution)/shard_map/ppermute | solution.py:477
  9.7 22.2 %collective-permute-start.2 = (bf16[3,656,128]{2,1,0:T(8,128)(2,1)S(1)}, bf16[3,656,128]{2,1,0:T(8,128)(2,1)S(1)}, u32[]{:S(2)}, u32[]{:S(2)}) collective-permute-start(bf16[3,656,128]{2,1,0:T(8,128)(2,1)S(1)} %pad_maximum_fusion.given.refs_0_), channel_id=1, source_target_pairs={{0,2},{1,3},{2,0},{3,1},{4,6},{5,7},{6,4},{7,5},{8,10},{9,11},{10,... | collective-permute-start | bytes 1511432 | tf_op jit(solution)/shard_map/ppermute | solution.py:477
  10.2 21.8 %collective-permute-start.1 = (bf16[3,656,128]{2,1,0:T(8,128)(2,1)S(1)}, bf16[3,656,128]{2,1,0:T(8,128)(2,1)S(1)}, u32[]{:S(2)}, u32[]{:S(2)}) collective-permute-start(bf16[3,656,128]{2,1,0:T(8,128)(2,1)S(1)} %pad_maximum_fusion.given.refs_0_), channel_id=1, source_target_pairs={{0,1},{1,0},{2,3},{3,2},{4,5},{5,4},{6,7},{7,6},{8,9},{9,8},{10,11... | collective-permute-start | bytes 1511432 | tf_op jit(solution)/shard_map/ppermute | solution.py:477
  10.7 26.4 %collective-permute-start = (bf16[3,656,128]{2,1,0:T(8,128)(2,1)S(1)}, bf16[3,656,128]{2,1,0:T(8,128)(2,1)S(1)}, u32[]{:S(2)}, u32[]{:S(2)}) collective-permute-start(bf16[3,656,128]{2,1,0:T(8,128)(2,1)S(1)} %pad_maximum_fusion.given.refs_0_), channel_id=1, source_target_pairs={{0,16},{1,17},{2,18},{3,19},{4,20},{5,21},{6,22},{7,23},{8,24},{9,... | collective-permute-start | bytes 1511432 | tf_op jit(solution)/shard_map/ppermute | solution.py:477
  22.6 36.1 %copy-start.4 = (bf16[3,656,128]{2,1,0:T(8,128)(2,1)}, bf16[3,656,128]{2,1,0:T(8,128)(2,1)S(1)}, u32[]{:S(2)}) copy-start(bf16[3,656,128]{2,1,0:T(8,128)(2,1)S(1)} %collective-permute-done.3.refs_3_) | copy-start | bytes 1511428
  22.6 19.6 %collective-permute-start.8 = (bf16[2,1,512,512]{3,2,1,0:T(8,128)(2,1)}, bf16[2,1,512,512]{3,2,1,0:T(8,128)(2,1)}, u32[]{:S(2)}, u32[]{:S(2)}) collective-permute-start(bf16[2,1,512,512]{3,2,1,0:T(8,128)(2,1)} %refs_4_.1), channel_id=1, source_target_pairs={{0,4},{1,5},{2,6},{3,7},{4,0},{5,1},{6,2},{7,3},{8,12},{9,13},{10,... | collective-permute-start | bytes 3145736 | tf_op jit(solution)/shard_map/ppermute | solution.py:477
  31.9 26.8 %copy-start.6 = (bf16[3,656,128]{2,1,0:T(8,128)(2,1)}, bf16[3,656,128]{2,1,0:T(8,128)(2,1)S(1)}, u32[]{:S(2)}) copy-start(bf16[3,656,128]{2,1,0:T(8,128)(2,1)S(1)} %collective-permute-done.2.refs_2_) | copy-start | bytes 1511428
  32.0 10.1 %copy-start.8 = (bf16[3,656,128]{2,1,0:T(8,128)(2,1)}, bf16[3,656,128]{2,1,0:T(8,128)(2,1)S(1)}, u32[]{:S(2)}) copy-start(bf16[3,656,128]{2,1,0:T(8,128)(2,1)S(1)} %collective-permute-done.1.refs_1_) | copy-start | bytes 1511428
  37.1 28.4 %copy-start.2 = (bf16[3,656,128]{2,1,0:T(8,128)(2,1)}, bf16[3,656,128]{2,1,0:T(8,128)(2,1)S(1)}, u32[]{:S(2)}) copy-start(bf16[3,656,128]{2,1,0:T(8,128)(2,1)S(1)} %collective-permute-done.given.refs_0_.refs_4_) | copy-start | bytes 1511428
  38.0 4.3 %collective-permute-start.9 = (bf16[2,1,512,512]{3,2,1,0:T(8,128)(2,1)}, bf16[2,1,512,512]{3,2,1,0:T(8,128)(2,1)}, u32[]{:S(2)}, u32[]{:S(2)}) collective-permute-start(bf16[2,1,512,512]{3,2,1,0:T(8,128)(2,1)} %collective-permute-done.4.refs_6_), channel_id=1, source_target_pairs={{0,4},{1,5},{2,6},{3,7},{4,0},{5,1},{6,2},{7,3},{8,12},{9,13},{10,... | collective-permute-start | bytes 3145736 | tf_op jit(solution)/shard_map/ppermute | solution.py:477
  38.6 27.0 %collective-permute-start.7 = (bf16[3,656,128]{2,1,0:T(8,128)(2,1)S(1)}, bf16[3,656,128]{2,1,0:T(8,128)(2,1)}, u32[]{:S(2)}, u32[]{:S(2)}) collective-permute-start(bf16[3,656,128]{2,1,0:T(8,128)(2,1)S(1)} %collective-permute-done.given.refs_0_.refs_4_), channel_id=1, source_target_pairs={{0,3},{1,2},{2,1},{3,0},{4,7},{5,6},{6,5},{7,4},{8,11},{9,10},{10,... | collective-permute-start | bytes 1511432 | tf_op jit(solution)/shard_map/ppermute | solution.py:477
  41.2 24.4 %collective-permute-start.6 = (bf16[3,656,128]{2,1,0:T(8,128)(2,1)S(1)}, bf16[3,656,128]{2,1,0:T(8,128)(2,1)}, u32[]{:S(2)}, u32[]{:S(2)}) collective-permute-start(bf16[3,656,128]{2,1,0:T(8,128)(2,1)S(1)} %collective-permute-done.given.refs_0_.refs_4_), channel_id=1, source_target_pairs={{0,2},{1,3},{2,0},{3,1},{4,6},{5,7},{6,4},{7,5},{8,10},{9,11},{10,... | collective-permute-start | bytes 1511432 | tf_op jit(solution)/shard_map/ppermute | solution.py:477
  41.7 23.9 %collective-permute-start.5 = (bf16[3,656,128]{2,1,0:T(8,128)(2,1)S(1)}, bf16[3,656,128]{2,1,0:T(8,128)(2,1)}, u32[]{:S(2)}, u32[]{:S(2)}) collective-permute-start(bf16[3,656,128]{2,1,0:T(8,128)(2,1)S(1)} %collective-permute-done.given.refs_0_.refs_4_), channel_id=1, source_target_pairs={{0,1},{1,0},{2,3},{3,2},{4,5},{5,4},{6,7},{7,6},{8,9},{9,8},{10,11... | collective-permute-start | bytes 1511432 | tf_op jit(solution)/shard_map/ppermute | solution.py:477
  42.3 23.4 %collective-permute-start.11 = (bf16[3,128,512]{2,1,0:T(8,128)(2,1)S(1)}, bf16[3,128,512]{2,1,0:T(8,128)(2,1)}, u32[]{:S(2)}, u32[]{:S(2)}) collective-permute-start(bf16[3,128,512]{2,1,0:T(8,128)(2,1)S(1)} %shard_map.96.own), channel_id=1, source_target_pairs={{0,24},{1,25},{2,26},{3,27},{4,28},{5,29},{6,30},{7,31},{8,16},{9,... | collective-permute-start | bytes 1179656 | tf_op jit(solution)/shard_map/ppermute | solution.py:477
  46.1 19.6 %collective-permute-start.10 = (bf16[3,128,512]{2,1,0:T(8,128)(2,1)S(1)}, bf16[3,128,512]{2,1,0:T(8,128)(2,1)}, u32[]{:S(2)}, u32[]{:S(2)}) collective-permute-start(bf16[3,128,512]{2,1,0:T(8,128)(2,1)S(1)} %shard_map.96.own), channel_id=1, source_target_pairs={{0,8},{1,9},{2,10},{3,11},{4,12},{5,13},{6,14},{7,15},{8,0},{9,1},... | collective-permute-start | bytes 1179656 | tf_op jit(solution)/shard_map/ppermute | solution.py:477
  58.6 7.0 %copy-start.3 = (bf16[6,128,512]{2,1,0:T(8,128)(2,1)}, bf16[6,128,512]{2,1,0:T(8,128)(2,1)S(1)}, u32[]{:S(2)}) copy-start(bf16[6,128,512]{2,1,0:T(8,128)(2,1)S(1)} %shard_map.97.refs_8_) | copy-start | bytes 2359300
  65.5 7.7 %copy-start.1 = (bf16[3,656,128]{2,1,0:T(8,128)(2,1)S(1)}, bf16[3,656,128]{2,1,0:T(8,128)(2,1)}, u32[]{:S(2)}) copy-start(bf16[3,656,128]{2,1,0:T(8,128)(2,1)} %copy-done) | copy-start | bytes 1511428
  65.5 7.7 %copy-start.5 = (bf16[3,656,128]{2,1,0:T(8,128)(2,1)S(1)}, bf16[3,656,128]{2,1,0:T(8,128)(2,1)}, u32[]{:S(2)}) copy-start(bf16[3,656,128]{2,1,0:T(8,128)(2,1)} %copy-done.4) | copy-start | bytes 1511428
  65.5 7.7 %copy-start.7 = (bf16[3,656,128]{2,1,0:T(8,128)(2,1)S(1)}, bf16[3,656,128]{2,1,0:T(8,128)(2,1)}, u32[]{:S(2)}) copy-start(bf16[3,656,128]{2,1,0:T(8,128)(2,1)} %copy-done.6) | copy-start | bytes 1511428
  65.6 7.7 %copy-start.9 = (bf16[3,656,128]{2,1,0:T(8,128)(2,1)S(1)}, bf16[3,656,128]{2,1,0:T(8,128)(2,1)}, u32[]{:S(2)}) copy-start(bf16[3,656,128]{2,1,0:T(8,128)(2,1)} %copy-done.8) | copy-start | bytes 1511428
  65.6 7.7 %copy-start.10 = (s32[4]{0:T(128)S(1)}, s32[4]{0:T(128)}, u32[]{:S(2)}) copy-start(s32[4]{0:T(128)} %get-tuple-element.38.sizes) | copy-start | bytes 52
  65.6 7.7 %copy-start.11 = (s32[320]{0:T(512)S(1)}, s32[320]{0:T(512)}, u32[]{:S(2)}) copy-start(s32[320]{0:T(512)} %get-tuple-element.40.entries) | copy-start | bytes 3844
  65.6 7.7 %copy-start.12 = (s32[24]{0:T(128)S(1)}, s32[24]{0:T(128)}, u32[]{:S(2)}) copy-start(s32[24]{0:T(128)} %get-tuple-element.37.slot_of) | copy-start | bytes 292
  65.6 7.7 %copy-start.13 = (s32[80]{0:T(128)S(1)}, s32[80]{0:T(128)}, u32[]{:S(2)}) copy-start(s32[80]{0:T(128)} %get-tuple-element.39.group_input) | copy-start | bytes 964
  65.7 7.5 %collective-permute-start.12 = (bf16[6,128,512]{2,1,0:T(8,128)(2,1)S(1)}, bf16[6,128,512]{2,1,0:T(8,128)(2,1)}, u32[]{:S(2)}, u32[]{:S(2)}) collective-permute-start(bf16[6,128,512]{2,1,0:T(8,128)(2,1)S(1)} %shard_map.97.refs_8_), channel_id=1, source_target_pairs={{0,4},{1,5},{2,6},{3,7},{4,0},{5,1},{6,2},{7,3},{8,12},{9,13},{10,... | collective-permute-start | bytes 2359304 | tf_op jit(solution)/shard_map/ppermute | solution.py:477
  65.8 7.4 %collective-permute-start.13 = (bf16[3,128,512]{2,1,0:T(8,128)(2,1)}, bf16[3,128,512]{2,1,0:T(8,128)(2,1)S(1)}, u32[]{:S(2)}, u32[]{:S(2)}) collective-permute-start(bf16[3,128,512]{2,1,0:T(8,128)(2,1)} %collective-permute-done.10.refs_9_), channel_id=1, source_target_pairs={{0,4},{1,5},{2,6},{3,7},{4,0},{5,1},{6,2},{7,3},{8,12},{9,13},{10,... | collective-permute-start | bytes 1179656 | tf_op jit(solution)/shard_map/ppermute | solution.py:477
  66.3 6.9 %collective-permute-start.14 = (bf16[3,128,512]{2,1,0:T(8,128)(2,1)}, bf16[3,128,512]{2,1,0:T(8,128)(2,1)S(1)}, u32[]{:S(2)}, u32[]{:S(2)}) collective-permute-start(bf16[3,128,512]{2,1,0:T(8,128)(2,1)} %collective-permute-done.11.refs_10_), channel_id=1, source_target_pairs={{0,4},{1,5},{2,6},{3,7},{4,0},{5,1},{6,2},{7,3},{8,12},{9,13},{10,... | collective-permute-start | bytes 1179656 | tf_op jit(solution)/shard_map/ppermute | solution.py:477
  85.6 3.3 %copy-start.14 = (f32[384,128]{1,0:T(8,128)S(1)}, f32[384,128]{1,0:T(8,128)}, u32[]{:S(2)}) copy-start(f32[384,128]{1,0:T(8,128)} %param.8) | copy-start | bytes 589828
  85.6 3.3 %copy-start.15 = (f32[384]{0:T(512)S(1)}, f32[384]{0:T(512)}, u32[]{:S(2)}) copy-start(f32[384]{0:T(512)} %param.9) | copy-start | bytes 4612
  85.7 1.8 %collective-permute-start.15 = (bf16[12,128,128]{2,1,0:T(8,128)(2,1)S(1)}, bf16[12,128,128]{2,1,0:T(8,128)(2,1)S(1)}, u32[]{:S(2)}, u32[]{:S(2)}) collective-permute-start(bf16[12,128,128]{2,1,0:T(8,128)(2,1)S(1)} %get-tuple-element.66), channel_id=1, source_target_pairs={{0,4},{1,5},{2,6},{3,7},{4,0},{5,1},{6,2},{7,3},{8,12},{9,13},{10,... | collective-permute-start | bytes 1179656 | tf_op jit(solution)/shard_map/ppermute | solution.py:477
  88.8 7.2 %collective-permute-start.16 = (bf16[2,3,128,128]{3,2,1,0:T(8,128)(2,1)S(1)}, bf16[2,3,128,128]{3,2,1,0:T(8,128)(2,1)S(1)}, u32[]{:S(2)}, u32[]{:S(2)}) collective-permute-start(bf16[2,3,128,128]{3,2,1,0:T(8,128)(2,1)S(1)} %pad_maximum_fusion.1), channel_id=1, source_target_pairs={{0,8},{1,9},{2,10},{3,11},{4,12},{5,13},{6,14},{7,15},{8,0},{9,1},... | collective-permute-start | bytes 589832 | tf_op jit(solution)/shard_map/ppermute | solution.py:477
  96.1 11.5 %collective-permute-start.17 = (bf16[2,3,128,128]{3,2,1,0:T(8,128)(2,1)S(1)}, bf16[2,3,128,128]{3,2,1,0:T(8,128)(2,1)S(1)}, u32[]{:S(2)}, u32[]{:S(2)}) collective-permute-start(bf16[2,3,128,128]{3,2,1,0:T(8,128)(2,1)S(1)} %fusion), channel_id=1, source_target_pairs={{0,16},{1,17},{2,18},{3,19},{4,20},{5,21},{6,22},{7,23},{8,24},{9,... | collective-permute-start | bytes 589832 | tf_op jit(solution)/shard_map/ppermute | solution.py:477
  107.7 8.8 %collective-permute-start.20 = (bf16[2,3,128,128]{3,2,1,0:T(8,128)(2,1)S(1)}, bf16[2,3,128,128]{3,2,1,0:T(8,128)(2,1)S(1)}, u32[]{:S(2)}, u32[]{:S(2)}) collective-permute-start(bf16[2,3,128,128]{3,2,1,0:T(8,128)(2,1)S(1)} %get-tuple-element.72.refs_0_), channel_id=1, source_target_pairs={{0,3},{1,2},{2,1},{3,0},{4,7},{5,6},{6,5},{7,4},{8,11},{9,10},{10,... | collective-permute-start | bytes 589832 | tf_op jit(solution)/shard_map/ppermute | solution.py:477
  107.8 11.1 %collective-permute-start.19 = (bf16[2,3,128,128]{3,2,1,0:T(8,128)(2,1)S(1)}, bf16[2,3,128,128]{3,2,1,0:T(8,128)(2,1)S(1)}, u32[]{:S(2)}, u32[]{:S(2)}) collective-permute-start(bf16[2,3,128,128]{3,2,1,0:T(8,128)(2,1)S(1)} %get-tuple-element.72.refs_0_), channel_id=1, source_target_pairs={{0,2},{1,3},{2,0},{3,1},{4,6},{5,7},{6,4},{7,5},{8,10},{9,11},{10,... | collective-permute-start | bytes 589832 | tf_op jit(solution)/shard_map/ppermute | solution.py:477
  109.3 9.6 %collective-permute-start.18 = (bf16[2,3,128,128]{3,2,1,0:T(8,128)(2,1)S(1)}, bf16[2,3,128,128]{3,2,1,0:T(8,128)(2,1)S(1)}, u32[]{:S(2)}, u32[]{:S(2)}) collective-permute-start(bf16[2,3,128,128]{3,2,1,0:T(8,128)(2,1)S(1)} %get-tuple-element.72.refs_0_), channel_id=1, source_target_pairs={{0,1},{1,0},{2,3},{3,2},{4,5},{5,4},{6,7},{7,6},{8,9},{9,8},{10,11... | collective-permute-start | bytes 589832 | tf_op jit(solution)/shard_map/ppermute | solution.py:477
  123.9 1.8 %collective-permute-start.21 = (bf16[12,128,128]{2,1,0:T(8,128)(2,1)S(1)}, bf16[12,128,128]{2,1,0:T(8,128)(2,1)S(1)}, u32[]{:S(2)}, u32[]{:S(2)}) collective-permute-start(bf16[12,128,128]{2,1,0:T(8,128)(2,1)S(1)} %get-tuple-element.69), channel_id=1, source_target_pairs={{0,4},{1,5},{2,6},{3,7},{4,0},{5,1},{6,2},{7,3},{8,12},{9,13},{10,... | collective-permute-start | bytes 1179656 | tf_op jit(solution)/shard_map/ppermute | solution.py:477
  125.8 6.3 %collective-permute-start.22 = (bf16[3,128,128]{2,1,0:T(8,128)(2,1)S(1)}, bf16[3,128,128]{2,1,0:T(8,128)(2,1)S(1)}, u32[]{:S(2)}, u32[]{:S(2)}) collective-permute-start(bf16[3,128,128]{2,1,0:T(8,128)(2,1)S(1)} %get-tuple-element.78), channel_id=1, source_target_pairs={{0,8},{1,9},{2,10},{3,11},{4,12},{5,13},{6,14},{7,15},{8,0},{9,1},... | collective-permute-start | bytes 294920 | tf_op jit(solution)/shard_map/ppermute | solution.py:477
  125.9 7.6 %collective-permute-start.24 = (bf16[3,128,128]{2,1,0:T(8,128)(2,1)S(1)}, bf16[3,128,128]{2,1,0:T(8,128)(2,1)S(1)}, u32[]{:S(2)}, u32[]{:S(2)}) collective-permute-start(bf16[3,128,128]{2,1,0:T(8,128)(2,1)S(1)} %get-tuple-element.79), channel_id=1, source_target_pairs={{0,24},{1,25},{2,26},{3,27},{4,28},{5,29},{6,30},{7,31},{8,16},{9,... | collective-permute-start | bytes 294920 | tf_op jit(solution)/shard_map/ppermute | solution.py:477
  127.3 11.0 %collective-permute-start.23 = (bf16[3,128,128]{2,1,0:T(8,128)(2,1)S(1)}, bf16[3,128,128]{2,1,0:T(8,128)(2,1)S(1)}, u32[]{:S(2)}, u32[]{:S(2)}) collective-permute-start(bf16[3,128,128]{2,1,0:T(8,128)(2,1)S(1)} %get-tuple-element.80), channel_id=1, source_target_pairs={{0,16},{1,17},{2,18},{3,19},{4,20},{5,21},{6,22},{7,23},{8,24},{9,... | collective-permute-start | bytes 294920 | tf_op jit(solution)/shard_map/ppermute | solution.py:477
